TPU v7x, 32 devices: a whole 2x2x4 slice. The times are simulated.
32 devices in a mesh: gx: 4 (over z), gy: 4 (over x, core), gz: 2 (over y).
Axes of the slice: x: 2, y: 2, z: 4, core: 2. Of those that a mesh axis runs over, the one named last changes fastest.
Arguments:
- positions: float32 [4, 4, 2, 3, 256], P('gx', 'gy', 'gz'), may hold values from 0 to 1
- species: int32 [4, 4, 2, 256], P('gx', 'gy', 'gz'), may hold values from 0 to 1
- start_block: float32 [4, 4, 2, 4, 3, 256], P('gx', 'gy', 'gz'), may hold values from -560 to 560
- neighbors: int32 [4, 4, 2, 6, 256], P('gx', 'gy', 'gz'), may hold values from 0 to 1151, as said below
- ghost_lists: int32 [8, 8, 4, 16], P('gx', 'gy', 'gz'), may hold values from 0 to 255
- embedding: float32 [2, 64], replicated, may hold values from 0.5 to 1.5
- radial_in: float32 [8, 128], replicated, may hold values from -2 to 2
- radial_out: float32 [128, 64], replicated, may hold values from -0.5 to 0.5
- readout: float32 [64], replicated, may hold values from -0.75 to 0.75
Outputs:
- next_block: float32 [4, 4, 2, 4, 3, 256], P('gx', 'gy', 'gz')
- diagonal_blocks: float32 [2, 4, 4], replicated
- offdiagonal_blocks: float32 [2, 4, 4], replicated
Inputs may be any that keep to these rules, and one draw needn't show every extreme that they name: `neighbors`: about two thirds of the slots name the device's own atoms, the rest ghost entries.
All inputs are finite; a program needn't handle non-finite values.
Results may differ from a plain program's by a relative error of at most 0.0003.
Values sent between devices are 32-bit elements; how exact they have to be, the bound alone decides.
No kernel may reach another device: no remote copies, remote signals or barrier semaphores. Data moves between devices by JAX's collectives and lax.ppermute only.
A program may use at most 192 MiB of HBM per device.

v0:
```python
import jax
import jax.numpy as jnp
import numpy as np
from jax import lax
from jax.sharding import PartitionSpec as P

PRODUCTS = 2


SOFTEN = 0.25
CUTOFF = 4.0
HIGHEST = lax.Precision.HIGHEST


def with_halo(x, sides, width):
    for axis, dim in sides:
        size, length = (lax.axis_size(axis), x.shape[dim])
        up = [(i, (i + 1) % size) for i in range(size)]
        down = [(j, i) for i, j in up]
        last = lax.slice_in_dim(x, length - width, length, axis=dim)
        first = lax.slice_in_dim(x, 0, width, axis=dim)
        before = lax.ppermute(last, axis, up)
        after = lax.ppermute(first, axis, down)
        x = jnp.concatenate([before, x, after], axis=dim)
    return x


def from_behind(value, axis, steps):
    count = lax.axis_size(axis)
    pairs = [(source, (source + steps) % count) for source in range(count)]
    return lax.ppermute(value, axis, pairs)


def ghost_layout():
    chosen = []
    moves = []
    octants = []
    for number in range(64):
        coords = (number // 16, number // 4 % 4, number % 4)
        if all((member in (1, 2) for member in coords)):
            continue
        chosen.append(number)
        moves.append([int(member == 3) - int(member == 0) for member in coords])
        octants.append([(member + 1) % 2 for member in coords])
    return (np.array(chosen), np.array(moves), np.array(octants))


def block_energy(atom_table, embed_table, centers, neighbor, radial_in, radial_out, readout):
    fanout = neighbor.shape[0]
    width_block = neighbor.shape[1]
    flat_neighbor = neighbor.reshape(-1)
    center_coords = jnp.take(atom_table, centers, axis=1)
    neighbor_coords = jnp.take(atom_table, flat_neighbor, axis=1).reshape(3, fanout, width_block)
    displace = neighbor_coords - center_coords[:, None, :]
    distance = jnp.sqrt(jnp.sum(displace * displace, axis=0) + SOFTEN)
    direction = displace / distance[None]
    envelope = (1.0 - (distance / CUTOFF) ** 2) ** 2
    orders = jnp.arange(1, radial_in.shape[0] + 1).astype(jnp.float32)
    flat_distance = distance.reshape(-1)
    bessel = (
        jnp.sin(orders[:, None] * (jnp.pi / CUTOFF) * flat_distance[None, :])
        / flat_distance[None, :]
    )
    hidden = jax.nn.silu(jnp.dot(radial_in.T, bessel, precision=HIGHEST))
    radial = jnp.dot(radial_out.T, hidden, precision=HIGHEST).reshape(-1, fanout, width_block)
    pairing = jnp.take(embed_table, centers, axis=1)[:, None, :] * jnp.take(
        embed_table, flat_neighbor, axis=1
    ).reshape(-1, fanout, width_block)
    feature = radial * envelope[None] * pairing
    harmonic = jnp.concatenate([jnp.ones((1, fanout, width_block), jnp.float32), direction], axis=0)
    environ = jnp.einsum("ckb,mkb->cmb", feature, harmonic, precision=HIGHEST) / fanout
    project = jnp.einsum("cmb,mkb->ckb", environ, harmonic, precision=HIGHEST)
    mixed_feature = feature * project
    return jnp.sum(readout[:, None, None] * jax.nn.silu(mixed_feature))


def table_hessian(
    atom_table, embed_table, centers, neighbor, tangents, radial_in, radial_out, readout
):

    def energy(coords):
        return block_energy(coords, embed_table, centers, neighbor, radial_in, radial_out, readout)

    forces = jax.grad(energy)

    def apply_one(tangent):
        return jax.jvp(forces, (atom_table,), (tangent,))[1]

    return jax.vmap(apply_one)(tangents)


def on_device(
    positions,
    species,
    start_block,
    neighbors,
    ghost_lists,
    embedding,
    radial_in,
    radial_out,
    readout,
):
    chosen, moves, octants = ghost_layout()
    atoms_dev = positions.shape[-1]
    ghosts = ghost_lists.shape[-1]
    vectors = start_block.shape[3]
    devices = lax.axis_size("gx") * lax.axis_size("gy") * lax.axis_size("gz")
    scale_ip = 1.0 / (3.0 * atoms_dev * devices)
    octant_picks = ghost_lists.reshape(-1)
    own_coords = positions[0, 0, 0]
    own_species = species[0, 0, 0].astype(jnp.float32)
    packed = jnp.concatenate([own_coords, own_species[None]], axis=0)
    octant_atoms = jnp.take(packed, octant_picks, axis=1).reshape(4, 2, 2, 2, ghosts)
    beside_all = with_halo(octant_atoms, (("gx", 1), ("gy", 2), ("gz", 3)), 1)
    ghost_atoms = jnp.take(beside_all.reshape(4, 64, ghosts), chosen, axis=1)
    offsets = jnp.asarray(moves.T, jnp.float32)
    ghost_coords = ghost_atoms[:3] + offsets[:, :, None]
    atom_table = jnp.concatenate([own_coords, ghost_coords.reshape(3, -1)], axis=1)
    species_table = jnp.concatenate([own_species, ghost_atoms[3].reshape(-1)])
    kinds = jnp.arange(embedding.shape[0]).astype(jnp.float32)
    onehot = (species_table[None, :] == kinds[:, None]).astype(jnp.float32)
    embed_table = jnp.dot(embedding.T, onehot, precision=HIGHEST)
    table_width = atom_table.shape[1]
    neighbor_all = neighbors[0, 0, 0]
    block_size = min(256, atoms_dev)
    block_count = atoms_dev // block_size
    rows_tan = 3 * vectors

    def mean_gram(left_rows, right_rows):
        return jnp.dot(left_rows, right_rows.T, precision=HIGHEST) * scale_ip

    initial = start_block[0, 0, 0].reshape(vectors, 3 * atoms_dev)
    factor = jnp.linalg.cholesky(lax.psum(mean_gram(initial, initial), ("gx", "gy", "gz")))
    current = jax.scipy.linalg.solve_triangular(factor, initial, lower=True)
    previous = jnp.zeros_like(current)
    diagonals = []
    couplings = []
    for step_number in range(PRODUCTS):
        flat_block = current.reshape(rows_tan, atoms_dev)
        octant_tangent = jnp.take(flat_block, octant_picks, axis=1).reshape(
            rows_tan, 2, 2, 2, ghosts
        )
        around_tangent = with_halo(octant_tangent, (("gx", 1), ("gy", 2), ("gz", 3)), 1)
        ghost_tangent = jnp.take(
            around_tangent.reshape(rows_tan, 64, ghosts), chosen, axis=1
        ).reshape(rows_tan, -1)
        tangents = jnp.concatenate([flat_block, ghost_tangent], axis=1).reshape(
            vectors, 3, table_width
        )

        def add_block(running, block_number):
            centers = block_number * block_size + jnp.arange(block_size, dtype=jnp.int32)
            return (
                running
                + table_hessian(
                    atom_table,
                    embed_table,
                    centers,
                    neighbor_all,
                    tangents,
                    radial_in,
                    radial_out,
                    readout,
                ),
                None,
            )

        summed = lax.scan(
            add_block,
            jnp.zeros((vectors, 3, table_width), jnp.float32),
            jnp.arange(block_count, dtype=jnp.int32),
        )[0]
        summed = summed.reshape(rows_tan, table_width)
        local_portion = summed[:, :atoms_dev]
        ghost_part = summed[:, atoms_dev:].reshape(rows_tan, chosen.shape[0], ghosts)
        cells_full = jnp.zeros((rows_tan, 64, ghosts), jnp.float32).at[:, chosen].set(ghost_part)
        cells_full = cells_full.reshape(rows_tan, 4, 4, 4, ghosts)
        from_below = from_behind(cells_full[:, 3], "gx", 1)
        from_above = from_behind(cells_full[:, 0], "gx", -1)
        section_one = cells_full[:, 1:3] + jnp.stack([from_below, from_above], axis=1)
        from_below = from_behind(section_one[:, :, 3], "gy", 1)
        from_above = from_behind(section_one[:, :, 0], "gy", -1)
        section_two = section_one[:, :, 1:3] + jnp.stack([from_below, from_above], axis=2)
        from_below = from_behind(section_two[:, :, :, 3], "gz", 1)
        from_above = from_behind(section_two[:, :, :, 0], "gz", -1)
        octant_partial_sums = section_two[:, :, :, 1:3] + jnp.stack(
            [from_below, from_above], axis=3
        )
        flat_sums = octant_partial_sums.reshape(rows_tan, -1)
        local_portion = local_portion.at[:, octant_picks].add(flat_sums)
        product_block = local_portion.reshape(vectors, 3 * atoms_dev)
        proj_current, proj_previous, gram_raw = lax.psum(
            (
                mean_gram(current, product_block),
                mean_gram(previous, product_block),
                mean_gram(product_block, product_block),
            ),
            ("gx", "gy", "gz"),
        )
        residue = (
            product_block
            - jnp.dot(proj_current.T, current, precision=HIGHEST)
            - jnp.dot(proj_previous.T, previous, precision=HIGHEST)
        )
        gram_matrix = (
            gram_raw
            - jnp.dot(proj_current.T, proj_current, precision=HIGHEST)
            - jnp.dot(proj_previous.T, proj_previous, precision=HIGHEST)
        )
        factor = jnp.linalg.cholesky(gram_matrix)
        previous, current = (
            current,
            jax.scipy.linalg.solve_triangular(factor, residue, lower=True),
        )
        diagonals.append(proj_current)
        couplings.append(factor.T)
    return (
        current.reshape(1, 1, 1, vectors, 3, atoms_dev),
        jnp.stack(diagonals),
        jnp.stack(couplings),
    )


def solution(mesh):
    return jax.shard_map(
        on_device,
        mesh=mesh,
        in_specs=(
            P("gx", "gy", "gz", None, None),
            P("gx", "gy", "gz", None),
            P("gx", "gy", "gz", None, None, None),
            P("gx", "gy", "gz", None, None),
            P("gx", "gy", "gz", None),
            P(),
            P(),
            P(),
            P(),
        ),
        out_specs=(P("gx", "gy", "gz", None, None, None), P(), P()),
        check_vma=False,
    )
```

profile of v0, /device:TPU:0, one launch (start us, length us, event | category | flops | bytes accessed | tf_op | source)
XLA Modules:
  0.0 1219.4 jit_solution(15173416916520515061)
XLA Ops:
  12.0 38.9 %psum.49 = f32[4,4]{0,1:T(4,128)S(1)} all-reduce(f32[4,4]{0,1:T(4,128)S(1)} %fusion.108), channel_id=1, replica_groups=mesh['gx'=4,'gy'=4,'gz'=2] {'gx','gy','gz'}, use_global_device_ids=true, to_apply=%region_0.1 | all-reduce | flops 16 | bytes 128 | tf_op jit(solution)/shard_map/psum | solution.py:133
  161.1 6.7 gather_fusion.5
  188.0 9.9 fusion.106
  197.9 6.3 fusion.104
  225.3 5.8 copy.866
  232.9 7.4 fusion.65
  245.3 8.6 multiply_add_fusion.3
  254.0 56.5 %fusion.10 = f32[256,4,6,4]{2,3,1,0:T(4,128)} fusion(f32[4,64,6,256]{1,2,0,3:T(8,128)S(1)} %get-tuple-element.272, f32[256,4,64]{2,1,0:T(4,128)S(1)} %convolution_multiply_fusion.1), kind=kOutput, calls=%fused_computation.37 | convolution fusion | flops 18874368 | bytes 1933312 | tf_op jit(solution)/shard_map/while/body/eval_jaxpr/vmap(jvp(transpose(jvp(cmb,mkb->ckb))))/dot_general | solution.py:72
  320.1 5.7 fusion.115
  325.8 56.8 %fusion.141 = f32[256,4,4,6]{3,1,2,0:T(4,128)} fusion(f32[256,4,64]{2,1,0:T(4,128)S(1)} %copy-done.50, f32[4,64,6,256]{1,2,0,3:T(8,128)S(1)} %copy-done.10, f32[64,6,256]{0,1,2:T(8,128)S(1)} %copy-done.19, f32[4,6,256]{1,0,2:T(4,128)S(1)} %copy-done.48, f32[64,6,256]{0,1,2:T(8,128)S(1)} %copy-done.7, f32[6,256]{0,1:T(8,128)S(1)} %copy-done.46), kind=kOutput, calls=%fused_computation.220 | convolution fusion | flops 20447232 | bytes 2750464 | tf_op jit(solution)/shard_map/while/body/eval_jaxpr/vmap(jvp(transpose(jvp(ckb,mkb->cmb))))/dot_general | solution.py:71
  382.6 15.5 %add_reduce_fusion.1 = (f32[4,6,256]{1,0,2:T(4,128)}, f32[4,64,6,256]{1,2,0,3:T(8,128)}) fusion(f32[4,64,6,256]{1,2,0,3:T(8,128)S(1)} %copy-done.10, f32[64,6,256]{0,1,2:T(8,128)S(1)} %copy-done.171, f32[64,6,256]{0,1,2:T(8,128)S(1)} %copy-done.7, f32[4,6,256]{1,0,2:T(4,128)S(1)} %copy-done.48, f32[6,256]{0,1:T(8,128)S(1)} %copy-done.46, ...), kind=kOutput, calls=%fused_computation.48 | convolution fusion | flops 31057920 | bytes 10615040 | tf_op jit(solution)/shard_map/while/body/eval_jaxpr/vmap(jvp(transpose(jvp(ckb,mkb->cmb))))/dot_general | solution.py:71
  405.7 7.6 convolution_bitcast_fusion.1
  426.3 9.0 fusion.168
  442.5 155.1 %scatter_fusion = f32[4,3,1152]{1,0,2:T(4,128)} fusion(f32[4,3,1152]{1,0,2:T(4,128)} %broadcast.878.clone.1, s32[1536]{0:T(1024)S(1)} %copy-done.113, f32[1536,4,3]{2,1,0:T(4,128)} %copy.905), kind=kCustom, calls=%fused_computation.16 | custom fusion | flops 18432 | bytes 227328 | tf_op jit(solution)/shard_map/while/body/eval_jaxpr/vmap(jvp(transpose(jvp(jit(_take)))))/scatter-add | solution.py:53
  599.2 26.4 %scatter_fusion.1 = f32[4,3,1152]{1,0,2:T(4,128)} fusion(f32[4,3,1152]{1,0,2:T(4,128)} %broadcast.878.clone.2, s32[256]{0:T(256)S(1)} %iota.87, f32[256,4,3]{2,1,0:T(4,128)} %copy.906), kind=kCustom, calls=%fused_computation.17 | custom fusion | flops 3072 | bytes 37888 | tf_op jit(solution)/shard_map/while/body/eval_jaxpr/vmap(jvp(transpose(jvp(jit(_take)))))/scatter-add | solution.py:52
  636.5 7.8 scatter_fusion.2
  669.0 38.9 %all-reduce.5 = (f32[4,4]{0,1:T(4,128)S(1)}, f32[4,4]{0,1:T(4,128)S(1)}, f32[4,4]{0,1:T(4,128)S(1)}) all-reduce(f32[4,4]{0,1:T(4,128)S(1)} %convolution_multiply_fusion.6, f32[4,4]{0,1:T(4,128)S(1)} %convolution_multiply_fusion.5, f32[4,4]{0,1:T(4,128)S(1)} %convolution_multiply_fusion.7), channel_id=1, replica_groups=mesh['gx'=4,'gy'=4,'gz'=2] {'gx','gy','gz'}, use_global_device_ids=true, to_apply=%region_19.32 | all-reduce | flops 48 | bytes 384 | tf_op jit(solution)/shard_map/psum | solution.py:192
  749.3 6.7 gather_fusion.12
  775.1 9.9 fusion.99
  785.0 5.9 fusion.97
  812.4 5.8 copy.939
  819.3 7.4 fusion.63
  831.7 8.6 multiply_add_fusion.1
  840.4 56.5 %fusion.4 = f32[256,4,6,4]{2,3,1,0:T(4,128)} fusion(f32[4,64,6,256]{1,2,0,3:T(8,128)S(1)} %get-tuple-element.274, f32[256,4,64]{2,1,0:T(4,128)S(1)} %convolution_multiply_fusion.1), kind=kOutput, calls=%fused_computation.29 | convolution fusion | flops 18874368 | bytes 1933312 | tf_op jit(solution)/shard_map/while/body/eval_jaxpr/vmap(jvp(transpose(jvp(cmb,mkb->ckb))))/dot_general | solution.py:72
  906.5 5.7 fusion.112
  912.2 56.8 %fusion.138 = f32[256,4,4,6]{3,1,2,0:T(4,128)} fusion(f32[256,4,64]{2,1,0:T(4,128)S(1)} %copy-done.51, f32[4,64,6,256]{1,2,0,3:T(8,128)S(1)} %copy-done.9, f32[4,6,256]{1,0,2:T(4,128)S(1)} %copy-done.47, f32[64,6,256]{0,1,2:T(8,128)S(1)} %copy-done.20, f32[64,6,256]{0,1,2:T(8,128)S(1)} %copy-done.8, f32[6,256]{0,1:T(8,128)S(1)} %copy-done.46), kind=kOutput, calls=%fused_computation.217 | convolution fusion | flops 20447232 | bytes 2750464 | tf_op jit(solution)/shard_map/while/body/eval_jaxpr/vmap(jvp(transpose(jvp(ckb,mkb->cmb))))/dot_general | solution.py:71
  969.0 15.5 %add_reduce_fusion = (f32[4,6,256]{1,0,2:T(4,128)}, f32[4,64,6,256]{1,2,0,3:T(8,128)}) fusion(f32[4,64,6,256]{1,2,0,3:T(8,128)S(1)} %copy-done.9, f32[64,6,256]{0,1,2:T(8,128)S(1)} %copy-done.172, f32[64,6,256]{0,1,2:T(8,128)S(1)} %copy-done.8, f32[4,6,256]{1,0,2:T(4,128)S(1)} %copy-done.47, f32[6,256]{0,1:T(8,128)S(1)} %copy-done.46, ...), kind=kOutput, calls=%fused_computation.44 | convolution fusion | flops 31057920 | bytes 10615040 | tf_op jit(solution)/shard_map/while/body/eval_jaxpr/vmap(jvp(transpose(jvp(ckb,mkb->cmb))))/dot_general | solution.py:71
  990.2 7.7 convolution_bitcast_fusion
  1007.6 7.8 fusion.166
  1019.3 99.2 %scatter_fusion.4 = f32[4,3,1152]{1,0,2:T(4,128)S(1)} fusion(f32[4,3,1152]{1,0,2:T(4,128)S(1)} %broadcast.878.clone, s32[1536]{0:T(1024)S(1)} %copy-done.114, f32[1536,4,3]{2,1,0:T(4,128)} %copy.974), kind=kCustom, calls=%fused_computation.20 | custom fusion | flops 18432 | bytes 227328 | tf_op jit(solution)/shard_map/while/body/eval_jaxpr/vmap(jvp(transpose(jvp(jit(_take)))))/scatter-add | solution.py:53
  1120.0 25.0 %scatter_fusion.5 = f32[4,3,1152]{1,0,2:T(4,128)} fusion(f32[4,3,1152]{1,0,2:T(4,128)} %broadcast.878.clone.3, s32[256]{0:T(256)S(1)} %iota.89, f32[256,4,3]{2,1,0:T(4,128)S(1)} %copy.975), kind=kCustom, calls=%fused_computation.21 | custom fusion | flops 3072 | bytes 37888 | tf_op jit(solution)/shard_map/while/body/eval_jaxpr/vmap(jvp(transpose(jvp(jit(_take)))))/scatter-add | solution.py:52
  1174.6 40.0 %all-reduce.4 = (f32[4,4]{0,1:T(4,128)S(1)}, f32[4,4]{0,1:T(4,128)S(1)}, f32[4,4]{0,1:T(4,128)S(1)}) all-reduce(f32[4,4]{0,1:T(4,128)S(1)} %convolution_multiply_fusion.3, f32[4,4]{0,1:T(4,128)S(1)} %convolution_multiply_fusion.2, f32[4,4]{0,1:T(4,128)S(1)} %convolution_multiply_fusion.4), channel_id=1, replica_groups=mesh['gx'=4,'gy'=4,'gz'=2] {'gx','gy','gz'}, use_global_device_ids=true, to_apply=%region_37.50 | all-reduce | flops 48 | bytes 384 | tf_op jit(solution)/shard_map/psum | solution.py:192
  (686 shorter events, 394.0 us)
Async XLA Ops:
  5.1 55.3 %collective-permute-start = (f32[4,1,2,2,16]{4,1,3,2,0:T(1,128)S(1)}, f32[4,1,2,2,16]{4,1,3,2,0:T(1,128)S(1)}, u32[]{:S(2)}, u32[]{:S(2)}) collective-permute-start(f32[4,1,2,2,16]{4,1,3,2,0:T(1,128)S(1)} %get-tuple-element.242), channel_id=1, source_target_pairs={{0,8},{8,16},{16,24},{24,0},{1,9},{9,17},{17,25},{25,1},{2,10},{10... | collective-permute-start | bytes 3080 | tf_op jit(solution)/shard_map/ppermute | solution.py:22
  8.2 52.2 %collective-permute-start.1 = (f32[4,1,2,2,16]{4,1,3,2,0:T(1,128)S(1)}, f32[4,1,2,2,16]{4,1,3,2,0:T(1,128)S(1)}, u32[]{:S(2)}, u32[]{:S(2)}) collective-permute-start(f32[4,1,2,2,16]{4,1,3,2,0:T(1,128)S(1)} %get-tuple-element.243), channel_id=1, source_target_pairs={{8,0},{16,8},{24,16},{0,24},{9,1},{17,9},{25,17},{1,25},{10,2},{18... | collective-permute-start | bytes 3080 | tf_op jit(solution)/shard_map/ppermute | solution.py:23
  55.0 11.2 collective-permute-start.6
  57.0 9.2 collective-permute-start.7
  60.4 3.2 collective-permute-start.2
  60.5 3.2 collective-permute-start.3
  63.7 4.9 collective-permute-start.4
  66.1 3.9 collective-permute-start.5
  66.9 68.5 %collective-permute-start.8 = (f32[12,4,1,2,16]{0,4,3,2,1:T(8,128)}, f32[12,4,1,2,16]{0,4,3,2,1:T(8,128)}, u32[]{:S(2)}, u32[]{:S(2)}) collective-permute-start(f32[12,4,1,2,16]{0,4,3,2,1:T(8,128)} %get-tuple-element.225), channel_id=1, source_target_pairs={{0,2},{2,4},{4,6},{6,0},{1,3},{3,5},{5,7},{7,1},{8,10},{10,12},{12... | collective-permute-start | bytes 18440 | tf_op jit(solution)/shard_map/ppermute | solution.py:22
  68.3 67.0 %collective-permute-start.9 = (f32[12,4,1,2,16]{0,4,3,2,1:T(8,128)}, f32[12,4,1,2,16]{0,4,3,2,1:T(8,128)}, u32[]{:S(2)}, u32[]{:S(2)}) collective-permute-start(f32[12,4,1,2,16]{0,4,3,2,1:T(8,128)} %get-tuple-element.226), channel_id=1, source_target_pairs={{2,0},{4,2},{6,4},{0,6},{3,1},{5,3},{7,5},{1,7},{10,8},{12,10},{14... | collective-permute-start | bytes 18440 | tf_op jit(solution)/shard_map/ppermute | solution.py:23
  82.7 353.0 %copy-start.62 = (f32[6,256]{1,0:T(8,128)}, f32[6,256]{1,0:T(8,128)S(1)}, u32[]{:S(2)}) copy-start(f32[6,256]{1,0:T(8,128)S(1)} %sqrt.140) | copy-start | bytes 18436
  82.7 353.0 %copy-start.60 = (f32[6,256]{1,0:T(8,128)}, f32[6,256]{1,0:T(8,128)S(1)}, u32[]{:S(2)}) copy-start(f32[6,256]{1,0:T(8,128)S(1)} %get-tuple-element.261) | copy-start | bytes 18436
  137.2 8.4 collective-permute-start.10
  137.8 7.8 collective-permute-start.11
  645.3 7.3 collective-permute-start.12
  645.5 7.1 collective-permute-start.13
  653.6 3.7 collective-permute-start.14
  653.7 3.7 collective-permute-start.15
  658.1 4.1 collective-permute-start.16
  659.5 4.2 collective-permute-start.17
  714.4 5.8 collective-permute-start.18
  715.9 4.3 collective-permute-start.19
  720.3 3.7 collective-permute-start.20
  720.3 4.2 collective-permute-start.21
  725.3 5.8 collective-permute-start.22
  727.0 6.8 collective-permute-start.23
  1153.2 8.4 collective-permute-start.24
  1154.2 8.6 collective-permute-start.25
  1162.9 3.7 collective-permute-start.26
  1162.9 3.7 collective-permute-start.27
  1166.7 4.0 collective-permute-start.28
  1168.5 4.0 collective-permute-start.29
  (172 other events, 3158.6 us)
where the time goes:
time: 1240 us; the launch traced here: 1220 us
  matrix products  460 us (37%)
  other arithmetic  369 us (30%)
  local copies, waits for them, and re-layouts  198 us (16%)
  blocking collectives  118 us (10%)
  starting transfers between devices  40.4 us (3%)
  waiting for transfers between devices  30.9 us (2%)
    scatter-add x2, other arithmetic, block_energy(): jnp.take(atom_table, flat_neighbor, axis=1).reshape(3, fanout, width_block)  254 us
    dot_general x15, matrix products, block_energy(): jnp.einsum('ckb,mkb->cmb', feature, harmonic, precision=HIGHEST) / fanout  202 us
    dot_general x15, matrix products, block_energy(): project = jnp.einsum('cmb,mkb->ckb', environ, harmonic, precision=HIGHEST)  189 us
    psum x2, blocking collectives, on_device(): lax.psum((mean_gram(current, product_block), mean_gram(previous, product_...  78.9 us
    scatter-add x2, other arithmetic, block_energy(): center_coords = jnp.take(atom_table, centers, axis=1)  51.4 us
    psum x1, blocking collectives, on_device(): lax.psum(mean_gram(initial, initial), ('gx', 'gy', 'gz'))  38.9 us
    dot_general x6, matrix products, block_energy(): hidden = jax.nn.silu(jnp.dot(radial_in.T, bessel, precision=HIGHEST))  32.2 us
    dot_general x6, matrix products, block_energy(): jnp.dot(radial_out.T, hidden, precision=HIGHEST)  31.6 us
  transfers between devices with their start and end apart: 30, of which 16 were waited for; matrix products, arithmetic and copies ran while one was open for 7% of the time, Pallas kernels for 0%

commit v1 on v0

v1 whole, which is shorter than its diff:
```python
import functools

import jax
import jax.numpy as jnp
import numpy as np
from jax import lax
from jax.experimental import pallas as pl
from jax.experimental.pallas import tpu as pltpu
from jax.sharding import PartitionSpec as P

SOFTEN = 0.25
CUTOFF = 4.0
HIGHEST = lax.Precision.HIGHEST
LANES = 128
GROUP = 8
AXES = ("gx", "gy", "gz")
VMEM_BYTES = 48 * 1024 * 1024


def swap_pairs(size, distance):
    return [(i, (i + distance) % size) for i in range(size)]


def octant_bit(shape, bit, ghosts):
    lane = lax.broadcasted_iota(jnp.int32, shape, 1) % (8 * ghosts)
    return (lane // ghosts // (4 >> bit)) % 2 == 1


def fetch_ghosts(x, bit, ghosts):
    axis = AXES[bit]
    size = lax.axis_size(axis)
    if size == 1:
        return x
    if size == 2:
        return lax.ppermute(x, axis, swap_pairs(2, 1))
    below = lax.ppermute(x, axis, swap_pairs(size, 1))
    above = lax.ppermute(x, axis, swap_pairs(size, -1))
    return jnp.where(octant_bit(x.shape, bit, ghosts), below, above)


def return_ghosts(x, bit, ghosts):
    axis = AXES[bit]
    size = lax.axis_size(axis)
    if size == 1:
        return x
    if size == 2:
        return lax.ppermute(x, axis, swap_pairs(2, 1))
    above = lax.ppermute(x, axis, swap_pairs(size, -1))
    below = lax.ppermute(x, axis, swap_pairs(size, 1))
    return jnp.where(octant_bit(x.shape, bit, ghosts), above, below)


def halo(octants, ghosts):
    first = fetch_ghosts(octants, 0, ghosts)
    level = jnp.concatenate([octants, first], axis=1)
    second = fetch_ghosts(level, 1, ghosts)
    level = jnp.concatenate([level, second], axis=1)
    third = fetch_ghosts(level, 2, ghosts)
    return first, second, third


def halo_back(first, second, third, ghosts):
    width = first.shape[1]
    got = return_ghosts(third, 2, ghosts)
    zero_part = got[:, :width]
    first = first + got[:, width : 2 * width]
    second = second + got[:, 2 * width :]
    got = return_ghosts(second, 1, ghosts)
    zero_part = zero_part + got[:, :width]
    first = first + got[:, width:]
    return zero_part + return_ghosts(first, 0, ghosts)


def sum_everywhere(x):
    for axis in AXES:
        size = lax.axis_size(axis)
        if size & (size - 1):
            x = lax.psum(x, axis)
            continue
        step = 1
        while step < size:
            x = x + lax.ppermute(x, axis, [(i, i ^ step) for i in range(size)])
            step *= 2
    return x


def rows(a):
    return slice(GROUP * a, GROUP * (a + 1))


def gather_lanes(table, index_row, group):
    lane = jnp.broadcast_to(index_row % LANES, (GROUP, LANES))
    tile = jnp.broadcast_to(index_row // LANES, (GROUP, LANES))
    out = None
    for number in range(table.shape[1] // LANES):
        source = table[rows(group), number * LANES : (number + 1) * LANES]
        picked = jnp.take_along_axis(source, lane, axis=1, mode="promise_in_bounds")
        out = picked if out is None else jnp.where(tile == number, picked, out)
    return out


def split_rows(y, vectors):
    high = y.astype(jnp.bfloat16).astype(jnp.float32)
    return high + pltpu.roll(y - high, vectors, 0)


def join_rows(y, vectors):
    return y + pltpu.roll(y, GROUP - vectors, 0)


def pack_kernel(pos_ref, spec_ref, block_ref, list_ref, own_ref, oct_ref):
    vectors = block_ref.shape[3]
    atoms = pos_ref.shape[-1]
    for a in range(3):
        parts = [block_ref[0, 0, 0, :, a, :], pos_ref[0, 0, 0, a : a + 1, :]]
        used = vectors + 1
        if a == 0:
            parts.append(spec_ref[0, 0].astype(jnp.float32))
            used += 1
        parts.append(jnp.zeros((GROUP - used, atoms), jnp.float32))
        own_ref[rows(a), :] = jnp.concatenate(parts, axis=0)
    pick_octants(own_ref, list_ref, oct_ref)


def pick_octants(own_ref, list_ref, oct_ref):
    for j in range(list_ref.shape[1] // LANES):
        cut = slice(j * LANES, (j + 1) * LANES)
        for a in range(3):
            oct_ref[rows(a), cut] = gather_lanes(own_ref, list_ref[:, cut], a)


def add_octants(own, octants, lists, vectors):
    atoms = own.shape[1]
    width = lists.shape[1]
    keep = lax.broadcasted_iota(jnp.int32, octants.shape, 0) < vectors
    packed = split_rows(jnp.where(keep, octants, 0.0), vectors).astype(jnp.bfloat16)
    onehot = lax.broadcasted_iota(jnp.int32, (atoms, width), 0) == lists
    spread = lax.dot_general(
        packed,
        jnp.where(onehot, 1.0, 0.0).astype(jnp.bfloat16),
        (((1,), (1,)), ((), ())),
        preferred_element_type=jnp.float32,
    )
    return own + join_rows(spread, vectors)


def fill_table(table, own_ref, ghost_refs, vectors, ghosts, shifted):
    atoms = own_ref.shape[1]
    table[:, :atoms] = own_ref[...]
    width = 8 * ghosts
    base = atoms
    kind = 1
    for ref in ghost_refs:
        for j in range(ref.shape[1] // width):
            part = ref[:, j * width : (j + 1) * width]
            if shifted:
                row = lax.broadcasted_iota(jnp.int32, part.shape, 0)
                for a in range(3):
                    if (kind >> a) & 1:
                        move = jnp.where(octant_bit(part.shape, a, ghosts), -1.0, 1.0)
                        part = part + jnp.where(row == GROUP * a + vectors, move, 0.0)
            table[:, base : base + width] = part
            base += width
            kind += 1


def gather_slot(table, idx_ref, k, atoms):
    pieces = [[] for _ in range(3)]
    for j in range(atoms // LANES):
        index_row = idx_ref[:, pl.ds(pl.multiple_of(k * atoms + j * LANES, LANES), LANES)]
        for a in range(3):
            pieces[a].append(gather_lanes(table, index_row, a))
    return [jnp.concatenate(p, axis=1) for p in pieces]


def slot_tangents(diff, unit, inv, tn, tdiff, lanes, vectors):
    tau = sum(unit[a] * diff[a] for a in range(3))
    nus = [(diff[a] - unit[a] * tau) * inv for a in range(3)]
    shape = tau.shape
    for v in range(vectors):
        for m, value in enumerate([tau] + nus):
            start = (v * 4 + m) * GROUP
            tn[start : start + GROUP, lanes] = jnp.broadcast_to(value[v : v + 1, :], shape)
    for a in range(3):
        tdiff[rows(a), lanes] = diff[a]
    tdiff[rows(3), lanes] = tau


def channel_products(f, f1, q, rp, rpp, unit, env, tn, acc, half, atoms, fanout, vectors):
    share = 1.0 / fanout
    rpf = [rp[k] * f[k] for k in range(fanout)]
    for v in range(vectors):

        def get(m, k):
            start = (v * 4 + m) * GROUP
            return tn[start : start + GROUP, pl.ds(k * atoms + half, LANES)]

        phi = [f1[k] * get(0, k) for k in range(fanout)]
        de = [share * sum(phi)]
        for a in range(3):
            de.append(
                share * sum(phi[k] * unit(a, k) + f[k] * get(1 + a, k) for k in range(fanout))
            )
        y = []
        hde = []
        for k in range(fanout):
            turn = de[0] + sum(unit(a, k) * de[1 + a] for a in range(3))
            hde.append(turn)
            bend = turn + sum(get(1 + a, k) * env[1 + a] for a in range(3))
            y.append(rpp[k] * (phi[k] * q[k] + f[k] * bend))
        w = [y[k] * f[k] + rp[k] * phi[k] for k in range(fanout)]
        total = [share * sum(w)]
        for a in range(3):
            total.append(
                share * sum(w[k] * unit(a, k) + rpf[k] * get(1 + a, k) for k in range(fanout))
            )
        for k in range(fanout):
            along = total[0] + sum(unit(a, k) * total[1 + a] for a in range(3))
            terms = [f1[k] * (y[k] * q[k] + rp[k] * hde[k] + along)]
            for a in range(3):
                terms.append(f[k] * (y[k] * env[1 + a] + rp[k] * de[1 + a] + total[1 + a]))
            for m in range(4):
                start = (v * 4 + m) * GROUP
                acc[start : start + GROUP, pl.ds(k * atoms + half, LANES)] += terms[m]


def finish_product(
    idx_ref, unit_ref, inv_ref, bend_ref, acc, tdiff, scat, center, own_out, ghost_out, vectors
):
    atoms = center.shape[1]
    fanout = idx_ref.shape[1] // atoms
    tiles = scat.shape[0] // (3 * GROUP)
    scat[...] = jnp.zeros_like(scat)
    center[...] = jnp.zeros_like(center)

    def slot(k, carry):
        lanes = pl.ds(pl.multiple_of(k * atoms, LANES), atoms)
        row = lax.broadcasted_iota(jnp.int32, (GROUP, atoms), 0)
        outs = []
        for m in range(4):
            value = jnp.zeros((GROUP, atoms), jnp.float32)
            for v in range(vectors):
                start = (v * 4 + m) * GROUP
                part = jnp.sum(acc[start : start + GROUP, lanes], axis=0, keepdims=True)
                value = jnp.where(row == v, part, value)
            outs.append(value)
        unit = [unit_ref[rows(a), lanes] for a in range(3)]
        inv = inv_ref[:, lanes]
        diff = [tdiff[rows(a), lanes] for a in range(3)]
        tau = tdiff[rows(3), lanes]
        bend = bend_ref[:, lanes]
        stretch, turn = bend[0:1], bend[1:2]
        mix = [bend[2 + a : 3 + a] for a in range(3)]
        inner = sum(unit[a] * outs[1 + a] for a in range(3))
        along = (
            outs[0]
            - inner * inv
            + (stretch - turn) * tau
            + sum(mix[a] * diff[a] for a in range(3))
        )
        packed = []
        for a in range(3):
            y = along * unit[a] + outs[1 + a] * inv + turn * diff[a] + mix[a] * tau
            y = jnp.where(row < vectors, y, 0.0)
            center[rows(a), :] -= y
            packed.append(split_rows(y, vectors))
        packed = jnp.concatenate(packed, axis=0)
        index_row = idx_ref[:, lanes]
        tile = index_row // LANES
        low = lax.broadcasted_iota(jnp.int32, (LANES, atoms), 0) == index_row % LANES
        left = jnp.concatenate(
            [jnp.where(tile == number, packed, 0.0) for number in range(tiles)], axis=0
        ).astype(jnp.bfloat16)
        right = jnp.where(low, 1.0, 0.0).astype(jnp.bfloat16)
        scat[...] += lax.dot_general(
            left, right, (((1,), (1,)), ((), ())), preferred_element_type=jnp.float32
        )
        return carry

    lax.fori_loop(0, fanout, slot, 0)
    own_tiles = atoms // LANES
    for number in range(tiles):
        for a in range(3):
            start = (number * 3 + a) * GROUP
            value = join_rows(scat[start : start + GROUP, :], vectors)
            if number < own_tiles:
                cut = slice(number * LANES, (number + 1) * LANES)
                own_out[rows(a), cut] = value + center[rows(a), cut]
            else:
                cut = number - own_tiles
                ghost_out[rows(a), cut * LANES : (cut + 1) * LANES] = value


def first_kernel(
    ghosts,
    vectors,
    idx_ref,
    own_ref,
    g1_ref,
    g2_ref,
    g3_ref,
    emb_ref,
    rin_ref,
    rout_ref,
    read_ref,
    own_out,
    ghost_out,
    unit_ref,
    inv_ref,
    bend_ref,
    f_ref,
    f1_ref,
    q_ref,
    rp_ref,
    rpp_ref,
    env_ref,
    table,
    f2_ref,
    tn,
    tdiff,
    acc,
    acc2,
    scat,
    center,
):
    atoms = own_ref.shape[1]
    fanout = idx_ref.shape[1] // atoms
    channels, species = emb_ref.shape
    basis = rin_ref.shape[1]
    fill_table(table, own_ref, (g1_ref, g2_ref, g3_ref), vectors, ghosts, True)

    def embed(kind):
        value = emb_ref[:, 0:1]
        for s in range(1, species):
            value = jnp.where(kind == float(s), emb_ref[:, s : s + 1], value)
        return value

    own_embed = embed(own_ref[vectors + 1 : vectors + 2, :])

    def slot(k, carry):
        lanes = pl.ds(pl.multiple_of(k * atoms, LANES), atoms)
        near = gather_slot(table, idx_ref, k, atoms)
        diff = [near[a] - own_ref[rows(a), :] for a in range(3)]
        delta = [
            jnp.broadcast_to(diff[a][vectors : vectors + 1, :], (GROUP, atoms)) for a in range(3)
        ]
        dist = jnp.sqrt(delta[0] * delta[0] + delta[1] * delta[1] + delta[2] * delta[2] + SOFTEN)
        inv = 1.0 / dist
        unit = [delta[a] * inv for a in range(3)]
        for a in range(3):
            unit_ref[rows(a), lanes] = unit[a]
        inv_ref[:, lanes] = inv
        slot_tangents(diff, unit, inv, tn, tdiff, lanes, vectors)
        one = dist[0:1]
        inv_one = inv[0:1]
        order = (lax.broadcasted_iota(jnp.int32, (basis, atoms), 0) + 1).astype(jnp.float32)
        turns = order * (one * (1.0 / CUTOFF))
        whole = jnp.floor(turns + 0.5)
        rest = turns - whole
        odd = whole - 2.0 * jnp.floor(whole * 0.5)
        sign = 1.0 - 2.0 * odd
        x = rest * np.float32(np.pi)
        x2 = x * x
        sine = x * (
            1.0
            + x2
            * (
                -1.0 / 6
                + x2
                * (1.0 / 120 + x2 * (-1.0 / 5040 + x2 * (1.0 / 362880 + x2 * (-1.0 / 39916800))))
            )
        )
        cosine = 1.0 + x2 * (
            -0.5
            + x2
            * (
                1.0 / 24
                + x2
                * (
                    -1.0 / 720
                    + x2 * (1.0 / 40320 + x2 * (-1.0 / 3628800 + x2 * (1.0 / 479001600)))
                )
            )
        )
        sine = sine * sign
        cosine = cosine * sign
        omega = order * np.float32(np.pi / CUTOFF)
        b0 = sine * inv_one
        b1 = (omega * cosine - b0) * inv_one
        b2 = -(omega * omega * sine + 2.0 * b1) * inv_one
        z = jnp.dot(
            rin_ref[...],
            jnp.concatenate([b0, b1, b2], axis=1),
            precision=HIGHEST,
            preferred_element_type=jnp.float32,
        )
        z0, z1, z2 = z[:, :atoms], z[:, atoms : 2 * atoms], z[:, 2 * atoms :]
        sig = 1.0 / (1.0 + jnp.exp(-z0))
        anti = 1.0 - sig
        slope = sig * (1.0 + z0 * anti)
        curve = sig * anti * (2.0 + z0 * (anti - sig))
        hidden = jnp.concatenate(
            [z0 * sig, slope * z1, curve * z1 * z1 + slope * z2], axis=1
        )
        radial = jnp.dot(
            rout_ref[...], hidden, precision=HIGHEST, preferred_element_type=jnp.float32
        )
        r0, r1, r2 = radial[:, :atoms], radial[:, atoms : 2 * atoms], radial[:, 2 * atoms :]
        square = one * one
        base = 1.0 - square * (1.0 / CUTOFF**2)
        v0 = base * base
        v1 = base * one * (-4.0 / CUTOFF**2)
        v2 = -4.0 / CUTOFF**2 + square * (12.0 / CUTOFF**4)
        pair = own_embed * embed(near[0][vectors + 1 : vectors + 2, :])
        f_ref[:, lanes] = pair * (r0 * v0)
        f1_ref[:, lanes] = pair * (r1 * v0 + r0 * v1)
        f2_ref[:, lanes] = pair * (r2 * v0 + 2.0 * (r1 * v1) + r0 * v2)
        return carry

    lax.fori_loop(0, fanout, slot, 0)
    acc[...] = jnp.zeros_like(acc)
    acc2[...] = jnp.zeros_like(acc2)
    halves = atoms // LANES
    share = 1.0 / fanout

    def tile(number, carry):
        start = pl.multiple_of((number // halves) * GROUP, GROUP)
        half = pl.multiple_of((number % halves) * LANES, LANES)
        here = pl.ds(start, GROUP)

        def cut(k):
            return pl.ds(pl.multiple_of(k * atoms + half, LANES), LANES)

        def unit(a, k):
            return unit_ref[rows(a), cut(k)]

        slots = range(fanout)
        f = [f_ref[here, cut(k)] for k in slots]
        f1 = [f1_ref[here, cut(k)] for k in slots]
        read = jnp.broadcast_to(read_ref[here, :], (GROUP, LANES))
        env = [share * sum(f)]
        for a in range(3):
            env.append(share * sum(f[k] * unit(a, k) for k in slots))
        q, rp, rpp = [], [], []
        for k in slots:
            project = env[0] + sum(unit(a, k) * env[1 + a] for a in range(3))
            x = f[k] * project
            sig = 1.0 / (1.0 + jnp.exp(-x))
            anti = 1.0 - sig
            q.append(project)
            rp.append(read * (sig * (1.0 + x * anti)))
            rpp.append(read * (sig * anti * (2.0 + x * (anti - sig))))
            q_ref[here, cut(k)] = q[k]
            rp_ref[here, cut(k)] = rp[k]
            rpp_ref[here, cut(k)] = rpp[k]
        for m in range(4):
            env_ref[pl.ds(m * channels + start, GROUP), pl.ds(half, LANES)] = env[m]
        rpf = [rp[k] * f[k] for k in slots]
        total = [share * sum(rpf)]
        for a in range(3):
            total.append(share * sum(rpf[k] * unit(a, k) for k in slots))
        for k in slots:
            g = [rp[k] * env[m] + total[m] for m in range(4)]
            gamma = g[0] + sum(unit(a, k) * g[1 + a] for a in range(3))
            terms = [f2_ref[here, cut(k)] * gamma, f1[k] * g[0]]
            terms += [f1[k] * g[1 + a] for a in range(3)]
            terms += [f[k] * g[1 + a] for a in range(3)]
            for m, term in enumerate(terms):
                acc2[m * GROUP : (m + 1) * GROUP, cut(k)] += term
        channel_products(
            f, f1, q, rp, rpp, unit, env, tn, acc, half, atoms, fanout, vectors
        )
        return carry

    lax.fori_loop(0, (channels // GROUP) * halves, tile, 0)

    def bend_slot(k, carry):
        lanes = pl.ds(pl.multiple_of(k * atoms, LANES), atoms)
        sums = [
            jnp.sum(acc2[m * GROUP : (m + 1) * GROUP, lanes], axis=0, keepdims=True)
            for m in range(8)
        ]
        inv = inv_ref[0:1, lanes]
        unit = [unit_ref[GROUP * a : GROUP * a + 1, lanes] for a in range(3)]
        up = sum(unit[a] * sums[2 + a] for a in range(3))
        uw = sum(unit[a] * sums[5 + a] for a in range(3))
        turn = (sums[1] + up - uw * inv) * inv
        mix = [
            ((sums[2 + a] - unit[a] * up) - (sums[5 + a] - unit[a] * uw) * inv) * inv
            for a in range(3)
        ]
        pad = jnp.zeros((GROUP - 5, atoms), jnp.float32)
        bend_ref[:, lanes] = jnp.concatenate([sums[0], turn] + mix + [pad], axis=0)
        return carry

    lax.fori_loop(0, fanout, bend_slot, 0)
    finish_product(
        idx_ref, unit_ref, inv_ref, bend_ref, acc, tdiff, scat, center, own_out, ghost_out, vectors
    )


def second_kernel(
    ghosts,
    vectors,
    idx_ref,
    own_ref,
    g1_ref,
    g2_ref,
    g3_ref,
    unit_ref,
    inv_ref,
    bend_ref,
    f_ref,
    f1_ref,
    q_ref,
    rp_ref,
    rpp_ref,
    env_ref,
    own_out,
    ghost_out,
    table,
    tn,
    tdiff,
    acc,
    scat,
    center,
):
    atoms = own_ref.shape[1]
    fanout = idx_ref.shape[1] // atoms
    channels = f_ref.shape[0]
    fill_table(table, own_ref, (g1_ref, g2_ref, g3_ref), vectors, ghosts, False)

    def slot(k, carry):
        lanes = pl.ds(pl.multiple_of(k * atoms, LANES), atoms)
        near = gather_slot(table, idx_ref, k, atoms)
        diff = [near[a] - own_ref[rows(a), :] for a in range(3)]
        unit = [unit_ref[rows(a), lanes] for a in range(3)]
        slot_tangents(diff, unit, inv_ref[:, lanes], tn, tdiff, lanes, vectors)
        return carry

    lax.fori_loop(0, fanout, slot, 0)
    acc[...] = jnp.zeros_like(acc)
    halves = atoms // LANES

    def tile(number, carry):
        start = pl.multiple_of((number // halves) * GROUP, GROUP)
        half = pl.multiple_of((number % halves) * LANES, LANES)
        here = pl.ds(start, GROUP)

        def cut(k):
            return pl.ds(pl.multiple_of(k * atoms + half, LANES), LANES)

        def unit(a, k):
            return unit_ref[rows(a), cut(k)]

        def load(ref):
            return [ref[here, cut(k)] for k in range(fanout)]

        env = [
            env_ref[pl.ds(m * channels + start, GROUP), pl.ds(half, LANES)] for m in range(4)
        ]
        channel_products(
            load(f_ref),
            load(f1_ref),
            load(q_ref),
            load(rp_ref),
            load(rpp_ref),
            unit,
            env,
            tn,
            acc,
            half,
            atoms,
            fanout,
            vectors,
        )
        return carry

    lax.fori_loop(0, (channels // GROUP) * halves, tile, 0)
    finish_product(
        idx_ref, unit_ref, inv_ref, bend_ref, acc, tdiff, scat, center, own_out, ghost_out, vectors
    )


def middle_kernel(vectors, own_ref, sums_ref, list_ref, full_ref, oct_ref):
    for a in range(3):
        full_ref[rows(a), :] = add_octants(
            own_ref[rows(a), :], sums_ref[rows(a), :], list_ref[...], vectors
        )
    pick_octants(full_ref, list_ref, oct_ref)


def gram_kernel(vectors, start_ref, first_ref, own_ref, sums_ref, list_ref, full_ref, gram_ref):
    total = jnp.zeros(gram_ref.shape, jnp.float32)
    for a in range(3):
        second = add_octants(own_ref[rows(a), :], sums_ref[rows(a), :], list_ref[...], vectors)
        full_ref[rows(a), :] = second
        stack = jnp.concatenate([start_ref[rows(a), :], first_ref[rows(a), :], second], axis=0)
        row = lax.broadcasted_iota(jnp.int32, stack.shape, 0)
        stack = jnp.where(row % GROUP < vectors, stack, 0.0)
        pad = jnp.zeros((gram_ref.shape[1] - stack.shape[0], stack.shape[1]), jnp.float32)
        total += lax.dot_general(
            stack,
            jnp.concatenate([stack, pad], axis=0),
            (((1,), (1,)), ((), ())),
            precision=HIGHEST,
            preferred_element_type=jnp.float32,
        )
    gram_ref[...] = total


def last_kernel(
    vectors, scale, start_ref, first_ref, second_ref, gram_ref, next_ref, diag_ref, off_ref
):
    shape = (GROUP, LANES)
    row = lax.broadcasted_iota(jnp.int32, shape, 0)
    lane = lax.broadcasted_iota(jnp.int32, shape, 1)
    inside = (row < vectors) & (lane < vectors)
    eye = jnp.where((row == lane) & inside, 1.0, 0.0)

    def block(i, j):
        part = gram_ref[rows(i), :]
        if j:
            part = pltpu.roll(part, LANES - GROUP * j, 1)
        return jnp.where(inside, part * scale, 0.0)

    def mul(x, y):
        return sum(x[:, k : k + 1] * y[k : k + 1, :] for k in range(vectors))

    def flip(x):
        out = jnp.zeros(shape, jnp.float32)
        for k in range(vectors):
            line = jnp.sum(eye * x[:, k : k + 1], axis=0, keepdims=True)
            out = jnp.where(row == k, line, out)
        return out

    def factor(m):
        upper = jnp.zeros(shape, jnp.float32)
        inverse = eye
        for j in range(vectors):
            scale_j = 1.0 / jnp.sqrt(m[j : j + 1, j : j + 1])
            column = m[:, j : j + 1] * scale_j
            line = m[j : j + 1, :] * scale_j
            upper = jnp.where((row == j) & (lane >= j), line, upper)
            m = m - column * line
            own = inverse[j : j + 1, :] * scale_j
            inverse = jnp.where(
                row == j, own, jnp.where(row > j, inverse - column * own, inverse)
            )
        return upper, inverse

    ss, su, uu = block(0, 0), block(0, 1), block(1, 1)
    sq, uq, qq = block(0, 2), block(1, 2), block(2, 2)
    qu = block(2, 1)
    _, p0 = factor(ss)
    p0t = flip(p0)
    a1 = mul(mul(p0, su), p0t)
    a1t = flip(a1)
    up1, p1 = factor(mul(mul(p0, uu), p0t) - mul(a1t, a1))
    b = mul(p1, p0)
    a = -mul(p1, mul(a1t, p0))
    at, bt = flip(a), flip(b)
    right_s = mul(su, at) + mul(sq, bt)
    right_u = mul(uu, at) + mul(uq, bt)
    right_q = mul(qu, at) + mul(qq, bt)
    a2 = mul(a, right_s) + mul(b, right_u)
    c2 = mul(p0, right_s)
    ww = mul(a, right_u) + mul(b, right_q)
    a2t, c2t = flip(a2), flip(c2)
    up2, p2 = factor(ww - mul(a2t, a2) - mul(c2t, c2))
    weights = (
        -mul(p2, mul(a2t, a) + mul(c2t, p0)),
        mul(p2, a - mul(a2t, b)),
        mul(p2, b),
    )
    small = (slice(0, vectors), slice(0, vectors))
    diag_ref[0] = a1[small]
    diag_ref[1] = a2[small]
    off_ref[0] = up1[small]
    off_ref[1] = up2[small]
    for comp in range(3):
        value = None
        for weight, ref in zip(weights, (start_ref, first_ref, second_ref)):
            for w in range(vectors):
                line = GROUP * comp + w
                term = weight[:, w : w + 1] * ref[line : line + 1, :]
                value = term if value is None else value + term
        next_ref[0, 0, 0, :, comp, :] = value[:vectors]


def call(body, outs, args, scratch=()):
    return pl.pallas_call(
        body,
        out_shape=[jax.ShapeDtypeStruct(shape, jnp.float32) for shape in outs],
        in_specs=[pl.BlockSpec(memory_space=pltpu.VMEM)] * len(args),
        out_specs=[pl.BlockSpec(memory_space=pltpu.VMEM)] * len(outs),
        scratch_shapes=[pltpu.VMEM(shape, jnp.float32) for shape in scratch],
        compiler_params=pltpu.CompilerParams(vmem_limit_bytes=VMEM_BYTES),
    )(*args)


def table_index(neighbors, atoms, ghosts):
    entry = neighbors - atoms
    cell = entry // ghosts
    number = cell
    kept = [n for n in range(64) if not all(m in (1, 2) for m in (n // 16, n // 4 % 4, n % 4))]
    previous = -1
    for position, n in enumerate(kept):
        if n - previous > 1:
            number = number + jnp.where(cell >= position, n - previous - 1, 0)
        previous = n
    member = (number // 16, number // 4 % 4, number % 4)
    kind = 0
    octant = 0
    for bit, m in enumerate(member):
        kind = kind + jnp.where((m == 0) | (m == 3), 1 << bit, 0)
        octant = 2 * octant + (m + 1) % 2
    place = atoms + (kind - 1) * (8 * ghosts) + octant * ghosts + entry % ghosts
    return jnp.where(neighbors < atoms, neighbors, place)


def on_device(
    positions,
    species,
    start_block,
    neighbors,
    ghost_lists,
    embedding,
    radial_in,
    radial_out,
    readout,
):
    atoms = positions.shape[-1]
    ghosts = ghost_lists.shape[-1]
    vectors = start_block.shape[3]
    fanout = neighbors.shape[3]
    channels = embedding.shape[1]
    devices = lax.axis_size("gx") * lax.axis_size("gy") * lax.axis_size("gz")
    scale = 1.0 / (3.0 * atoms * devices)
    width = 8 * ghosts
    high = 3 * GROUP
    edges = fanout * atoms
    lists = ghost_lists.reshape(1, width)
    index = table_index(neighbors.reshape(1, -1), atoms, ghosts)
    table_width = atoms + 7 * width
    tiles = table_width // LANES

    own, octants = call(
        pack_kernel,
        [(high, atoms), (high, width)],
        (positions, species, start_block, lists),
    )
    ghost_parts = halo(octants, ghosts)
    shared = [
        (vectors * 4 * GROUP, edges),
        (4 * GROUP, edges),
        (vectors * 4 * GROUP, edges),
    ]
    tail = [(tiles * high, LANES), (high, atoms)]
    saved_shapes = [
        (high, edges),
        (GROUP, edges),
        (GROUP, edges),
        (channels, edges),
        (channels, edges),
        (channels, edges),
        (channels, edges),
        (channels, edges),
        (4 * channels, atoms),
    ]
    results = call(
        functools.partial(first_kernel, ghosts, vectors),
        [(high, atoms), (high, 7 * width)] + saved_shapes,
        (index, own) + ghost_parts
        + (embedding.T, radial_in.T, radial_out.T, readout.reshape(-1, 1)),
        [(high, table_width), (channels, edges)] + shared + [(8 * GROUP, edges)] + tail,
    )
    own_terms, ghost_terms, saved = results[0], results[1], results[2:]

    def back(terms):
        return halo_back(
            terms[:, :width], terms[:, width : 3 * width], terms[:, 3 * width :], ghosts
        )

    first, octants = call(
        functools.partial(middle_kernel, vectors),
        [(high, atoms), (high, width)],
        (own_terms, back(ghost_terms), lists),
    )
    ghost_parts = halo(octants, ghosts)
    own_terms, ghost_terms = call(
        functools.partial(second_kernel, ghosts, vectors),
        [(high, atoms), (high, 7 * width)],
        (index, first) + ghost_parts + tuple(saved),
        [(high, table_width)] + shared + tail,
    )
    second, gram = call(
        functools.partial(gram_kernel, vectors),
        [(high, atoms), (high, LANES)],
        (own, first, own_terms, back(ghost_terms), lists),
    )
    gram = sum_everywhere(gram)
    return tuple(
        call(
            functools.partial(last_kernel, vectors, scale),
            [(1, 1, 1, vectors, 3, atoms), (2, vectors, vectors), (2, vectors, vectors)],
            (own, first, second, gram),
        )
    )


def solution(mesh):
    return jax.shard_map(
        on_device,
        mesh=mesh,
        in_specs=(
            P("gx", "gy", "gz", None, None),
            P("gx", "gy", "gz", None),
            P("gx", "gy", "gz", None, None, None),
            P("gx", "gy", "gz", None, None),
            P("gx", "gy", "gz", None),
            P(),
            P(),
            P(),
            P(),
        ),
        out_specs=(P("gx", "gy", "gz", None, None, None), P(), P()),
        check_vma=False,
    )
```

time: 1240 us -> 109 us (0.09); the launches traced: 1220 us -> 109 us
  matrix products: 460 us -> 0 us
  other arithmetic: 369 us -> 0.55 us
  local copies, waits for them, and re-layouts: 198 us -> 4.41 us
  blocking collectives: 118 us -> 0 us
  Pallas kernels: 0 us -> 27.6 us
  waiting for transfers between devices: 30.9 us -> 44 us
    dot_general x58 -> x0, matrix products: 458 us -> none  [the longest x15 202 us: block_energy(): jnp.einsum('ckb,mkb->cmb', feature, harmonic, precision=HIGHEST) / fanout]
    scatter-add x6 -> x0, other arithmetic: 309 us -> none  [the longest x2 254 us: block_energy(): jnp.take(atom_table, flat_neighbor, axis=1).reshape(3, fanout, width_block)]
    psum x3 -> x0, blocking collectives: 118 us -> none  [the longest x2 78.9 us: on_device(): lax.psum((mean_gram(current, product_block), mean_gram(previous, product_...]
    gather x17 -> x0, local copies, waits for them, and re-layouts: 45.1 us -> none  [the longest x5 23.5 us: block_energy(): jnp.take(atom_table, flat_neighbor, axis=1).reshape(3, fanout, width_block)]
    reshape x24 -> x2, local copies, waits for them, and re-layouts: 35.8 us -> 0.87 us  [the longest x1 0.78 us: on_device(): lists = ghost_lists.reshape(1, width)]
    pallas_call x0 -> x6, Pallas kernels: none -> 27.6 us  [call(): pl.pallas_call(body, out_shape=[jax.ShapeDtypeStruct(shape, jnp.float32)...]
    dot_general x9 -> x0, local copies, waits for them, and re-layouts: 20 us -> none  [the longest x4 11.4 us: block_energy(): jnp.einsum('ckb,mkb->cmb', feature, harmonic, precision=HIGHEST) / fanout]
    concatenate x11 -> x0, local copies, waits for them, and re-layouts: 18.5 us -> none  [the longest x6 13.5 us: on_device(): jnp.concatenate([flat_block, ghost_tangent], axis=1)]
  transfers between devices with their start and end apart: 30 -> 25, of which waited for: 16 -> 21; matrix products, arithmetic and copies ran while one was open for 7% -> 1% of each run, Pallas kernels for 0% -> 0%
where the time goes in v1:
time: 109 us
  waiting for transfers between devices  44 us (40%)
  starting transfers between devices  31.7 us (29%)
  Pallas kernels  27.6 us (25%)
  local copies, waits for them, and re-layouts  4.41 us (4%)
    pallas_call x6, Pallas kernels, call(): pl.pallas_call(body, out_shape=[jax.ShapeDtypeStruct(shape, jnp.float32)...  27.6 us
    ppermute x4, waiting for transfers between devices, fetch_ghosts(): below = lax.ppermute(x, axis, swap_pairs(size, 1))  12 us
    ppermute x5, waiting for transfers between devices, sum_everywhere(): x = x + lax.ppermute(x, axis, [(i, i ^ step) for i in range(size)])  11.9 us
    ppermute x4, starting transfers between devices, return_ghosts(): above = lax.ppermute(x, axis, swap_pairs(size, -1))  11.1 us
    ppermute x4, starting transfers between devices, fetch_ghosts(): above = lax.ppermute(x, axis, swap_pairs(size, -1))  9.05 us
    ppermute x4, waiting for transfers between devices, return_ghosts(): below = lax.ppermute(x, axis, swap_pairs(size, 1))  6.35 us
    ppermute x2, waiting for transfers between devices, return_ghosts(): return lax.ppermute(x, axis, swap_pairs(2, 1))  5.74 us
    ppermute x5, starting transfers between devices, sum_everywhere(): x = x + lax.ppermute(x, axis, [(i, i ^ step) for i in range(size)])  4.99 us
  transfers between devices with their start and end apart: 25, of which 21 were waited for; matrix products, arithmetic and copies ran while one was open for 1% of the time, Pallas kernels for 0%

profile of v1, /device:TPU:0, one launch (start us, length us, event | category | flops | bytes accessed | tf_op | source)
XLA Modules:
  0.0 109.1 jit_solution(5840036889713269497)
XLA Ops:
  2.2 5.1 %collective-permute-start.1 = (f32[24,128]{1,0:T(8,128)S(1)}, f32[24,128]{1,0:T(8,128)S(1)}, u32[]{:S(2)}, u32[]{:S(2)}) collective-permute-start(f32[24,128]{1,0:T(8,128)S(1)} %get-tuple-element.23), channel_id=1, source_target_pairs={{0,24},{8,0},{16,8},{24,16},{1,25},{9,1},{17,9},{25,17},{2,26},{10... | collective-permute-start | bytes 36872 | tf_op jit(solution)/shard_map/ppermute | solution.py:37
  7.3 1.4 %collective-permute-done.1 = f32[24,128]{1,0:T(8,128)S(1)} collective-permute-done((f32[24,128]{1,0:T(8,128)S(1)}, f32[24,128]{1,0:T(8,128)S(1)}, u32[]{:S(2)}, u32[]{:S(2)}) %collective-permute-start.1) | collective-permute-done | bytes 12320 | tf_op jit(solution)/shard_map/ppermute | solution.py:37
  8.7 4.1 %collective-permute-done = f32[24,128]{1,0:T(8,128)S(1)} collective-permute-done((f32[24,128]{1,0:T(8,128)S(1)}, f32[24,128]{1,0:T(8,128)S(1)}, u32[]{:S(2)}, u32[]{:S(2)}) %collective-permute-start) | collective-permute-done | bytes 12320 | tf_op jit(solution)/shard_map/ppermute | solution.py:36
  14.4 2.0 %collective-permute-done.2 = f32[24,256]{1,0:T(8,128)S(1)} collective-permute-done((f32[24,256]{1,0:T(8,128)S(1)}, f32[24,256]{1,0:T(8,128)S(1)}, u32[]{:S(2)}, u32[]{:S(2)}) %collective-permute-start.2) | collective-permute-done | bytes 24608 | tf_op jit(solution)/shard_map/ppermute | solution.py:36
  16.5 1.6 %collective-permute-start.4 = (f32[24,512]{1,0:T(8,128)S(1)}, f32[24,512]{1,0:T(8,128)S(1)}, u32[]{:S(2)}, u32[]{:S(2)}) collective-permute-start(f32[24,512]{1,0:T(8,128)S(1)} %pad_maximum_fusion), channel_id=1, source_target_pairs={{0,1},{1,0},{2,3},{3,2},{4,5},{5,4},{6,7},{7,6},{8,9},{9,8},{10,11... | collective-permute-start | bytes 147464 | tf_op jit(solution)/shard_map/ppermute | solution.py:35
  21.0 15.6 %shard_map.113 = (f32[24,256]{1,0:T(8,128)S(1)}, f32[24,896]{1,0:T(8,128)S(1)}, f32[24,1536]{1,0:T(8,128)S(1)}, f32[8,1536]{1,0:T(8,128)S(1)}, f32[8,1536]{1,0:T...) custom-call(s32[1,1536]{1,0:T(1,128)S(1)} %compare_select_fusion.idx, ...), custom_call_target="tpu_custom_call" | custom-call | tf_op jit(solution)/shard_map/pallas_call | solution.py:692
  36.6 1.3 %collective-permute-start.5 = (f32[24,512]{1,0:T(8,128)S(1)}, f32[24,512]{1,0:T(8,128)S(1)}, u32[]{:S(2)}, u32[]{:S(2)}) collective-permute-start(f32[24,512]{1,0:T(8,128)S(1)} %slice.48), channel_id=1, source_target_pairs={{0,1},{1,0},{2,3},{3,2},{4,5},{5,4},{6,7},{7,6},{8,9},{9,8},{10,11... | collective-permute-start | bytes 147464 | tf_op jit(solution)/shard_map/ppermute | solution.py:47
  37.9 2.9 %collective-permute-done.5 = f32[24,512]{1,0:T(8,128)S(1)} collective-permute-done((f32[24,512]{1,0:T(8,128)S(1)}, f32[24,512]{1,0:T(8,128)S(1)}, u32[]{:S(2)}, u32[]{:S(2)}) %collective-permute-start.5) | collective-permute-done | bytes 49184 | tf_op jit(solution)/shard_map/ppermute | solution.py:47
  40.7 1.7 %collective-permute-start.6 = (f32[24,256]{1,0:T(8,128)S(1)}, f32[24,256]{1,0:T(8,128)S(1)}, u32[]{:S(2)}, u32[]{:S(2)}) collective-permute-start(f32[24,256]{1,0:T(8,128)S(1)} %slice_add_fusion.1), channel_id=1, source_target_pairs={{0,6},{2,0},{4,2},{6,4},{1,7},{3,1},{5,3},{7,5},{8,14},{10,8},{12,... | collective-permute-start | bytes 73736 | tf_op jit(solution)/shard_map/ppermute | solution.py:48
  42.5 1.5 %collective-permute-done.7 = f32[24,256]{1,0:T(8,128)S(1)} collective-permute-done((f32[24,256]{1,0:T(8,128)S(1)}, f32[24,256]{1,0:T(8,128)S(1)}, u32[]{:S(2)}, u32[]{:S(2)}) %collective-permute-start.7) | collective-permute-done | bytes 24608 | tf_op jit(solution)/shard_map/ppermute | solution.py:49
  44.1 3.8 %collective-permute-start.8 = (f32[24,128]{1,0:T(8,128)S(1)}, f32[24,128]{1,0:T(8,128)S(1)}, u32[]{:S(2)}, u32[]{:S(2)}) collective-permute-start(f32[24,128]{1,0:T(8,128)S(1)} %slice_add_fusion.5), channel_id=1, source_target_pairs={{0,24},{8,0},{16,8},{24,16},{1,25},{9,1},{17,9},{25,17},{2,26},{10... | collective-permute-start | bytes 36872 | tf_op jit(solution)/shard_map/ppermute | solution.py:48
  47.9 1.7 %collective-permute-done.9 = f32[24,128]{1,0:T(8,128)S(1)} collective-permute-done((f32[24,128]{1,0:T(8,128)S(1)}, f32[24,128]{1,0:T(8,128)S(1)}, u32[]{:S(2)}, u32[]{:S(2)}) %collective-permute-start.9) | collective-permute-done | bytes 12320 | tf_op jit(solution)/shard_map/ppermute | solution.py:49
  49.9 3.9 %collective-permute-start.11 = (f32[24,128]{1,0:T(8,128)S(1)}, f32[24,128]{1,0:T(8,128)S(1)}, u32[]{:S(2)}, u32[]{:S(2)}) collective-permute-start(f32[24,128]{1,0:T(8,128)S(1)} %get-tuple-element.27), channel_id=1, source_target_pairs={{0,24},{8,0},{16,8},{24,16},{1,25},{9,1},{17,9},{25,17},{2,26},{10... | collective-permute-start | bytes 36872 | tf_op jit(solution)/shard_map/ppermute | solution.py:37
  53.8 1.4 %collective-permute-done.11 = f32[24,128]{1,0:T(8,128)S(1)} collective-permute-done((f32[24,128]{1,0:T(8,128)S(1)}, f32[24,128]{1,0:T(8,128)S(1)}, u32[]{:S(2)}, u32[]{:S(2)}) %collective-permute-start.11) | collective-permute-done | bytes 12320 | tf_op jit(solution)/shard_map/ppermute | solution.py:37
  55.2 4.1 %collective-permute-done.10 = f32[24,128]{1,0:T(8,128)S(1)} collective-permute-done((f32[24,128]{1,0:T(8,128)S(1)}, f32[24,128]{1,0:T(8,128)S(1)}, u32[]{:S(2)}, u32[]{:S(2)}) %collective-permute-start.10) | collective-permute-done | bytes 12320 | tf_op jit(solution)/shard_map/ppermute | solution.py:36
  60.9 1.8 %collective-permute-done.12 = f32[24,256]{1,0:T(8,128)S(1)} collective-permute-done((f32[24,256]{1,0:T(8,128)S(1)}, f32[24,256]{1,0:T(8,128)S(1)}, u32[]{:S(2)}, u32[]{:S(2)}) %collective-permute-start.12) | collective-permute-done | bytes 24608 | tf_op jit(solution)/shard_map/ppermute | solution.py:36
  62.7 1.3 %collective-permute-start.14 = (f32[24,512]{1,0:T(8,128)S(1)}, f32[24,512]{1,0:T(8,128)S(1)}, u32[]{:S(2)}, u32[]{:S(2)}) collective-permute-start(f32[24,512]{1,0:T(8,128)S(1)} %pad_maximum_fusion.1), channel_id=1, source_target_pairs={{0,1},{1,0},{2,3},{3,2},{4,5},{5,4},{6,7},{7,6},{8,9},{9,8},{10,11... | collective-permute-start | bytes 147464 | tf_op jit(solution)/shard_map/ppermute | solution.py:35
  64.0 2.9 %collective-permute-done.14.g3_ref = f32[24,512]{1,0:T(8,128)S(1)} collective-permute-done((f32[24,512]{1,0:T(8,128)S(1)}, f32[24,512]{1,0:T(8,128)S(1)}, u32[]{:S(2)}, u32[]{:S(2)}) %collective-permute-start.14) | collective-permute-done | bytes 49184 | tf_op jit(solution)/shard_map/ppermute | solution.py:35
  66.8 8.9 %shard_map.115 = (f32[24,256]{1,0:T(8,128)S(1)}, f32[24,896]{1,0:T(8,128)S(1)}) custom-call(s32[1,1536]{1,0:T(1,128)S(1)} %compare_select_fusion.idx_ref, f32[24,256]{1,0:T(8,128)S(1)} %get-tuple-element.26.own_ref.first_ref, f32[24,128]{1,0:T(8,128)S(1)} %fusion.35.g1_ref, f32[24,256]{1,0:T(8,128)S(1)} %fusion.38.g2_ref, ...), custom_call_target="tpu_custom_call" | custom-call | tf_op jit(solution)/shard_map/pallas_call | solution.py:692
  75.7 1.3 %collective-permute-start.15 = (f32[24,512]{1,0:T(8,128)S(1)}, f32[24,512]{1,0:T(8,128)S(1)}, u32[]{:S(2)}, u32[]{:S(2)}) collective-permute-start(f32[24,512]{1,0:T(8,128)S(1)} %slice.56), channel_id=1, source_target_pairs={{0,1},{1,0},{2,3},{3,2},{4,5},{5,4},{6,7},{7,6},{8,9},{9,8},{10,11... | collective-permute-start | bytes 147464 | tf_op jit(solution)/shard_map/ppermute | solution.py:47
  77.0 2.9 %collective-permute-done.15 = f32[24,512]{1,0:T(8,128)S(1)} collective-permute-done((f32[24,512]{1,0:T(8,128)S(1)}, f32[24,512]{1,0:T(8,128)S(1)}, u32[]{:S(2)}, u32[]{:S(2)}) %collective-permute-start.15) | collective-permute-done | bytes 49184 | tf_op jit(solution)/shard_map/ppermute | solution.py:47
  79.9 1.7 %collective-permute-start.16 = (f32[24,256]{1,0:T(8,128)S(1)}, f32[24,256]{1,0:T(8,128)S(1)}, u32[]{:S(2)}, u32[]{:S(2)}) collective-permute-start(f32[24,256]{1,0:T(8,128)S(1)} %slice_add_fusion), channel_id=1, source_target_pairs={{0,6},{2,0},{4,2},{6,4},{1,7},{3,1},{5,3},{7,5},{8,14},{10,8},{12,... | collective-permute-start | bytes 73736 | tf_op jit(solution)/shard_map/ppermute | solution.py:48
  81.6 1.5 %collective-permute-done.17 = f32[24,256]{1,0:T(8,128)S(1)} collective-permute-done((f32[24,256]{1,0:T(8,128)S(1)}, f32[24,256]{1,0:T(8,128)S(1)}, u32[]{:S(2)}, u32[]{:S(2)}) %collective-permute-start.17) | collective-permute-done | bytes 24608 | tf_op jit(solution)/shard_map/ppermute | solution.py:49
  83.3 3.8 %collective-permute-start.18 = (f32[24,128]{1,0:T(8,128)S(1)}, f32[24,128]{1,0:T(8,128)S(1)}, u32[]{:S(2)}, u32[]{:S(2)}) collective-permute-start(f32[24,128]{1,0:T(8,128)S(1)} %slice_add_fusion.2), channel_id=1, source_target_pairs={{0,24},{8,0},{16,8},{24,16},{1,25},{9,1},{17,9},{25,17},{2,26},{10... | collective-permute-start | bytes 36872 | tf_op jit(solution)/shard_map/ppermute | solution.py:48
  87.1 1.7 %collective-permute-done.19 = f32[24,128]{1,0:T(8,128)S(1)} collective-permute-done((f32[24,128]{1,0:T(8,128)S(1)}, f32[24,128]{1,0:T(8,128)S(1)}, u32[]{:S(2)}, u32[]{:S(2)}) %collective-permute-start.19) | collective-permute-done | bytes 12320 | tf_op jit(solution)/shard_map/ppermute | solution.py:49
  89.3 3.7 %collective-permute-done.20 = f32[24,128]{1,0:T(8,128)S(1)} collective-permute-done((f32[24,128]{1,0:T(8,128)S(1)}, f32[24,128]{1,0:T(8,128)S(1)}, u32[]{:S(2)}, u32[]{:S(2)}) %collective-permute-start.20) | collective-permute-done | bytes 12320 | tf_op jit(solution)/shard_map/ppermute | solution.py:82
  93.0 2.4 %collective-permute-start.21 = (f32[24,128]{1,0:T(8,128)S(1)}, f32[24,128]{1,0:T(8,128)S(1)}, u32[]{:S(2)}, u32[]{:S(2)}) collective-permute-start(f32[24,128]{1,0:T(8,128)S(1)} %add.426), channel_id=1, source_target_pairs={{0,16},{8,24},{16,0},{24,8},{1,17},{9,25},{17,1},{25,9},{2,18},{10... | collective-permute-start | bytes 36872 | tf_op jit(solution)/shard_map/ppermute | solution.py:82
  95.4 2.2 %collective-permute-done.21 = f32[24,128]{1,0:T(8,128)S(1)} collective-permute-done((f32[24,128]{1,0:T(8,128)S(1)}, f32[24,128]{1,0:T(8,128)S(1)}, u32[]{:S(2)}, u32[]{:S(2)}) %collective-permute-start.21) | collective-permute-done | bytes 12320 | tf_op jit(solution)/shard_map/ppermute | solution.py:82
  98.8 1.3 %collective-permute-start.23 = (f32[24,128]{1,0:T(8,128)S(1)}, f32[24,128]{1,0:T(8,128)S(1)}, u32[]{:S(2)}, u32[]{:S(2)}) collective-permute-start(f32[24,128]{1,0:T(8,128)S(1)} %add.428), channel_id=1, source_target_pairs={{0,4},{2,6},{4,0},{6,2},{1,5},{3,7},{5,1},{7,3},{8,12},{10,14},{12... | collective-permute-start | bytes 36872 | tf_op jit(solution)/shard_map/ppermute | solution.py:82
  100.1 2.4 %collective-permute-done.23 = f32[24,128]{1,0:T(8,128)S(1)} collective-permute-done((f32[24,128]{1,0:T(8,128)S(1)}, f32[24,128]{1,0:T(8,128)S(1)}, u32[]{:S(2)}, u32[]{:S(2)}) %collective-permute-start.23) | collective-permute-done | bytes 12320 | tf_op jit(solution)/shard_map/ppermute | solution.py:82
  103.7 2.5 %collective-permute-done.24 = f32[24,128]{1,0:T(8,128)S(1)} collective-permute-done((f32[24,128]{1,0:T(8,128)S(1)}, f32[24,128]{1,0:T(8,128)S(1)}, u32[]{:S(2)}, u32[]{:S(2)}) %collective-permute-start.24) | collective-permute-done | bytes 12320 | tf_op jit(solution)/shard_map/ppermute | solution.py:82
  106.2 2.3 %shard_map.117 = (f32[1,1,1,4,3,256]{5,4,3,2,1,0:T(4,128)S(1)}, f32[2,4,4]{2,1,0:T(4,128)}, f32[2,4,4]{2,1,0:T(4,128)}) custom-call(f32[24,256]{1,0:T(8,128)S(1)} %get-tuple-element.22.own_ref.start_ref, f32[24,256]{1,0:T(8,128)S(1)} %get-tuple-element.26.own_ref.first_ref, f32[24,256]{1,0:T(8,128)S(1)} %get-tuple-element.39.second_ref, ...), custom_call_target="tpu_custom_call" | custom-call | tf_op jit(solution)/shard_map/pallas_call | solution.py:692
  (73 shorter events, 11.8 us)
Async XLA Ops:
  0.6 0.8 copy-start.4
  1.4 0.7 copy-start.1
  2.2 6.5 %collective-permute-start.1 = (f32[24,128]{1,0:T(8,128)S(1)}, f32[24,128]{1,0:T(8,128)S(1)}, u32[]{:S(2)}, u32[]{:S(2)}) collective-permute-start(f32[24,128]{1,0:T(8,128)S(1)} %get-tuple-element.23), channel_id=1, source_target_pairs={{0,24},{8,0},{16,8},{24,16},{1,25},{9,1},{17,9},{25,17},{2,26},{10... | collective-permute-start | bytes 36872 | tf_op jit(solution)/shard_map/ppermute | solution.py:37
  7.3 5.5 %collective-permute-start = (f32[24,128]{1,0:T(8,128)S(1)}, f32[24,128]{1,0:T(8,128)S(1)}, u32[]{:S(2)}, u32[]{:S(2)}) collective-permute-start(f32[24,128]{1,0:T(8,128)S(1)} %get-tuple-element.23), channel_id=1, source_target_pairs={{0,8},{8,16},{16,24},{24,0},{1,9},{9,17},{17,25},{25,1},{2,10},{10... | collective-permute-start | bytes 36872 | tf_op jit(solution)/shard_map/ppermute | solution.py:36
  12.8 1.6 %collective-permute-start.3 = (f32[24,256]{1,0:T(8,128)S(1)}, f32[24,256]{1,0:T(8,128)S(1)}, u32[]{:S(2)}, u32[]{:S(2)}) collective-permute-start(f32[24,256]{1,0:T(8,128)S(1)} %pad_maximum_fusion.2), channel_id=1, source_target_pairs={{0,6},{2,0},{4,2},{6,4},{1,7},{3,1},{5,3},{7,5},{8,14},{10,8},{12,... | collective-permute-start | bytes 73736 | tf_op jit(solution)/shard_map/ppermute | solution.py:37
  12.9 3.5 %collective-permute-start.2 = (f32[24,256]{1,0:T(8,128)S(1)}, f32[24,256]{1,0:T(8,128)S(1)}, u32[]{:S(2)}, u32[]{:S(2)}) collective-permute-start(f32[24,256]{1,0:T(8,128)S(1)} %pad_maximum_fusion.2), channel_id=1, source_target_pairs={{0,2},{2,4},{4,6},{6,0},{1,3},{3,5},{5,7},{7,1},{8,10},{10,12},{12... | collective-permute-start | bytes 73736 | tf_op jit(solution)/shard_map/ppermute | solution.py:36
  16.5 1.6 %copy-start.2 = (s32[1,1,1,6,256]{4,2,3,1,0:T(1,128)S(1)}, s32[1,1,1,6,256]{4,2,3,1,0:T(1,128)}, u32[]{:S(2)}) copy-start(s32[1,1,1,6,256]{4,2,3,1,0:T(1,128)} %param.12) | copy-start | bytes 18436
  16.5 4.2 %collective-permute-start.4 = (f32[24,512]{1,0:T(8,128)S(1)}, f32[24,512]{1,0:T(8,128)S(1)}, u32[]{:S(2)}, u32[]{:S(2)}) collective-permute-start(f32[24,512]{1,0:T(8,128)S(1)} %pad_maximum_fusion), channel_id=1, source_target_pairs={{0,1},{1,0},{2,3},{3,2},{4,5},{5,4},{6,7},{7,6},{8,9},{9,8},{10,11... | collective-permute-start | bytes 147464 | tf_op jit(solution)/shard_map/ppermute | solution.py:35
  18.1 0.7 copy-start.5
  18.9 0.7 copy-start.6
  19.5 0.7 copy-start.3
  20.2 0.8 copy-start
  36.6 4.2 %collective-permute-start.5 = (f32[24,512]{1,0:T(8,128)S(1)}, f32[24,512]{1,0:T(8,128)S(1)}, u32[]{:S(2)}, u32[]{:S(2)}) collective-permute-start(f32[24,512]{1,0:T(8,128)S(1)} %slice.48), channel_id=1, source_target_pairs={{0,1},{1,0},{2,3},{3,2},{4,5},{5,4},{6,7},{7,6},{8,9},{9,8},{10,11... | collective-permute-start | bytes 147464 | tf_op jit(solution)/shard_map/ppermute | solution.py:47
  40.7 3.3 %collective-permute-start.7 = (f32[24,256]{1,0:T(8,128)S(1)}, f32[24,256]{1,0:T(8,128)S(1)}, u32[]{:S(2)}, u32[]{:S(2)}) collective-permute-start(f32[24,256]{1,0:T(8,128)S(1)} %slice_add_fusion.1), channel_id=1, source_target_pairs={{0,2},{2,4},{4,6},{6,0},{1,3},{3,5},{5,7},{7,1},{8,10},{10,12},{12... | collective-permute-start | bytes 73736 | tf_op jit(solution)/shard_map/ppermute | solution.py:49
  40.7 3.3 %collective-permute-start.6 = (f32[24,256]{1,0:T(8,128)S(1)}, f32[24,256]{1,0:T(8,128)S(1)}, u32[]{:S(2)}, u32[]{:S(2)}) collective-permute-start(f32[24,256]{1,0:T(8,128)S(1)} %slice_add_fusion.1), channel_id=1, source_target_pairs={{0,6},{2,0},{4,2},{6,4},{1,7},{3,1},{5,3},{7,5},{8,14},{10,8},{12,... | collective-permute-start | bytes 73736 | tf_op jit(solution)/shard_map/ppermute | solution.py:48
  44.0 5.5 %collective-permute-start.9 = (f32[24,128]{1,0:T(8,128)S(1)}, f32[24,128]{1,0:T(8,128)S(1)}, u32[]{:S(2)}, u32[]{:S(2)}) collective-permute-start(f32[24,128]{1,0:T(8,128)S(1)} %slice_add_fusion.5), channel_id=1, source_target_pairs={{0,8},{8,16},{16,24},{24,0},{1,9},{9,17},{17,25},{25,1},{2,10},{10... | collective-permute-start | bytes 36872 | tf_op jit(solution)/shard_map/ppermute | solution.py:49
  44.1 5.5 %collective-permute-start.8 = (f32[24,128]{1,0:T(8,128)S(1)}, f32[24,128]{1,0:T(8,128)S(1)}, u32[]{:S(2)}, u32[]{:S(2)}) collective-permute-start(f32[24,128]{1,0:T(8,128)S(1)} %slice_add_fusion.5), channel_id=1, source_target_pairs={{0,24},{8,0},{16,8},{24,16},{1,25},{9,1},{17,9},{25,17},{2,26},{10... | collective-permute-start | bytes 36872 | tf_op jit(solution)/shard_map/ppermute | solution.py:48
  49.9 5.3 %collective-permute-start.11 = (f32[24,128]{1,0:T(8,128)S(1)}, f32[24,128]{1,0:T(8,128)S(1)}, u32[]{:S(2)}, u32[]{:S(2)}) collective-permute-start(f32[24,128]{1,0:T(8,128)S(1)} %get-tuple-element.27), channel_id=1, source_target_pairs={{0,24},{8,0},{16,8},{24,16},{1,25},{9,1},{17,9},{25,17},{2,26},{10... | collective-permute-start | bytes 36872 | tf_op jit(solution)/shard_map/ppermute | solution.py:37
  53.7 5.5 %collective-permute-start.10 = (f32[24,128]{1,0:T(8,128)S(1)}, f32[24,128]{1,0:T(8,128)S(1)}, u32[]{:S(2)}, u32[]{:S(2)}) collective-permute-start(f32[24,128]{1,0:T(8,128)S(1)} %get-tuple-element.27), channel_id=1, source_target_pairs={{0,8},{8,16},{16,24},{24,0},{1,9},{9,17},{17,25},{25,1},{2,10},{10... | collective-permute-start | bytes 36872 | tf_op jit(solution)/shard_map/ppermute | solution.py:36
  59.3 1.6 %collective-permute-start.13 = (f32[24,256]{1,0:T(8,128)S(1)}, f32[24,256]{1,0:T(8,128)S(1)}, u32[]{:S(2)}, u32[]{:S(2)}) collective-permute-start(f32[24,256]{1,0:T(8,128)S(1)} %pad_maximum_fusion.3), channel_id=1, source_target_pairs={{0,6},{2,0},{4,2},{6,4},{1,7},{3,1},{5,3},{7,5},{8,14},{10,8},{12,... | collective-permute-start | bytes 73736 | tf_op jit(solution)/shard_map/ppermute | solution.py:37
  59.3 3.3 %collective-permute-start.12 = (f32[24,256]{1,0:T(8,128)S(1)}, f32[24,256]{1,0:T(8,128)S(1)}, u32[]{:S(2)}, u32[]{:S(2)}) collective-permute-start(f32[24,256]{1,0:T(8,128)S(1)} %pad_maximum_fusion.3), channel_id=1, source_target_pairs={{0,2},{2,4},{4,6},{6,0},{1,3},{3,5},{5,7},{7,1},{8,10},{10,12},{12... | collective-permute-start | bytes 73736 | tf_op jit(solution)/shard_map/ppermute | solution.py:36
  62.7 4.2 %collective-permute-start.14 = (f32[24,512]{1,0:T(8,128)S(1)}, f32[24,512]{1,0:T(8,128)S(1)}, u32[]{:S(2)}, u32[]{:S(2)}) collective-permute-start(f32[24,512]{1,0:T(8,128)S(1)} %pad_maximum_fusion.1), channel_id=1, source_target_pairs={{0,1},{1,0},{2,3},{3,2},{4,5},{5,4},{6,7},{7,6},{8,9},{9,8},{10,11... | collective-permute-start | bytes 147464 | tf_op jit(solution)/shard_map/ppermute | solution.py:35
  75.7 4.2 %collective-permute-start.15 = (f32[24,512]{1,0:T(8,128)S(1)}, f32[24,512]{1,0:T(8,128)S(1)}, u32[]{:S(2)}, u32[]{:S(2)}) collective-permute-start(f32[24,512]{1,0:T(8,128)S(1)} %slice.56), channel_id=1, source_target_pairs={{0,1},{1,0},{2,3},{3,2},{4,5},{5,4},{6,7},{7,6},{8,9},{9,8},{10,11... | collective-permute-start | bytes 147464 | tf_op jit(solution)/shard_map/ppermute | solution.py:47
  79.9 3.3 %collective-permute-start.17 = (f32[24,256]{1,0:T(8,128)S(1)}, f32[24,256]{1,0:T(8,128)S(1)}, u32[]{:S(2)}, u32[]{:S(2)}) collective-permute-start(f32[24,256]{1,0:T(8,128)S(1)} %slice_add_fusion), channel_id=1, source_target_pairs={{0,2},{2,4},{4,6},{6,0},{1,3},{3,5},{5,7},{7,1},{8,10},{10,12},{12... | collective-permute-start | bytes 73736 | tf_op jit(solution)/shard_map/ppermute | solution.py:49
  79.9 3.3 %collective-permute-start.16 = (f32[24,256]{1,0:T(8,128)S(1)}, f32[24,256]{1,0:T(8,128)S(1)}, u32[]{:S(2)}, u32[]{:S(2)}) collective-permute-start(f32[24,256]{1,0:T(8,128)S(1)} %slice_add_fusion), channel_id=1, source_target_pairs={{0,6},{2,0},{4,2},{6,4},{1,7},{3,1},{5,3},{7,5},{8,14},{10,8},{12,... | collective-permute-start | bytes 73736 | tf_op jit(solution)/shard_map/ppermute | solution.py:48
  83.2 5.5 %collective-permute-start.19 = (f32[24,128]{1,0:T(8,128)S(1)}, f32[24,128]{1,0:T(8,128)S(1)}, u32[]{:S(2)}, u32[]{:S(2)}) collective-permute-start(f32[24,128]{1,0:T(8,128)S(1)} %slice_add_fusion.2), channel_id=1, source_target_pairs={{0,8},{8,16},{16,24},{24,0},{1,9},{9,17},{17,25},{25,1},{2,10},{10... | collective-permute-start | bytes 36872 | tf_op jit(solution)/shard_map/ppermute | solution.py:49
  83.3 5.5 %collective-permute-start.18 = (f32[24,128]{1,0:T(8,128)S(1)}, f32[24,128]{1,0:T(8,128)S(1)}, u32[]{:S(2)}, u32[]{:S(2)}) collective-permute-start(f32[24,128]{1,0:T(8,128)S(1)} %slice_add_fusion.2), channel_id=1, source_target_pairs={{0,24},{8,0},{16,8},{24,16},{1,25},{9,1},{17,9},{25,17},{2,26},{10... | collective-permute-start | bytes 36872 | tf_op jit(solution)/shard_map/ppermute | solution.py:48
  89.3 3.7 %collective-permute-start.20 = (f32[24,128]{1,0:T(8,128)S(1)}, f32[24,128]{1,0:T(8,128)S(1)}, u32[]{:S(2)}, u32[]{:S(2)}) collective-permute-start(f32[24,128]{1,0:T(8,128)S(1)} %get-tuple-element.40), channel_id=1, source_target_pairs={{0,8},{8,0},{16,24},{24,16},{1,9},{9,1},{17,25},{25,17},{2,10},{10... | collective-permute-start | bytes 36872 | tf_op jit(solution)/shard_map/ppermute | solution.py:82
  93.0 4.6 %collective-permute-start.21 = (f32[24,128]{1,0:T(8,128)S(1)}, f32[24,128]{1,0:T(8,128)S(1)}, u32[]{:S(2)}, u32[]{:S(2)}) collective-permute-start(f32[24,128]{1,0:T(8,128)S(1)} %add.426), channel_id=1, source_target_pairs={{0,16},{8,24},{16,0},{24,8},{1,17},{9,25},{17,1},{25,9},{2,18},{10... | collective-permute-start | bytes 36872 | tf_op jit(solution)/shard_map/ppermute | solution.py:82
  97.6 1.2 %collective-permute-start.22 = (f32[24,128]{1,0:T(8,128)S(1)}, f32[24,128]{1,0:T(8,128)S(1)}, u32[]{:S(2)}, u32[]{:S(2)}) collective-permute-start(f32[24,128]{1,0:T(8,128)S(1)} %add.427), channel_id=1, source_target_pairs={{0,2},{2,0},{4,6},{6,4},{1,3},{3,1},{5,7},{7,5},{8,10},{10,8},{12,... | collective-permute-start | bytes 36872 | tf_op jit(solution)/shard_map/ppermute | solution.py:82
  98.8 3.7 %collective-permute-start.23 = (f32[24,128]{1,0:T(8,128)S(1)}, f32[24,128]{1,0:T(8,128)S(1)}, u32[]{:S(2)}, u32[]{:S(2)}) collective-permute-start(f32[24,128]{1,0:T(8,128)S(1)} %add.428), channel_id=1, source_target_pairs={{0,4},{2,6},{4,0},{6,2},{1,5},{3,7},{5,1},{7,3},{8,12},{10,14},{12... | collective-permute-start | bytes 36872 | tf_op jit(solution)/shard_map/ppermute | solution.py:82
  102.5 3.7 %collective-permute-start.24 = (f32[24,128]{1,0:T(8,128)S(1)}, f32[24,128]{1,0:T(8,128)S(1)}, u32[]{:S(2)}, u32[]{:S(2)}) collective-permute-start(f32[24,128]{1,0:T(8,128)S(1)} %add.429), channel_id=1, source_target_pairs={{0,1},{1,0},{2,3},{3,2},{4,5},{5,4},{6,7},{7,6},{8,9},{9,8},{10,11... | collective-permute-start | bytes 36872 | tf_op jit(solution)/shard_map/ppermute | solution.py:82

commit v2 on v1

--- a/solution.py
+++ b/solution.py
@@ -26,6 +26,22 @@
     return (lane // ghosts // (4 >> bit)) % 2 == 1
 
 
+def pair_exchange(x, axis, distances):
+    size = lax.axis_size(axis)
+    return [lax.ppermute(x, axis, [(i, i ^ d) for i in range(size)]) for d in distances]
+
+
+def ring_sides(x, bit):
+    axis = AXES[bit]
+    size = lax.axis_size(axis)
+    if size == 4:
+        near, far = pair_exchange(x, axis, (1, 3))
+        return near, far, lax.axis_index(axis) % 2 == 1
+    above = lax.ppermute(x, axis, swap_pairs(size, -1))
+    below = lax.ppermute(x, axis, swap_pairs(size, 1))
+    return above, below, False
+
+
 def fetch_ghosts(x, bit, ghosts):
     axis = AXES[bit]
     size = lax.axis_size(axis)
@@ -33,9 +49,8 @@
         return x
     if size == 2:
         return lax.ppermute(x, axis, swap_pairs(2, 1))
-    below = lax.ppermute(x, axis, swap_pairs(size, 1))
-    above = lax.ppermute(x, axis, swap_pairs(size, -1))
-    return jnp.where(octant_bit(x.shape, bit, ghosts), below, above)
+    near, far, odd = ring_sides(x, bit)
+    return jnp.where(octant_bit(x.shape, bit, ghosts) ^ odd, far, near)
 
 
 def return_ghosts(x, bit, ghosts):
@@ -45,34 +60,27 @@
         return x
     if size == 2:
         return lax.ppermute(x, axis, swap_pairs(2, 1))
-    above = lax.ppermute(x, axis, swap_pairs(size, -1))
-    below = lax.ppermute(x, axis, swap_pairs(size, 1))
-    return jnp.where(octant_bit(x.shape, bit, ghosts), above, below)
-
-
-def halo(octants, ghosts):
-    first = fetch_ghosts(octants, 0, ghosts)
-    level = jnp.concatenate([octants, first], axis=1)
+    near, far, odd = ring_sides(x, bit)
+    return jnp.where(octant_bit(x.shape, bit, ghosts) ^ odd, near, far)
+
+
+def spread_outer(level, ghosts):
     second = fetch_ghosts(level, 1, ghosts)
     level = jnp.concatenate([level, second], axis=1)
-    third = fetch_ghosts(level, 2, ghosts)
-    return first, second, third
-
-
-def halo_back(first, second, third, ghosts):
-    width = first.shape[1]
-    got = return_ghosts(third, 2, ghosts)
-    zero_part = got[:, :width]
-    first = first + got[:, width : 2 * width]
-    second = second + got[:, 2 * width :]
+    return second, fetch_ghosts(level, 2, ghosts)
+
+
+def return_outer(terms, width, ghosts):
+    got = return_ghosts(terms[:, 3 * width :], 2, ghosts)
+    inner = got[:, :width]
+    first = terms[:, :width] + got[:, width : 2 * width]
+    second = terms[:, width : 3 * width] + got[:, 2 * width :]
     got = return_ghosts(second, 1, ghosts)
-    zero_part = zero_part + got[:, :width]
-    first = first + got[:, width:]
-    return zero_part + return_ghosts(first, 0, ghosts)
-
-
-def sum_everywhere(x):
-    for axis in AXES:
+    return inner + got[:, :width], first + got[:, width:]
+
+
+def sum_over(x, axes):
+    for axis in axes:
         size = lax.axis_size(axis)
         if size & (size - 1):
             x = lax.psum(x, axis)
@@ -99,6 +107,13 @@
     return out
 
 
+def column(line):
+    size = line.shape[1]
+    shape = (size, size)
+    same = lax.broadcasted_iota(jnp.int32, shape, 0) == lax.broadcasted_iota(jnp.int32, shape, 1)
+    return jnp.sum(jnp.where(same, line, 0.0), axis=1, keepdims=True)
+
+
 def split_rows(y, vectors):
     high = y.astype(jnp.bfloat16).astype(jnp.float32)
     return high + pltpu.roll(y - high, vectors, 0)
@@ -108,17 +123,19 @@
     return y + pltpu.roll(y, GROUP - vectors, 0)
 
 
-def pack_kernel(pos_ref, spec_ref, block_ref, list_ref, own_ref, oct_ref):
-    vectors = block_ref.shape[3]
+def pack_kernel(pos_ref, spec_ref, block_ref, raw_ref, own_ref, oct_ref, list_ref):
+    vectors = block_ref.shape[4]
     atoms = pos_ref.shape[-1]
     for a in range(3):
-        parts = [block_ref[0, 0, 0, :, a, :], pos_ref[0, 0, 0, a : a + 1, :]]
+        parts = [block_ref[0, 0, 0, a], pos_ref[0, 0, 0, a : a + 1, :]]
         used = vectors + 1
         if a == 0:
             parts.append(spec_ref[0, 0].astype(jnp.float32))
             used += 1
         parts.append(jnp.zeros((GROUP - used, atoms), jnp.float32))
         own_ref[rows(a), :] = jnp.concatenate(parts, axis=0)
+    pieces = [raw_ref[n // 4, n // 2 % 2, n % 2 : n % 2 + 1, :] for n in range(8)]
+    list_ref[...] = jnp.concatenate(pieces, axis=1)
     pick_octants(own_ref, list_ref, oct_ref)
 
 
@@ -150,8 +167,8 @@
     width = 8 * ghosts
     base = atoms
     kind = 1
-    for ref in ghost_refs:
-        for j in range(ref.shape[1] // width):
+    for number, ref in enumerate(ghost_refs):
+        for j in range(number == 0, ref.shape[1] // width):
             part = ref[:, j * width : (j + 1) * width]
             if shifted:
                 row = lax.broadcasted_iota(jnp.int32, part.shape, 0)
@@ -225,7 +242,7 @@
 
 
 def finish_product(
-    idx_ref, unit_ref, inv_ref, bend_ref, acc, tdiff, scat, center, own_out, ghost_out, vectors
+    idx_ref, unit_ref, inv_ref, bend_ref, acc, tdiff, scat, center, own_out, ghost_out, vectors, gram=None
 ):
     atoms = center.shape[1]
     fanout = idx_ref.shape[1] // atoms
@@ -236,6 +253,7 @@
     def slot(k, carry):
         lanes = pl.ds(pl.multiple_of(k * atoms, LANES), atoms)
         row = lax.broadcasted_iota(jnp.int32, (GROUP, atoms), 0)
+        zero = jnp.zeros((GROUP, atoms), jnp.float32)
         outs = []
         for m in range(4):
             value = jnp.zeros((GROUP, atoms), jnp.float32)
@@ -263,6 +281,14 @@
             y = along * unit[a] + outs[1 + a] * inv + turn * diff[a] + mix[a] * tau
             y = jnp.where(row < vectors, y, 0.0)
             center[rows(a), :] -= y
+            if gram is not None:
+                gram[...] += lax.dot_general(
+                    jnp.where(row < vectors, diff[a], 0.0),
+                    jnp.concatenate([y] + [zero] * (LANES // GROUP - 1), axis=0),
+                    (((1,), (1,)), ((), ())),
+                    precision=HIGHEST,
+                    preferred_element_type=jnp.float32,
+                )
             packed.append(split_rows(y, vectors))
         packed = jnp.concatenate(packed, axis=0)
         index_row = idx_ref[:, lanes]
@@ -316,6 +342,7 @@
     env_ref,
     table,
     f2_ref,
+    read_col,
     tn,
     tdiff,
     acc,
@@ -325,14 +352,17 @@
 ):
     atoms = own_ref.shape[1]
     fanout = idx_ref.shape[1] // atoms
-    channels, species = emb_ref.shape
-    basis = rin_ref.shape[1]
+    species, channels = emb_ref.shape
+    basis = rin_ref.shape[0]
+    embeds = [column(emb_ref[s : s + 1, :]) for s in range(species)]
+    readout = column(read_ref[...])
+    read_col[...] = jnp.broadcast_to(readout, read_col.shape)
     fill_table(table, own_ref, (g1_ref, g2_ref, g3_ref), vectors, ghosts, True)
 
     def embed(kind):
-        value = emb_ref[:, 0:1]
+        value = embeds[0]
         for s in range(1, species):
-            value = jnp.where(kind == float(s), emb_ref[:, s : s + 1], value)
+            value = jnp.where(kind == float(s), embeds[s], value)
         return value
 
     own_embed = embed(own_ref[vectors + 1 : vectors + 2, :])
@@ -388,9 +418,10 @@
         b0 = sine * inv_one
         b1 = (omega * cosine - b0) * inv_one
         b2 = -(omega * omega * sine + 2.0 * b1) * inv_one
-        z = jnp.dot(
+        z = lax.dot_general(
             rin_ref[...],
             jnp.concatenate([b0, b1, b2], axis=1),
+            (((0,), (0,)), ((), ())),
             precision=HIGHEST,
             preferred_element_type=jnp.float32,
         )
@@ -437,7 +468,7 @@
         slots = range(fanout)
         f = [f_ref[here, cut(k)] for k in slots]
         f1 = [f1_ref[here, cut(k)] for k in slots]
-        read = jnp.broadcast_to(read_ref[here, :], (GROUP, LANES))
+        read = read_col[here, :]
         env = [share * sum(f)]
         for a in range(3):
             env.append(share * sum(f[k] * unit(a, k) for k in slots))
@@ -518,6 +549,7 @@
     env_ref,
     own_out,
     ghost_out,
+    gram_out,
     table,
     tn,
     tdiff,
@@ -540,6 +572,7 @@
 
     lax.fori_loop(0, fanout, slot, 0)
     acc[...] = jnp.zeros_like(acc)
+    gram_out[...] = jnp.zeros_like(gram_out)
     halves = atoms // LANES
 
     def tile(number, carry):
@@ -578,7 +611,18 @@
 
     lax.fori_loop(0, (channels // GROUP) * halves, tile, 0)
     finish_product(
-        idx_ref, unit_ref, inv_ref, bend_ref, acc, tdiff, scat, center, own_out, ghost_out, vectors
+        idx_ref,
+        unit_ref,
+        inv_ref,
+        bend_ref,
+        acc,
+        tdiff,
+        scat,
+        center,
+        own_out,
+        ghost_out,
+        vectors,
+        gram_out,
     )
 
 
@@ -588,6 +632,22 @@
             own_ref[rows(a), :], sums_ref[rows(a), :], list_ref[...], vectors
         )
     pick_octants(full_ref, list_ref, oct_ref)
+
+
+def inner(x, y, pad_to=LANES):
+    pad = jnp.zeros((pad_to - y.shape[0], y.shape[1]), jnp.float32)
+    return lax.dot_general(
+        x,
+        jnp.concatenate([y, pad], axis=0),
+        (((1,), (1,)), ((), ())),
+        precision=HIGHEST,
+        preferred_element_type=jnp.float32,
+    )
+
+
+def only_vectors(x, vectors):
+    row = lax.broadcasted_iota(jnp.int32, x.shape, 0)
+    return jnp.where(row % GROUP < vectors, x, 0.0)
 
 
 def gram_kernel(vectors, start_ref, first_ref, own_ref, sums_ref, list_ref, full_ref, gram_ref):
@@ -596,17 +656,133 @@
         second = add_octants(own_ref[rows(a), :], sums_ref[rows(a), :], list_ref[...], vectors)
         full_ref[rows(a), :] = second
         stack = jnp.concatenate([start_ref[rows(a), :], first_ref[rows(a), :], second], axis=0)
-        row = lax.broadcasted_iota(jnp.int32, stack.shape, 0)
-        stack = jnp.where(row % GROUP < vectors, stack, 0.0)
-        pad = jnp.zeros((gram_ref.shape[1] - stack.shape[0], stack.shape[1]), jnp.float32)
-        total += lax.dot_general(
-            stack,
-            jnp.concatenate([stack, pad], axis=0),
-            (((1,), (1,)), ((), ())),
-            precision=HIGHEST,
-            preferred_element_type=jnp.float32,
-        )
+        stack = only_vectors(stack, vectors)
+        total += inner(stack, stack)
     gram_ref[...] = total
+
+
+def packet_start(vectors, own_ref, sums_ref, ghost_ref, list_ref, part_ref, packet_ref):
+    width = list_ref.shape[1]
+    for a in range(3):
+        part_ref[rows(a), :] = add_octants(
+            own_ref[rows(a), :], sums_ref[rows(a), :], list_ref[...], vectors
+        )
+    mark = vectors + 1
+    for j in range(width // LANES):
+        cut = slice(j * LANES, (j + 1) * LANES)
+        for a in range(3):
+            value = gather_lanes(part_ref, list_ref[:, cut], a)
+            if a == 0:
+                row = lax.broadcasted_iota(jnp.int32, value.shape, 0)
+                value = jnp.where(row == mark, list_ref[:, cut].astype(jnp.float32), value)
+            packet_ref[rows(a), cut] = value
+    packet_ref[:, width : 2 * width] = ghost_ref[...]
+
+
+def arriving(side, packets, n, a, width):
+    cut = slice(width, 2 * width)
+    after, before = packets[(n + 1) % 4], packets[(n + 3) % 4]
+    return jnp.where(side > 0.5, after[rows(a), cut], before[rows(a), cut])
+
+
+def packet_lists(packet, vectors, width):
+    mark = vectors + 1
+    return packet[mark : mark + 1, :width].astype(jnp.int32)
+
+
+def start_kernel(vectors, own_ref, sums_ref, ghost_ref, list_ref, part_ref, packet_ref):
+    packet_start(vectors, own_ref, sums_ref, ghost_ref, list_ref, part_ref, packet_ref)
+
+
+def merge_kernel(
+    vectors, side_ref, part_ref, p0_ref, p1_ref, p2_ref, p3_ref, full_ref, level_ref, spread
+):
+    width = p0_ref.shape[1] // 2
+    side = side_ref[...]
+    packets = (p0_ref, p1_ref, p2_ref, p3_ref)
+    lists = [packet_lists(p, vectors, width) for p in packets]
+    for a in range(3):
+        full_ref[rows(a), :] = add_octants(
+            part_ref[rows(a), :], arriving(side, packets, 0, a, width), lists[0], vectors
+        )
+    near = []
+    for n in (1, 3):
+        for a in range(3):
+            zero = jnp.zeros((GROUP, part_ref.shape[1]), jnp.float32)
+            spread[rows(a), :] = add_octants(
+                zero, arriving(side, packets, n, a, width), lists[n], vectors
+            )
+        values = []
+        for a in range(3):
+            pieces = [
+                gather_lanes(spread, lists[n][:, j * LANES : (j + 1) * LANES], a)
+                for j in range(width // LANES)
+            ]
+            values.append(packets[n][rows(a), :width] + jnp.concatenate(pieces, axis=1))
+        near.append(values)
+    for a in range(3):
+        for j in range(width // LANES):
+            cut = slice(j * LANES, (j + 1) * LANES)
+            level_ref[rows(a), cut] = gather_lanes(full_ref, lists[0][:, cut], a)
+        level_ref[rows(a), width : 2 * width] = jnp.where(side > 0.5, near[1][a], near[0][a])
+
+
+def gram_start_kernel(
+    vectors,
+    start_ref,
+    first_ref,
+    own_ref,
+    sums_ref,
+    ghost_ref,
+    list_ref,
+    edge_ref,
+    part_ref,
+    packet_ref,
+):
+    packet_start(vectors, own_ref, sums_ref, ghost_ref, list_ref, part_ref, packet_ref)
+    width = list_ref.shape[1]
+    total = jnp.zeros((3 * GROUP, LANES), jnp.float32)
+    for a in range(3):
+        stack = jnp.concatenate(
+            [start_ref[rows(a), :], first_ref[rows(a), :], part_ref[rows(a), :]], axis=0
+        )
+        stack = only_vectors(stack, vectors)
+        total += inner(stack, stack)
+    edge = pltpu.roll(edge_ref[...], 2 * GROUP, 1)
+    lane = lax.broadcasted_iota(jnp.int32, edge.shape, 1)
+    cut = slice(2 * width, 2 * width + LANES)
+    packet_ref[rows(0), cut] = total[rows(0)]
+    packet_ref[rows(1), cut] = jnp.where(lane // GROUP == 2, edge, total[rows(1)])
+    packet_ref[rows(2), cut] = total[rows(2)]
+
+
+def gram_merge_kernel(
+    vectors, side_ref, part_ref, p0_ref, p1_ref, p2_ref, p3_ref, full_ref, gram_ref
+):
+    width = (p0_ref.shape[1] - LANES) // 2
+    side = side_ref[...]
+    packets = (p0_ref, p1_ref, p2_ref, p3_ref)
+    shares = []
+    for n in range(4):
+        lists = packet_lists(packets[n], vectors, width)
+        extra = jnp.zeros((GROUP, LANES), jnp.float32)
+        for a in range(3):
+            terms = only_vectors(arriving(side, packets, n, a, width), vectors)
+            values = only_vectors(packets[n][rows(a), :width], vectors)
+            zero = jnp.zeros((GROUP, part_ref.shape[1]), jnp.float32)
+            spread = only_vectors(add_octants(zero, terms, lists, vectors), vectors)
+            extra += inner(terms, values) + inner(values, terms) + inner(spread, spread)
+            if n == 0:
+                full_ref[rows(a), :] = part_ref[rows(a), :] + spread
+        share = packets[n][:, 2 * width : 2 * width + LANES]
+        shares.append((share, pltpu.roll(extra, 2 * GROUP, 1)))
+
+    def add(x, y):
+        return x[0] + y[0], x[1] + y[1]
+
+    share, extra = add(add(shares[0], shares[1]), add(shares[2], shares[3]))
+    gram_ref[0 : 2 * GROUP, :] = share[0 : 2 * GROUP]
+    gram_ref[rows(2), :] = share[rows(2)] + extra
 
 
 def last_kernel(
@@ -650,8 +826,8 @@
         return upper, inverse
 
     ss, su, uu = block(0, 0), block(0, 1), block(1, 1)
-    sq, uq, qq = block(0, 2), block(1, 2), block(2, 2)
-    qu = block(2, 1)
+    uq, qq = block(1, 2), block(2, 2)
+    sq, qu = uu, uq
     _, p0 = factor(ss)
     p0t = flip(p0)
     a1 = mul(mul(p0, su), p0t)
@@ -685,13 +861,14 @@
                 line = GROUP * comp + w
                 term = weight[:, w : w + 1] * ref[line : line + 1, :]
                 value = term if value is None else value + term
-        next_ref[0, 0, 0, :, comp, :] = value[:vectors]
+        next_ref[0, 0, 0, comp] = value[:vectors]
 
 
 def call(body, outs, args, scratch=()):
+    outs = [shape if isinstance(shape[0], tuple) else (shape, jnp.float32) for shape in outs]
     return pl.pallas_call(
         body,
-        out_shape=[jax.ShapeDtypeStruct(shape, jnp.float32) for shape in outs],
+        out_shape=[jax.ShapeDtypeStruct(shape, kind) for shape, kind in outs],
         in_specs=[pl.BlockSpec(memory_space=pltpu.VMEM)] * len(args),
         out_specs=[pl.BlockSpec(memory_space=pltpu.VMEM)] * len(outs),
         scratch_shapes=[pltpu.VMEM(shape, jnp.float32) for shape in scratch],
@@ -740,17 +917,25 @@
     width = 8 * ghosts
     high = 3 * GROUP
     edges = fanout * atoms
-    lists = ghost_lists.reshape(1, width)
     index = table_index(neighbors.reshape(1, -1), atoms, ghosts)
     table_width = atoms + 7 * width
     tiles = table_width // LANES
-
-    own, octants = call(
+    ring = lax.axis_size("gx") == 4
+    side = (octant_bit((GROUP, width), 0, ghosts) ^ (lax.axis_index("gx") % 2 == 1)).astype(
+        jnp.float32
+    )
+
+    own, octants, lists = call(
         pack_kernel,
-        [(high, atoms), (high, width)],
-        (positions, species, start_block, lists),
+        [(high, atoms), (high, width), ((1, width), jnp.int32)],
+        (positions, species, start_block.transpose(0, 1, 2, 4, 3, 5), ghost_lists),
     )
-    ghost_parts = halo(octants, ghosts)
+
+    def spread(level):
+        if level.shape[1] == width:
+            level = jnp.concatenate([level, fetch_ghosts(level, 0, ghosts)], axis=1)
+        return (level,) + spread_outer(level, ghosts)
+
     shared = [
         (vectors * 4 * GROUP, edges),
         (4 * GROUP, edges),
@@ -771,42 +956,69 @@
     results = call(
         functools.partial(first_kernel, ghosts, vectors),
         [(high, atoms), (high, 7 * width)] + saved_shapes,
-        (index, own) + ghost_parts
-        + (embedding.T, radial_in.T, radial_out.T, readout.reshape(-1, 1)),
-        [(high, table_width), (channels, edges)] + shared + [(8 * GROUP, edges)] + tail,
+        (index, own)
+        + spread(octants)
+        + (embedding, radial_in, radial_out.T, readout.reshape(1, -1)),
+        [(high, table_width), (channels, edges), (channels, LANES)]
+        + shared
+        + [(8 * GROUP, edges)]
+        + tail,
     )
     own_terms, ghost_terms, saved = results[0], results[1], results[2:]
 
-    def back(terms):
-        return halo_back(
-            terms[:, :width], terms[:, width : 3 * width], terms[:, 3 * width :], ghosts
-        )
-
-    first, octants = call(
-        functools.partial(middle_kernel, vectors),
-        [(high, atoms), (high, width)],
-        (own_terms, back(ghost_terms), lists),
-    )
-    ghost_parts = halo(octants, ghosts)
-    own_terms, ghost_terms = call(
+    sums, beside = return_outer(ghost_terms, width, ghosts)
+    if ring:
+        part, packet = call(
+            functools.partial(start_kernel, vectors),
+            [(high, atoms), (high, 2 * width)],
+            (own_terms, sums, beside, lists),
+        )
+        others = pair_exchange(packet, "gx", (1, 2, 3))
+        first, level = call(
+            functools.partial(merge_kernel, vectors),
+            [(high, atoms), (high, 2 * width)],
+            (side, part, packet, *others),
+            [(high, atoms)],
+        )
+    else:
+        first, level = call(
+            functools.partial(middle_kernel, vectors),
+            [(high, atoms), (high, width)],
+            (own_terms, sums + return_ghosts(beside, 0, ghosts), lists),
+        )
+    own_terms, ghost_terms, edge_gram = call(
         functools.partial(second_kernel, ghosts, vectors),
-        [(high, atoms), (high, 7 * width)],
-        (index, first) + ghost_parts + tuple(saved),
+        [(high, atoms), (high, 7 * width), (GROUP, LANES)],
+        (index, first) + spread(level) + tuple(saved),
         [(high, table_width)] + shared + tail,
     )
-    second, gram = call(
-        functools.partial(gram_kernel, vectors),
-        [(high, atoms), (high, LANES)],
-        (own, first, own_terms, back(ghost_terms), lists),
+    sums, beside = return_outer(ghost_terms, width, ghosts)
+    if ring:
+        part, packet = call(
+            functools.partial(gram_start_kernel, vectors),
+            [(high, atoms), (high, 2 * width + LANES)],
+            (own, first, own_terms, sums, beside, lists, edge_gram),
+        )
+        others = pair_exchange(packet, "gx", (1, 2, 3))
+        second, gram = call(
+            functools.partial(gram_merge_kernel, vectors),
+            [(high, atoms), (high, LANES)],
+            (side, part, packet, *others),
+        )
+        gram = sum_over(gram, AXES[1:])
+    else:
+        second, gram = call(
+            functools.partial(gram_kernel, vectors),
+            [(high, atoms), (high, LANES)],
+            (own, first, own_terms, sums + return_ghosts(beside, 0, ghosts), lists),
+        )
+        gram = sum_over(gram, AXES)
+    following, diagonal, off = call(
+        functools.partial(last_kernel, vectors, scale),
+        [(1, 1, 1, 3, vectors, atoms), (2, vectors, vectors), (2, vectors, vectors)],
+        (own, first, second, gram),
     )
-    gram = sum_everywhere(gram)
-    return tuple(
-        call(
-            functools.partial(last_kernel, vectors, scale),
-            [(1, 1, 1, vectors, 3, atoms), (2, vectors, vectors), (2, vectors, vectors)],
-            (own, first, second, gram),
-        )
-    )
+    return following.transpose(0, 1, 2, 4, 3, 5), diagonal, off
 
 
 def solution(mesh):

time: 109 us -> 96 us (0.88)
  waiting for transfers between devices: 44 us -> 33.4 us
  starting transfers between devices: 31.7 us -> 28.7 us
  Pallas kernels: 27.6 us -> 29.5 us
  local copies, waits for them, and re-layouts: 4.41 us -> 2.78 us
    ppermute x21 -> x19, waiting for transfers between devices: 35.1 us -> 23.4 us  [the longest x16 17.5 us: pair_exchange(): lax.ppermute(x, axis, [(i, i ^ d) for i in range(size)])]
    ppermute x21 -> x19, starting transfers between devices: 26.3 us -> 22.4 us  [the longest x16 19.7 us: pair_exchange(): lax.ppermute(x, axis, [(i, i ^ d) for i in range(size)])]
    pallas_call x6 -> x8, Pallas kernels: 27.6 us -> 29.5 us  [call(): pl.pallas_call(body, out_shape=[jax.ShapeDtypeStruct(shape, kind) for sha...]
    ppermute x2, waiting for transfers between devices: 3.21 us -> 4.88 us  [fetch_ghosts(): return lax.ppermute(x, axis, swap_pairs(2, 1))]
    unnamed x18 -> x17, local copies, waits for them, and re-layouts: 2.92 us -> 2.77 us
  transfers between devices with their start and end apart: 25 -> 23, of which waited for: 21 -> 18; matrix products, arithmetic and copies ran while one was open for 1% -> 0% of each run, Pallas kernels for 0% -> 0%
where the time goes in v2:
time: 96 us; the launch traced here: 95.7 us
  waiting for transfers between devices  33.4 us (35%)
  Pallas kernels  29.5 us (31%)
  starting transfers between devices  28.7 us (30%)
  local copies, waits for them, and re-layouts  2.78 us (3%)
    pallas_call x8, Pallas kernels, call(): pl.pallas_call(body, out_shape=[jax.ShapeDtypeStruct(shape, kind) for sha...  29.5 us
    ppermute x16, starting transfers between devices, pair_exchange(): lax.ppermute(x, axis, [(i, i ^ d) for i in range(size)])  19.7 us
    ppermute x16, waiting for transfers between devices, pair_exchange(): lax.ppermute(x, axis, [(i, i ^ d) for i in range(size)])  17.5 us
    ppermute x3, waiting for transfers between devices, sum_over(): x = x + lax.ppermute(x, axis, [(i, i ^ step) for i in range(size)])  5.88 us
    ppermute x2, waiting for transfers between devices, return_ghosts(): return lax.ppermute(x, axis, swap_pairs(2, 1))  5.14 us
    ppermute x2, waiting for transfers between devices, fetch_ghosts(): return lax.ppermute(x, axis, swap_pairs(2, 1))  4.88 us
    ppermute x2, starting transfers between devices, fetch_ghosts(): return lax.ppermute(x, axis, swap_pairs(2, 1))  3.17 us
    ppermute x2, starting transfers between devices, return_ghosts(): return lax.ppermute(x, axis, swap_pairs(2, 1))  3.17 us
  transfers between devices with their start and end apart: 23, of which 18 were waited for; matrix products, arithmetic and copies ran while one was open for 0% of the time, Pallas kernels for 0%

profile of v2, /device:TPU:0, one launch (start us, length us, event | category | flops | bytes accessed | tf_op | source)
XLA Modules:
  0.0 95.7 jit_solution(15432929527353972743)
XLA Ops:
  2.9 5.1 %collective-permute-start = (f32[24,128]{1,0:T(8,128)S(1)}, f32[24,128]{1,0:T(8,128)S(1)}, u32[]{:S(2)}, u32[]{:S(2)}) collective-permute-start(f32[24,128]{1,0:T(8,128)S(1)} %get-tuple-element.32), channel_id=1, source_target_pairs={{0,24},{8,16},{16,8},{24,0},{1,25},{9,17},{17,9},{25,1},{2,26},{10... | collective-permute-start | bytes 36872 | tf_op jit(solution)/shard_map/ppermute | solution.py:31
  8.0 1.6 %collective-permute-done = f32[24,128]{1,0:T(8,128)S(1)} collective-permute-done((f32[24,128]{1,0:T(8,128)S(1)}, f32[24,128]{1,0:T(8,128)S(1)}, u32[]{:S(2)}, u32[]{:S(2)}) %collective-permute-start) | collective-permute-done | bytes 12320 | tf_op jit(solution)/shard_map/ppermute | solution.py:31
  9.6 2.0 %collective-permute-done.1 = f32[24,128]{1,0:T(8,128)S(1)} collective-permute-done((f32[24,128]{1,0:T(8,128)S(1)}, f32[24,128]{1,0:T(8,128)S(1)}, u32[]{:S(2)}, u32[]{:S(2)}) %collective-permute-start.1) | collective-permute-done | bytes 12320 | tf_op jit(solution)/shard_map/ppermute | solution.py:31
  11.8 1.6 %collective-permute-start.3 = (f32[24,256]{1,0:T(8,128)S(1)}, f32[24,256]{1,0:T(8,128)S(1)}, u32[]{:S(2)}, u32[]{:S(2)}) collective-permute-start(f32[24,256]{1,0:T(8,128)S(1)} %pad_maximum_fusion.2.g1_ref), channel_id=1, source_target_pairs={{0,2},{2,0},{4,6},{6,4},{1,3},{3,1},{5,7},{7,5},{8,10},{10,8},{12,... | collective-permute-start | bytes 73736 | tf_op jit(solution)/shard_map/ppermute | solution.py:31
  13.4 1.9 %collective-permute-done.2 = f32[24,256]{1,0:T(8,128)S(1)} collective-permute-done((f32[24,256]{1,0:T(8,128)S(1)}, f32[24,256]{1,0:T(8,128)S(1)}, u32[]{:S(2)}, u32[]{:S(2)}) %collective-permute-start.2) | collective-permute-done | bytes 24608 | tf_op jit(solution)/shard_map/ppermute | solution.py:31
  15.3 1.6 %collective-permute-start.4 = (f32[24,512]{1,0:T(8,128)S(1)}, f32[24,512]{1,0:T(8,128)S(1)}, u32[]{:S(2)}, u32[]{:S(2)}) collective-permute-start(f32[24,512]{1,0:T(8,128)S(1)} %pad_maximum_fusion), channel_id=1, source_target_pairs={{0,1},{1,0},{2,3},{3,2},{4,5},{5,4},{6,7},{7,6},{8,9},{9,8},{10,11... | collective-permute-start | bytes 147464 | tf_op jit(solution)/shard_map/ppermute | solution.py:51
  17.1 2.3 %collective-permute-done.4.g3_ref = f32[24,512]{1,0:T(8,128)S(1)} collective-permute-done((f32[24,512]{1,0:T(8,128)S(1)}, f32[24,512]{1,0:T(8,128)S(1)}, u32[]{:S(2)}, u32[]{:S(2)}) %collective-permute-start.4) | collective-permute-done | bytes 49184 | tf_op jit(solution)/shard_map/ppermute | solution.py:51
  20.1 15.2 %shard_map.113 = (f32[24,256]{1,0:T(8,128)S(1)}, f32[24,896]{1,0:T(8,128)S(1)}, f32[24,1536]{1,0:T(8,128)S(1)}, f32[8,1536]{1,0:T(8,128)S(1)}, f32[8,1536]{1,0:T...) custom-call(s32[1,1536]{1,0:T(1,128)S(1)} %compare_select_fusion.idx, ...), custom_call_target="tpu_custom_call" | custom-call | tf_op jit(solution)/shard_map/pallas_call | solution.py:869
  35.3 1.6 %collective-permute-start.5 = (f32[24,512]{1,0:T(8,128)S(1)}, f32[24,512]{1,0:T(8,128)S(1)}, u32[]{:S(2)}, u32[]{:S(2)}) collective-permute-start(f32[24,512]{1,0:T(8,128)S(1)} %slice.48), channel_id=1, source_target_pairs={{0,1},{1,0},{2,3},{3,2},{4,5},{5,4},{6,7},{7,6},{8,9},{9,8},{10,11... | collective-permute-start | bytes 147464 | tf_op jit(solution)/shard_map/ppermute | solution.py:62
  36.9 2.6 %collective-permute-done.5 = f32[24,512]{1,0:T(8,128)S(1)} collective-permute-done((f32[24,512]{1,0:T(8,128)S(1)}, f32[24,512]{1,0:T(8,128)S(1)}, u32[]{:S(2)}, u32[]{:S(2)}) %collective-permute-start.5) | collective-permute-done | bytes 49184 | tf_op jit(solution)/shard_map/ppermute | solution.py:62
  39.5 1.4 %collective-permute-start.7 = (f32[24,256]{1,0:T(8,128)S(1)}, f32[24,256]{1,0:T(8,128)S(1)}, u32[]{:S(2)}, u32[]{:S(2)}) collective-permute-start(f32[24,256]{1,0:T(8,128)S(1)} %slice_add_fusion.1), channel_id=1, source_target_pairs={{0,6},{2,4},{4,2},{6,0},{1,7},{3,5},{5,3},{7,1},{8,14},{10,12},{12... | collective-permute-start | bytes 73736 | tf_op jit(solution)/shard_map/ppermute | solution.py:31
  40.9 1.9 %collective-permute-done.7 = f32[24,256]{1,0:T(8,128)S(1)} collective-permute-done((f32[24,256]{1,0:T(8,128)S(1)}, f32[24,256]{1,0:T(8,128)S(1)}, u32[]{:S(2)}, u32[]{:S(2)}) %collective-permute-start.7) | collective-permute-done | bytes 24608 | tf_op jit(solution)/shard_map/ppermute | solution.py:31
  43.1 1.8 %collective-permute-start.10 = (f32[24,256]{1,0:T(8,128)S(1)}, f32[24,256]{1,0:T(8,128)S(1)}, u32[]{:S(2)}, u32[]{:S(2)}) collective-permute-start(f32[24,256]{1,0:T(8,128)S(1)} %get-tuple-element.37.p0_ref), channel_id=1, source_target_pairs={{0,24},{8,16},{16,8},{24,0},{1,25},{9,17},{17,9},{25,1},{2,26},{10... | collective-permute-start | bytes 73736 | tf_op jit(solution)/shard_map/ppermute | solution.py:31
  44.9 2.6 %collective-permute-start.9 = (f32[24,256]{1,0:T(8,128)S(1)}, f32[24,256]{1,0:T(8,128)S(1)}, u32[]{:S(2)}, u32[]{:S(2)}) collective-permute-start(f32[24,256]{1,0:T(8,128)S(1)} %get-tuple-element.37.p0_ref), channel_id=1, source_target_pairs={{0,16},{8,24},{16,0},{24,8},{1,17},{9,25},{17,1},{25,9},{2,18},{10... | collective-permute-start | bytes 73736 | tf_op jit(solution)/shard_map/ppermute | solution.py:31
  47.5 1.3 %collective-permute-done.10.p3_ref = f32[24,256]{1,0:T(8,128)S(1)} collective-permute-done((f32[24,256]{1,0:T(8,128)S(1)}, f32[24,256]{1,0:T(8,128)S(1)}, u32[]{:S(2)}, u32[]{:S(2)}) %collective-permute-start.10) | collective-permute-done | bytes 24608 | tf_op jit(solution)/shard_map/ppermute | solution.py:31
  50.1 1.3 %collective-permute-start.12 = (f32[24,256]{1,0:T(8,128)S(1)}, f32[24,256]{1,0:T(8,128)S(1)}, u32[]{:S(2)}, u32[]{:S(2)}) collective-permute-start(f32[24,256]{1,0:T(8,128)S(1)} %get-tuple-element.39.g1_ref), channel_id=1, source_target_pairs={{0,2},{2,0},{4,6},{6,4},{1,3},{3,1},{5,7},{7,5},{8,10},{10,8},{12,... | collective-permute-start | bytes 73736 | tf_op jit(solution)/shard_map/ppermute | solution.py:31
  51.4 2.0 %collective-permute-done.11 = f32[24,256]{1,0:T(8,128)S(1)} collective-permute-done((f32[24,256]{1,0:T(8,128)S(1)}, f32[24,256]{1,0:T(8,128)S(1)}, u32[]{:S(2)}, u32[]{:S(2)}) %collective-permute-start.11) | collective-permute-done | bytes 24608 | tf_op jit(solution)/shard_map/ppermute | solution.py:31
  53.4 1.6 %collective-permute-start.13 = (f32[24,512]{1,0:T(8,128)S(1)}, f32[24,512]{1,0:T(8,128)S(1)}, u32[]{:S(2)}, u32[]{:S(2)}) collective-permute-start(f32[24,512]{1,0:T(8,128)S(1)} %pad_maximum_fusion.1), channel_id=1, source_target_pairs={{0,1},{1,0},{2,3},{3,2},{4,5},{5,4},{6,7},{7,6},{8,9},{9,8},{10,11... | collective-permute-start | bytes 147464 | tf_op jit(solution)/shard_map/ppermute | solution.py:51
  55.0 2.6 %collective-permute-done.13.g3_ref = f32[24,512]{1,0:T(8,128)S(1)} collective-permute-done((f32[24,512]{1,0:T(8,128)S(1)}, f32[24,512]{1,0:T(8,128)S(1)}, u32[]{:S(2)}, u32[]{:S(2)}) %collective-permute-start.13) | collective-permute-done | bytes 49184 | tf_op jit(solution)/shard_map/ppermute | solution.py:51
  57.6 9.3 %shard_map.116 = (f32[24,256]{1,0:T(8,128)S(1)}, f32[24,896]{1,0:T(8,128)S(1)}, f32[8,128]{1,0:T(8,128)S(1)}) custom-call(s32[1,1536]{1,0:T(1,128)S(1)} %compare_select_fusion.idx_ref, f32[24,256]{1,0:T(8,128)S(1)} %get-tuple-element.38.own_ref.first_ref, f32[24,256]{1,0:T(8,128)S(1)} %get-tuple-element.39.g1_ref, f32[24,256]{1,0:T(8,128)S(1)} %fusion.48.g2_ref, ...), custom_call_target="tpu_custom_call" | custom-call | tf_op jit(solution)/shard_map/pallas_call | solution.py:869
  66.9 1.6 %collective-permute-start.14 = (f32[24,512]{1,0:T(8,128)S(1)}, f32[24,512]{1,0:T(8,128)S(1)}, u32[]{:S(2)}, u32[]{:S(2)}) collective-permute-start(f32[24,512]{1,0:T(8,128)S(1)} %slice.56), channel_id=1, source_target_pairs={{0,1},{1,0},{2,3},{3,2},{4,5},{5,4},{6,7},{7,6},{8,9},{9,8},{10,11... | collective-permute-start | bytes 147464 | tf_op jit(solution)/shard_map/ppermute | solution.py:62
  68.5 2.6 %collective-permute-done.14 = f32[24,512]{1,0:T(8,128)S(1)} collective-permute-done((f32[24,512]{1,0:T(8,128)S(1)}, f32[24,512]{1,0:T(8,128)S(1)}, u32[]{:S(2)}, u32[]{:S(2)}) %collective-permute-start.14) | collective-permute-done | bytes 49184 | tf_op jit(solution)/shard_map/ppermute | solution.py:62
  71.0 1.3 %collective-permute-start.16 = (f32[24,256]{1,0:T(8,128)S(1)}, f32[24,256]{1,0:T(8,128)S(1)}, u32[]{:S(2)}, u32[]{:S(2)}) collective-permute-start(f32[24,256]{1,0:T(8,128)S(1)} %slice_add_fusion), channel_id=1, source_target_pairs={{0,6},{2,4},{4,2},{6,0},{1,7},{3,5},{5,3},{7,1},{8,14},{10,12},{12... | collective-permute-start | bytes 73736 | tf_op jit(solution)/shard_map/ppermute | solution.py:31
  72.3 2.0 %collective-permute-done.16 = f32[24,256]{1,0:T(8,128)S(1)} collective-permute-done((f32[24,256]{1,0:T(8,128)S(1)}, f32[24,256]{1,0:T(8,128)S(1)}, u32[]{:S(2)}, u32[]{:S(2)}) %collective-permute-start.16) | collective-permute-done | bytes 24608 | tf_op jit(solution)/shard_map/ppermute | solution.py:31
  74.9 2.0 %collective-permute-start.17 = (f32[24,384]{1,0:T(8,128)S(1)}, f32[24,384]{1,0:T(8,128)S(1)}, u32[]{:S(2)}, u32[]{:S(2)}) collective-permute-start(f32[24,384]{1,0:T(8,128)S(1)} %get-tuple-element.53.p0_ref), channel_id=1, source_target_pairs={{0,8},{8,0},{16,24},{24,16},{1,9},{9,1},{17,25},{25,17},{2,10},{10... | collective-permute-start | bytes 110600 | tf_op jit(solution)/shard_map/ppermute | solution.py:31
  77.5 1.8 %collective-permute-start.19 = (f32[24,384]{1,0:T(8,128)S(1)}, f32[24,384]{1,0:T(8,128)S(1)}, u32[]{:S(2)}, u32[]{:S(2)}) collective-permute-start(f32[24,384]{1,0:T(8,128)S(1)} %get-tuple-element.53.p0_ref), channel_id=1, source_target_pairs={{0,24},{8,16},{16,8},{24,0},{1,25},{9,17},{17,9},{25,1},{2,26},{10... | collective-permute-start | bytes 110600 | tf_op jit(solution)/shard_map/ppermute | solution.py:31
  79.3 3.5 %collective-permute-done.18.p2_ref = f32[24,384]{1,0:T(8,128)S(1)} collective-permute-done((f32[24,384]{1,0:T(8,128)S(1)}, f32[24,384]{1,0:T(8,128)S(1)}, u32[]{:S(2)}, u32[]{:S(2)}) %collective-permute-start.18) | collective-permute-done | bytes 36896 | tf_op jit(solution)/shard_map/ppermute | solution.py:31
  83.3 1.4 %shard_map.118 = (f32[24,256]{1,0:T(8,128)S(1)}, f32[24,128]{1,0:T(8,128)S(1)}) custom-call(f32[8,128]{1,0:T(8,128)S(1)} %fusion.45.side_ref, f32[24,256]{1,0:T(8,128)S(1)} %get-tuple-element.52.part_ref, f32[24,384]{1,0:T(8,128)S(1)} %get-tuple-element.53.p0_ref, f32[24,384]{1,0:T(8,128)S(1)} %collective-permute-done.17.p1_ref, ...), custom_call_target="tpu_custom_call" | custom-call | tf_op jit(solution)/shard_map/pallas_call | solution.py:869
  87.1 2.5 %collective-permute-done.21 = f32[24,128]{1,0:T(8,128)S(1)} collective-permute-done((f32[24,128]{1,0:T(8,128)S(1)}, f32[24,128]{1,0:T(8,128)S(1)}, u32[]{:S(2)}, u32[]{:S(2)}) %collective-permute-start.21) | collective-permute-done | bytes 12320 | tf_op jit(solution)/shard_map/ppermute | solution.py:90
  89.6 1.5 %collective-permute-start.22 = (f32[24,128]{1,0:T(8,128)S(1)}, f32[24,128]{1,0:T(8,128)S(1)}, u32[]{:S(2)}, u32[]{:S(2)}) collective-permute-start(f32[24,128]{1,0:T(8,128)S(1)} %add.404), channel_id=1, source_target_pairs={{0,1},{1,0},{2,3},{3,2},{4,5},{5,4},{6,7},{7,6},{8,9},{9,8},{10,11... | collective-permute-start | bytes 36872 | tf_op jit(solution)/shard_map/ppermute | solution.py:90
  91.1 2.2 %collective-permute-done.22 = f32[24,128]{1,0:T(8,128)S(1)} collective-permute-done((f32[24,128]{1,0:T(8,128)S(1)}, f32[24,128]{1,0:T(8,128)S(1)}, u32[]{:S(2)}, u32[]{:S(2)}) %collective-permute-start.22) | collective-permute-done | bytes 12320 | tf_op jit(solution)/shard_map/ppermute | solution.py:90
  93.3 2.5 %shard_map.119 = (f32[1,1,1,3,4,256]{5,4,3,2,1,0:T(4,128)}, f32[2,4,4]{2,1,0:T(4,128)}, f32[2,4,4]{2,1,0:T(4,128)}) custom-call(f32[24,256]{1,0:T(8,128)S(1)} %get-tuple-element.31.own_ref.start_ref, f32[24,256]{1,0:T(8,128)S(1)} %get-tuple-element.38.own_ref.first_ref, f32[24,256]{1,0:T(8,128)S(1)} %get-tuple-element.54.second_ref, f32[24,128]{1,0:T(8,128)S(1)} %add.405.gram_ref), custom_call_target="tpu_custom_call" | custom-call | tf_op jit(solution)/shard_map/pallas_call | solution.py:869
  (62 shorter events, 9.1 us)
Async XLA Ops:
  0.6 0.7 copy-start.2
  1.3 0.7 copy-start.5
  2.0 0.7 copy-start.1
  2.9 6.7 %collective-permute-start = (f32[24,128]{1,0:T(8,128)S(1)}, f32[24,128]{1,0:T(8,128)S(1)}, u32[]{:S(2)}, u32[]{:S(2)}) collective-permute-start(f32[24,128]{1,0:T(8,128)S(1)} %get-tuple-element.32), channel_id=1, source_target_pairs={{0,24},{8,16},{16,8},{24,0},{1,25},{9,17},{17,9},{25,1},{2,26},{10... | collective-permute-start | bytes 36872 | tf_op jit(solution)/shard_map/ppermute | solution.py:31
  7.9 3.7 %collective-permute-start.1 = (f32[24,128]{1,0:T(8,128)S(1)}, f32[24,128]{1,0:T(8,128)S(1)}, u32[]{:S(2)}, u32[]{:S(2)}) collective-permute-start(f32[24,128]{1,0:T(8,128)S(1)} %get-tuple-element.32), channel_id=1, source_target_pairs={{0,8},{8,0},{16,24},{24,16},{1,9},{9,1},{17,25},{25,17},{2,10},{10... | collective-permute-start | bytes 36872 | tf_op jit(solution)/shard_map/ppermute | solution.py:31
  11.7 3.5 %collective-permute-start.2 = (f32[24,256]{1,0:T(8,128)S(1)}, f32[24,256]{1,0:T(8,128)S(1)}, u32[]{:S(2)}, u32[]{:S(2)}) collective-permute-start(f32[24,256]{1,0:T(8,128)S(1)} %pad_maximum_fusion.2.g1_ref), channel_id=1, source_target_pairs={{0,6},{2,4},{4,2},{6,0},{1,7},{3,5},{5,3},{7,1},{8,14},{10,12},{12... | collective-permute-start | bytes 73736 | tf_op jit(solution)/shard_map/ppermute | solution.py:31
  11.8 3.5 %collective-permute-start.3 = (f32[24,256]{1,0:T(8,128)S(1)}, f32[24,256]{1,0:T(8,128)S(1)}, u32[]{:S(2)}, u32[]{:S(2)}) collective-permute-start(f32[24,256]{1,0:T(8,128)S(1)} %pad_maximum_fusion.2.g1_ref), channel_id=1, source_target_pairs={{0,2},{2,0},{4,6},{6,4},{1,3},{3,1},{5,7},{7,5},{8,10},{10,8},{12,... | collective-permute-start | bytes 73736 | tf_op jit(solution)/shard_map/ppermute | solution.py:31
  15.2 1.6 %copy-start.7 = (s32[1,1,1,6,256]{4,2,3,1,0:T(1,128)S(1)}, s32[1,1,1,6,256]{4,2,3,1,0:T(1,128)}, u32[]{:S(2)}) copy-start(s32[1,1,1,6,256]{4,2,3,1,0:T(1,128)} %param.12) | copy-start | bytes 18436
  15.3 4.2 %copy-start = (f32[128,64]{0,1:T(8,128)S(1)}, f32[128,64]{0,1:T(8,128)}, u32[]{:S(2)}) copy-start(f32[128,64]{0,1:T(8,128)} %param.16) | copy-start | bytes 98308
  15.3 4.2 %collective-permute-start.4 = (f32[24,512]{1,0:T(8,128)S(1)}, f32[24,512]{1,0:T(8,128)S(1)}, u32[]{:S(2)}, u32[]{:S(2)}) collective-permute-start(f32[24,512]{1,0:T(8,128)S(1)} %pad_maximum_fusion), channel_id=1, source_target_pairs={{0,1},{1,0},{2,3},{3,2},{4,5},{5,4},{6,7},{7,6},{8,9},{9,8},{10,11... | collective-permute-start | bytes 147464 | tf_op jit(solution)/shard_map/ppermute | solution.py:51
  17.1 2.3 %copy-start.3 = (f32[8,128]{1,0:T(8,128)S(1)}, f32[8,128]{1,0:T(8,128)}, u32[]{:S(2)}) copy-start(f32[8,128]{1,0:T(8,128)} %rin_ref.1) | copy-start | bytes 12292
  19.4 0.7 copy-start.4
  19.4 0.7 copy-start.6
  35.3 4.2 %collective-permute-start.5 = (f32[24,512]{1,0:T(8,128)S(1)}, f32[24,512]{1,0:T(8,128)S(1)}, u32[]{:S(2)}, u32[]{:S(2)}) collective-permute-start(f32[24,512]{1,0:T(8,128)S(1)} %slice.48), channel_id=1, source_target_pairs={{0,1},{1,0},{2,3},{3,2},{4,5},{5,4},{6,7},{7,6},{8,9},{9,8},{10,11... | collective-permute-start | bytes 147464 | tf_op jit(solution)/shard_map/ppermute | solution.py:62
  39.5 1.4 %collective-permute-start.6 = (f32[24,256]{1,0:T(8,128)S(1)}, f32[24,256]{1,0:T(8,128)S(1)}, u32[]{:S(2)}, u32[]{:S(2)}) collective-permute-start(f32[24,256]{1,0:T(8,128)S(1)} %slice_add_fusion.1), channel_id=1, source_target_pairs={{0,2},{2,0},{4,6},{6,4},{1,3},{3,1},{5,7},{7,5},{8,10},{10,8},{12,... | collective-permute-start | bytes 73736 | tf_op jit(solution)/shard_map/ppermute | solution.py:31
  39.5 3.3 %collective-permute-start.7 = (f32[24,256]{1,0:T(8,128)S(1)}, f32[24,256]{1,0:T(8,128)S(1)}, u32[]{:S(2)}, u32[]{:S(2)}) collective-permute-start(f32[24,256]{1,0:T(8,128)S(1)} %slice_add_fusion.1), channel_id=1, source_target_pairs={{0,6},{2,4},{4,2},{6,0},{1,7},{3,5},{5,3},{7,1},{8,14},{10,12},{12... | collective-permute-start | bytes 73736 | tf_op jit(solution)/shard_map/ppermute | solution.py:31
  43.1 5.7 %collective-permute-start.10 = (f32[24,256]{1,0:T(8,128)S(1)}, f32[24,256]{1,0:T(8,128)S(1)}, u32[]{:S(2)}, u32[]{:S(2)}) collective-permute-start(f32[24,256]{1,0:T(8,128)S(1)} %get-tuple-element.37.p0_ref), channel_id=1, source_target_pairs={{0,24},{8,16},{16,8},{24,0},{1,25},{9,17},{17,9},{25,1},{2,26},{10... | collective-permute-start | bytes 73736 | tf_op jit(solution)/shard_map/ppermute | solution.py:31
  44.9 4.3 %collective-permute-start.8 = (f32[24,256]{1,0:T(8,128)S(1)}, f32[24,256]{1,0:T(8,128)S(1)}, u32[]{:S(2)}, u32[]{:S(2)}) collective-permute-start(f32[24,256]{1,0:T(8,128)S(1)} %get-tuple-element.37.p0_ref), channel_id=1, source_target_pairs={{0,8},{8,0},{16,24},{24,16},{1,9},{9,1},{17,25},{25,17},{2,10},{10... | collective-permute-start | bytes 73736 | tf_op jit(solution)/shard_map/ppermute | solution.py:31
  44.9 4.7 %collective-permute-start.9 = (f32[24,256]{1,0:T(8,128)S(1)}, f32[24,256]{1,0:T(8,128)S(1)}, u32[]{:S(2)}, u32[]{:S(2)}) collective-permute-start(f32[24,256]{1,0:T(8,128)S(1)} %get-tuple-element.37.p0_ref), channel_id=1, source_target_pairs={{0,16},{8,24},{16,0},{24,8},{1,17},{9,25},{17,1},{25,9},{2,18},{10... | collective-permute-start | bytes 73736 | tf_op jit(solution)/shard_map/ppermute | solution.py:31
  50.0 3.4 %collective-permute-start.11 = (f32[24,256]{1,0:T(8,128)S(1)}, f32[24,256]{1,0:T(8,128)S(1)}, u32[]{:S(2)}, u32[]{:S(2)}) collective-permute-start(f32[24,256]{1,0:T(8,128)S(1)} %get-tuple-element.39.g1_ref), channel_id=1, source_target_pairs={{0,6},{2,4},{4,2},{6,0},{1,7},{3,5},{5,3},{7,1},{8,14},{10,12},{12... | collective-permute-start | bytes 73736 | tf_op jit(solution)/shard_map/ppermute | solution.py:31
  50.1 3.2 %collective-permute-start.12 = (f32[24,256]{1,0:T(8,128)S(1)}, f32[24,256]{1,0:T(8,128)S(1)}, u32[]{:S(2)}, u32[]{:S(2)}) collective-permute-start(f32[24,256]{1,0:T(8,128)S(1)} %get-tuple-element.39.g1_ref), channel_id=1, source_target_pairs={{0,2},{2,0},{4,6},{6,4},{1,3},{3,1},{5,7},{7,5},{8,10},{10,8},{12,... | collective-permute-start | bytes 73736 | tf_op jit(solution)/shard_map/ppermute | solution.py:31
  53.4 4.2 %collective-permute-start.13 = (f32[24,512]{1,0:T(8,128)S(1)}, f32[24,512]{1,0:T(8,128)S(1)}, u32[]{:S(2)}, u32[]{:S(2)}) collective-permute-start(f32[24,512]{1,0:T(8,128)S(1)} %pad_maximum_fusion.1), channel_id=1, source_target_pairs={{0,1},{1,0},{2,3},{3,2},{4,5},{5,4},{6,7},{7,6},{8,9},{9,8},{10,11... | collective-permute-start | bytes 147464 | tf_op jit(solution)/shard_map/ppermute | solution.py:51
  66.9 4.2 %collective-permute-start.14 = (f32[24,512]{1,0:T(8,128)S(1)}, f32[24,512]{1,0:T(8,128)S(1)}, u32[]{:S(2)}, u32[]{:S(2)}) collective-permute-start(f32[24,512]{1,0:T(8,128)S(1)} %slice.56), channel_id=1, source_target_pairs={{0,1},{1,0},{2,3},{3,2},{4,5},{5,4},{6,7},{7,6},{8,9},{9,8},{10,11... | collective-permute-start | bytes 147464 | tf_op jit(solution)/shard_map/ppermute | solution.py:62
  71.0 1.3 %collective-permute-start.15 = (f32[24,256]{1,0:T(8,128)S(1)}, f32[24,256]{1,0:T(8,128)S(1)}, u32[]{:S(2)}, u32[]{:S(2)}) collective-permute-start(f32[24,256]{1,0:T(8,128)S(1)} %slice_add_fusion), channel_id=1, source_target_pairs={{0,2},{2,0},{4,6},{6,4},{1,3},{3,1},{5,7},{7,5},{8,10},{10,8},{12,... | collective-permute-start | bytes 73736 | tf_op jit(solution)/shard_map/ppermute | solution.py:31
  71.0 3.3 %collective-permute-start.16 = (f32[24,256]{1,0:T(8,128)S(1)}, f32[24,256]{1,0:T(8,128)S(1)}, u32[]{:S(2)}, u32[]{:S(2)}) collective-permute-start(f32[24,256]{1,0:T(8,128)S(1)} %slice_add_fusion), channel_id=1, source_target_pairs={{0,6},{2,4},{4,2},{6,0},{1,7},{3,5},{5,3},{7,1},{8,14},{10,12},{12... | collective-permute-start | bytes 73736 | tf_op jit(solution)/shard_map/ppermute | solution.py:31
  74.9 4.4 %collective-permute-start.17 = (f32[24,384]{1,0:T(8,128)S(1)}, f32[24,384]{1,0:T(8,128)S(1)}, u32[]{:S(2)}, u32[]{:S(2)}) collective-permute-start(f32[24,384]{1,0:T(8,128)S(1)} %get-tuple-element.53.p0_ref), channel_id=1, source_target_pairs={{0,8},{8,0},{16,24},{24,16},{1,9},{9,1},{17,25},{25,17},{2,10},{10... | collective-permute-start | bytes 110600 | tf_op jit(solution)/shard_map/ppermute | solution.py:31
  76.9 5.9 %collective-permute-start.18 = (f32[24,384]{1,0:T(8,128)S(1)}, f32[24,384]{1,0:T(8,128)S(1)}, u32[]{:S(2)}, u32[]{:S(2)}) collective-permute-start(f32[24,384]{1,0:T(8,128)S(1)} %get-tuple-element.53.p0_ref), channel_id=1, source_target_pairs={{0,16},{8,24},{16,0},{24,8},{1,17},{9,25},{17,1},{25,9},{2,18},{10... | collective-permute-start | bytes 110600 | tf_op jit(solution)/shard_map/ppermute | solution.py:31
  77.5 5.8 %collective-permute-start.19 = (f32[24,384]{1,0:T(8,128)S(1)}, f32[24,384]{1,0:T(8,128)S(1)}, u32[]{:S(2)}, u32[]{:S(2)}) collective-permute-start(f32[24,384]{1,0:T(8,128)S(1)} %get-tuple-element.53.p0_ref), channel_id=1, source_target_pairs={{0,24},{8,16},{16,8},{24,0},{1,25},{9,17},{17,9},{25,1},{2,26},{10... | collective-permute-start | bytes 110600 | tf_op jit(solution)/shard_map/ppermute | solution.py:31
  84.7 1.2 %collective-permute-start.20 = (f32[24,128]{1,0:T(8,128)S(1)}, f32[24,128]{1,0:T(8,128)S(1)}, u32[]{:S(2)}, u32[]{:S(2)}) collective-permute-start(f32[24,128]{1,0:T(8,128)S(1)} %get-tuple-element.55), channel_id=1, source_target_pairs={{0,2},{2,0},{4,6},{6,4},{1,3},{3,1},{5,7},{7,5},{8,10},{10,8},{12,... | collective-permute-start | bytes 36872 | tf_op jit(solution)/shard_map/ppermute | solution.py:90
  85.9 3.7 %collective-permute-start.21 = (f32[24,128]{1,0:T(8,128)S(1)}, f32[24,128]{1,0:T(8,128)S(1)}, u32[]{:S(2)}, u32[]{:S(2)}) collective-permute-start(f32[24,128]{1,0:T(8,128)S(1)} %add.403), channel_id=1, source_target_pairs={{0,4},{2,6},{4,0},{6,2},{1,5},{3,7},{5,1},{7,3},{8,12},{10,14},{12... | collective-permute-start | bytes 36872 | tf_op jit(solution)/shard_map/ppermute | solution.py:90
  89.6 3.7 %collective-permute-start.22 = (f32[24,128]{1,0:T(8,128)S(1)}, f32[24,128]{1,0:T(8,128)S(1)}, u32[]{:S(2)}, u32[]{:S(2)}) collective-permute-start(f32[24,128]{1,0:T(8,128)S(1)} %add.404), channel_id=1, source_target_pairs={{0,1},{1,0},{2,3},{3,2},{4,5},{5,4},{6,7},{7,6},{8,9},{9,8},{10,11... | collective-permute-start | bytes 36872 | tf_op jit(solution)/shard_map/ppermute | solution.py:90

commit v3 on v2

--- a/solution.py
+++ b/solution.py
@@ -1,4 +1,5 @@
 import functools
+import math
 
 import jax
 import jax.numpy as jnp
@@ -190,131 +191,230 @@
     return [jnp.concatenate(p, axis=1) for p in pieces]
 
 
-def slot_tangents(diff, unit, inv, tn, tdiff, lanes, vectors):
-    tau = sum(unit[a] * diff[a] for a in range(3))
-    nus = [(diff[a] - unit[a] * tau) * inv for a in range(3)]
-    shape = tau.shape
+def pair_list(fanout):
+    return [(k, l) for k in range(fanout) for l in range(k, fanout)]
+
+
+def lookup(table, fanout):
+    where = {pair: n for n, pair in enumerate(pair_list(fanout))}
+    return lambda k, l: table[where[min(k, l), max(k, l)]]
+
+
+def sum_rows(parts):
+    row = lax.broadcasted_iota(jnp.int32, parts[0].shape, 0)
+    if len(parts) != 4 or GROUP != 8:
+        out = jnp.zeros_like(parts[0])
+        for n, part in enumerate(parts):
+            out = jnp.where(row == n, jnp.sum(part, axis=0, keepdims=True), out)
+        return out
+    fold = [part + pltpu.roll(part, 4, 0) for part in parts]
+    low = row < 4
+    lead = jnp.where(low, fold[0], fold[1])
+    rest = jnp.where(low, fold[2], fold[3])
+    both = jnp.where(row % 4 < 2, lead + pltpu.roll(lead, 6, 0), rest + pltpu.roll(rest, 2, 0))
+    even = both + pltpu.roll(both, 7, 0)
+    odd = both + pltpu.roll(both, 1, 0)
+    return jnp.where(row % 2 == 1, pltpu.roll(odd, 4, 0), even)
+
+
+def dot3(x, y):
+    return x[0] * y[0] + x[1] * y[1] + x[2] * y[2]
+
+
+def slot_cut(k, atoms):
+    return slice(k * atoms, (k + 1) * atoms)
+
+
+def tile_rows(n):
+    return slice(GROUP * n, GROUP * (n + 1))
+
+
+def tangents(diffs, units, invs, tn, changes, vectors):
+    fanout = len(diffs)
+    pairs = pair_list(fanout)
+    per_vector = fanout + len(pairs)
+    taus = [dot3(units[k], diffs[k]) for k in range(fanout)]
+    turns = [
+        [(diffs[k][a] - units[k][a] * taus[k]) * invs[k] for a in range(3)] for k in range(fanout)
+    ]
+    values = list(taus)
+    for k, l in pairs:
+        half = dot3(units[k], turns[l])
+        values.append(2.0 * half if k == l else half + dot3(units[l], turns[k]))
+    for n, value in enumerate(values):
+        changes[tile_rows(n), :] = value
+        for v in range(vectors):
+            tn[tile_rows(v * per_vector + n), :] = jnp.broadcast_to(
+                value[v : v + 1, :], value.shape
+            )
+
+
+def channel_products(f, f1, q, rp, rpp, cosine, tn, acc, lanes, fanout, vectors):
+    pairs = pair_list(fanout)
+    per_vector = fanout + len(pairs)
+    slots = range(fanout)
+    rpp_q = [rpp[k] * q[k] for k in slots]
+    rpp_f = [rpp[k] * f[k] for k in slots]
     for v in range(vectors):
-        for m, value in enumerate([tau] + nus):
-            start = (v * 4 + m) * GROUP
-            tn[start : start + GROUP, lanes] = jnp.broadcast_to(value[v : v + 1, :], shape)
-    for a in range(3):
-        tdiff[rows(a), lanes] = diff[a]
-    tdiff[rows(3), lanes] = tau
-
-
-def channel_products(f, f1, q, rp, rpp, unit, env, tn, acc, half, atoms, fanout, vectors):
-    share = 1.0 / fanout
-    rpf = [rp[k] * f[k] for k in range(fanout)]
-    for v in range(vectors):
-
-        def get(m, k):
-            start = (v * 4 + m) * GROUP
-            return tn[start : start + GROUP, pl.ds(k * atoms + half, LANES)]
-
-        phi = [f1[k] * get(0, k) for k in range(fanout)]
-        de = [share * sum(phi)]
-        for a in range(3):
-            de.append(
-                share * sum(phi[k] * unit(a, k) + f[k] * get(1 + a, k) for k in range(fanout))
-            )
-        y = []
-        hde = []
-        for k in range(fanout):
-            turn = de[0] + sum(unit(a, k) * de[1 + a] for a in range(3))
-            hde.append(turn)
-            bend = turn + sum(get(1 + a, k) * env[1 + a] for a in range(3))
-            y.append(rpp[k] * (phi[k] * q[k] + f[k] * bend))
-        w = [y[k] * f[k] + rp[k] * phi[k] for k in range(fanout)]
-        total = [share * sum(w)]
-        for a in range(3):
-            total.append(
-                share * sum(w[k] * unit(a, k) + rpf[k] * get(1 + a, k) for k in range(fanout))
-            )
-        for k in range(fanout):
-            along = total[0] + sum(unit(a, k) * total[1 + a] for a in range(3))
-            terms = [f1[k] * (y[k] * q[k] + rp[k] * hde[k] + along)]
+        base = v * per_vector
+
+        def tangent(n):
+            return tn[tile_rows(base + n), lanes]
+
+        phi = [f1[k] * tangent(k) for k in slots]
+        index = {pair: fanout + n for n, pair in enumerate(pairs)}
+        dq = []
+        for k in slots:
+            total = None
+            for l in slots:
+                term = phi[l] * cosine(k, l) + f[l] * tangent(index[min(k, l), max(k, l)])
+                total = term if total is None else total + term
+            dq.append(total)
+        y = [phi[k] * rpp_q[k] + dq[k] * rpp_f[k] for k in slots]
+        w = [y[k] * f[k] + rp[k] * phi[k] for k in slots]
+        for k in slots:
+            total = y[k] * q[k] + rp[k] * dq[k]
+            for l in slots:
+                total = total + w[l] * cosine(k, l)
+            acc[tile_rows(base + k), lanes] += f1[k] * total
+        for n, (k, l) in enumerate(pairs):
+            term = w[k] * f[l] if k == l else w[k] * f[l] + w[l] * f[k]
+            acc[tile_rows(base + fanout + n), lanes] += term
+
+
+def finish_product(
+    idx_ref, low_ref, unit_ref, inv_ref, sums_ref, acc, changes, diffs, own_out, ghost_out, vectors
+):
+    atoms = own_out.shape[1]
+    fanout = idx_ref.shape[1] // atoms
+    tiles = (atoms + ghost_out.shape[1]) // LANES
+    pairs = pair_list(fanout)
+    per_vector = fanout + len(pairs)
+    slots = range(fanout)
+    row = lax.broadcasted_iota(jnp.int32, (GROUP, atoms), 0)
+    outs = [
+        sum_rows([acc[tile_rows(v * per_vector + n), :] for v in range(vectors)])
+        for n in range(per_vector)
+    ]
+    taus = [changes[tile_rows(k), :] for k in slots]
+    turned = lookup([changes[tile_rows(fanout + n), :] for n in range(len(pairs))], fanout)
+    bent = lookup(outs[fanout:], fanout)
+    units = [[unit_ref[rows(a), slot_cut(k, atoms)] for a in range(3)] for k in slots]
+    invs = [inv_ref[:, slot_cut(k, atoms)] for k in slots]
+    turns = [
+        [(diffs[k][a] - units[k][a] * taus[k]) * invs[k] for a in range(3)] for k in slots
+    ]
+
+    def base_sum(n):
+        line = (n // 4) * GROUP + n % 4
+        return sums_ref[line : line + 1, :]
+
+    stretch = [base_sum(k) for k in slots]
+    curve = [base_sum(fanout + k) for k in slots]
+    weight = lookup([base_sum(2 * fanout + n) for n in range(len(pairs))], fanout)
+    mixed = [[base_sum(2 * fanout + len(pairs) + k * fanout + l) for l in slots] for k in slots]
+    center = [jnp.zeros((GROUP, atoms), jnp.float32) for _ in range(3)]
+    shifted = [jnp.zeros((GROUP, atoms), jnp.float32) for _ in range(vectors)]
+    left = []
+    for k in slots:
+        along = outs[k] + curve[k] * taus[k]
+        force = [0.0, 0.0, 0.0]
+        change = [0.0, 0.0, 0.0]
+        for l in slots:
+            along = along + turned(k, l) * mixed[k][l]
+            bend = bent(k, l) + taus[l] * mixed[l][k] + taus[k] * mixed[k][l]
+            pull = weight(k, l)
+            if k == l:
+                bend = bend + bent(k, l)
+                pull = pull + pull
             for a in range(3):
-                terms.append(f[k] * (y[k] * env[1 + a] + rp[k] * de[1 + a] + total[1 + a]))
-            for m in range(4):
-                start = (v * 4 + m) * GROUP
-                acc[start : start + GROUP, pl.ds(k * atoms + half, LANES)] += terms[m]
-
-
-def finish_product(
-    idx_ref, unit_ref, inv_ref, bend_ref, acc, tdiff, scat, center, own_out, ghost_out, vectors, gram=None
-):
-    atoms = center.shape[1]
-    fanout = idx_ref.shape[1] // atoms
-    tiles = scat.shape[0] // (3 * GROUP)
-    scat[...] = jnp.zeros_like(scat)
-    center[...] = jnp.zeros_like(center)
-
-    def slot(k, carry):
-        lanes = pl.ds(pl.multiple_of(k * atoms, LANES), atoms)
-        row = lax.broadcasted_iota(jnp.int32, (GROUP, atoms), 0)
-        zero = jnp.zeros((GROUP, atoms), jnp.float32)
-        outs = []
-        for m in range(4):
-            value = jnp.zeros((GROUP, atoms), jnp.float32)
-            for v in range(vectors):
-                start = (v * 4 + m) * GROUP
-                part = jnp.sum(acc[start : start + GROUP, lanes], axis=0, keepdims=True)
-                value = jnp.where(row == v, part, value)
-            outs.append(value)
-        unit = [unit_ref[rows(a), lanes] for a in range(3)]
-        inv = inv_ref[:, lanes]
-        diff = [tdiff[rows(a), lanes] for a in range(3)]
-        tau = tdiff[rows(3), lanes]
-        bend = bend_ref[:, lanes]
-        stretch, turn = bend[0:1], bend[1:2]
-        mix = [bend[2 + a : 3 + a] for a in range(3)]
-        inner = sum(unit[a] * outs[1 + a] for a in range(3))
+                force[a] = force[a] + pull * units[l][a]
+                change[a] = change[a] + bend * units[l][a] + pull * turns[l][a]
+        flat = dot3(units[k], force)
+        inv = invs[k]
         along = (
-            outs[0]
-            - inner * inv
-            + (stretch - turn) * tau
-            + sum(mix[a] * diff[a] for a in range(3))
-        )
+            along
+            - (dot3(units[k], change) + dot3(turns[k], force)) * inv
+            + taus[k] * flat * (inv * inv)
+        )
+        keep = stretch[k] - flat * inv
         packed = []
         for a in range(3):
-            y = along * unit[a] + outs[1 + a] * inv + turn * diff[a] + mix[a] * tau
+            y = (
+                along * units[k][a]
+                + keep * turns[k][a]
+                + (change[a] - taus[k] * inv * force[a]) * inv
+            )
             y = jnp.where(row < vectors, y, 0.0)
-            center[rows(a), :] -= y
-            if gram is not None:
-                gram[...] += lax.dot_general(
-                    jnp.where(row < vectors, diff[a], 0.0),
-                    jnp.concatenate([y] + [zero] * (LANES // GROUP - 1), axis=0),
-                    (((1,), (1,)), ((), ())),
-                    precision=HIGHEST,
-                    preferred_element_type=jnp.float32,
-                )
+            center[a] = center[a] - y
+            for n in range(vectors):
+                other = y if n == 0 else pltpu.roll(y, n, 0)
+                if n:
+                    other = other + pltpu.roll(y, GROUP - vectors + n, 0)
+                shifted[n] = shifted[n] + other * diffs[k][a]
             packed.append(split_rows(y, vectors))
         packed = jnp.concatenate(packed, axis=0)
-        index_row = idx_ref[:, lanes]
-        tile = index_row // LANES
-        low = lax.broadcasted_iota(jnp.int32, (LANES, atoms), 0) == index_row % LANES
-        left = jnp.concatenate(
-            [jnp.where(tile == number, packed, 0.0) for number in range(tiles)], axis=0
-        ).astype(jnp.bfloat16)
-        right = jnp.where(low, 1.0, 0.0).astype(jnp.bfloat16)
-        scat[...] += lax.dot_general(
-            left, right, (((1,), (1,)), ((), ())), preferred_element_type=jnp.float32
-        )
-        return carry
-
-    lax.fori_loop(0, fanout, slot, 0)
+        tile = idx_ref[:, slot_cut(k, atoms)] // LANES
+        left.append(
+            jnp.concatenate(
+                [jnp.where(tile == number, packed, 0.0) for number in range(tiles)], axis=0
+            ).astype(jnp.bfloat16)
+        )
+    spread = lax.dot_general(
+        jnp.concatenate(left, axis=1),
+        low_ref[...],
+        (((1,), (1,)), ((), ())),
+        preferred_element_type=jnp.float32,
+    )
     own_tiles = atoms // LANES
     for number in range(tiles):
         for a in range(3):
-            start = (number * 3 + a) * GROUP
-            value = join_rows(scat[start : start + GROUP, :], vectors)
+            value = join_rows(spread[tile_rows(number * 3 + a)], vectors)
             if number < own_tiles:
                 cut = slice(number * LANES, (number + 1) * LANES)
-                own_out[rows(a), cut] = value + center[rows(a), cut]
+                own_out[rows(a), cut] = value + center[a][:, cut]
             else:
                 cut = number - own_tiles
                 ghost_out[rows(a), cut * LANES : (cut + 1) * LANES] = value
+    return shifted
+
+
+def split_parts(x):
+    high = x.astype(jnp.bfloat16).astype(jnp.float32)
+    rest = x - high
+    middle = rest.astype(jnp.bfloat16).astype(jnp.float32)
+    low = (rest - middle).astype(jnp.bfloat16).astype(jnp.float32)
+    return high, middle, low
+
+
+def silu_slopes(x):
+    sig = 0.5 + 0.5 * jnp.tanh(0.5 * x)
+    anti = 1.0 - sig
+    return sig, sig * (1.0 + x * anti), sig * anti * (2.0 + x * (anti - sig))
+
+
+def half_turns(dist, inv, basis):
+    shape = (basis, dist.shape[1])
+    order = (lax.broadcasted_iota(jnp.int32, shape, 0) + 1).astype(jnp.float32)
+    turns = order * (dist * (1.0 / CUTOFF))
+    whole = jnp.floor(turns + 0.5)
+    sign = 1.0 - 2.0 * (whole - 2.0 * jnp.floor(whole * 0.5))
+    x = (turns - whole) * np.float32(np.pi)
+    x2 = x * x
+
+    def series(terms):
+        value = terms[-1]
+        for term in terms[-2::-1]:
+            value = term + x2 * value
+        return value
+
+    sine = sign * x * series([(-1.0) ** n / math.factorial(2 * n + 1) for n in range(6)])
+    cosine = sign * series([(-1.0) ** n / math.factorial(2 * n) for n in range(7)])
+    omega = order * np.float32(np.pi / CUTOFF)
+    b0 = sine * inv
+    b1 = (omega * cosine - b0) * inv
+    b2 = -(omega * omega * sine + 2.0 * b1) * inv
+    return jnp.concatenate([b0, b1, b2], axis=1)
 
 
 def first_kernel(
@@ -331,32 +431,32 @@
     read_ref,
     own_out,
     ghost_out,
+    low_out,
     unit_ref,
     inv_ref,
-    bend_ref,
+    sums_ref,
+    cos_ref,
     f_ref,
     f1_ref,
     q_ref,
     rp_ref,
     rpp_ref,
-    env_ref,
     table,
     f2_ref,
     read_col,
     tn,
-    tdiff,
+    changes,
     acc,
     acc2,
-    scat,
-    center,
 ):
     atoms = own_ref.shape[1]
     fanout = idx_ref.shape[1] // atoms
     species, channels = emb_ref.shape
-    basis = rin_ref.shape[0]
+    basis, hidden_units = rin_ref.shape
+    pairs = pair_list(fanout)
+    slots = range(fanout)
     embeds = [column(emb_ref[s : s + 1, :]) for s in range(species)]
-    readout = column(read_ref[...])
-    read_col[...] = jnp.broadcast_to(readout, read_col.shape)
+    read_col[...] = jnp.broadcast_to(column(read_ref[...]), read_col.shape)
     fill_table(table, own_ref, (g1_ref, g2_ref, g3_ref), vectors, ghosts, True)
 
     def embed(kind):
@@ -366,76 +466,53 @@
         return value
 
     own_embed = embed(own_ref[vectors + 1 : vectors + 2, :])
-
-    def slot(k, carry):
-        lanes = pl.ds(pl.multiple_of(k * atoms, LANES), atoms)
+    low = lax.broadcasted_iota(jnp.int32, (LANES, idx_ref.shape[1]), 0) == idx_ref[...] % LANES
+    low_out[...] = jnp.where(low, 1.0, 0.0).astype(jnp.bfloat16)
+
+    high, middle, rest = split_parts(rin_ref[...])
+    stack = [high, middle, rest, high, middle, high]
+    pad = LANES * (-(-(6 * basis) // LANES)) - 6 * basis
+    stack = jnp.concatenate(stack + [jnp.zeros((pad, hidden_units), jnp.float32)], axis=0)
+    inward = jnp.transpose(stack)[:, : 6 * basis].astype(jnp.bfloat16)
+    high, rest, _ = split_parts(rout_ref[...])
+    outward = jnp.concatenate(
+        [jnp.concatenate([high, high], axis=1), jnp.concatenate([rest, rest], axis=1)], axis=0
+    ).astype(jnp.bfloat16)
+
+    diffs, units, invs = [], [], []
+    for k in slots:
+        cut = slot_cut(k, atoms)
         near = gather_slot(table, idx_ref, k, atoms)
         diff = [near[a] - own_ref[rows(a), :] for a in range(3)]
         delta = [
             jnp.broadcast_to(diff[a][vectors : vectors + 1, :], (GROUP, atoms)) for a in range(3)
         ]
-        dist = jnp.sqrt(delta[0] * delta[0] + delta[1] * delta[1] + delta[2] * delta[2] + SOFTEN)
+        dist = jnp.sqrt(dot3(delta, delta) + SOFTEN)
         inv = 1.0 / dist
         unit = [delta[a] * inv for a in range(3)]
         for a in range(3):
-            unit_ref[rows(a), lanes] = unit[a]
-        inv_ref[:, lanes] = inv
-        slot_tangents(diff, unit, inv, tn, tdiff, lanes, vectors)
+            unit_ref[rows(a), cut] = unit[a]
+        inv_ref[:, cut] = inv
+        diffs.append(diff)
+        units.append(unit)
+        invs.append(inv)
         one = dist[0:1]
-        inv_one = inv[0:1]
-        order = (lax.broadcasted_iota(jnp.int32, (basis, atoms), 0) + 1).astype(jnp.float32)
-        turns = order * (one * (1.0 / CUTOFF))
-        whole = jnp.floor(turns + 0.5)
-        rest = turns - whole
-        odd = whole - 2.0 * jnp.floor(whole * 0.5)
-        sign = 1.0 - 2.0 * odd
-        x = rest * np.float32(np.pi)
-        x2 = x * x
-        sine = x * (
-            1.0
-            + x2
-            * (
-                -1.0 / 6
-                + x2
-                * (1.0 / 120 + x2 * (-1.0 / 5040 + x2 * (1.0 / 362880 + x2 * (-1.0 / 39916800))))
-            )
-        )
-        cosine = 1.0 + x2 * (
-            -0.5
-            + x2
-            * (
-                1.0 / 24
-                + x2
-                * (
-                    -1.0 / 720
-                    + x2 * (1.0 / 40320 + x2 * (-1.0 / 3628800 + x2 * (1.0 / 479001600)))
-                )
-            )
-        )
-        sine = sine * sign
-        cosine = cosine * sign
-        omega = order * np.float32(np.pi / CUTOFF)
-        b0 = sine * inv_one
-        b1 = (omega * cosine - b0) * inv_one
-        b2 = -(omega * omega * sine + 2.0 * b1) * inv_one
-        z = lax.dot_general(
-            rin_ref[...],
-            jnp.concatenate([b0, b1, b2], axis=1),
-            (((0,), (0,)), ((), ())),
-            precision=HIGHEST,
+        radii = half_turns(one, inv[0:1], basis)
+        high, middle, rest = split_parts(radii)
+        z = jnp.dot(
+            inward,
+            jnp.concatenate([high, high, high, middle, middle, rest], axis=0).astype(jnp.bfloat16),
             preferred_element_type=jnp.float32,
         )
         z0, z1, z2 = z[:, :atoms], z[:, atoms : 2 * atoms], z[:, 2 * atoms :]
-        sig = 1.0 / (1.0 + jnp.exp(-z0))
-        anti = 1.0 - sig
-        slope = sig * (1.0 + z0 * anti)
-        curve = sig * anti * (2.0 + z0 * (anti - sig))
-        hidden = jnp.concatenate(
-            [z0 * sig, slope * z1, curve * z1 * z1 + slope * z2], axis=1
-        )
+        sig, slope, curve = silu_slopes(z0)
+        hidden = jnp.concatenate([z0 * sig, slope * z1, curve * z1 * z1 + slope * z2], axis=1)
+        high = hidden.astype(jnp.bfloat16)
+        rest = (hidden - high.astype(jnp.float32)).astype(jnp.bfloat16)
         radial = jnp.dot(
-            rout_ref[...], hidden, precision=HIGHEST, preferred_element_type=jnp.float32
-        )
+            outward, jnp.concatenate([high, rest], axis=0), preferred_element_type=jnp.float32
+        )
+        radial = radial[:channels] + radial[channels:]
         r0, r1, r2 = radial[:, :atoms], radial[:, atoms : 2 * atoms], radial[:, 2 * atoms :]
         square = one * one
         base = 1.0 - square * (1.0 / CUTOFF**2)
@@ -443,90 +520,63 @@
         v1 = base * one * (-4.0 / CUTOFF**2)
         v2 = -4.0 / CUTOFF**2 + square * (12.0 / CUTOFF**4)
         pair = own_embed * embed(near[0][vectors + 1 : vectors + 2, :])
-        f_ref[:, lanes] = pair * (r0 * v0)
-        f1_ref[:, lanes] = pair * (r1 * v0 + r0 * v1)
-        f2_ref[:, lanes] = pair * (r2 * v0 + 2.0 * (r1 * v1) + r0 * v2)
-        return carry
-
-    lax.fori_loop(0, fanout, slot, 0)
+        f_ref[:, cut] = pair * (r0 * v0)
+        f1_ref[:, cut] = pair * (r1 * v0 + r0 * v1)
+        f2_ref[:, cut] = pair * (r2 * v0 + 2.0 * (r1 * v1) + r0 * v2)
+    for n, (k, l) in enumerate(pairs):
+        cos_ref[tile_rows(n), :] = 1.0 + dot3(units[k], units[l])
+    tangents(diffs, units, invs, tn, changes, vectors)
     acc[...] = jnp.zeros_like(acc)
     acc2[...] = jnp.zeros_like(acc2)
-    halves = atoms // LANES
     share = 1.0 / fanout
 
     def tile(number, carry):
-        start = pl.multiple_of((number // halves) * GROUP, GROUP)
-        half = pl.multiple_of((number % halves) * LANES, LANES)
-        here = pl.ds(start, GROUP)
-
-        def cut(k):
-            return pl.ds(pl.multiple_of(k * atoms + half, LANES), LANES)
-
-        def unit(a, k):
-            return unit_ref[rows(a), cut(k)]
-
-        slots = range(fanout)
-        f = [f_ref[here, cut(k)] for k in slots]
-        f1 = [f1_ref[here, cut(k)] for k in slots]
-        read = read_col[here, :]
-        env = [share * sum(f)]
-        for a in range(3):
-            env.append(share * sum(f[k] * unit(a, k) for k in slots))
-        q, rp, rpp = [], [], []
-        for k in slots:
-            project = env[0] + sum(unit(a, k) * env[1 + a] for a in range(3))
-            x = f[k] * project
-            sig = 1.0 / (1.0 + jnp.exp(-x))
-            anti = 1.0 - sig
-            q.append(project)
-            rp.append(read * (sig * (1.0 + x * anti)))
-            rpp.append(read * (sig * anti * (2.0 + x * (anti - sig))))
-            q_ref[here, cut(k)] = q[k]
-            rp_ref[here, cut(k)] = rp[k]
-            rpp_ref[here, cut(k)] = rpp[k]
-        for m in range(4):
-            env_ref[pl.ds(m * channels + start, GROUP), pl.ds(half, LANES)] = env[m]
-        rpf = [rp[k] * f[k] for k in slots]
-        total = [share * sum(rpf)]
-        for a in range(3):
-            total.append(share * sum(rpf[k] * unit(a, k) for k in slots))
-        for k in slots:
-            g = [rp[k] * env[m] + total[m] for m in range(4)]
-            gamma = g[0] + sum(unit(a, k) * g[1 + a] for a in range(3))
-            terms = [f2_ref[here, cut(k)] * gamma, f1[k] * g[0]]
-            terms += [f1[k] * g[1 + a] for a in range(3)]
-            terms += [f[k] * g[1 + a] for a in range(3)]
-            for m, term in enumerate(terms):
-                acc2[m * GROUP : (m + 1) * GROUP, cut(k)] += term
-        channel_products(
-            f, f1, q, rp, rpp, unit, env, tn, acc, half, atoms, fanout, vectors
-        )
+        here = pl.ds(pl.multiple_of(number * GROUP, GROUP), GROUP)
+        for half in range(atoms // LANES):
+            lanes = slice(half * LANES, (half + 1) * LANES)
+            cuts = [slice(k * atoms + half * LANES, k * atoms + (half + 1) * LANES) for k in slots]
+            cosine = lookup([cos_ref[tile_rows(n), lanes] for n in range(len(pairs))], fanout)
+            f = [f_ref[here, cut] for cut in cuts]
+            f1 = [f1_ref[here, cut] for cut in cuts]
+            read = read_col[here, :] * share
+            q, rp, rpp = [], [], []
+            for k in slots:
+                project = sum(f[l] * cosine(k, l) for l in slots)
+                _, slope, curve = silu_slopes(f[k] * project * share)
+                q.append(project)
+                rp.append(read * slope)
+                rpp.append(read * share * curve)
+                q_ref[here, cuts[k]] = q[k]
+                rp_ref[here, cuts[k]] = rp[k]
+                rpp_ref[here, cuts[k]] = rpp[k]
+            m = [rp[k] * f[k] for k in slots]
+            slope = [rp[k] * q[k] + sum(m[l] * cosine(k, l) for l in slots) for k in slots]
+            terms = [slope[k] * f1[k] for k in slots]
+            terms += [slope[k] * f2_ref[here, cuts[k]] for k in slots]
+            terms += [m[k] * f[l] if k == l else m[k] * f[l] + m[l] * f[k] for k, l in pairs]
+            terms += [f1[k] * m[l] for k in slots for l in slots]
+            for n, term in enumerate(terms):
+                acc2[tile_rows(n), lanes] += term
+            channel_products(f, f1, q, rp, rpp, cosine, tn, acc, lanes, fanout, vectors)
         return carry
 
-    lax.fori_loop(0, (channels // GROUP) * halves, tile, 0)
-
-    def bend_slot(k, carry):
-        lanes = pl.ds(pl.multiple_of(k * atoms, LANES), atoms)
-        sums = [
-            jnp.sum(acc2[m * GROUP : (m + 1) * GROUP, lanes], axis=0, keepdims=True)
-            for m in range(8)
-        ]
-        inv = inv_ref[0:1, lanes]
-        unit = [unit_ref[GROUP * a : GROUP * a + 1, lanes] for a in range(3)]
-        up = sum(unit[a] * sums[2 + a] for a in range(3))
-        uw = sum(unit[a] * sums[5 + a] for a in range(3))
-        turn = (sums[1] + up - uw * inv) * inv
-        mix = [
-            ((sums[2 + a] - unit[a] * up) - (sums[5 + a] - unit[a] * uw) * inv) * inv
-            for a in range(3)
-        ]
-        pad = jnp.zeros((GROUP - 5, atoms), jnp.float32)
-        bend_ref[:, lanes] = jnp.concatenate([sums[0], turn] + mix + [pad], axis=0)
-        return carry
-
-    lax.fori_loop(0, fanout, bend_slot, 0)
+    lax.fori_loop(0, channels // GROUP, tile, 0)
+    count = acc2.shape[0] // GROUP
+    for n in range(0, count, 4):
+        parts = [acc2[tile_rows(min(n + j, count - 1)), :] for j in range(4)]
+        sums_ref[tile_rows(n // 4), :] = sum_rows(parts)
     finish_product(
-        idx_ref, unit_ref, inv_ref, bend_ref, acc, tdiff, scat, center, own_out, ghost_out, vectors
+        idx_ref,
+        low_out,
+        unit_ref,
+        inv_ref,
+        sums_ref,
+        acc,
+        changes,
+        diffs,
+        own_out,
+        ghost_out,
+        vectors,
     )
 
 
@@ -538,92 +588,72 @@
     g1_ref,
     g2_ref,
     g3_ref,
+    low_ref,
     unit_ref,
     inv_ref,
-    bend_ref,
+    sums_ref,
+    cos_ref,
     f_ref,
     f1_ref,
     q_ref,
     rp_ref,
     rpp_ref,
-    env_ref,
     own_out,
     ghost_out,
     gram_out,
     table,
     tn,
-    tdiff,
+    changes,
     acc,
-    scat,
-    center,
 ):
     atoms = own_ref.shape[1]
     fanout = idx_ref.shape[1] // atoms
     channels = f_ref.shape[0]
+    pairs = pair_list(fanout)
+    slots = range(fanout)
     fill_table(table, own_ref, (g1_ref, g2_ref, g3_ref), vectors, ghosts, False)
-
-    def slot(k, carry):
-        lanes = pl.ds(pl.multiple_of(k * atoms, LANES), atoms)
+    diffs = []
+    for k in slots:
         near = gather_slot(table, idx_ref, k, atoms)
-        diff = [near[a] - own_ref[rows(a), :] for a in range(3)]
-        unit = [unit_ref[rows(a), lanes] for a in range(3)]
-        slot_tangents(diff, unit, inv_ref[:, lanes], tn, tdiff, lanes, vectors)
+        diffs.append([near[a] - own_ref[rows(a), :] for a in range(3)])
+    units = [[unit_ref[rows(a), slot_cut(k, atoms)] for a in range(3)] for k in slots]
+    invs = [inv_ref[:, slot_cut(k, atoms)] for k in slots]
+    tangents(diffs, units, invs, tn, changes, vectors)
+    acc[...] = jnp.zeros_like(acc)
+
+    def tile(number, carry):
+        here = pl.ds(pl.multiple_of(number * GROUP, GROUP), GROUP)
+        for half in range(atoms // LANES):
+            lanes = slice(half * LANES, (half + 1) * LANES)
+            cuts = [slice(k * atoms + half * LANES, k * atoms + (half + 1) * LANES) for k in slots]
+            cosine = lookup([cos_ref[tile_rows(n), lanes] for n in range(len(pairs))], fanout)
+            parts = [
+                [ref[here, cut] for cut in cuts] for ref in (f_ref, f1_ref, q_ref, rp_ref, rpp_ref)
+            ]
+            channel_products(*parts, cosine, tn, acc, lanes, fanout, vectors)
         return carry
 
-    lax.fori_loop(0, fanout, slot, 0)
-    acc[...] = jnp.zeros_like(acc)
-    gram_out[...] = jnp.zeros_like(gram_out)
-    halves = atoms // LANES
-
-    def tile(number, carry):
-        start = pl.multiple_of((number // halves) * GROUP, GROUP)
-        half = pl.multiple_of((number % halves) * LANES, LANES)
-        here = pl.ds(start, GROUP)
-
-        def cut(k):
-            return pl.ds(pl.multiple_of(k * atoms + half, LANES), LANES)
-
-        def unit(a, k):
-            return unit_ref[rows(a), cut(k)]
-
-        def load(ref):
-            return [ref[here, cut(k)] for k in range(fanout)]
-
-        env = [
-            env_ref[pl.ds(m * channels + start, GROUP), pl.ds(half, LANES)] for m in range(4)
-        ]
-        channel_products(
-            load(f_ref),
-            load(f1_ref),
-            load(q_ref),
-            load(rp_ref),
-            load(rpp_ref),
-            unit,
-            env,
-            tn,
-            acc,
-            half,
-            atoms,
-            fanout,
-            vectors,
-        )
-        return carry
-
-    lax.fori_loop(0, (channels // GROUP) * halves, tile, 0)
-    finish_product(
+    lax.fori_loop(0, channels // GROUP, tile, 0)
+    shifted = finish_product(
         idx_ref,
+        low_ref,
         unit_ref,
         inv_ref,
-        bend_ref,
+        sums_ref,
         acc,
-        tdiff,
-        scat,
-        center,
+        changes,
+        diffs,
         own_out,
         ghost_out,
         vectors,
-        gram_out,
-    )
+    )
+    row = lax.broadcasted_iota(jnp.int32, gram_out.shape, 0)
+    lane = lax.broadcasted_iota(jnp.int32, gram_out.shape, 1)
+    total = jnp.zeros(gram_out.shape, jnp.float32)
+    for n in range(vectors):
+        value = jnp.sum(shifted[n], axis=1, keepdims=True)
+        total = jnp.where(lane == (row + vectors - n) % vectors, value, total)
+    gram_out[...] = jnp.where((row < vectors) & (lane < vectors), total, 0.0)
 
 
 def middle_kernel(vectors, own_ref, sums_ref, list_ref, full_ref, oct_ref):
@@ -919,7 +949,6 @@
     edges = fanout * atoms
     index = table_index(neighbors.reshape(1, -1), atoms, ghosts)
     table_width = atoms + 7 * width
-    tiles = table_width // LANES
     ring = lax.axis_size("gx") == 4
     side = (octant_bit((GROUP, width), 0, ghosts) ^ (lax.axis_index("gx") % 2 == 1)).astype(
         jnp.float32
@@ -936,23 +965,20 @@
             level = jnp.concatenate([level, fetch_ghosts(level, 0, ghosts)], axis=1)
         return (level,) + spread_outer(level, ghosts)
 
+    pairs = len(pair_list(fanout))
     shared = [
-        (vectors * 4 * GROUP, edges),
-        (4 * GROUP, edges),
-        (vectors * 4 * GROUP, edges),
+        (vectors * (fanout + pairs) * GROUP, atoms),
+        ((fanout + pairs) * GROUP, atoms),
+        (vectors * (fanout + pairs) * GROUP, atoms),
     ]
-    tail = [(tiles * high, LANES), (high, atoms)]
+    base_sums = 2 * fanout + pairs + fanout * fanout
     saved_shapes = [
+        ((LANES, edges), jnp.bfloat16),
         (high, edges),
         (GROUP, edges),
-        (GROUP, edges),
-        (channels, edges),
-        (channels, edges),
-        (channels, edges),
-        (channels, edges),
-        (channels, edges),
-        (4 * channels, atoms),
-    ]
+        (GROUP * (-(-base_sums // 4)), atoms),
+        (pairs * GROUP, atoms),
+    ] + [(channels, edges)] * 5
     results = call(
         functools.partial(first_kernel, ghosts, vectors),
         [(high, atoms), (high, 7 * width)] + saved_shapes,
@@ -961,8 +987,7 @@
         + (embedding, radial_in, radial_out.T, readout.reshape(1, -1)),
         [(high, table_width), (channels, edges), (channels, LANES)]
         + shared
-        + [(8 * GROUP, edges)]
-        + tail,
+        + [(base_sums * GROUP, atoms)],
     )
     own_terms, ghost_terms, saved = results[0], results[1], results[2:]
 
@@ -990,7 +1015,7 @@
         functools.partial(second_kernel, ghosts, vectors),
         [(high, atoms), (high, 7 * width), (GROUP, LANES)],
         (index, first) + spread(level) + tuple(saved),
-        [(high, table_width)] + shared + tail,
+        [(high, table_width)] + shared,
     )
     sums, beside = return_outer(ghost_terms, width, ghosts)
     if ring:

time: 96 us -> 84 us (0.88)
  Pallas kernels: 29.5 us -> 17.5 us
    pallas_call x8, Pallas kernels: 29.5 us -> 17.5 us  [call(): pl.pallas_call(body, out_shape=[jax.ShapeDtypeStruct(shape, kind) for sha...]
where the time goes in v3:
time: 84 us; the launch traced here: 83.7 us
  waiting for transfers between devices  33.4 us (40%)
  starting transfers between devices  28.7 us (34%)
  Pallas kernels  17.5 us (21%)
  local copies, waits for them, and re-layouts  2.78 us (3%)
    ppermute x16, starting transfers between devices, pair_exchange(): lax.ppermute(x, axis, [(i, i ^ d) for i in range(size)])  19.7 us
    ppermute x16, waiting for transfers between devices, pair_exchange(): lax.ppermute(x, axis, [(i, i ^ d) for i in range(size)])  17.5 us
    pallas_call x8, Pallas kernels, call(): pl.pallas_call(body, out_shape=[jax.ShapeDtypeStruct(shape, kind) for sha...  17.5 us
    ppermute x3, waiting for transfers between devices, sum_over(): x = x + lax.ppermute(x, axis, [(i, i ^ step) for i in range(size)])  5.89 us
    ppermute x2, waiting for transfers between devices, return_ghosts(): return lax.ppermute(x, axis, swap_pairs(2, 1))  5.13 us
    ppermute x2, waiting for transfers between devices, fetch_ghosts(): return lax.ppermute(x, axis, swap_pairs(2, 1))  4.88 us
    ppermute x2, starting transfers between devices, return_ghosts(): return lax.ppermute(x, axis, swap_pairs(2, 1))  3.18 us
    ppermute x2, starting transfers between devices, fetch_ghosts(): return lax.ppermute(x, axis, swap_pairs(2, 1))  3.17 us
  transfers between devices with their start and end apart: 23, of which 18 were waited for; matrix products, arithmetic and copies ran while one was open for 0% of the time, Pallas kernels for 0%

profile of v3, /device:TPU:0, one launch (start us, length us, event | category | flops | bytes accessed | tf_op | source)
XLA Modules:
  0.0 83.7 jit_solution(16044894497914928703)
XLA Ops:
  2.9 5.1 %collective-permute-start = (f32[24,128]{1,0:T(8,128)S(1)}, f32[24,128]{1,0:T(8,128)S(1)}, u32[]{:S(2)}, u32[]{:S(2)}) collective-permute-start(f32[24,128]{1,0:T(8,128)S(1)} %get-tuple-element.33), channel_id=1, source_target_pairs={{0,24},{8,16},{16,8},{24,0},{1,25},{9,17},{17,9},{25,1},{2,26},{10... | collective-permute-start | bytes 36872 | tf_op jit(solution)/shard_map/ppermute | solution.py:32
  8.0 1.6 %collective-permute-done = f32[24,128]{1,0:T(8,128)S(1)} collective-permute-done((f32[24,128]{1,0:T(8,128)S(1)}, f32[24,128]{1,0:T(8,128)S(1)}, u32[]{:S(2)}, u32[]{:S(2)}) %collective-permute-start) | collective-permute-done | bytes 12320 | tf_op jit(solution)/shard_map/ppermute | solution.py:32
  9.6 2.0 %collective-permute-done.1 = f32[24,128]{1,0:T(8,128)S(1)} collective-permute-done((f32[24,128]{1,0:T(8,128)S(1)}, f32[24,128]{1,0:T(8,128)S(1)}, u32[]{:S(2)}, u32[]{:S(2)}) %collective-permute-start.1) | collective-permute-done | bytes 12320 | tf_op jit(solution)/shard_map/ppermute | solution.py:32
  11.8 1.6 %collective-permute-start.3 = (f32[24,256]{1,0:T(8,128)S(1)}, f32[24,256]{1,0:T(8,128)S(1)}, u32[]{:S(2)}, u32[]{:S(2)}) collective-permute-start(f32[24,256]{1,0:T(8,128)S(1)} %pad_maximum_fusion.2.g1_ref), channel_id=1, source_target_pairs={{0,2},{2,0},{4,6},{6,4},{1,3},{3,1},{5,7},{7,5},{8,10},{10,8},{12,... | collective-permute-start | bytes 73736 | tf_op jit(solution)/shard_map/ppermute | solution.py:32
  13.4 1.9 %collective-permute-done.2 = f32[24,256]{1,0:T(8,128)S(1)} collective-permute-done((f32[24,256]{1,0:T(8,128)S(1)}, f32[24,256]{1,0:T(8,128)S(1)}, u32[]{:S(2)}, u32[]{:S(2)}) %collective-permute-start.2) | collective-permute-done | bytes 24608 | tf_op jit(solution)/shard_map/ppermute | solution.py:32
  15.3 1.6 %collective-permute-start.4 = (f32[24,512]{1,0:T(8,128)S(1)}, f32[24,512]{1,0:T(8,128)S(1)}, u32[]{:S(2)}, u32[]{:S(2)}) collective-permute-start(f32[24,512]{1,0:T(8,128)S(1)} %pad_maximum_fusion), channel_id=1, source_target_pairs={{0,1},{1,0},{2,3},{3,2},{4,5},{5,4},{6,7},{7,6},{8,9},{9,8},{10,11... | collective-permute-start | bytes 147464 | tf_op jit(solution)/shard_map/ppermute | solution.py:52
  17.1 2.3 %collective-permute-done.4.g3_ref = f32[24,512]{1,0:T(8,128)S(1)} collective-permute-done((f32[24,512]{1,0:T(8,128)S(1)}, f32[24,512]{1,0:T(8,128)S(1)}, u32[]{:S(2)}, u32[]{:S(2)}) %collective-permute-start.4) | collective-permute-done | bytes 49184 | tf_op jit(solution)/shard_map/ppermute | solution.py:52
  20.1 7.7 %shard_map.113 = (f32[24,256]{1,0:T(8,128)S(1)}, f32[24,896]{1,0:T(8,128)S(1)}, bf16[128,1536]{1,0:T(8,128)(2,1)S(1)}, f32[24,1536]{1,0:T(8,128)S(1)}, f32[8,153...) custom-call(s32[1,1536]{1,0:T(1,128)S(1)} %compare_select_fusion.idx, ...), custom_call_target="tpu_custom_call" | custom-call | tf_op jit(solution)/shard_map/pallas_call | solution.py:899
  27.9 1.6 %collective-permute-start.5 = (f32[24,512]{1,0:T(8,128)S(1)}, f32[24,512]{1,0:T(8,128)S(1)}, u32[]{:S(2)}, u32[]{:S(2)}) collective-permute-start(f32[24,512]{1,0:T(8,128)S(1)} %slice.48), channel_id=1, source_target_pairs={{0,1},{1,0},{2,3},{3,2},{4,5},{5,4},{6,7},{7,6},{8,9},{9,8},{10,11... | collective-permute-start | bytes 147464 | tf_op jit(solution)/shard_map/ppermute | solution.py:63
  29.5 2.6 %collective-permute-done.5 = f32[24,512]{1,0:T(8,128)S(1)} collective-permute-done((f32[24,512]{1,0:T(8,128)S(1)}, f32[24,512]{1,0:T(8,128)S(1)}, u32[]{:S(2)}, u32[]{:S(2)}) %collective-permute-start.5) | collective-permute-done | bytes 49184 | tf_op jit(solution)/shard_map/ppermute | solution.py:63
  32.1 1.4 %collective-permute-start.7 = (f32[24,256]{1,0:T(8,128)S(1)}, f32[24,256]{1,0:T(8,128)S(1)}, u32[]{:S(2)}, u32[]{:S(2)}) collective-permute-start(f32[24,256]{1,0:T(8,128)S(1)} %slice_add_fusion.1), channel_id=1, source_target_pairs={{0,6},{2,4},{4,2},{6,0},{1,7},{3,5},{5,3},{7,1},{8,14},{10,12},{12... | collective-permute-start | bytes 73736 | tf_op jit(solution)/shard_map/ppermute | solution.py:32
  33.4 1.9 %collective-permute-done.7 = f32[24,256]{1,0:T(8,128)S(1)} collective-permute-done((f32[24,256]{1,0:T(8,128)S(1)}, f32[24,256]{1,0:T(8,128)S(1)}, u32[]{:S(2)}, u32[]{:S(2)}) %collective-permute-start.7) | collective-permute-done | bytes 24608 | tf_op jit(solution)/shard_map/ppermute | solution.py:32
  35.7 1.8 %collective-permute-start.10 = (f32[24,256]{1,0:T(8,128)S(1)}, f32[24,256]{1,0:T(8,128)S(1)}, u32[]{:S(2)}, u32[]{:S(2)}) collective-permute-start(f32[24,256]{1,0:T(8,128)S(1)} %get-tuple-element.38.p0_ref), channel_id=1, source_target_pairs={{0,24},{8,16},{16,8},{24,0},{1,25},{9,17},{17,9},{25,1},{2,26},{10... | collective-permute-start | bytes 73736 | tf_op jit(solution)/shard_map/ppermute | solution.py:32
  37.5 2.6 %collective-permute-start.9 = (f32[24,256]{1,0:T(8,128)S(1)}, f32[24,256]{1,0:T(8,128)S(1)}, u32[]{:S(2)}, u32[]{:S(2)}) collective-permute-start(f32[24,256]{1,0:T(8,128)S(1)} %get-tuple-element.38.p0_ref), channel_id=1, source_target_pairs={{0,16},{8,24},{16,0},{24,8},{1,17},{9,25},{17,1},{25,9},{2,18},{10... | collective-permute-start | bytes 73736 | tf_op jit(solution)/shard_map/ppermute | solution.py:32
  40.1 1.3 %collective-permute-done.10.p3_ref = f32[24,256]{1,0:T(8,128)S(1)} collective-permute-done((f32[24,256]{1,0:T(8,128)S(1)}, f32[24,256]{1,0:T(8,128)S(1)}, u32[]{:S(2)}, u32[]{:S(2)}) %collective-permute-start.10) | collective-permute-done | bytes 24608 | tf_op jit(solution)/shard_map/ppermute | solution.py:32
  42.7 1.3 %collective-permute-start.12 = (f32[24,256]{1,0:T(8,128)S(1)}, f32[24,256]{1,0:T(8,128)S(1)}, u32[]{:S(2)}, u32[]{:S(2)}) collective-permute-start(f32[24,256]{1,0:T(8,128)S(1)} %get-tuple-element.40.g1_ref), channel_id=1, source_target_pairs={{0,2},{2,0},{4,6},{6,4},{1,3},{3,1},{5,7},{7,5},{8,10},{10,8},{12,... | collective-permute-start | bytes 73736 | tf_op jit(solution)/shard_map/ppermute | solution.py:32
  44.0 2.0 %collective-permute-done.11 = f32[24,256]{1,0:T(8,128)S(1)} collective-permute-done((f32[24,256]{1,0:T(8,128)S(1)}, f32[24,256]{1,0:T(8,128)S(1)}, u32[]{:S(2)}, u32[]{:S(2)}) %collective-permute-start.11) | collective-permute-done | bytes 24608 | tf_op jit(solution)/shard_map/ppermute | solution.py:32
  46.0 1.6 %collective-permute-start.13 = (f32[24,512]{1,0:T(8,128)S(1)}, f32[24,512]{1,0:T(8,128)S(1)}, u32[]{:S(2)}, u32[]{:S(2)}) collective-permute-start(f32[24,512]{1,0:T(8,128)S(1)} %pad_maximum_fusion.1), channel_id=1, source_target_pairs={{0,1},{1,0},{2,3},{3,2},{4,5},{5,4},{6,7},{7,6},{8,9},{9,8},{10,11... | collective-permute-start | bytes 147464 | tf_op jit(solution)/shard_map/ppermute | solution.py:52
  47.6 2.6 %collective-permute-done.13.g3_ref = f32[24,512]{1,0:T(8,128)S(1)} collective-permute-done((f32[24,512]{1,0:T(8,128)S(1)}, f32[24,512]{1,0:T(8,128)S(1)}, u32[]{:S(2)}, u32[]{:S(2)}) %collective-permute-start.13) | collective-permute-done | bytes 49184 | tf_op jit(solution)/shard_map/ppermute | solution.py:52
  50.2 4.7 %shard_map.116 = (f32[24,256]{1,0:T(8,128)S(1)}, f32[24,896]{1,0:T(8,128)S(1)}, f32[8,128]{1,0:T(8,128)S(1)}) custom-call(s32[1,1536]{1,0:T(1,128)S(1)} %compare_select_fusion.idx_ref, f32[24,256]{1,0:T(8,128)S(1)} %get-tuple-element.39.own_ref.first_ref, f32[24,256]{1,0:T(8,128)S(1)} %get-tuple-element.40.g1_ref, f32[24,256]{1,0:T(8,128)S(1)} %fusion.48.g2_ref, ...), custom_call_target="tpu_custom_call" | custom-call | tf_op jit(solution)/shard_map/pallas_call | solution.py:899
  54.9 1.6 %collective-permute-start.14 = (f32[24,512]{1,0:T(8,128)S(1)}, f32[24,512]{1,0:T(8,128)S(1)}, u32[]{:S(2)}, u32[]{:S(2)}) collective-permute-start(f32[24,512]{1,0:T(8,128)S(1)} %slice.56), channel_id=1, source_target_pairs={{0,1},{1,0},{2,3},{3,2},{4,5},{5,4},{6,7},{7,6},{8,9},{9,8},{10,11... | collective-permute-start | bytes 147464 | tf_op jit(solution)/shard_map/ppermute | solution.py:63
  56.4 2.6 %collective-permute-done.14 = f32[24,512]{1,0:T(8,128)S(1)} collective-permute-done((f32[24,512]{1,0:T(8,128)S(1)}, f32[24,512]{1,0:T(8,128)S(1)}, u32[]{:S(2)}, u32[]{:S(2)}) %collective-permute-start.14) | collective-permute-done | bytes 49184 | tf_op jit(solution)/shard_map/ppermute | solution.py:63
  59.0 1.3 %collective-permute-start.16 = (f32[24,256]{1,0:T(8,128)S(1)}, f32[24,256]{1,0:T(8,128)S(1)}, u32[]{:S(2)}, u32[]{:S(2)}) collective-permute-start(f32[24,256]{1,0:T(8,128)S(1)} %slice_add_fusion), channel_id=1, source_target_pairs={{0,6},{2,4},{4,2},{6,0},{1,7},{3,5},{5,3},{7,1},{8,14},{10,12},{12... | collective-permute-start | bytes 73736 | tf_op jit(solution)/shard_map/ppermute | solution.py:32
  60.3 2.0 %collective-permute-done.16 = f32[24,256]{1,0:T(8,128)S(1)} collective-permute-done((f32[24,256]{1,0:T(8,128)S(1)}, f32[24,256]{1,0:T(8,128)S(1)}, u32[]{:S(2)}, u32[]{:S(2)}) %collective-permute-start.16) | collective-permute-done | bytes 24608 | tf_op jit(solution)/shard_map/ppermute | solution.py:32
  62.8 2.0 %collective-permute-start.17 = (f32[24,384]{1,0:T(8,128)S(1)}, f32[24,384]{1,0:T(8,128)S(1)}, u32[]{:S(2)}, u32[]{:S(2)}) collective-permute-start(f32[24,384]{1,0:T(8,128)S(1)} %get-tuple-element.55.p0_ref), channel_id=1, source_target_pairs={{0,8},{8,0},{16,24},{24,16},{1,9},{9,1},{17,25},{25,17},{2,10},{10... | collective-permute-start | bytes 110600 | tf_op jit(solution)/shard_map/ppermute | solution.py:32
  65.5 1.8 %collective-permute-start.19 = (f32[24,384]{1,0:T(8,128)S(1)}, f32[24,384]{1,0:T(8,128)S(1)}, u32[]{:S(2)}, u32[]{:S(2)}) collective-permute-start(f32[24,384]{1,0:T(8,128)S(1)} %get-tuple-element.55.p0_ref), channel_id=1, source_target_pairs={{0,24},{8,16},{16,8},{24,0},{1,25},{9,17},{17,9},{25,1},{2,26},{10... | collective-permute-start | bytes 110600 | tf_op jit(solution)/shard_map/ppermute | solution.py:32
  67.3 3.5 %collective-permute-done.18.p2_ref = f32[24,384]{1,0:T(8,128)S(1)} collective-permute-done((f32[24,384]{1,0:T(8,128)S(1)}, f32[24,384]{1,0:T(8,128)S(1)}, u32[]{:S(2)}, u32[]{:S(2)}) %collective-permute-start.18) | collective-permute-done | bytes 36896 | tf_op jit(solution)/shard_map/ppermute | solution.py:32
  71.3 1.4 %shard_map.118 = (f32[24,256]{1,0:T(8,128)S(1)}, f32[24,128]{1,0:T(8,128)S(1)}) custom-call(f32[8,128]{1,0:T(8,128)S(1)} %fusion.45.side_ref, f32[24,256]{1,0:T(8,128)S(1)} %get-tuple-element.54.part_ref, f32[24,384]{1,0:T(8,128)S(1)} %get-tuple-element.55.p0_ref, f32[24,384]{1,0:T(8,128)S(1)} %collective-permute-done.17.p1_ref, ...), custom_call_target="tpu_custom_call" | custom-call | tf_op jit(solution)/shard_map/pallas_call | solution.py:899
  75.0 2.5 %collective-permute-done.21 = f32[24,128]{1,0:T(8,128)S(1)} collective-permute-done((f32[24,128]{1,0:T(8,128)S(1)}, f32[24,128]{1,0:T(8,128)S(1)}, u32[]{:S(2)}, u32[]{:S(2)}) %collective-permute-start.21) | collective-permute-done | bytes 12320 | tf_op jit(solution)/shard_map/ppermute | solution.py:91
  77.6 1.5 %collective-permute-start.22 = (f32[24,128]{1,0:T(8,128)S(1)}, f32[24,128]{1,0:T(8,128)S(1)}, u32[]{:S(2)}, u32[]{:S(2)}) collective-permute-start(f32[24,128]{1,0:T(8,128)S(1)} %add.404), channel_id=1, source_target_pairs={{0,1},{1,0},{2,3},{3,2},{4,5},{5,4},{6,7},{7,6},{8,9},{9,8},{10,11... | collective-permute-start | bytes 36872 | tf_op jit(solution)/shard_map/ppermute | solution.py:91
  79.1 2.2 %collective-permute-done.22 = f32[24,128]{1,0:T(8,128)S(1)} collective-permute-done((f32[24,128]{1,0:T(8,128)S(1)}, f32[24,128]{1,0:T(8,128)S(1)}, u32[]{:S(2)}, u32[]{:S(2)}) %collective-permute-start.22) | collective-permute-done | bytes 12320 | tf_op jit(solution)/shard_map/ppermute | solution.py:91
  81.3 2.5 %shard_map.119 = (f32[1,1,1,3,4,256]{5,4,3,2,1,0:T(4,128)}, f32[2,4,4]{2,1,0:T(4,128)}, f32[2,4,4]{2,1,0:T(4,128)}) custom-call(f32[24,256]{1,0:T(8,128)S(1)} %get-tuple-element.32.own_ref.start_ref, f32[24,256]{1,0:T(8,128)S(1)} %get-tuple-element.39.own_ref.first_ref, f32[24,256]{1,0:T(8,128)S(1)} %get-tuple-element.56.second_ref, f32[24,128]{1,0:T(8,128)S(1)} %add.405.gram_ref), custom_call_target="tpu_custom_call" | custom-call | tf_op jit(solution)/shard_map/pallas_call | solution.py:899
  (62 shorter events, 9.1 us)
Async XLA Ops:
  0.6 0.7 copy-start.2
  1.3 0.7 copy-start.5
  2.0 0.7 copy-start.1
  2.9 6.7 %collective-permute-start = (f32[24,128]{1,0:T(8,128)S(1)}, f32[24,128]{1,0:T(8,128)S(1)}, u32[]{:S(2)}, u32[]{:S(2)}) collective-permute-start(f32[24,128]{1,0:T(8,128)S(1)} %get-tuple-element.33), channel_id=1, source_target_pairs={{0,24},{8,16},{16,8},{24,0},{1,25},{9,17},{17,9},{25,1},{2,26},{10... | collective-permute-start | bytes 36872 | tf_op jit(solution)/shard_map/ppermute | solution.py:32
  7.9 3.7 %collective-permute-start.1 = (f32[24,128]{1,0:T(8,128)S(1)}, f32[24,128]{1,0:T(8,128)S(1)}, u32[]{:S(2)}, u32[]{:S(2)}) collective-permute-start(f32[24,128]{1,0:T(8,128)S(1)} %get-tuple-element.33), channel_id=1, source_target_pairs={{0,8},{8,0},{16,24},{24,16},{1,9},{9,1},{17,25},{25,17},{2,10},{10... | collective-permute-start | bytes 36872 | tf_op jit(solution)/shard_map/ppermute | solution.py:32
  11.7 3.5 %collective-permute-start.2 = (f32[24,256]{1,0:T(8,128)S(1)}, f32[24,256]{1,0:T(8,128)S(1)}, u32[]{:S(2)}, u32[]{:S(2)}) collective-permute-start(f32[24,256]{1,0:T(8,128)S(1)} %pad_maximum_fusion.2.g1_ref), channel_id=1, source_target_pairs={{0,6},{2,4},{4,2},{6,0},{1,7},{3,5},{5,3},{7,1},{8,14},{10,12},{12... | collective-permute-start | bytes 73736 | tf_op jit(solution)/shard_map/ppermute | solution.py:32
  11.8 3.5 %collective-permute-start.3 = (f32[24,256]{1,0:T(8,128)S(1)}, f32[24,256]{1,0:T(8,128)S(1)}, u32[]{:S(2)}, u32[]{:S(2)}) collective-permute-start(f32[24,256]{1,0:T(8,128)S(1)} %pad_maximum_fusion.2.g1_ref), channel_id=1, source_target_pairs={{0,2},{2,0},{4,6},{6,4},{1,3},{3,1},{5,7},{7,5},{8,10},{10,8},{12,... | collective-permute-start | bytes 73736 | tf_op jit(solution)/shard_map/ppermute | solution.py:32
  15.2 1.6 %copy-start.7 = (s32[1,1,1,6,256]{4,2,3,1,0:T(1,128)S(1)}, s32[1,1,1,6,256]{4,2,3,1,0:T(1,128)}, u32[]{:S(2)}) copy-start(s32[1,1,1,6,256]{4,2,3,1,0:T(1,128)} %param.12) | copy-start | bytes 18436
  15.3 4.2 %copy-start = (f32[128,64]{0,1:T(8,128)S(1)}, f32[128,64]{0,1:T(8,128)}, u32[]{:S(2)}) copy-start(f32[128,64]{0,1:T(8,128)} %param.16) | copy-start | bytes 98308
  15.3 4.2 %collective-permute-start.4 = (f32[24,512]{1,0:T(8,128)S(1)}, f32[24,512]{1,0:T(8,128)S(1)}, u32[]{:S(2)}, u32[]{:S(2)}) collective-permute-start(f32[24,512]{1,0:T(8,128)S(1)} %pad_maximum_fusion), channel_id=1, source_target_pairs={{0,1},{1,0},{2,3},{3,2},{4,5},{5,4},{6,7},{7,6},{8,9},{9,8},{10,11... | collective-permute-start | bytes 147464 | tf_op jit(solution)/shard_map/ppermute | solution.py:52
  17.1 2.3 %copy-start.3 = (f32[8,128]{1,0:T(8,128)S(1)}, f32[8,128]{1,0:T(8,128)}, u32[]{:S(2)}) copy-start(f32[8,128]{1,0:T(8,128)} %rin_ref.1) | copy-start | bytes 12292
  19.4 0.7 copy-start.4
  19.4 0.7 copy-start.6
  27.9 4.2 %collective-permute-start.5 = (f32[24,512]{1,0:T(8,128)S(1)}, f32[24,512]{1,0:T(8,128)S(1)}, u32[]{:S(2)}, u32[]{:S(2)}) collective-permute-start(f32[24,512]{1,0:T(8,128)S(1)} %slice.48), channel_id=1, source_target_pairs={{0,1},{1,0},{2,3},{3,2},{4,5},{5,4},{6,7},{7,6},{8,9},{9,8},{10,11... | collective-permute-start | bytes 147464 | tf_op jit(solution)/shard_map/ppermute | solution.py:63
  32.1 1.4 %collective-permute-start.6 = (f32[24,256]{1,0:T(8,128)S(1)}, f32[24,256]{1,0:T(8,128)S(1)}, u32[]{:S(2)}, u32[]{:S(2)}) collective-permute-start(f32[24,256]{1,0:T(8,128)S(1)} %slice_add_fusion.1), channel_id=1, source_target_pairs={{0,2},{2,0},{4,6},{6,4},{1,3},{3,1},{5,7},{7,5},{8,10},{10,8},{12,... | collective-permute-start | bytes 73736 | tf_op jit(solution)/shard_map/ppermute | solution.py:32
  32.1 3.3 %collective-permute-start.7 = (f32[24,256]{1,0:T(8,128)S(1)}, f32[24,256]{1,0:T(8,128)S(1)}, u32[]{:S(2)}, u32[]{:S(2)}) collective-permute-start(f32[24,256]{1,0:T(8,128)S(1)} %slice_add_fusion.1), channel_id=1, source_target_pairs={{0,6},{2,4},{4,2},{6,0},{1,7},{3,5},{5,3},{7,1},{8,14},{10,12},{12... | collective-permute-start | bytes 73736 | tf_op jit(solution)/shard_map/ppermute | solution.py:32
  35.7 5.7 %collective-permute-start.10 = (f32[24,256]{1,0:T(8,128)S(1)}, f32[24,256]{1,0:T(8,128)S(1)}, u32[]{:S(2)}, u32[]{:S(2)}) collective-permute-start(f32[24,256]{1,0:T(8,128)S(1)} %get-tuple-element.38.p0_ref), channel_id=1, source_target_pairs={{0,24},{8,16},{16,8},{24,0},{1,25},{9,17},{17,9},{25,1},{2,26},{10... | collective-permute-start | bytes 73736 | tf_op jit(solution)/shard_map/ppermute | solution.py:32
  37.5 4.3 %collective-permute-start.8 = (f32[24,256]{1,0:T(8,128)S(1)}, f32[24,256]{1,0:T(8,128)S(1)}, u32[]{:S(2)}, u32[]{:S(2)}) collective-permute-start(f32[24,256]{1,0:T(8,128)S(1)} %get-tuple-element.38.p0_ref), channel_id=1, source_target_pairs={{0,8},{8,0},{16,24},{24,16},{1,9},{9,1},{17,25},{25,17},{2,10},{10... | collective-permute-start | bytes 73736 | tf_op jit(solution)/shard_map/ppermute | solution.py:32
  37.5 4.7 %collective-permute-start.9 = (f32[24,256]{1,0:T(8,128)S(1)}, f32[24,256]{1,0:T(8,128)S(1)}, u32[]{:S(2)}, u32[]{:S(2)}) collective-permute-start(f32[24,256]{1,0:T(8,128)S(1)} %get-tuple-element.38.p0_ref), channel_id=1, source_target_pairs={{0,16},{8,24},{16,0},{24,8},{1,17},{9,25},{17,1},{25,9},{2,18},{10... | collective-permute-start | bytes 73736 | tf_op jit(solution)/shard_map/ppermute | solution.py:32
  42.6 3.4 %collective-permute-start.11 = (f32[24,256]{1,0:T(8,128)S(1)}, f32[24,256]{1,0:T(8,128)S(1)}, u32[]{:S(2)}, u32[]{:S(2)}) collective-permute-start(f32[24,256]{1,0:T(8,128)S(1)} %get-tuple-element.40.g1_ref), channel_id=1, source_target_pairs={{0,6},{2,4},{4,2},{6,0},{1,7},{3,5},{5,3},{7,1},{8,14},{10,12},{12... | collective-permute-start | bytes 73736 | tf_op jit(solution)/shard_map/ppermute | solution.py:32
  42.7 3.2 %collective-permute-start.12 = (f32[24,256]{1,0:T(8,128)S(1)}, f32[24,256]{1,0:T(8,128)S(1)}, u32[]{:S(2)}, u32[]{:S(2)}) collective-permute-start(f32[24,256]{1,0:T(8,128)S(1)} %get-tuple-element.40.g1_ref), channel_id=1, source_target_pairs={{0,2},{2,0},{4,6},{6,4},{1,3},{3,1},{5,7},{7,5},{8,10},{10,8},{12,... | collective-permute-start | bytes 73736 | tf_op jit(solution)/shard_map/ppermute | solution.py:32
  46.0 4.2 %collective-permute-start.13 = (f32[24,512]{1,0:T(8,128)S(1)}, f32[24,512]{1,0:T(8,128)S(1)}, u32[]{:S(2)}, u32[]{:S(2)}) collective-permute-start(f32[24,512]{1,0:T(8,128)S(1)} %pad_maximum_fusion.1), channel_id=1, source_target_pairs={{0,1},{1,0},{2,3},{3,2},{4,5},{5,4},{6,7},{7,6},{8,9},{9,8},{10,11... | collective-permute-start | bytes 147464 | tf_op jit(solution)/shard_map/ppermute | solution.py:52
  54.9 4.2 %collective-permute-start.14 = (f32[24,512]{1,0:T(8,128)S(1)}, f32[24,512]{1,0:T(8,128)S(1)}, u32[]{:S(2)}, u32[]{:S(2)}) collective-permute-start(f32[24,512]{1,0:T(8,128)S(1)} %slice.56), channel_id=1, source_target_pairs={{0,1},{1,0},{2,3},{3,2},{4,5},{5,4},{6,7},{7,6},{8,9},{9,8},{10,11... | collective-permute-start | bytes 147464 | tf_op jit(solution)/shard_map/ppermute | solution.py:63
  59.0 1.3 %collective-permute-start.15 = (f32[24,256]{1,0:T(8,128)S(1)}, f32[24,256]{1,0:T(8,128)S(1)}, u32[]{:S(2)}, u32[]{:S(2)}) collective-permute-start(f32[24,256]{1,0:T(8,128)S(1)} %slice_add_fusion), channel_id=1, source_target_pairs={{0,2},{2,0},{4,6},{6,4},{1,3},{3,1},{5,7},{7,5},{8,10},{10,8},{12,... | collective-permute-start | bytes 73736 | tf_op jit(solution)/shard_map/ppermute | solution.py:32
  59.0 3.3 %collective-permute-start.16 = (f32[24,256]{1,0:T(8,128)S(1)}, f32[24,256]{1,0:T(8,128)S(1)}, u32[]{:S(2)}, u32[]{:S(2)}) collective-permute-start(f32[24,256]{1,0:T(8,128)S(1)} %slice_add_fusion), channel_id=1, source_target_pairs={{0,6},{2,4},{4,2},{6,0},{1,7},{3,5},{5,3},{7,1},{8,14},{10,12},{12... | collective-permute-start | bytes 73736 | tf_op jit(solution)/shard_map/ppermute | solution.py:32
  62.8 4.4 %collective-permute-start.17 = (f32[24,384]{1,0:T(8,128)S(1)}, f32[24,384]{1,0:T(8,128)S(1)}, u32[]{:S(2)}, u32[]{:S(2)}) collective-permute-start(f32[24,384]{1,0:T(8,128)S(1)} %get-tuple-element.55.p0_ref), channel_id=1, source_target_pairs={{0,8},{8,0},{16,24},{24,16},{1,9},{9,1},{17,25},{25,17},{2,10},{10... | collective-permute-start | bytes 110600 | tf_op jit(solution)/shard_map/ppermute | solution.py:32
  64.9 5.9 %collective-permute-start.18 = (f32[24,384]{1,0:T(8,128)S(1)}, f32[24,384]{1,0:T(8,128)S(1)}, u32[]{:S(2)}, u32[]{:S(2)}) collective-permute-start(f32[24,384]{1,0:T(8,128)S(1)} %get-tuple-element.55.p0_ref), channel_id=1, source_target_pairs={{0,16},{8,24},{16,0},{24,8},{1,17},{9,25},{17,1},{25,9},{2,18},{10... | collective-permute-start | bytes 110600 | tf_op jit(solution)/shard_map/ppermute | solution.py:32
  65.5 5.8 %collective-permute-start.19 = (f32[24,384]{1,0:T(8,128)S(1)}, f32[24,384]{1,0:T(8,128)S(1)}, u32[]{:S(2)}, u32[]{:S(2)}) collective-permute-start(f32[24,384]{1,0:T(8,128)S(1)} %get-tuple-element.55.p0_ref), channel_id=1, source_target_pairs={{0,24},{8,16},{16,8},{24,0},{1,25},{9,17},{17,9},{25,1},{2,26},{10... | collective-permute-start | bytes 110600 | tf_op jit(solution)/shard_map/ppermute | solution.py:32
  72.7 1.2 %collective-permute-start.20 = (f32[24,128]{1,0:T(8,128)S(1)}, f32[24,128]{1,0:T(8,128)S(1)}, u32[]{:S(2)}, u32[]{:S(2)}) collective-permute-start(f32[24,128]{1,0:T(8,128)S(1)} %get-tuple-element.57), channel_id=1, source_target_pairs={{0,2},{2,0},{4,6},{6,4},{1,3},{3,1},{5,7},{7,5},{8,10},{10,8},{12,... | collective-permute-start | bytes 36872 | tf_op jit(solution)/shard_map/ppermute | solution.py:91
  73.9 3.7 %collective-permute-start.21 = (f32[24,128]{1,0:T(8,128)S(1)}, f32[24,128]{1,0:T(8,128)S(1)}, u32[]{:S(2)}, u32[]{:S(2)}) collective-permute-start(f32[24,128]{1,0:T(8,128)S(1)} %add.403), channel_id=1, source_target_pairs={{0,4},{2,6},{4,0},{6,2},{1,5},{3,7},{5,1},{7,3},{8,12},{10,14},{12... | collective-permute-start | bytes 36872 | tf_op jit(solution)/shard_map/ppermute | solution.py:91
  77.6 3.7 %collective-permute-start.22 = (f32[24,128]{1,0:T(8,128)S(1)}, f32[24,128]{1,0:T(8,128)S(1)}, u32[]{:S(2)}, u32[]{:S(2)}) collective-permute-start(f32[24,128]{1,0:T(8,128)S(1)} %add.404), channel_id=1, source_target_pairs={{0,1},{1,0},{2,3},{3,2},{4,5},{5,4},{6,7},{7,6},{8,9},{9,8},{10,11... | collective-permute-start | bytes 36872 | tf_op jit(solution)/shard_map/ppermute | solution.py:91

commit v4 on v3

--- a/solution.py
+++ b/solution.py
@@ -124,11 +124,27 @@
     return y + pltpu.roll(y, GROUP - vectors, 0)
 
 
-def pack_kernel(pos_ref, spec_ref, block_ref, raw_ref, own_ref, oct_ref, list_ref):
+def pack_kernel(pos_hbm, spec_hbm, block_hbm, raw_hbm, own_ref, oct_ref, list_ref, *scratch):
+    pos_ref, spec_ref, block_ref, raw_ref, sems = scratch
+    copies = [
+        pltpu.make_async_copy(source, target, sems.at[n])
+        for n, (source, target) in enumerate(
+            (
+                (pos_hbm, pos_ref),
+                (spec_hbm, spec_ref),
+                (block_hbm, block_ref),
+                (raw_hbm, raw_ref),
+            )
+        )
+    ]
+    for copy in copies:
+        copy.start()
+    for copy in copies:
+        copy.wait()
     vectors = block_ref.shape[4]
     atoms = pos_ref.shape[-1]
     for a in range(3):
-        parts = [block_ref[0, 0, 0, a], pos_ref[0, 0, 0, a : a + 1, :]]
+        parts = [block_ref[0, 0, 0, a], pos_ref[a]]
         used = vectors + 1
         if a == 0:
             parts.append(spec_ref[0, 0].astype(jnp.float32))
@@ -138,6 +154,30 @@
     pieces = [raw_ref[n // 4, n // 2 % 2, n % 2 : n % 2 + 1, :] for n in range(8)]
     list_ref[...] = jnp.concatenate(pieces, axis=1)
     pick_octants(own_ref, list_ref, oct_ref)
+
+
+def prepare_kernel(
+    atoms, ghosts, near_ref, emb_ref, rin_ref, rout_ref, read_ref, idx_ref, low_ref, in_ref, out_ref, col_ref
+):
+    index = table_index(near_ref[...], atoms, ghosts)
+    idx_ref[...] = index
+    low = lax.broadcasted_iota(jnp.int32, low_ref.shape, 0) == index % LANES
+    low_ref[...] = jnp.where(low, 1.0, 0.0).astype(jnp.bfloat16)
+    high, middle, rest = split_parts(rin_ref[...])
+    stack = [high, middle, rest, high, middle, high]
+    pad = in_ref.shape[1] - 6 * rin_ref.shape[0]
+    stack = jnp.concatenate(stack + [jnp.zeros((pad, rin_ref.shape[1]), jnp.float32)], axis=0)
+    in_ref[...] = jnp.transpose(stack).astype(jnp.bfloat16)
+    high, rest, _ = split_parts(rout_ref[...])
+    out_ref[...] = jnp.concatenate(
+        [jnp.concatenate([high, high], axis=1), jnp.concatenate([rest, rest], axis=1)], axis=0
+    ).astype(jnp.bfloat16)
+    species = emb_ref.shape[0]
+    lane = lax.broadcasted_iota(jnp.int32, col_ref.shape, 1)
+    columns = jnp.broadcast_to(column(read_ref[...]), col_ref.shape)
+    for n in range(species):
+        columns = jnp.where(lane == n, column(emb_ref[n : n + 1, :]), columns)
+    col_ref[...] = columns
 
 
 def pick_octants(own_ref, list_ref, oct_ref):
@@ -420,18 +460,19 @@
 def first_kernel(
     ghosts,
     vectors,
+    basis,
+    species,
     idx_ref,
     own_ref,
     g1_ref,
     g2_ref,
     g3_ref,
-    emb_ref,
-    rin_ref,
-    rout_ref,
-    read_ref,
+    low_ref,
+    in_ref,
+    out_ref,
+    col_ref,
     own_out,
     ghost_out,
-    low_out,
     unit_ref,
     inv_ref,
     sums_ref,
@@ -451,34 +492,22 @@
 ):
     atoms = own_ref.shape[1]
     fanout = idx_ref.shape[1] // atoms
-    species, channels = emb_ref.shape
-    basis, hidden_units = rin_ref.shape
+    channels = col_ref.shape[0]
     pairs = pair_list(fanout)
     slots = range(fanout)
-    embeds = [column(emb_ref[s : s + 1, :]) for s in range(species)]
-    read_col[...] = jnp.broadcast_to(column(read_ref[...]), read_col.shape)
+    embeds = [col_ref[:, n : n + 1] for n in range(species)]
+    read_col[...] = jnp.broadcast_to(col_ref[:, species : species + 1], read_col.shape)
     fill_table(table, own_ref, (g1_ref, g2_ref, g3_ref), vectors, ghosts, True)
 
     def embed(kind):
         value = embeds[0]
-        for s in range(1, species):
-            value = jnp.where(kind == float(s), embeds[s], value)
+        for n in range(1, species):
+            value = jnp.where(kind == float(n), embeds[n], value)
         return value
 
     own_embed = embed(own_ref[vectors + 1 : vectors + 2, :])
-    low = lax.broadcasted_iota(jnp.int32, (LANES, idx_ref.shape[1]), 0) == idx_ref[...] % LANES
-    low_out[...] = jnp.where(low, 1.0, 0.0).astype(jnp.bfloat16)
-
-    high, middle, rest = split_parts(rin_ref[...])
-    stack = [high, middle, rest, high, middle, high]
-    pad = LANES * (-(-(6 * basis) // LANES)) - 6 * basis
-    stack = jnp.concatenate(stack + [jnp.zeros((pad, hidden_units), jnp.float32)], axis=0)
-    inward = jnp.transpose(stack)[:, : 6 * basis].astype(jnp.bfloat16)
-    high, rest, _ = split_parts(rout_ref[...])
-    outward = jnp.concatenate(
-        [jnp.concatenate([high, high], axis=1), jnp.concatenate([rest, rest], axis=1)], axis=0
-    ).astype(jnp.bfloat16)
-
+    inward = in_ref[:, : 6 * basis]
+    outward = out_ref[...]
     diffs, units, invs = [], [], []
     for k in slots:
         cut = slot_cut(k, atoms)
@@ -567,7 +596,7 @@
         sums_ref[tile_rows(n // 4), :] = sum_rows(parts)
     finish_product(
         idx_ref,
-        low_out,
+        low_ref,
         unit_ref,
         inv_ref,
         sums_ref,
@@ -647,13 +676,7 @@
         ghost_out,
         vectors,
     )
-    row = lax.broadcasted_iota(jnp.int32, gram_out.shape, 0)
-    lane = lax.broadcasted_iota(jnp.int32, gram_out.shape, 1)
-    total = jnp.zeros(gram_out.shape, jnp.float32)
-    for n in range(vectors):
-        value = jnp.sum(shifted[n], axis=1, keepdims=True)
-        total = jnp.where(lane == (row + vectors - n) % vectors, value, total)
-    gram_out[...] = jnp.where((row < vectors) & (lane < vectors), total, 0.0)
+    gram_out[...] = from_shifted(shifted, vectors)
 
 
 def middle_kernel(vectors, own_ref, sums_ref, list_ref, full_ref, oct_ref):
@@ -680,15 +703,24 @@
     return jnp.where(row % GROUP < vectors, x, 0.0)
 
 
+def pack_gram(total, edge):
+    lane = lax.broadcasted_iota(jnp.int32, (GROUP, LANES), 1)
+    out = total[rows(0)]
+    out = jnp.where(lane >= 2 * GROUP, pltpu.roll(total[rows(1)], GROUP, 1), out)
+    if edge is not None:
+        out = jnp.where(lane >= 3 * GROUP, pltpu.roll(edge, 3 * GROUP, 1), out)
+    return jnp.where(lane >= 4 * GROUP, pltpu.roll(total[rows(2)], 2 * GROUP, 1), out)
+
+
 def gram_kernel(vectors, start_ref, first_ref, own_ref, sums_ref, list_ref, full_ref, gram_ref):
-    total = jnp.zeros(gram_ref.shape, jnp.float32)
+    total = jnp.zeros((3 * GROUP, LANES), jnp.float32)
     for a in range(3):
         second = add_octants(own_ref[rows(a), :], sums_ref[rows(a), :], list_ref[...], vectors)
         full_ref[rows(a), :] = second
         stack = jnp.concatenate([start_ref[rows(a), :], first_ref[rows(a), :], second], axis=0)
         stack = only_vectors(stack, vectors)
         total += inner(stack, stack)
-    gram_ref[...] = total
+    gram_ref[...] = pack_gram(total, None)
 
 
 def packet_start(vectors, own_ref, sums_ref, ghost_ref, list_ref, part_ref, packet_ref):
@@ -778,41 +810,71 @@
         )
         stack = only_vectors(stack, vectors)
         total += inner(stack, stack)
-    edge = pltpu.roll(edge_ref[...], 2 * GROUP, 1)
-    lane = lax.broadcasted_iota(jnp.int32, edge.shape, 1)
     cut = slice(2 * width, 2 * width + LANES)
-    packet_ref[rows(0), cut] = total[rows(0)]
-    packet_ref[rows(1), cut] = jnp.where(lane // GROUP == 2, edge, total[rows(1)])
-    packet_ref[rows(2), cut] = total[rows(2)]
+    packet_ref[rows(0), cut] = pack_gram(total, edge_ref[...])
+    packet_ref[GROUP : 3 * GROUP, cut] = jnp.zeros((2 * GROUP, LANES), jnp.float32)
+
+
+def shifted_products(x, y, vectors):
+    return [x * (pltpu.roll(y, n, 0) if n else y) for n in range(vectors)]
+
+
+def from_shifted(shifted, vectors):
+    shape = (GROUP, LANES)
+    row = lax.broadcasted_iota(jnp.int32, shape, 0)
+    lane = lax.broadcasted_iota(jnp.int32, shape, 1)
+    total = jnp.zeros(shape, jnp.float32)
+    for n in range(vectors):
+        value = jnp.sum(shifted[n], axis=1, keepdims=True)
+        total = jnp.where(lane == (row + vectors - n) % vectors, value, total)
+    return jnp.where((row < vectors) & (lane < vectors), total, 0.0)
 
 
 def gram_merge_kernel(
-    vectors, side_ref, part_ref, p0_ref, p1_ref, p2_ref, p3_ref, full_ref, gram_ref
+    vectors, side_ref, part_ref, p0_ref, p1_ref, p2_ref, p3_ref, full_ref, gram_ref, spread
 ):
     width = (p0_ref.shape[1] - LANES) // 2
+    atoms = part_ref.shape[1]
     side = side_ref[...]
     packets = (p0_ref, p1_ref, p2_ref, p3_ref)
     shares = []
     for n in range(4):
         lists = packet_lists(packets[n], vectors, width)
-        extra = jnp.zeros((GROUP, LANES), jnp.float32)
+        terms = [only_vectors(arriving(side, packets, n, a, width), vectors) for a in range(3)]
+        packed = jnp.concatenate([split_rows(t, vectors) for t in terms], axis=0)
+        onehot = lax.broadcasted_iota(jnp.int32, (atoms, width), 0) == lists
+        placed = lax.dot_general(
+            packed.astype(jnp.bfloat16),
+            jnp.where(onehot, 1.0, 0.0).astype(jnp.bfloat16),
+            (((1,), (1,)), ((), ())),
+            preferred_element_type=jnp.float32,
+        )
+        total = None
         for a in range(3):
-            terms = only_vectors(arriving(side, packets, n, a, width), vectors)
-            values = only_vectors(packets[n][rows(a), :width], vectors)
-            zero = jnp.zeros((GROUP, part_ref.shape[1]), jnp.float32)
-            spread = only_vectors(add_octants(zero, terms, lists, vectors), vectors)
-            extra += inner(terms, values) + inner(values, terms) + inner(spread, spread)
+            value = join_rows(placed[rows(a)], vectors)
+            spread[rows(a), :] = value
             if n == 0:
-                full_ref[rows(a), :] = part_ref[rows(a), :] + spread
-        share = packets[n][:, 2 * width : 2 * width + LANES]
-        shares.append((share, pltpu.roll(extra, 2 * GROUP, 1)))
+                full_ref[rows(a), :] = part_ref[rows(a), :] + value
+            at = only_vectors(packets[n][rows(a), :width], vectors)
+            at = at + pltpu.roll(at, vectors, 0)
+            back = jnp.concatenate(
+                [
+                    gather_lanes(spread, lists[:, j * LANES : (j + 1) * LANES], a)
+                    for j in range(width // LANES)
+                ],
+                axis=1,
+            )
+            found = shifted_products(terms[a], at + at + back, vectors)
+            total = found if total is None else [x + y for x, y in zip(total, found)]
+        shares.append([packets[n][rows(0), 2 * width : 2 * width + LANES]] + total)
 
     def add(x, y):
-        return x[0] + y[0], x[1] + y[1]
-
-    share, extra = add(add(shares[0], shares[1]), add(shares[2], shares[3]))
-    gram_ref[0 : 2 * GROUP, :] = share[0 : 2 * GROUP]
-    gram_ref[rows(2), :] = share[rows(2)] + extra
+        return [p + q for p, q in zip(x, y)]
+
+    total = add(add(shares[0], shares[1]), add(shares[2], shares[3]))
+    gram = total[0] + pltpu.roll(from_shifted(total[1:], vectors), 4 * GROUP, 1)
+    for n in range(gram_ref.shape[0]):
+        gram_ref[n] = gram
 
 
 def last_kernel(
@@ -823,12 +885,19 @@
     lane = lax.broadcasted_iota(jnp.int32, shape, 1)
     inside = (row < vectors) & (lane < vectors)
     eye = jnp.where((row == lane) & inside, 1.0, 0.0)
-
-    def block(i, j):
-        part = gram_ref[rows(i), :]
-        if j:
-            part = pltpu.roll(part, LANES - GROUP * j, 1)
-        return jnp.where(inside, part * scale, 0.0)
+    levels = [gram_ref[n] for n in range(gram_ref.shape[0])]
+    while len(levels) > 1:
+        levels = [sum(levels[n : n + 2]) for n in range(0, len(levels), 2)]
+    gram = levels[0] * scale
+
+    def block(x, n):
+        return jnp.where(inside, pltpu.roll(x, LANES - GROUP * n, 1) if n else x, 0.0)
+
+    def beside(*parts):
+        out = parts[0]
+        for n, part in enumerate(parts[1:]):
+            out = out + pltpu.roll(part, GROUP * (n + 1), 1)
+        return out
 
     def mul(x, y):
         return sum(x[:, k : k + 1] * y[k : k + 1, :] for k in range(vectors))
@@ -840,44 +909,33 @@
             out = jnp.where(row == k, line, out)
         return out
 
-    def factor(m):
-        upper = jnp.zeros(shape, jnp.float32)
-        inverse = eye
+    def solve(m):
         for j in range(vectors):
-            scale_j = 1.0 / jnp.sqrt(m[j : j + 1, j : j + 1])
-            column = m[:, j : j + 1] * scale_j
-            line = m[j : j + 1, :] * scale_j
-            upper = jnp.where((row == j) & (lane >= j), line, upper)
-            m = m - column * line
-            own = inverse[j : j + 1, :] * scale_j
-            inverse = jnp.where(
-                row == j, own, jnp.where(row > j, inverse - column * own, inverse)
+            inverse = lax.rsqrt(m[j : j + 1, j : j + 1])
+            line = m[j : j + 1, :] * inverse
+            m = jnp.where(
+                row == j, line, jnp.where(row > j, m - (m[:, j : j + 1] * inverse) * line, m)
             )
-        return upper, inverse
-
-    ss, su, uu = block(0, 0), block(0, 1), block(1, 1)
-    uq, qq = block(1, 2), block(2, 2)
-    sq, qu = uu, uq
-    _, p0 = factor(ss)
+        return jnp.where((lane >= row) & inside, m, 0.0), m
+
+    ss, su, uu, uq, qq = (block(gram, n) for n in range(5))
+    qq = 0.5 * (qq + flip(qq))
+    _, m = solve(beside(ss, su, uu, eye))
+    p0 = block(m, 3)
     p0t = flip(p0)
-    a1 = mul(mul(p0, su), p0t)
-    a1t = flip(a1)
-    up1, p1 = factor(mul(mul(p0, uu), p0t) - mul(a1t, a1))
-    b = mul(p1, p0)
-    a = -mul(p1, mul(a1t, p0))
+    a1 = mul(block(m, 1), p0t)
+    up1, m = solve(beside(mul(block(m, 2), p0t) - mul(a1, a1), p0, mul(a1, p0)))
+    b, a = block(m, 1), -block(m, 2)
     at, bt = flip(a), flip(b)
-    right_s = mul(su, at) + mul(sq, bt)
+    known = mul(up1, beside(flip(up1), p0))
+    right_s = mul(su, at) + mul(uu, bt)
     right_u = mul(uu, at) + mul(uq, bt)
-    right_q = mul(qu, at) + mul(qq, bt)
+    right_q = mul(uq, at) + mul(qq, bt)
     a2 = mul(a, right_s) + mul(b, right_u)
-    c2 = mul(p0, right_s)
     ww = mul(a, right_u) + mul(b, right_q)
-    a2t, c2t = flip(a2), flip(c2)
-    up2, p2 = factor(ww - mul(a2t, a2) - mul(c2t, c2))
-    weights = (
-        -mul(p2, mul(a2t, a) + mul(c2t, p0)),
-        mul(p2, a - mul(a2t, b)),
-        mul(p2, b),
+    moved = mul(a2, beside(a2, a, b)) + known
+    up2, m = solve(
+        beside(ww - block(moved, 0), -block(moved, 1), a - block(moved, 2), b)
     )
     small = (slice(0, vectors), slice(0, vectors))
     diag_ref[0] = a1[small]
@@ -886,22 +944,29 @@
     off_ref[1] = up2[small]
     for comp in range(3):
         value = None
-        for weight, ref in zip(weights, (start_ref, first_ref, second_ref)):
+        for n, ref in enumerate((start_ref, first_ref, second_ref)):
             for w in range(vectors):
                 line = GROUP * comp + w
-                term = weight[:, w : w + 1] * ref[line : line + 1, :]
+                place = GROUP * (n + 1) + w
+                term = m[:, place : place + 1] * ref[line : line + 1, :]
                 value = term if value is None else value + term
         next_ref[0, 0, 0, comp] = value[:vectors]
 
 
-def call(body, outs, args, scratch=()):
+def call(body, outs, args, scratch=(), flops=0, spaces=pltpu.VMEM):
     outs = [shape if isinstance(shape[0], tuple) else (shape, jnp.float32) for shape in outs]
     return pl.pallas_call(
         body,
         out_shape=[jax.ShapeDtypeStruct(shape, kind) for shape, kind in outs],
-        in_specs=[pl.BlockSpec(memory_space=pltpu.VMEM)] * len(args),
+        in_specs=[pl.BlockSpec(memory_space=spaces)] * len(args),
         out_specs=[pl.BlockSpec(memory_space=pltpu.VMEM)] * len(outs),
-        scratch_shapes=[pltpu.VMEM(shape, jnp.float32) for shape in scratch],
+        scratch_shapes=[
+            pltpu.VMEM(shape, jnp.float32) if isinstance(shape, tuple) else shape
+            for shape in scratch
+        ],
+        cost_estimate=pl.CostEstimate(flops=flops, bytes_accessed=0, transcendentals=0)
+        if flops
+        else None,
         compiler_params=pltpu.CompilerParams(vmem_limit_bytes=VMEM_BYTES),
     )(*args)
 
@@ -947,17 +1012,39 @@
     width = 8 * ghosts
     high = 3 * GROUP
     edges = fanout * atoms
-    index = table_index(neighbors.reshape(1, -1), atoms, ghosts)
     table_width = atoms + 7 * width
     ring = lax.axis_size("gx") == 4
+    others_count = lax.axis_size("gy") * lax.axis_size("gz")
     side = (octant_bit((GROUP, width), 0, ghosts) ^ (lax.axis_index("gx") % 2 == 1)).astype(
         jnp.float32
     )
 
+    inputs = (
+        positions.transpose(0, 1, 3, 2, 4).reshape(3, 1, atoms),
+        species,
+        start_block.transpose(0, 1, 2, 4, 3, 5),
+        ghost_lists,
+    )
     own, octants, lists = call(
         pack_kernel,
         [(high, atoms), (high, width), ((1, width), jnp.int32)],
-        (positions, species, start_block.transpose(0, 1, 2, 4, 3, 5), ghost_lists),
+        inputs,
+        [pltpu.VMEM(x.shape, x.dtype) for x in inputs]
+        + [pltpu.SemaphoreType.DMA((len(inputs),))],
+        spaces=pl.ANY,
+    )
+    basis, hidden = radial_in.shape
+    index, low, inward, outward, columns = call(
+        functools.partial(prepare_kernel, atoms, ghosts),
+        [
+            ((1, edges), jnp.int32),
+            ((LANES, edges), jnp.bfloat16),
+            ((hidden, LANES * (-(-6 * basis // LANES))), jnp.bfloat16),
+            ((2 * channels, 2 * hidden), jnp.bfloat16),
+            (channels, LANES),
+        ],
+        (neighbors.reshape(1, -1), embedding, radial_in, radial_out.T, readout.reshape(1, -1)),
+        flops=2_000_000,
     )
 
     def spread(level):
@@ -973,18 +1060,17 @@
     ]
     base_sums = 2 * fanout + pairs + fanout * fanout
     saved_shapes = [
-        ((LANES, edges), jnp.bfloat16),
         (high, edges),
         (GROUP, edges),
         (GROUP * (-(-base_sums // 4)), atoms),
         (pairs * GROUP, atoms),
     ] + [(channels, edges)] * 5
     results = call(
-        functools.partial(first_kernel, ghosts, vectors),
+        functools.partial(first_kernel, ghosts, vectors, basis, embedding.shape[0]),
         [(high, atoms), (high, 7 * width)] + saved_shapes,
         (index, own)
         + spread(octants)
-        + (embedding, radial_in, radial_out.T, readout.reshape(1, -1)),
+        + (low, inward, outward, columns),
         [(high, table_width), (channels, edges), (channels, LANES)]
         + shared
         + [(base_sums * GROUP, atoms)],
@@ -1014,7 +1100,7 @@
     own_terms, ghost_terms, edge_gram = call(
         functools.partial(second_kernel, ghosts, vectors),
         [(high, atoms), (high, 7 * width), (GROUP, LANES)],
-        (index, first) + spread(level) + tuple(saved),
+        (index, first) + spread(level) + (low,) + tuple(saved),
         [(high, table_width)] + shared,
     )
     sums, beside = return_outer(ghost_terms, width, ghosts)
@@ -1027,17 +1113,18 @@
         others = pair_exchange(packet, "gx", (1, 2, 3))
         second, gram = call(
             functools.partial(gram_merge_kernel, vectors),
-            [(high, atoms), (high, LANES)],
+            [(high, atoms), (others_count, GROUP, LANES)],
             (side, part, packet, *others),
-        )
-        gram = sum_over(gram, AXES[1:])
+            [(high, atoms)],
+        )
+        gram = lax.all_to_all(gram, AXES[1:], 0, 0, tiled=True)
     else:
         second, gram = call(
             functools.partial(gram_kernel, vectors),
-            [(high, atoms), (high, LANES)],
+            [(high, atoms), (GROUP, LANES)],
             (own, first, own_terms, sums + return_ghosts(beside, 0, ghosts), lists),
         )
-        gram = sum_over(gram, AXES)
+        gram = sum_over(gram, AXES)[None]
     following, diagonal, off = call(
         functools.partial(last_kernel, vectors, scale),
         [(1, 1, 1, 3, vectors, atoms), (2, vectors, vectors), (2, vectors, vectors)],

time: 84 us -> 82.3 us (0.980)
  blocking collectives: 0 us -> 7.93 us
  waiting for transfers between devices: 33.4 us -> 26.9 us
  starting transfers between devices: 28.7 us -> 26 us
  Pallas kernels: 17.5 us -> 16.6 us
    all_to_all x0 -> x1, blocking collectives: none -> 7.93 us  [on_device(): gram = lax.all_to_all(gram, AXES[1:], 0, 0, tiled=True)]
    ppermute x3 -> x0, waiting for transfers between devices: 5.89 us -> none  [sum_over(): x = x + lax.ppermute(x, axis, [(i, i ^ step) for i in range(size)])]
    ppermute x3 -> x0, starting transfers between devices: 2.7 us -> none  [sum_over(): x = x + lax.ppermute(x, axis, [(i, i ^ step) for i in range(size)])]
    pallas_call x8 -> x9, Pallas kernels: 17.5 us -> 16.6 us  [call(): pl.pallas_call(body, out_shape=[jax.ShapeDtypeStruct(shape, kind) for sha...]
    unnamed x17 -> x18, local copies, waits for them, and re-layouts: 2.77 us -> 3.43 us
  transfers between devices with their start and end apart: 23 -> 20, of which waited for: 18 -> 15; matrix products, arithmetic and copies ran while one was open for 0% -> 0% of each run, Pallas kernels for 0% -> 0%
where the time goes in v4:
time: 82.3 us; the launch traced here: 82 us
  waiting for transfers between devices  26.9 us (33%)
  starting transfers between devices  26 us (32%)
  Pallas kernels  16.6 us (20%)
  blocking collectives  7.93 us (10%)
  local copies, waits for them, and re-layouts  3.44 us (4%)
    ppermute x16, starting transfers between devices, pair_exchange(): lax.ppermute(x, axis, [(i, i ^ d) for i in range(size)])  19.7 us
    ppermute x16, waiting for transfers between devices, pair_exchange(): lax.ppermute(x, axis, [(i, i ^ d) for i in range(size)])  17.5 us
    pallas_call x9, Pallas kernels, call(): pl.pallas_call(body, out_shape=[jax.ShapeDtypeStruct(shape, kind) for sha...  16.6 us
    all_to_all x1, blocking collectives, on_device(): gram = lax.all_to_all(gram, AXES[1:], 0, 0, tiled=True)  7.93 us
    ppermute x2, waiting for transfers between devices, return_ghosts(): return lax.ppermute(x, axis, swap_pairs(2, 1))  5.14 us
    ppermute x2, waiting for transfers between devices, fetch_ghosts(): return lax.ppermute(x, axis, swap_pairs(2, 1))  4.26 us
    unnamed x18, local copies, waits for them, and re-layouts  3.43 us
    ppermute x2, starting transfers between devices, fetch_ghosts(): return lax.ppermute(x, axis, swap_pairs(2, 1))  3.17 us
  transfers between devices with their start and end apart: 20, of which 15 were waited for; matrix products, arithmetic and copies ran while one was open for 0% of the time, Pallas kernels for 0%

profile of v4, /device:TPU:0, one launch (start us, length us, event | category | flops | bytes accessed | tf_op | source)
XLA Modules:
  0.0 82.0 jit_solution(10703050251575476597)
XLA Ops:
  1.3 0.7 copy-done.1
  2.0 0.7 copy-done.3
  2.7 0.7 copy-done.6
  3.6 5.1 %collective-permute-start = (f32[24,128]{1,0:T(8,128)S(1)}, f32[24,128]{1,0:T(8,128)S(1)}, u32[]{:S(2)}, u32[]{:S(2)}) collective-permute-start(f32[24,128]{1,0:T(8,128)S(1)} %get-tuple-element.38), channel_id=1, source_target_pairs={{0,24},{8,16},{16,8},{24,0},{1,25},{9,17},{17,9},{25,1},{2,26},{10... | collective-permute-start | bytes 36872 | tf_op jit(solution)/shard_map/ppermute | solution.py:32
  8.8 1.6 %collective-permute-done = f32[24,128]{1,0:T(8,128)S(1)} collective-permute-done((f32[24,128]{1,0:T(8,128)S(1)}, f32[24,128]{1,0:T(8,128)S(1)}, u32[]{:S(2)}, u32[]{:S(2)}) %collective-permute-start) | collective-permute-done | bytes 12320 | tf_op jit(solution)/shard_map/ppermute | solution.py:32
  10.4 2.0 %collective-permute-done.1 = f32[24,128]{1,0:T(8,128)S(1)} collective-permute-done((f32[24,128]{1,0:T(8,128)S(1)}, f32[24,128]{1,0:T(8,128)S(1)}, u32[]{:S(2)}, u32[]{:S(2)}) %collective-permute-start.1) | collective-permute-done | bytes 12320 | tf_op jit(solution)/shard_map/ppermute | solution.py:32
  12.6 1.6 %collective-permute-start.3 = (f32[24,256]{1,0:T(8,128)S(1)}, f32[24,256]{1,0:T(8,128)S(1)}, u32[]{:S(2)}, u32[]{:S(2)}) collective-permute-start(f32[24,256]{1,0:T(8,128)S(1)} %pad_maximum_fusion.2.g1_ref), channel_id=1, source_target_pairs={{0,2},{2,0},{4,6},{6,4},{1,3},{3,1},{5,7},{7,5},{8,10},{10,8},{12,... | collective-permute-start | bytes 73736 | tf_op jit(solution)/shard_map/ppermute | solution.py:32
  14.1 1.9 %collective-permute-done.2 = f32[24,256]{1,0:T(8,128)S(1)} collective-permute-done((f32[24,256]{1,0:T(8,128)S(1)}, f32[24,256]{1,0:T(8,128)S(1)}, u32[]{:S(2)}, u32[]{:S(2)}) %collective-permute-start.2) | collective-permute-done | bytes 24608 | tf_op jit(solution)/shard_map/ppermute | solution.py:32
  16.1 1.6 %collective-permute-start.4 = (f32[24,512]{1,0:T(8,128)S(1)}, f32[24,512]{1,0:T(8,128)S(1)}, u32[]{:S(2)}, u32[]{:S(2)}) collective-permute-start(f32[24,512]{1,0:T(8,128)S(1)} %pad_maximum_fusion), channel_id=1, source_target_pairs={{0,1},{1,0},{2,3},{3,2},{4,5},{5,4},{6,7},{7,6},{8,9},{9,8},{10,11... | collective-permute-start | bytes 147464 | tf_op jit(solution)/shard_map/ppermute | solution.py:52
  18.6 1.7 %collective-permute-done.4.g3_ref = f32[24,512]{1,0:T(8,128)S(1)} collective-permute-done((f32[24,512]{1,0:T(8,128)S(1)}, f32[24,512]{1,0:T(8,128)S(1)}, u32[]{:S(2)}, u32[]{:S(2)}) %collective-permute-start.4) | collective-permute-done | bytes 49184 | tf_op jit(solution)/shard_map/ppermute | solution.py:52
  20.2 7.6 %shard_map.114 = (f32[24,256]{1,0:T(8,128)S(1)}, f32[24,896]{1,0:T(8,128)S(1)}, f32[24,1536]{1,0:T(8,128)S(1)}, f32[8,1536]{1,0:T(8,128)S(1)}, f32[144,256]{1,0:...) custom-call(s32[1,1536]{1,0:T(1,128)S(1)} %get-tuple-element.37.idx_, ...), custom_call_target="tpu_custom_call" | custom-call | tf_op jit(solution)/shard_map/pallas_call | solution.py:958
  27.8 1.6 %collective-permute-start.5 = (f32[24,512]{1,0:T(8,128)S(1)}, f32[24,512]{1,0:T(8,128)S(1)}, u32[]{:S(2)}, u32[]{:S(2)}) collective-permute-start(f32[24,512]{1,0:T(8,128)S(1)} %slice.48), channel_id=1, source_target_pairs={{0,1},{1,0},{2,3},{3,2},{4,5},{5,4},{6,7},{7,6},{8,9},{9,8},{10,11... | collective-permute-start | bytes 147464 | tf_op jit(solution)/shard_map/ppermute | solution.py:63
  29.4 2.6 %collective-permute-done.5 = f32[24,512]{1,0:T(8,128)S(1)} collective-permute-done((f32[24,512]{1,0:T(8,128)S(1)}, f32[24,512]{1,0:T(8,128)S(1)}, u32[]{:S(2)}, u32[]{:S(2)}) %collective-permute-start.5) | collective-permute-done | bytes 49184 | tf_op jit(solution)/shard_map/ppermute | solution.py:63
  32.0 1.4 %collective-permute-start.7 = (f32[24,256]{1,0:T(8,128)S(1)}, f32[24,256]{1,0:T(8,128)S(1)}, u32[]{:S(2)}, u32[]{:S(2)}) collective-permute-start(f32[24,256]{1,0:T(8,128)S(1)} %slice_add_fusion.1), channel_id=1, source_target_pairs={{0,6},{2,4},{4,2},{6,0},{1,7},{3,5},{5,3},{7,1},{8,14},{10,12},{12... | collective-permute-start | bytes 73736 | tf_op jit(solution)/shard_map/ppermute | solution.py:32
  33.4 1.9 %collective-permute-done.7 = f32[24,256]{1,0:T(8,128)S(1)} collective-permute-done((f32[24,256]{1,0:T(8,128)S(1)}, f32[24,256]{1,0:T(8,128)S(1)}, u32[]{:S(2)}, u32[]{:S(2)}) %collective-permute-start.7) | collective-permute-done | bytes 24608 | tf_op jit(solution)/shard_map/ppermute | solution.py:32
  35.6 1.8 %collective-permute-start.10 = (f32[24,256]{1,0:T(8,128)S(1)}, f32[24,256]{1,0:T(8,128)S(1)}, u32[]{:S(2)}, u32[]{:S(2)}) collective-permute-start(f32[24,256]{1,0:T(8,128)S(1)} %get-tuple-element.47.p0_ref), channel_id=1, source_target_pairs={{0,24},{8,16},{16,8},{24,0},{1,25},{9,17},{17,9},{25,1},{2,26},{10... | collective-permute-start | bytes 73736 | tf_op jit(solution)/shard_map/ppermute | solution.py:32
  37.4 2.6 %collective-permute-start.9 = (f32[24,256]{1,0:T(8,128)S(1)}, f32[24,256]{1,0:T(8,128)S(1)}, u32[]{:S(2)}, u32[]{:S(2)}) collective-permute-start(f32[24,256]{1,0:T(8,128)S(1)} %get-tuple-element.47.p0_ref), channel_id=1, source_target_pairs={{0,16},{8,24},{16,0},{24,8},{1,17},{9,25},{17,1},{25,9},{2,18},{10... | collective-permute-start | bytes 73736 | tf_op jit(solution)/shard_map/ppermute | solution.py:32
  40.1 1.3 %collective-permute-done.10.p3_ref = f32[24,256]{1,0:T(8,128)S(1)} collective-permute-done((f32[24,256]{1,0:T(8,128)S(1)}, f32[24,256]{1,0:T(8,128)S(1)}, u32[]{:S(2)}, u32[]{:S(2)}) %collective-permute-start.10) | collective-permute-done | bytes 24608 | tf_op jit(solution)/shard_map/ppermute | solution.py:32
  42.7 1.3 %collective-permute-start.12 = (f32[24,256]{1,0:T(8,128)S(1)}, f32[24,256]{1,0:T(8,128)S(1)}, u32[]{:S(2)}, u32[]{:S(2)}) collective-permute-start(f32[24,256]{1,0:T(8,128)S(1)} %get-tuple-element.49.g1_ref), channel_id=1, source_target_pairs={{0,2},{2,0},{4,6},{6,4},{1,3},{3,1},{5,7},{7,5},{8,10},{10,8},{12,... | collective-permute-start | bytes 73736 | tf_op jit(solution)/shard_map/ppermute | solution.py:32
  43.9 2.0 %collective-permute-done.11 = f32[24,256]{1,0:T(8,128)S(1)} collective-permute-done((f32[24,256]{1,0:T(8,128)S(1)}, f32[24,256]{1,0:T(8,128)S(1)}, u32[]{:S(2)}, u32[]{:S(2)}) %collective-permute-start.11) | collective-permute-done | bytes 24608 | tf_op jit(solution)/shard_map/ppermute | solution.py:32
  45.9 1.6 %collective-permute-start.13 = (f32[24,512]{1,0:T(8,128)S(1)}, f32[24,512]{1,0:T(8,128)S(1)}, u32[]{:S(2)}, u32[]{:S(2)}) collective-permute-start(f32[24,512]{1,0:T(8,128)S(1)} %pad_maximum_fusion.1), channel_id=1, source_target_pairs={{0,1},{1,0},{2,3},{3,2},{4,5},{5,4},{6,7},{7,6},{8,9},{9,8},{10,11... | collective-permute-start | bytes 147464 | tf_op jit(solution)/shard_map/ppermute | solution.py:52
  47.5 2.6 %collective-permute-done.13.g3_ref = f32[24,512]{1,0:T(8,128)S(1)} collective-permute-done((f32[24,512]{1,0:T(8,128)S(1)}, f32[24,512]{1,0:T(8,128)S(1)}, u32[]{:S(2)}, u32[]{:S(2)}) %collective-permute-start.13) | collective-permute-done | bytes 49184 | tf_op jit(solution)/shard_map/ppermute | solution.py:52
  50.1 4.6 %shard_map.117 = (f32[24,256]{1,0:T(8,128)S(1)}, f32[24,896]{1,0:T(8,128)S(1)}, f32[8,128]{1,0:T(8,128)S(1)}) custom-call(s32[1,1536]{1,0:T(1,128)S(1)} %get-tuple-element.37.idx_ref, f32[24,256]{1,0:T(8,128)S(1)} %get-tuple-element.48.own_ref.first_ref, f32[24,256]{1,0:T(8,128)S(1)} %get-tuple-element.49.g1_ref, f32[24,256]{1,0:T(8,128)S(1)} %fusion.34.g2_ref, ...), custom_call_target="tpu_custom_call" | custom-call | tf_op jit(solution)/shard_map/pallas_call | solution.py:958
  54.7 1.6 %collective-permute-start.14 = (f32[24,512]{1,0:T(8,128)S(1)}, f32[24,512]{1,0:T(8,128)S(1)}, u32[]{:S(2)}, u32[]{:S(2)}) collective-permute-start(f32[24,512]{1,0:T(8,128)S(1)} %slice.56), channel_id=1, source_target_pairs={{0,1},{1,0},{2,3},{3,2},{4,5},{5,4},{6,7},{7,6},{8,9},{9,8},{10,11... | collective-permute-start | bytes 147464 | tf_op jit(solution)/shard_map/ppermute | solution.py:63
  56.3 2.6 %collective-permute-done.14 = f32[24,512]{1,0:T(8,128)S(1)} collective-permute-done((f32[24,512]{1,0:T(8,128)S(1)}, f32[24,512]{1,0:T(8,128)S(1)}, u32[]{:S(2)}, u32[]{:S(2)}) %collective-permute-start.14) | collective-permute-done | bytes 49184 | tf_op jit(solution)/shard_map/ppermute | solution.py:63
  58.9 1.3 %collective-permute-start.16 = (f32[24,256]{1,0:T(8,128)S(1)}, f32[24,256]{1,0:T(8,128)S(1)}, u32[]{:S(2)}, u32[]{:S(2)}) collective-permute-start(f32[24,256]{1,0:T(8,128)S(1)} %slice_add_fusion), channel_id=1, source_target_pairs={{0,6},{2,4},{4,2},{6,0},{1,7},{3,5},{5,3},{7,1},{8,14},{10,12},{12... | collective-permute-start | bytes 73736 | tf_op jit(solution)/shard_map/ppermute | solution.py:32
  60.2 2.0 %collective-permute-done.16 = f32[24,256]{1,0:T(8,128)S(1)} collective-permute-done((f32[24,256]{1,0:T(8,128)S(1)}, f32[24,256]{1,0:T(8,128)S(1)}, u32[]{:S(2)}, u32[]{:S(2)}) %collective-permute-start.16) | collective-permute-done | bytes 24608 | tf_op jit(solution)/shard_map/ppermute | solution.py:32
  62.7 2.0 %collective-permute-start.17 = (f32[24,384]{1,0:T(8,128)S(1)}, f32[24,384]{1,0:T(8,128)S(1)}, u32[]{:S(2)}, u32[]{:S(2)}) collective-permute-start(f32[24,384]{1,0:T(8,128)S(1)} %get-tuple-element.63.p0_ref), channel_id=1, source_target_pairs={{0,8},{8,0},{16,24},{24,16},{1,9},{9,1},{17,25},{25,17},{2,10},{10... | collective-permute-start | bytes 110600 | tf_op jit(solution)/shard_map/ppermute | solution.py:32
  65.3 1.8 %collective-permute-start.19 = (f32[24,384]{1,0:T(8,128)S(1)}, f32[24,384]{1,0:T(8,128)S(1)}, u32[]{:S(2)}, u32[]{:S(2)}) collective-permute-start(f32[24,384]{1,0:T(8,128)S(1)} %get-tuple-element.63.p0_ref), channel_id=1, source_target_pairs={{0,24},{8,16},{16,8},{24,0},{1,25},{9,17},{17,9},{25,1},{2,26},{10... | collective-permute-start | bytes 110600 | tf_op jit(solution)/shard_map/ppermute | solution.py:32
  67.1 3.5 %collective-permute-done.18.p2_ref = f32[24,384]{1,0:T(8,128)S(1)} collective-permute-done((f32[24,384]{1,0:T(8,128)S(1)}, f32[24,384]{1,0:T(8,128)S(1)}, u32[]{:S(2)}, u32[]{:S(2)}) %collective-permute-start.18) | collective-permute-done | bytes 36896 | tf_op jit(solution)/shard_map/ppermute | solution.py:32
  71.6 7.9 %all_to_all.5.gram_ref = f32[8,8,128]{2,1,0:T(8,128)S(1)} all-to-all(f32[8,8,128]{2,1,0:T(8,128)S(1)} %get-tuple-element.65), channel_id=1, replica_groups=mesh['gx'=4,'gy'=4,'gz'=2] {'gy','gz'}, dimensions={0} | all-to-all | bytes 65536 | tf_op jit(solution)/shard_map/all_to_all | solution.py:1120
  79.5 2.5 %shard_map.120 = (f32[1,1,1,3,4,256]{5,4,3,2,1,0:T(4,128)}, f32[2,4,4]{2,1,0:T(4,128)}, f32[2,4,4]{2,1,0:T(4,128)}) custom-call(f32[24,256]{1,0:T(8,128)S(1)} %get-tuple-element.36.own_ref.start_ref, f32[24,256]{1,0:T(8,128)S(1)} %get-tuple-element.48.own_ref.first_ref, f32[24,256]{1,0:T(8,128)S(1)} %get-tuple-element.64.second_ref, ...), custom_call_target="tpu_custom_call" | custom-call | tf_op jit(solution)/shard_map/pallas_call | solution.py:958
  (55 shorter events, 5.7 us)
Async XLA Ops:
  0.6 0.7 copy-start.5
  1.3 0.7 copy-start.1
  2.0 0.7 copy-start.3
  2.7 0.7 copy-start.6
  3.6 6.8 %collective-permute-start = (f32[24,128]{1,0:T(8,128)S(1)}, f32[24,128]{1,0:T(8,128)S(1)}, u32[]{:S(2)}, u32[]{:S(2)}) collective-permute-start(f32[24,128]{1,0:T(8,128)S(1)} %get-tuple-element.38), channel_id=1, source_target_pairs={{0,24},{8,16},{16,8},{24,0},{1,25},{9,17},{17,9},{25,1},{2,26},{10... | collective-permute-start | bytes 36872 | tf_op jit(solution)/shard_map/ppermute | solution.py:32
  8.7 3.7 %collective-permute-start.1 = (f32[24,128]{1,0:T(8,128)S(1)}, f32[24,128]{1,0:T(8,128)S(1)}, u32[]{:S(2)}, u32[]{:S(2)}) collective-permute-start(f32[24,128]{1,0:T(8,128)S(1)} %get-tuple-element.38), channel_id=1, source_target_pairs={{0,8},{8,0},{16,24},{24,16},{1,9},{9,1},{17,25},{25,17},{2,10},{10... | collective-permute-start | bytes 36872 | tf_op jit(solution)/shard_map/ppermute | solution.py:32
  12.5 3.5 %collective-permute-start.2 = (f32[24,256]{1,0:T(8,128)S(1)}, f32[24,256]{1,0:T(8,128)S(1)}, u32[]{:S(2)}, u32[]{:S(2)}) collective-permute-start(f32[24,256]{1,0:T(8,128)S(1)} %pad_maximum_fusion.2.g1_ref), channel_id=1, source_target_pairs={{0,6},{2,4},{4,2},{6,0},{1,7},{3,5},{5,3},{7,1},{8,14},{10,12},{12... | collective-permute-start | bytes 73736 | tf_op jit(solution)/shard_map/ppermute | solution.py:32
  12.6 3.5 %collective-permute-start.3 = (f32[24,256]{1,0:T(8,128)S(1)}, f32[24,256]{1,0:T(8,128)S(1)}, u32[]{:S(2)}, u32[]{:S(2)}) collective-permute-start(f32[24,256]{1,0:T(8,128)S(1)} %pad_maximum_fusion.2.g1_ref), channel_id=1, source_target_pairs={{0,2},{2,0},{4,6},{6,4},{1,3},{3,1},{5,7},{7,5},{8,10},{10,8},{12,... | collective-permute-start | bytes 73736 | tf_op jit(solution)/shard_map/ppermute | solution.py:32
  16.0 1.6 %copy-start = (f32[128,64]{0,1:T(8,128)S(1)}, f32[128,64]{0,1:T(8,128)}, u32[]{:S(2)}) copy-start(f32[128,64]{0,1:T(8,128)} %param.16) | copy-start | bytes 98308
  16.1 1.6 %copy-start.2 = (s32[1,1,1,6,256]{4,2,3,1,0:T(1,128)S(1)}, s32[1,1,1,6,256]{4,2,3,1,0:T(1,128)}, u32[]{:S(2)}) copy-start(s32[1,1,1,6,256]{4,2,3,1,0:T(1,128)} %param.12) | copy-start | bytes 18436
  16.1 1.6 %copy-start.4 = (f32[8,128]{1,0:T(8,128)S(1)}, f32[8,128]{1,0:T(8,128)}, u32[]{:S(2)}) copy-start(f32[8,128]{1,0:T(8,128)} %rin_ref.1) | copy-start | bytes 12292
  16.1 4.2 %collective-permute-start.4 = (f32[24,512]{1,0:T(8,128)S(1)}, f32[24,512]{1,0:T(8,128)S(1)}, u32[]{:S(2)}, u32[]{:S(2)}) collective-permute-start(f32[24,512]{1,0:T(8,128)S(1)} %pad_maximum_fusion), channel_id=1, source_target_pairs={{0,1},{1,0},{2,3},{3,2},{4,5},{5,4},{6,7},{7,6},{8,9},{9,8},{10,11... | collective-permute-start | bytes 147464 | tf_op jit(solution)/shard_map/ppermute | solution.py:52
  17.7 0.7 copy-start.7
  17.7 0.7 copy-start.8
  27.8 4.2 %collective-permute-start.5 = (f32[24,512]{1,0:T(8,128)S(1)}, f32[24,512]{1,0:T(8,128)S(1)}, u32[]{:S(2)}, u32[]{:S(2)}) collective-permute-start(f32[24,512]{1,0:T(8,128)S(1)} %slice.48), channel_id=1, source_target_pairs={{0,1},{1,0},{2,3},{3,2},{4,5},{5,4},{6,7},{7,6},{8,9},{9,8},{10,11... | collective-permute-start | bytes 147464 | tf_op jit(solution)/shard_map/ppermute | solution.py:63
  32.0 1.4 %collective-permute-start.6 = (f32[24,256]{1,0:T(8,128)S(1)}, f32[24,256]{1,0:T(8,128)S(1)}, u32[]{:S(2)}, u32[]{:S(2)}) collective-permute-start(f32[24,256]{1,0:T(8,128)S(1)} %slice_add_fusion.1), channel_id=1, source_target_pairs={{0,2},{2,0},{4,6},{6,4},{1,3},{3,1},{5,7},{7,5},{8,10},{10,8},{12,... | collective-permute-start | bytes 73736 | tf_op jit(solution)/shard_map/ppermute | solution.py:32
  32.0 3.3 %collective-permute-start.7 = (f32[24,256]{1,0:T(8,128)S(1)}, f32[24,256]{1,0:T(8,128)S(1)}, u32[]{:S(2)}, u32[]{:S(2)}) collective-permute-start(f32[24,256]{1,0:T(8,128)S(1)} %slice_add_fusion.1), channel_id=1, source_target_pairs={{0,6},{2,4},{4,2},{6,0},{1,7},{3,5},{5,3},{7,1},{8,14},{10,12},{12... | collective-permute-start | bytes 73736 | tf_op jit(solution)/shard_map/ppermute | solution.py:32
  35.6 5.8 %collective-permute-start.10 = (f32[24,256]{1,0:T(8,128)S(1)}, f32[24,256]{1,0:T(8,128)S(1)}, u32[]{:S(2)}, u32[]{:S(2)}) collective-permute-start(f32[24,256]{1,0:T(8,128)S(1)} %get-tuple-element.47.p0_ref), channel_id=1, source_target_pairs={{0,24},{8,16},{16,8},{24,0},{1,25},{9,17},{17,9},{25,1},{2,26},{10... | collective-permute-start | bytes 73736 | tf_op jit(solution)/shard_map/ppermute | solution.py:32
  37.4 4.4 %collective-permute-start.8 = (f32[24,256]{1,0:T(8,128)S(1)}, f32[24,256]{1,0:T(8,128)S(1)}, u32[]{:S(2)}, u32[]{:S(2)}) collective-permute-start(f32[24,256]{1,0:T(8,128)S(1)} %get-tuple-element.47.p0_ref), channel_id=1, source_target_pairs={{0,8},{8,0},{16,24},{24,16},{1,9},{9,1},{17,25},{25,17},{2,10},{10... | collective-permute-start | bytes 73736 | tf_op jit(solution)/shard_map/ppermute | solution.py:32
  37.4 4.7 %collective-permute-start.9 = (f32[24,256]{1,0:T(8,128)S(1)}, f32[24,256]{1,0:T(8,128)S(1)}, u32[]{:S(2)}, u32[]{:S(2)}) collective-permute-start(f32[24,256]{1,0:T(8,128)S(1)} %get-tuple-element.47.p0_ref), channel_id=1, source_target_pairs={{0,16},{8,24},{16,0},{24,8},{1,17},{9,25},{17,1},{25,9},{2,18},{10... | collective-permute-start | bytes 73736 | tf_op jit(solution)/shard_map/ppermute | solution.py:32
  42.5 3.4 %collective-permute-start.11 = (f32[24,256]{1,0:T(8,128)S(1)}, f32[24,256]{1,0:T(8,128)S(1)}, u32[]{:S(2)}, u32[]{:S(2)}) collective-permute-start(f32[24,256]{1,0:T(8,128)S(1)} %get-tuple-element.49.g1_ref), channel_id=1, source_target_pairs={{0,6},{2,4},{4,2},{6,0},{1,7},{3,5},{5,3},{7,1},{8,14},{10,12},{12... | collective-permute-start | bytes 73736 | tf_op jit(solution)/shard_map/ppermute | solution.py:32
  42.7 3.2 %collective-permute-start.12 = (f32[24,256]{1,0:T(8,128)S(1)}, f32[24,256]{1,0:T(8,128)S(1)}, u32[]{:S(2)}, u32[]{:S(2)}) collective-permute-start(f32[24,256]{1,0:T(8,128)S(1)} %get-tuple-element.49.g1_ref), channel_id=1, source_target_pairs={{0,2},{2,0},{4,6},{6,4},{1,3},{3,1},{5,7},{7,5},{8,10},{10,8},{12,... | collective-permute-start | bytes 73736 | tf_op jit(solution)/shard_map/ppermute | solution.py:32
  45.9 4.2 %collective-permute-start.13 = (f32[24,512]{1,0:T(8,128)S(1)}, f32[24,512]{1,0:T(8,128)S(1)}, u32[]{:S(2)}, u32[]{:S(2)}) collective-permute-start(f32[24,512]{1,0:T(8,128)S(1)} %pad_maximum_fusion.1), channel_id=1, source_target_pairs={{0,1},{1,0},{2,3},{3,2},{4,5},{5,4},{6,7},{7,6},{8,9},{9,8},{10,11... | collective-permute-start | bytes 147464 | tf_op jit(solution)/shard_map/ppermute | solution.py:52
  54.7 4.2 %collective-permute-start.14 = (f32[24,512]{1,0:T(8,128)S(1)}, f32[24,512]{1,0:T(8,128)S(1)}, u32[]{:S(2)}, u32[]{:S(2)}) collective-permute-start(f32[24,512]{1,0:T(8,128)S(1)} %slice.56), channel_id=1, source_target_pairs={{0,1},{1,0},{2,3},{3,2},{4,5},{5,4},{6,7},{7,6},{8,9},{9,8},{10,11... | collective-permute-start | bytes 147464 | tf_op jit(solution)/shard_map/ppermute | solution.py:63
  58.9 1.3 %collective-permute-start.15 = (f32[24,256]{1,0:T(8,128)S(1)}, f32[24,256]{1,0:T(8,128)S(1)}, u32[]{:S(2)}, u32[]{:S(2)}) collective-permute-start(f32[24,256]{1,0:T(8,128)S(1)} %slice_add_fusion), channel_id=1, source_target_pairs={{0,2},{2,0},{4,6},{6,4},{1,3},{3,1},{5,7},{7,5},{8,10},{10,8},{12,... | collective-permute-start | bytes 73736 | tf_op jit(solution)/shard_map/ppermute | solution.py:32
  58.9 3.3 %collective-permute-start.16 = (f32[24,256]{1,0:T(8,128)S(1)}, f32[24,256]{1,0:T(8,128)S(1)}, u32[]{:S(2)}, u32[]{:S(2)}) collective-permute-start(f32[24,256]{1,0:T(8,128)S(1)} %slice_add_fusion), channel_id=1, source_target_pairs={{0,6},{2,4},{4,2},{6,0},{1,7},{3,5},{5,3},{7,1},{8,14},{10,12},{12... | collective-permute-start | bytes 73736 | tf_op jit(solution)/shard_map/ppermute | solution.py:32
  62.7 4.4 %collective-permute-start.17 = (f32[24,384]{1,0:T(8,128)S(1)}, f32[24,384]{1,0:T(8,128)S(1)}, u32[]{:S(2)}, u32[]{:S(2)}) collective-permute-start(f32[24,384]{1,0:T(8,128)S(1)} %get-tuple-element.63.p0_ref), channel_id=1, source_target_pairs={{0,8},{8,0},{16,24},{24,16},{1,9},{9,1},{17,25},{25,17},{2,10},{10... | collective-permute-start | bytes 110600 | tf_op jit(solution)/shard_map/ppermute | solution.py:32
  64.8 5.9 %collective-permute-start.18 = (f32[24,384]{1,0:T(8,128)S(1)}, f32[24,384]{1,0:T(8,128)S(1)}, u32[]{:S(2)}, u32[]{:S(2)}) collective-permute-start(f32[24,384]{1,0:T(8,128)S(1)} %get-tuple-element.63.p0_ref), channel_id=1, source_target_pairs={{0,16},{8,24},{16,0},{24,8},{1,17},{9,25},{17,1},{25,9},{2,18},{10... | collective-permute-start | bytes 110600 | tf_op jit(solution)/shard_map/ppermute | solution.py:32
  65.3 5.8 %collective-permute-start.19 = (f32[24,384]{1,0:T(8,128)S(1)}, f32[24,384]{1,0:T(8,128)S(1)}, u32[]{:S(2)}, u32[]{:S(2)}) collective-permute-start(f32[24,384]{1,0:T(8,128)S(1)} %get-tuple-element.63.p0_ref), channel_id=1, source_target_pairs={{0,24},{8,16},{16,8},{24,0},{1,25},{9,17},{17,9},{25,1},{2,26},{10... | collective-permute-start | bytes 110600 | tf_op jit(solution)/shard_map/ppermute | solution.py:32

commit v5 on v4

--- a/solution.py
+++ b/solution.py
@@ -62,7 +62,7 @@
     if size == 2:
         return lax.ppermute(x, axis, swap_pairs(2, 1))
     near, far, odd = ring_sides(x, bit)
-    return jnp.where(octant_bit(x.shape, bit, ghosts) ^ odd, near, far)
+    return jnp.where(octant_bit(x.shape, bit, ghosts) == odd, far, near)
 
 
 def spread_outer(level, ghosts):
@@ -91,6 +91,20 @@
             x = x + lax.ppermute(x, axis, [(i, i ^ step) for i in range(size)])
             step *= 2
     return x
+
+
+def sum_across(x):
+    axes = AXES[1:]
+    sizes = [lax.axis_size(axis) for axis in axes]
+    if sizes != [4, 2]:
+        return [sum_over(x, axes)]
+    x = x + pair_exchange(x, axes[0], (1,))[0]
+    count = sizes[0] * sizes[1]
+    terms = [
+        lax.ppermute(x, axes, [(i, i ^ d) for i in range(count)])
+        for d in (2 * sizes[1], 1, 2 * sizes[1] + 1)
+    ]
+    return [x] + terms
 
 
 def rows(a):
@@ -831,7 +845,7 @@
 
 
 def gram_merge_kernel(
-    vectors, side_ref, part_ref, p0_ref, p1_ref, p2_ref, p3_ref, full_ref, gram_ref, spread
+    vectors, side_ref, p3_ref, p2_ref, part_ref, p0_ref, p1_ref, full_ref, gram_ref, spread
 ):
     width = (p0_ref.shape[1] - LANES) // 2
     atoms = part_ref.shape[1]
@@ -872,20 +886,18 @@
         return [p + q for p, q in zip(x, y)]
 
     total = add(add(shares[0], shares[1]), add(shares[2], shares[3]))
-    gram = total[0] + pltpu.roll(from_shifted(total[1:], vectors), 4 * GROUP, 1)
-    for n in range(gram_ref.shape[0]):
-        gram_ref[n] = gram
-
-
-def last_kernel(
-    vectors, scale, start_ref, first_ref, second_ref, gram_ref, next_ref, diag_ref, off_ref
-):
+    gram_ref[...] = total[0] + pltpu.roll(from_shifted(total[1:], vectors), 4 * GROUP, 1)
+
+
+def last_kernel(vectors, scale, start_ref, first_ref, second_ref, *refs):
+    gram_refs, refs = refs[:-7], refs[-7:]
+    next_hbm, diag_hbm, off_hbm, next_ref, diag_ref, off_ref, sems = refs
     shape = (GROUP, LANES)
     row = lax.broadcasted_iota(jnp.int32, shape, 0)
     lane = lax.broadcasted_iota(jnp.int32, shape, 1)
     inside = (row < vectors) & (lane < vectors)
     eye = jnp.where((row == lane) & inside, 1.0, 0.0)
-    levels = [gram_ref[n] for n in range(gram_ref.shape[0])]
+    levels = [ref[...] for ref in gram_refs]
     while len(levels) > 1:
         levels = [sum(levels[n : n + 2]) for n in range(0, len(levels), 2)]
     gram = levels[0] * scale
@@ -942,6 +954,12 @@
     diag_ref[1] = a2[small]
     off_ref[0] = up1[small]
     off_ref[1] = up2[small]
+    copies = [
+        pltpu.make_async_copy(diag_ref, diag_hbm, sems.at[0]),
+        pltpu.make_async_copy(off_ref, off_hbm, sems.at[1]),
+    ]
+    for copy in copies:
+        copy.start()
     for comp in range(3):
         value = None
         for n, ref in enumerate((start_ref, first_ref, second_ref)):
@@ -951,15 +969,19 @@
                 term = m[:, place : place + 1] * ref[line : line + 1, :]
                 value = term if value is None else value + term
         next_ref[0, 0, 0, comp] = value[:vectors]
-
-
-def call(body, outs, args, scratch=(), flops=0, spaces=pltpu.VMEM):
+    copies.append(pltpu.make_async_copy(next_ref, next_hbm, sems.at[2]))
+    copies[-1].start()
+    for copy in copies:
+        copy.wait()
+
+
+def call(body, outs, args, scratch=(), flops=0, spaces=pltpu.VMEM, out_spaces=pltpu.VMEM):
     outs = [shape if isinstance(shape[0], tuple) else (shape, jnp.float32) for shape in outs]
     return pl.pallas_call(
         body,
         out_shape=[jax.ShapeDtypeStruct(shape, kind) for shape, kind in outs],
         in_specs=[pl.BlockSpec(memory_space=spaces)] * len(args),
-        out_specs=[pl.BlockSpec(memory_space=pltpu.VMEM)] * len(outs),
+        out_specs=[pl.BlockSpec(memory_space=out_spaces)] * len(outs),
         scratch_shapes=[
             pltpu.VMEM(shape, jnp.float32) if isinstance(shape, tuple) else shape
             for shape in scratch
@@ -1014,7 +1036,6 @@
     edges = fanout * atoms
     table_width = atoms + 7 * width
     ring = lax.axis_size("gx") == 4
-    others_count = lax.axis_size("gy") * lax.axis_size("gz")
     side = (octant_bit((GROUP, width), 0, ghosts) ^ (lax.axis_index("gx") % 2 == 1)).astype(
         jnp.float32
     )
@@ -1031,7 +1052,7 @@
         inputs,
         [pltpu.VMEM(x.shape, x.dtype) for x in inputs]
         + [pltpu.SemaphoreType.DMA((len(inputs),))],
-        spaces=pl.ANY,
+        spaces=pltpu.HBM,
     )
     basis, hidden = radial_in.shape
     index, low, inward, outward, columns = call(
@@ -1113,22 +1134,25 @@
         others = pair_exchange(packet, "gx", (1, 2, 3))
         second, gram = call(
             functools.partial(gram_merge_kernel, vectors),
-            [(high, atoms), (others_count, GROUP, LANES)],
-            (side, part, packet, *others),
+            [(high, atoms), (GROUP, LANES)],
+            (side, *others[:0:-1], part, packet, others[0]),
             [(high, atoms)],
         )
-        gram = lax.all_to_all(gram, AXES[1:], 0, 0, tiled=True)
+        gram = sum_across(gram)
     else:
         second, gram = call(
             functools.partial(gram_kernel, vectors),
             [(high, atoms), (GROUP, LANES)],
             (own, first, own_terms, sums + return_ghosts(beside, 0, ghosts), lists),
         )
-        gram = sum_over(gram, AXES)[None]
+        gram = [sum_over(gram, AXES)]
+    shapes = [(1, 1, 1, 3, vectors, atoms), (2, vectors, vectors), (2, vectors, vectors)]
     following, diagonal, off = call(
         functools.partial(last_kernel, vectors, scale),
-        [(1, 1, 1, 3, vectors, atoms), (2, vectors, vectors), (2, vectors, vectors)],
-        (own, first, second, gram),
+        shapes,
+        (own, first, second, *gram),
+        shapes + [pltpu.SemaphoreType.DMA((len(shapes),))],
+        out_spaces=pltpu.HBM,
     )
     return following.transpose(0, 1, 2, 4, 3, 5), diagonal, off
 

time: 82.3 us -> 81.7 us (level)
  blocking collectives: 7.93 us -> 0 us
  waiting for transfers between devices: 26.9 us -> 31.1 us
  starting transfers between devices: 26 us -> 29.1 us
    all_to_all x1 -> x0, blocking collectives: 7.93 us -> none  [on_device(): gram = lax.all_to_all(gram, AXES[1:], 0, 0, tiled=True)]
    ppermute x0 -> x3, waiting for transfers between devices: none -> 3.72 us  [sum_across(): lax.ppermute(x, axes, [(i, i ^ d) for i in range(count)])]
    ppermute x0 -> x3, starting transfers between devices: none -> 3.49 us  [sum_across(): lax.ppermute(x, axes, [(i, i ^ d) for i in range(count)])]
    ppermute x16 -> x17, waiting for transfers between devices: 17.5 us -> 18 us  [pair_exchange(): lax.ppermute(x, axis, [(i, i ^ d) for i in range(size)])]
    ppermute x16 -> x17, starting transfers between devices: 19.7 us -> 19.3 us  [pair_exchange(): lax.ppermute(x, axis, [(i, i ^ d) for i in range(size)])]
  transfers between devices with their start and end apart: 20 -> 24, of which waited for: 15 -> 20; matrix products, arithmetic and copies ran while one was open for 0% -> 0% of each run, Pallas kernels for 0% -> 0%
where the time goes in v5:
time: 81.7 us; the launch traced here: 81.4 us
  waiting for transfers between devices  31.1 us (38%)
  starting transfers between devices  29.1 us (36%)
  Pallas kernels  16.6 us (20%)
  local copies, waits for them, and re-layouts  3.44 us (4%)
  between operations  0.83 us (1%)
    ppermute x17, starting transfers between devices, pair_exchange(): lax.ppermute(x, axis, [(i, i ^ d) for i in range(size)])  19.3 us
    ppermute x17, waiting for transfers between devices, pair_exchange(): lax.ppermute(x, axis, [(i, i ^ d) for i in range(size)])  18 us
    pallas_call x9, Pallas kernels, call(): pl.pallas_call(body, out_shape=[jax.ShapeDtypeStruct(shape, kind) for sha...  16.6 us
    ppermute x2, waiting for transfers between devices, return_ghosts(): return lax.ppermute(x, axis, swap_pairs(2, 1))  5.16 us
    ppermute x2, waiting for transfers between devices, fetch_ghosts(): return lax.ppermute(x, axis, swap_pairs(2, 1))  4.27 us
    ppermute x3, waiting for transfers between devices, sum_across(): lax.ppermute(x, axes, [(i, i ^ d) for i in range(count)])  3.72 us
    ppermute x3, starting transfers between devices, sum_across(): lax.ppermute(x, axes, [(i, i ^ d) for i in range(count)])  3.49 us
    unnamed x18, local copies, waits for them, and re-layouts  3.43 us
  transfers between devices with their start and end apart: 24, of which 20 were waited for; matrix products, arithmetic and copies ran while one was open for 0% of the time, Pallas kernels for 0%

profile of v5, /device:TPU:0, one launch (start us, length us, event | category | flops | bytes accessed | tf_op | source)
XLA Modules:
  0.0 81.4 jit_solution(4587930411782223039)
XLA Ops:
  3.6 5.1 %collective-permute-start = (f32[24,128]{1,0:T(8,128)S(1)}, f32[24,128]{1,0:T(8,128)S(1)}, u32[]{:S(2)}, u32[]{:S(2)}) collective-permute-start(f32[24,128]{1,0:T(8,128)S(1)} %get-tuple-element.38), channel_id=1, source_target_pairs={{0,24},{8,16},{16,8},{24,0},{1,25},{9,17},{17,9},{25,1},{2,26},{10... | collective-permute-start | bytes 36872 | tf_op jit(solution)/shard_map/ppermute | solution.py:32
  8.8 1.6 %collective-permute-done = f32[24,128]{1,0:T(8,128)S(1)} collective-permute-done((f32[24,128]{1,0:T(8,128)S(1)}, f32[24,128]{1,0:T(8,128)S(1)}, u32[]{:S(2)}, u32[]{:S(2)}) %collective-permute-start) | collective-permute-done | bytes 12320 | tf_op jit(solution)/shard_map/ppermute | solution.py:32
  10.4 2.0 %collective-permute-done.1 = f32[24,128]{1,0:T(8,128)S(1)} collective-permute-done((f32[24,128]{1,0:T(8,128)S(1)}, f32[24,128]{1,0:T(8,128)S(1)}, u32[]{:S(2)}, u32[]{:S(2)}) %collective-permute-start.1) | collective-permute-done | bytes 12320 | tf_op jit(solution)/shard_map/ppermute | solution.py:32
  12.6 1.6 %collective-permute-start.3 = (f32[24,256]{1,0:T(8,128)S(1)}, f32[24,256]{1,0:T(8,128)S(1)}, u32[]{:S(2)}, u32[]{:S(2)}) collective-permute-start(f32[24,256]{1,0:T(8,128)S(1)} %pad_maximum_fusion.2.g1_ref), channel_id=1, source_target_pairs={{0,2},{2,0},{4,6},{6,4},{1,3},{3,1},{5,7},{7,5},{8,10},{10,8},{12,... | collective-permute-start | bytes 73736 | tf_op jit(solution)/shard_map/ppermute | solution.py:32
  14.1 1.9 %collective-permute-done.2 = f32[24,256]{1,0:T(8,128)S(1)} collective-permute-done((f32[24,256]{1,0:T(8,128)S(1)}, f32[24,256]{1,0:T(8,128)S(1)}, u32[]{:S(2)}, u32[]{:S(2)}) %collective-permute-start.2) | collective-permute-done | bytes 24608 | tf_op jit(solution)/shard_map/ppermute | solution.py:32
  16.1 1.6 %collective-permute-start.4 = (f32[24,512]{1,0:T(8,128)S(1)}, f32[24,512]{1,0:T(8,128)S(1)}, u32[]{:S(2)}, u32[]{:S(2)}) collective-permute-start(f32[24,512]{1,0:T(8,128)S(1)} %pad_maximum_fusion), channel_id=1, source_target_pairs={{0,1},{1,0},{2,3},{3,2},{4,5},{5,4},{6,7},{7,6},{8,9},{9,8},{10,11... | collective-permute-start | bytes 147464 | tf_op jit(solution)/shard_map/ppermute | solution.py:52
  18.6 1.7 %collective-permute-done.4.g3_ref = f32[24,512]{1,0:T(8,128)S(1)} collective-permute-done((f32[24,512]{1,0:T(8,128)S(1)}, f32[24,512]{1,0:T(8,128)S(1)}, u32[]{:S(2)}, u32[]{:S(2)}) %collective-permute-start.4) | collective-permute-done | bytes 49184 | tf_op jit(solution)/shard_map/ppermute | solution.py:52
  20.2 7.6 %shard_map.114 = (f32[24,256]{1,0:T(8,128)S(1)}, f32[24,896]{1,0:T(8,128)S(1)}, f32[24,1536]{1,0:T(8,128)S(1)}, f32[8,1536]{1,0:T(8,128)S(1)}, f32[144,256]{1,0:...) custom-call(s32[1,1536]{1,0:T(1,128)S(1)} %get-tuple-element.37.idx_, ...), custom_call_target="tpu_custom_call" | custom-call | tf_op jit(solution)/shard_map/pallas_call | solution.py:980
  27.8 1.6 %collective-permute-start.5 = (f32[24,512]{1,0:T(8,128)S(1)}, f32[24,512]{1,0:T(8,128)S(1)}, u32[]{:S(2)}, u32[]{:S(2)}) collective-permute-start(f32[24,512]{1,0:T(8,128)S(1)} %slice.48), channel_id=1, source_target_pairs={{0,1},{1,0},{2,3},{3,2},{4,5},{5,4},{6,7},{7,6},{8,9},{9,8},{10,11... | collective-permute-start | bytes 147464 | tf_op jit(solution)/shard_map/ppermute | solution.py:63
  29.4 2.6 %collective-permute-done.5 = f32[24,512]{1,0:T(8,128)S(1)} collective-permute-done((f32[24,512]{1,0:T(8,128)S(1)}, f32[24,512]{1,0:T(8,128)S(1)}, u32[]{:S(2)}, u32[]{:S(2)}) %collective-permute-start.5) | collective-permute-done | bytes 49184 | tf_op jit(solution)/shard_map/ppermute | solution.py:63
  32.0 1.4 %collective-permute-start.7 = (f32[24,256]{1,0:T(8,128)S(1)}, f32[24,256]{1,0:T(8,128)S(1)}, u32[]{:S(2)}, u32[]{:S(2)}) collective-permute-start(f32[24,256]{1,0:T(8,128)S(1)} %slice_add_fusion.1), channel_id=1, source_target_pairs={{0,2},{2,0},{4,6},{6,4},{1,3},{3,1},{5,7},{7,5},{8,10},{10,8},{12,... | collective-permute-start | bytes 73736 | tf_op jit(solution)/shard_map/ppermute | solution.py:32
  33.4 2.0 %collective-permute-done.6 = f32[24,256]{1,0:T(8,128)S(1)} collective-permute-done((f32[24,256]{1,0:T(8,128)S(1)}, f32[24,256]{1,0:T(8,128)S(1)}, u32[]{:S(2)}, u32[]{:S(2)}) %collective-permute-start.6) | collective-permute-done | bytes 24608 | tf_op jit(solution)/shard_map/ppermute | solution.py:32
  35.6 1.8 %collective-permute-start.10 = (f32[24,256]{1,0:T(8,128)S(1)}, f32[24,256]{1,0:T(8,128)S(1)}, u32[]{:S(2)}, u32[]{:S(2)}) collective-permute-start(f32[24,256]{1,0:T(8,128)S(1)} %get-tuple-element.47.p0_ref), channel_id=1, source_target_pairs={{0,24},{8,16},{16,8},{24,0},{1,25},{9,17},{17,9},{25,1},{2,26},{10... | collective-permute-start | bytes 73736 | tf_op jit(solution)/shard_map/ppermute | solution.py:32
  37.5 2.6 %collective-permute-start.9 = (f32[24,256]{1,0:T(8,128)S(1)}, f32[24,256]{1,0:T(8,128)S(1)}, u32[]{:S(2)}, u32[]{:S(2)}) collective-permute-start(f32[24,256]{1,0:T(8,128)S(1)} %get-tuple-element.47.p0_ref), channel_id=1, source_target_pairs={{0,16},{8,24},{16,0},{24,8},{1,17},{9,25},{17,1},{25,9},{2,18},{10... | collective-permute-start | bytes 73736 | tf_op jit(solution)/shard_map/ppermute | solution.py:32
  40.1 1.2 %collective-permute-done.10.p3_ref = f32[24,256]{1,0:T(8,128)S(1)} collective-permute-done((f32[24,256]{1,0:T(8,128)S(1)}, f32[24,256]{1,0:T(8,128)S(1)}, u32[]{:S(2)}, u32[]{:S(2)}) %collective-permute-start.10) | collective-permute-done | bytes 24608 | tf_op jit(solution)/shard_map/ppermute | solution.py:32
  43.9 2.1 %collective-permute-done.11 = f32[24,256]{1,0:T(8,128)S(1)} collective-permute-done((f32[24,256]{1,0:T(8,128)S(1)}, f32[24,256]{1,0:T(8,128)S(1)}, u32[]{:S(2)}, u32[]{:S(2)}) %collective-permute-start.11) | collective-permute-done | bytes 24608 | tf_op jit(solution)/shard_map/ppermute | solution.py:32
  46.0 1.6 %collective-permute-start.13 = (f32[24,512]{1,0:T(8,128)S(1)}, f32[24,512]{1,0:T(8,128)S(1)}, u32[]{:S(2)}, u32[]{:S(2)}) collective-permute-start(f32[24,512]{1,0:T(8,128)S(1)} %pad_maximum_fusion.1), channel_id=1, source_target_pairs={{0,1},{1,0},{2,3},{3,2},{4,5},{5,4},{6,7},{7,6},{8,9},{9,8},{10,11... | collective-permute-start | bytes 147464 | tf_op jit(solution)/shard_map/ppermute | solution.py:52
  47.6 2.6 %collective-permute-done.13.g3_ref = f32[24,512]{1,0:T(8,128)S(1)} collective-permute-done((f32[24,512]{1,0:T(8,128)S(1)}, f32[24,512]{1,0:T(8,128)S(1)}, u32[]{:S(2)}, u32[]{:S(2)}) %collective-permute-start.13) | collective-permute-done | bytes 49184 | tf_op jit(solution)/shard_map/ppermute | solution.py:52
  50.2 4.6 %shard_map.117 = (f32[24,256]{1,0:T(8,128)S(1)}, f32[24,896]{1,0:T(8,128)S(1)}, f32[8,128]{1,0:T(8,128)S(1)}) custom-call(s32[1,1536]{1,0:T(1,128)S(1)} %get-tuple-element.37.idx_ref, f32[24,256]{1,0:T(8,128)S(1)} %get-tuple-element.48.own_ref.first_ref, f32[24,256]{1,0:T(8,128)S(1)} %get-tuple-element.49.g1_ref, f32[24,256]{1,0:T(8,128)S(1)} %xor_select_fusion.g2_ref, ...), custom_call_target="tpu_custom_call" | custom-call | tf_op jit(solution)/shard_map/pallas_call | solution.py:980
  54.8 1.6 %collective-permute-start.14 = (f32[24,512]{1,0:T(8,128)S(1)}, f32[24,512]{1,0:T(8,128)S(1)}, u32[]{:S(2)}, u32[]{:S(2)}) collective-permute-start(f32[24,512]{1,0:T(8,128)S(1)} %slice.56), channel_id=1, source_target_pairs={{0,1},{1,0},{2,3},{3,2},{4,5},{5,4},{6,7},{7,6},{8,9},{9,8},{10,11... | collective-permute-start | bytes 147464 | tf_op jit(solution)/shard_map/ppermute | solution.py:63
  56.3 2.6 %collective-permute-done.14 = f32[24,512]{1,0:T(8,128)S(1)} collective-permute-done((f32[24,512]{1,0:T(8,128)S(1)}, f32[24,512]{1,0:T(8,128)S(1)}, u32[]{:S(2)}, u32[]{:S(2)}) %collective-permute-start.14) | collective-permute-done | bytes 49184 | tf_op jit(solution)/shard_map/ppermute | solution.py:63
  58.9 1.2 %collective-permute-start.16 = (f32[24,256]{1,0:T(8,128)S(1)}, f32[24,256]{1,0:T(8,128)S(1)}, u32[]{:S(2)}, u32[]{:S(2)}) collective-permute-start(f32[24,256]{1,0:T(8,128)S(1)} %slice_add_fusion), channel_id=1, source_target_pairs={{0,2},{2,0},{4,6},{6,4},{1,3},{3,1},{5,7},{7,5},{8,10},{10,8},{12,... | collective-permute-start | bytes 73736 | tf_op jit(solution)/shard_map/ppermute | solution.py:32
  60.1 2.1 %collective-permute-done.15 = f32[24,256]{1,0:T(8,128)S(1)} collective-permute-done((f32[24,256]{1,0:T(8,128)S(1)}, f32[24,256]{1,0:T(8,128)S(1)}, u32[]{:S(2)}, u32[]{:S(2)}) %collective-permute-start.15) | collective-permute-done | bytes 24608 | tf_op jit(solution)/shard_map/ppermute | solution.py:32
  62.7 2.0 %collective-permute-start.17 = (f32[24,384]{1,0:T(8,128)S(1)}, f32[24,384]{1,0:T(8,128)S(1)}, u32[]{:S(2)}, u32[]{:S(2)}) collective-permute-start(f32[24,384]{1,0:T(8,128)S(1)} %get-tuple-element.62.p0_ref), channel_id=1, source_target_pairs={{0,24},{8,16},{16,8},{24,0},{1,25},{9,17},{17,9},{25,1},{2,26},{10... | collective-permute-start | bytes 110600 | tf_op jit(solution)/shard_map/ppermute | solution.py:32
  64.8 1.3 %collective-permute-start.18 = (f32[24,384]{1,0:T(8,128)S(1)}, f32[24,384]{1,0:T(8,128)S(1)}, u32[]{:S(2)}, u32[]{:S(2)}) collective-permute-start(f32[24,384]{1,0:T(8,128)S(1)} %get-tuple-element.62.p0_ref), channel_id=1, source_target_pairs={{0,16},{8,24},{16,0},{24,8},{1,17},{9,25},{17,1},{25,9},{2,18},{10... | collective-permute-start | bytes 110600 | tf_op jit(solution)/shard_map/ppermute | solution.py:32
  67.1 1.8 %collective-permute-done.17.p3_ref = f32[24,384]{1,0:T(8,128)S(1)} collective-permute-done((f32[24,384]{1,0:T(8,128)S(1)}, f32[24,384]{1,0:T(8,128)S(1)}, u32[]{:S(2)}, u32[]{:S(2)}) %collective-permute-start.17) | collective-permute-done | bytes 36896 | tf_op jit(solution)/shard_map/ppermute | solution.py:32
  70.5 1.2 %collective-permute-done.20 = f32[8,128]{1,0:T(8,128)S(1)} collective-permute-done((f32[8,128]{1,0:T(8,128)S(1)}, f32[8,128]{1,0:T(8,128)S(1)}, u32[]{:S(2)}, u32[]{:S(2)}) %collective-permute-start.20) | collective-permute-done | bytes 4128 | tf_op jit(solution)/shard_map/ppermute | solution.py:32
  71.7 1.2 %collective-permute-start.21 = (f32[8,128]{1,0:T(8,128)S(1)}, f32[8,128]{1,0:T(8,128)S(1)}, u32[]{:S(2)}, u32[]{:S(2)}) collective-permute-start(f32[8,128]{1,0:T(8,128)S(1)} %add.108.refs_0_), channel_id=1, source_target_pairs={{0,4},{1,5},{2,6},{3,7},{4,0},{5,1},{6,2},{7,3},{8,12},{9,13},{10,... | collective-permute-start | bytes 12296 | tf_op jit(solution)/shard_map/ppermute | solution.py:104
  72.9 1.5 %collective-permute-start.22 = (f32[8,128]{1,0:T(8,128)S(1)}, f32[8,128]{1,0:T(8,128)S(1)}, u32[]{:S(2)}, u32[]{:S(2)}) collective-permute-start(f32[8,128]{1,0:T(8,128)S(1)} %add.108.refs_0_), channel_id=1, source_target_pairs={{0,1},{1,0},{2,3},{3,2},{4,5},{5,4},{6,7},{7,6},{8,9},{9,8},{10,11... | collective-permute-start | bytes 12296 | tf_op jit(solution)/shard_map/ppermute | solution.py:104
  75.3 1.2 %collective-permute-done.22.refs_2_ = f32[8,128]{1,0:T(8,128)S(1)} collective-permute-done((f32[8,128]{1,0:T(8,128)S(1)}, f32[8,128]{1,0:T(8,128)S(1)}, u32[]{:S(2)}, u32[]{:S(2)}) %collective-permute-start.22) | collective-permute-done | bytes 4128 | tf_op jit(solution)/shard_map/ppermute | solution.py:104
  76.5 2.4 %collective-permute-done.23.refs_3_ = f32[8,128]{1,0:T(8,128)S(1)} collective-permute-done((f32[8,128]{1,0:T(8,128)S(1)}, f32[8,128]{1,0:T(8,128)S(1)}, u32[]{:S(2)}, u32[]{:S(2)}) %collective-permute-start.23) | collective-permute-done | bytes 4128 | tf_op jit(solution)/shard_map/ppermute | solution.py:104
  78.9 2.5 %shard_map.120 = (f32[1,1,1,3,4,256]{5,4,3,2,1,0:T(4,128)}, f32[2,4,4]{2,1,0:T(4,128)}, f32[2,4,4]{2,1,0:T(4,128)}) custom-call(f32[24,256]{1,0:T(8,128)S(1)} %get-tuple-element.36.own_ref.start_ref, f32[24,256]{1,0:T(8,128)S(1)} %get-tuple-element.48.own_ref.first_ref, f32[24,256]{1,0:T(8,128)S(1)} %get-tuple-element.64.second_ref, ...), custom_call_target="tpu_custom_call" | custom-call | tf_op jit(solution)/shard_map/pallas_call | solution.py:980
  (63 shorter events, 11.0 us)
Async XLA Ops:
  0.6 0.7 copy-start.5
  1.3 0.7 copy-start.1
  2.0 0.7 copy-start.3
  2.7 0.7 copy-start.6
  3.6 6.8 %collective-permute-start = (f32[24,128]{1,0:T(8,128)S(1)}, f32[24,128]{1,0:T(8,128)S(1)}, u32[]{:S(2)}, u32[]{:S(2)}) collective-permute-start(f32[24,128]{1,0:T(8,128)S(1)} %get-tuple-element.38), channel_id=1, source_target_pairs={{0,24},{8,16},{16,8},{24,0},{1,25},{9,17},{17,9},{25,1},{2,26},{10... | collective-permute-start | bytes 36872 | tf_op jit(solution)/shard_map/ppermute | solution.py:32
  8.7 3.7 %collective-permute-start.1 = (f32[24,128]{1,0:T(8,128)S(1)}, f32[24,128]{1,0:T(8,128)S(1)}, u32[]{:S(2)}, u32[]{:S(2)}) collective-permute-start(f32[24,128]{1,0:T(8,128)S(1)} %get-tuple-element.38), channel_id=1, source_target_pairs={{0,8},{8,0},{16,24},{24,16},{1,9},{9,1},{17,25},{25,17},{2,10},{10... | collective-permute-start | bytes 36872 | tf_op jit(solution)/shard_map/ppermute | solution.py:32
  12.5 3.5 %collective-permute-start.2 = (f32[24,256]{1,0:T(8,128)S(1)}, f32[24,256]{1,0:T(8,128)S(1)}, u32[]{:S(2)}, u32[]{:S(2)}) collective-permute-start(f32[24,256]{1,0:T(8,128)S(1)} %pad_maximum_fusion.2.g1_ref), channel_id=1, source_target_pairs={{0,6},{2,4},{4,2},{6,0},{1,7},{3,5},{5,3},{7,1},{8,14},{10,12},{12... | collective-permute-start | bytes 73736 | tf_op jit(solution)/shard_map/ppermute | solution.py:32
  12.6 3.5 %collective-permute-start.3 = (f32[24,256]{1,0:T(8,128)S(1)}, f32[24,256]{1,0:T(8,128)S(1)}, u32[]{:S(2)}, u32[]{:S(2)}) collective-permute-start(f32[24,256]{1,0:T(8,128)S(1)} %pad_maximum_fusion.2.g1_ref), channel_id=1, source_target_pairs={{0,2},{2,0},{4,6},{6,4},{1,3},{3,1},{5,7},{7,5},{8,10},{10,8},{12,... | collective-permute-start | bytes 73736 | tf_op jit(solution)/shard_map/ppermute | solution.py:32
  16.0 1.6 %copy-start = (f32[128,64]{0,1:T(8,128)S(1)}, f32[128,64]{0,1:T(8,128)}, u32[]{:S(2)}) copy-start(f32[128,64]{0,1:T(8,128)} %param.16) | copy-start | bytes 98308
  16.1 1.6 %copy-start.2 = (s32[1,1,1,6,256]{4,2,3,1,0:T(1,128)S(1)}, s32[1,1,1,6,256]{4,2,3,1,0:T(1,128)}, u32[]{:S(2)}) copy-start(s32[1,1,1,6,256]{4,2,3,1,0:T(1,128)} %param.12) | copy-start | bytes 18436
  16.1 1.6 %copy-start.4 = (f32[8,128]{1,0:T(8,128)S(1)}, f32[8,128]{1,0:T(8,128)}, u32[]{:S(2)}) copy-start(f32[8,128]{1,0:T(8,128)} %rin_ref.1) | copy-start | bytes 12292
  16.1 4.2 %collective-permute-start.4 = (f32[24,512]{1,0:T(8,128)S(1)}, f32[24,512]{1,0:T(8,128)S(1)}, u32[]{:S(2)}, u32[]{:S(2)}) collective-permute-start(f32[24,512]{1,0:T(8,128)S(1)} %pad_maximum_fusion), channel_id=1, source_target_pairs={{0,1},{1,0},{2,3},{3,2},{4,5},{5,4},{6,7},{7,6},{8,9},{9,8},{10,11... | collective-permute-start | bytes 147464 | tf_op jit(solution)/shard_map/ppermute | solution.py:52
  17.7 0.7 copy-start.8
  27.8 4.2 %collective-permute-start.5 = (f32[24,512]{1,0:T(8,128)S(1)}, f32[24,512]{1,0:T(8,128)S(1)}, u32[]{:S(2)}, u32[]{:S(2)}) collective-permute-start(f32[24,512]{1,0:T(8,128)S(1)} %slice.48), channel_id=1, source_target_pairs={{0,1},{1,0},{2,3},{3,2},{4,5},{5,4},{6,7},{7,6},{8,9},{9,8},{10,11... | collective-permute-start | bytes 147464 | tf_op jit(solution)/shard_map/ppermute | solution.py:63
  32.0 3.3 %collective-permute-start.6 = (f32[24,256]{1,0:T(8,128)S(1)}, f32[24,256]{1,0:T(8,128)S(1)}, u32[]{:S(2)}, u32[]{:S(2)}) collective-permute-start(f32[24,256]{1,0:T(8,128)S(1)} %slice_add_fusion.1), channel_id=1, source_target_pairs={{0,6},{2,4},{4,2},{6,0},{1,7},{3,5},{5,3},{7,1},{8,14},{10,12},{12... | collective-permute-start | bytes 73736 | tf_op jit(solution)/shard_map/ppermute | solution.py:32
  32.0 3.3 %collective-permute-start.7 = (f32[24,256]{1,0:T(8,128)S(1)}, f32[24,256]{1,0:T(8,128)S(1)}, u32[]{:S(2)}, u32[]{:S(2)}) collective-permute-start(f32[24,256]{1,0:T(8,128)S(1)} %slice_add_fusion.1), channel_id=1, source_target_pairs={{0,2},{2,0},{4,6},{6,4},{1,3},{3,1},{5,7},{7,5},{8,10},{10,8},{12,... | collective-permute-start | bytes 73736 | tf_op jit(solution)/shard_map/ppermute | solution.py:32
  35.6 5.7 %collective-permute-start.10 = (f32[24,256]{1,0:T(8,128)S(1)}, f32[24,256]{1,0:T(8,128)S(1)}, u32[]{:S(2)}, u32[]{:S(2)}) collective-permute-start(f32[24,256]{1,0:T(8,128)S(1)} %get-tuple-element.47.p0_ref), channel_id=1, source_target_pairs={{0,24},{8,16},{16,8},{24,0},{1,25},{9,17},{17,9},{25,1},{2,26},{10... | collective-permute-start | bytes 73736 | tf_op jit(solution)/shard_map/ppermute | solution.py:32
  37.5 4.1 %collective-permute-start.8 = (f32[24,256]{1,0:T(8,128)S(1)}, f32[24,256]{1,0:T(8,128)S(1)}, u32[]{:S(2)}, u32[]{:S(2)}) collective-permute-start(f32[24,256]{1,0:T(8,128)S(1)} %get-tuple-element.47.p0_ref), channel_id=1, source_target_pairs={{0,8},{8,0},{16,24},{24,16},{1,9},{9,1},{17,25},{25,17},{2,10},{10... | collective-permute-start | bytes 73736 | tf_op jit(solution)/shard_map/ppermute | solution.py:32
  37.5 4.9 %collective-permute-start.9 = (f32[24,256]{1,0:T(8,128)S(1)}, f32[24,256]{1,0:T(8,128)S(1)}, u32[]{:S(2)}, u32[]{:S(2)}) collective-permute-start(f32[24,256]{1,0:T(8,128)S(1)} %get-tuple-element.47.p0_ref), channel_id=1, source_target_pairs={{0,16},{8,24},{16,0},{24,8},{1,17},{9,25},{17,1},{25,9},{2,18},{10... | collective-permute-start | bytes 73736 | tf_op jit(solution)/shard_map/ppermute | solution.py:32
  42.7 3.3 %collective-permute-start.11 = (f32[24,256]{1,0:T(8,128)S(1)}, f32[24,256]{1,0:T(8,128)S(1)}, u32[]{:S(2)}, u32[]{:S(2)}) collective-permute-start(f32[24,256]{1,0:T(8,128)S(1)} %get-tuple-element.49.g1_ref), channel_id=1, source_target_pairs={{0,6},{2,4},{4,2},{6,0},{1,7},{3,5},{5,3},{7,1},{8,14},{10,12},{12... | collective-permute-start | bytes 73736 | tf_op jit(solution)/shard_map/ppermute | solution.py:32
  42.7 3.2 %collective-permute-start.12 = (f32[24,256]{1,0:T(8,128)S(1)}, f32[24,256]{1,0:T(8,128)S(1)}, u32[]{:S(2)}, u32[]{:S(2)}) collective-permute-start(f32[24,256]{1,0:T(8,128)S(1)} %get-tuple-element.49.g1_ref), channel_id=1, source_target_pairs={{0,2},{2,0},{4,6},{6,4},{1,3},{3,1},{5,7},{7,5},{8,10},{10,8},{12,... | collective-permute-start | bytes 73736 | tf_op jit(solution)/shard_map/ppermute | solution.py:32
  46.0 4.2 %collective-permute-start.13 = (f32[24,512]{1,0:T(8,128)S(1)}, f32[24,512]{1,0:T(8,128)S(1)}, u32[]{:S(2)}, u32[]{:S(2)}) collective-permute-start(f32[24,512]{1,0:T(8,128)S(1)} %pad_maximum_fusion.1), channel_id=1, source_target_pairs={{0,1},{1,0},{2,3},{3,2},{4,5},{5,4},{6,7},{7,6},{8,9},{9,8},{10,11... | collective-permute-start | bytes 147464 | tf_op jit(solution)/shard_map/ppermute | solution.py:52
  54.8 4.2 %collective-permute-start.14 = (f32[24,512]{1,0:T(8,128)S(1)}, f32[24,512]{1,0:T(8,128)S(1)}, u32[]{:S(2)}, u32[]{:S(2)}) collective-permute-start(f32[24,512]{1,0:T(8,128)S(1)} %slice.56), channel_id=1, source_target_pairs={{0,1},{1,0},{2,3},{3,2},{4,5},{5,4},{6,7},{7,6},{8,9},{9,8},{10,11... | collective-permute-start | bytes 147464 | tf_op jit(solution)/shard_map/ppermute | solution.py:63
  58.9 3.3 %collective-permute-start.15 = (f32[24,256]{1,0:T(8,128)S(1)}, f32[24,256]{1,0:T(8,128)S(1)}, u32[]{:S(2)}, u32[]{:S(2)}) collective-permute-start(f32[24,256]{1,0:T(8,128)S(1)} %slice_add_fusion), channel_id=1, source_target_pairs={{0,6},{2,4},{4,2},{6,0},{1,7},{3,5},{5,3},{7,1},{8,14},{10,12},{12... | collective-permute-start | bytes 73736 | tf_op jit(solution)/shard_map/ppermute | solution.py:32
  58.9 3.3 %collective-permute-start.16 = (f32[24,256]{1,0:T(8,128)S(1)}, f32[24,256]{1,0:T(8,128)S(1)}, u32[]{:S(2)}, u32[]{:S(2)}) collective-permute-start(f32[24,256]{1,0:T(8,128)S(1)} %slice_add_fusion), channel_id=1, source_target_pairs={{0,2},{2,0},{4,6},{6,4},{1,3},{3,1},{5,7},{7,5},{8,10},{10,8},{12,... | collective-permute-start | bytes 73736 | tf_op jit(solution)/shard_map/ppermute | solution.py:32
  62.7 6.2 %collective-permute-start.17 = (f32[24,384]{1,0:T(8,128)S(1)}, f32[24,384]{1,0:T(8,128)S(1)}, u32[]{:S(2)}, u32[]{:S(2)}) collective-permute-start(f32[24,384]{1,0:T(8,128)S(1)} %get-tuple-element.62.p0_ref), channel_id=1, source_target_pairs={{0,24},{8,16},{16,8},{24,0},{1,25},{9,17},{17,9},{25,1},{2,26},{10... | collective-permute-start | bytes 110600 | tf_op jit(solution)/shard_map/ppermute | solution.py:32
  64.8 4.9 %collective-permute-start.18 = (f32[24,384]{1,0:T(8,128)S(1)}, f32[24,384]{1,0:T(8,128)S(1)}, u32[]{:S(2)}, u32[]{:S(2)}) collective-permute-start(f32[24,384]{1,0:T(8,128)S(1)} %get-tuple-element.62.p0_ref), channel_id=1, source_target_pairs={{0,16},{8,24},{16,0},{24,8},{1,17},{9,25},{17,1},{25,9},{2,18},{10... | collective-permute-start | bytes 110600 | tf_op jit(solution)/shard_map/ppermute | solution.py:32
  66.1 4.0 %collective-permute-start.19 = (f32[24,384]{1,0:T(8,128)S(1)}, f32[24,384]{1,0:T(8,128)S(1)}, u32[]{:S(2)}, u32[]{:S(2)}) collective-permute-start(f32[24,384]{1,0:T(8,128)S(1)} %get-tuple-element.62.p0_ref), channel_id=1, source_target_pairs={{0,8},{8,0},{16,24},{24,16},{1,9},{9,1},{17,25},{25,17},{2,10},{10... | collective-permute-start | bytes 110600 | tf_op jit(solution)/shard_map/ppermute | solution.py:32
  70.5 1.2 %collective-permute-start.20 = (f32[8,128]{1,0:T(8,128)S(1)}, f32[8,128]{1,0:T(8,128)S(1)}, u32[]{:S(2)}, u32[]{:S(2)}) collective-permute-start(f32[8,128]{1,0:T(8,128)S(1)} %get-tuple-element.65), channel_id=1, source_target_pairs={{0,2},{2,0},{4,6},{6,4},{1,3},{3,1},{5,7},{7,5},{8,10},{10,8},{12,... | collective-permute-start | bytes 12296 | tf_op jit(solution)/shard_map/ppermute | solution.py:32
  71.7 3.6 %collective-permute-start.21 = (f32[8,128]{1,0:T(8,128)S(1)}, f32[8,128]{1,0:T(8,128)S(1)}, u32[]{:S(2)}, u32[]{:S(2)}) collective-permute-start(f32[8,128]{1,0:T(8,128)S(1)} %add.108.refs_0_), channel_id=1, source_target_pairs={{0,4},{1,5},{2,6},{3,7},{4,0},{5,1},{6,2},{7,3},{8,12},{9,13},{10,... | collective-permute-start | bytes 12296 | tf_op jit(solution)/shard_map/ppermute | solution.py:104
  72.9 3.6 %collective-permute-start.22 = (f32[8,128]{1,0:T(8,128)S(1)}, f32[8,128]{1,0:T(8,128)S(1)}, u32[]{:S(2)}, u32[]{:S(2)}) collective-permute-start(f32[8,128]{1,0:T(8,128)S(1)} %add.108.refs_0_), channel_id=1, source_target_pairs={{0,1},{1,0},{2,3},{3,2},{4,5},{5,4},{6,7},{7,6},{8,9},{9,8},{10,11... | collective-permute-start | bytes 12296 | tf_op jit(solution)/shard_map/ppermute | solution.py:104
  74.4 4.5 %collective-permute-start.23 = (f32[8,128]{1,0:T(8,128)S(1)}, f32[8,128]{1,0:T(8,128)S(1)}, u32[]{:S(2)}, u32[]{:S(2)}) collective-permute-start(f32[8,128]{1,0:T(8,128)S(1)} %add.108.refs_0_), channel_id=1, source_target_pairs={{0,5},{1,4},{2,7},{3,6},{4,1},{5,0},{6,3},{7,2},{8,13},{9,12},{10,... | collective-permute-start | bytes 12296 | tf_op jit(solution)/shard_map/ppermute | solution.py:104
  (1 other events, 0.7 us)

commit v6 on v5

--- a/solution.py
+++ b/solution.py
@@ -168,6 +168,10 @@
     pieces = [raw_ref[n // 4, n // 2 % 2, n % 2 : n % 2 + 1, :] for n in range(8)]
     list_ref[...] = jnp.concatenate(pieces, axis=1)
     pick_octants(own_ref, list_ref, oct_ref)
+    row = lax.broadcasted_iota(jnp.int32, (GROUP, list_ref.shape[1]), 0)
+    oct_ref[rows(0), :] = jnp.where(
+        row == vectors + 2, list_ref[...].astype(jnp.float32), oct_ref[rows(0), :]
+    )
 
 
 def prepare_kernel(
@@ -220,20 +224,23 @@
     atoms = own_ref.shape[1]
     table[:, :atoms] = own_ref[...]
     width = 8 * ghosts
-    base = atoms
-    kind = 1
-    for number, ref in enumerate(ghost_refs):
-        for j in range(number == 0, ref.shape[1] // width):
-            part = ref[:, j * width : (j + 1) * width]
-            if shifted:
-                row = lax.broadcasted_iota(jnp.int32, part.shape, 0)
-                for a in range(3):
-                    if (kind >> a) & 1:
-                        move = jnp.where(octant_bit(part.shape, a, ghosts), -1.0, 1.0)
-                        part = part + jnp.where(row == GROUP * a + vectors, move, 0.0)
-            table[:, base : base + width] = part
-            base += width
-            kind += 1
+    places = [
+        (ref, j * width) for ref in ghost_refs for j in range(ref.shape[1] // width)
+    ]
+    if len(ghost_refs) == 2:
+        places = [places[n] for n in (0, 1, 4, 5, 2, 3, 6, 7)]
+    for kind, (ref, start) in enumerate(places):
+        if kind == 0:
+            continue
+        part = ref[:, start : start + width]
+        if shifted:
+            row = lax.broadcasted_iota(jnp.int32, part.shape, 0)
+            for a in range(3):
+                if (kind >> a) & 1:
+                    move = jnp.where(octant_bit(part.shape, a, ghosts), -1.0, 1.0)
+                    part = part + jnp.where(row == GROUP * a + vectors, move, 0.0)
+        base = atoms + (kind - 1) * width
+        table[:, base : base + width] = part
 
 
 def gather_slot(table, idx_ref, k, atoms):
@@ -337,11 +344,11 @@
 
 
 def finish_product(
-    idx_ref, low_ref, unit_ref, inv_ref, sums_ref, acc, changes, diffs, own_out, ghost_out, vectors
+    idx_ref, low_ref, unit_ref, inv_ref, sums_ref, acc, changes, diffs, terms_out, vectors
 ):
-    atoms = own_out.shape[1]
-    fanout = idx_ref.shape[1] // atoms
-    tiles = (atoms + ghost_out.shape[1]) // LANES
+    fanout = len(diffs)
+    atoms = idx_ref.shape[1] // fanout
+    tiles = terms_out.shape[1] // LANES
     pairs = pair_list(fanout)
     per_vector = fanout + len(pairs)
     slots = range(fanout)
@@ -424,12 +431,10 @@
     for number in range(tiles):
         for a in range(3):
             value = join_rows(spread[tile_rows(number * 3 + a)], vectors)
+            cut = slice(number * LANES, (number + 1) * LANES)
             if number < own_tiles:
-                cut = slice(number * LANES, (number + 1) * LANES)
-                own_out[rows(a), cut] = value + center[a][:, cut]
-            else:
-                cut = number - own_tiles
-                ghost_out[rows(a), cut * LANES : (cut + 1) * LANES] = value
+                value = value + center[a][:, cut]
+            terms_out[rows(a), cut] = value
     return shifted
 
 
@@ -485,8 +490,7 @@
     in_ref,
     out_ref,
     col_ref,
-    own_out,
-    ghost_out,
+    terms_out,
     unit_ref,
     inv_ref,
     sums_ref,
@@ -617,44 +621,21 @@
         acc,
         changes,
         diffs,
-        own_out,
-        ghost_out,
+        terms_out,
         vectors,
     )
 
 
-def second_kernel(
-    ghosts,
-    vectors,
-    idx_ref,
-    own_ref,
-    g1_ref,
-    g2_ref,
-    g3_ref,
-    low_ref,
-    unit_ref,
-    inv_ref,
-    sums_ref,
-    cos_ref,
-    f_ref,
-    f1_ref,
-    q_ref,
-    rp_ref,
-    rpp_ref,
-    own_out,
-    ghost_out,
-    gram_out,
-    table,
-    tn,
-    changes,
-    acc,
-):
+def second_kernel(ghosts, vectors, levels, idx_ref, own_ref, *refs):
+    ghost_refs, refs = refs[:levels], refs[levels:]
+    low_ref, unit_ref, inv_ref, sums_ref, cos_ref, f_ref, f1_ref, q_ref, rp_ref, rpp_ref = refs[:10]
+    terms_out, gram_out, table, tn, changes, acc = refs[10:]
     atoms = own_ref.shape[1]
     fanout = idx_ref.shape[1] // atoms
     channels = f_ref.shape[0]
     pairs = pair_list(fanout)
     slots = range(fanout)
-    fill_table(table, own_ref, (g1_ref, g2_ref, g3_ref), vectors, ghosts, False)
+    fill_table(table, own_ref, ghost_refs, vectors, ghosts, False)
     diffs = []
     for k in slots:
         near = gather_slot(table, idx_ref, k, atoms)
@@ -686,8 +667,7 @@
         acc,
         changes,
         diffs,
-        own_out,
-        ghost_out,
+        terms_out,
         vectors,
     )
     gram_out[...] = from_shifted(shifted, vectors)
@@ -889,84 +869,371 @@
     gram_ref[...] = total[0] + pltpu.roll(from_shifted(total[1:], vectors), 4 * GROUP, 1)
 
 
+def pair_sums(mine, other, got, width, atoms):
+    def tile(ref, kind, a):
+        start = atoms + (kind - 1) * width
+        return ref[rows(a), start : start + width]
+
+    def back(n, a):
+        return got[rows(a), n * width : (n + 1) * width]
+
+    def pick(first, second, n):
+        return (
+            [first[rows(a), :atoms] for a in range(3)],
+            [tile(second, 4, a) + back(n, a) for a in range(3)],
+            [tile(first, 1, a) + tile(second, 5, a) + back(n + 1, a) for a in range(3)],
+        )
+
+    return pick(mine, other, 0), pick(other, mine, 2)
+
+
+def pair_packet(vectors, mine, other, got, lists, parts, packet, ghosts_width):
+    atoms = parts[0].shape[1]
+    mark = vectors + 1
+    for n, (own, sums, beside) in enumerate(pair_sums(mine, other, got, ghosts_width, atoms)):
+        base = 2 * n * ghosts_width
+        for a in range(3):
+            parts[n][rows(a), :] = add_octants(own[a], sums[a], lists[n], vectors)
+        for a in range(3):
+            packet[rows(a), base + ghosts_width : base + 2 * ghosts_width] = beside[a]
+            for j in range(ghosts_width // LANES):
+                cut = slice(j * LANES, (j + 1) * LANES)
+                value = gather_lanes(parts[n], lists[n][:, cut], a)
+                if a == 0:
+                    row = lax.broadcasted_iota(jnp.int32, value.shape, 0)
+                    value = jnp.where(row == mark, lists[n][:, cut].astype(jnp.float32), value)
+                packet[rows(a), base + j * LANES : base + (j + 1) * LANES] = value
+
+
+def pair_lists(vectors, list_ref, beyond_ref):
+    row = vectors + 2
+    width = list_ref.shape[1]
+    return list_ref[...], beyond_ref[row : row + 1, :width].astype(jnp.int32)
+
+
+def pair_start_kernel(
+    vectors, mine, other, got, list_ref, beyond_ref, part_ref, packet_ref, beyond_part
+):
+    pair_packet(
+        vectors,
+        mine,
+        other,
+        got,
+        pair_lists(vectors, list_ref, beyond_ref),
+        (part_ref, beyond_part),
+        packet_ref,
+        list_ref.shape[1],
+    )
+
+
+def placed_terms(side, packets, n, half, lists, atoms, width, vectors):
+    start = (2 * half + 1) * width
+    after, before = packets[(n + 1) % 4], packets[(n + 3) % 4]
+    terms = [
+        only_vectors(
+            jnp.where(
+                side > 0.5,
+                after[rows(a), start : start + width],
+                before[rows(a), start : start + width],
+            ),
+            vectors,
+        )
+        for a in range(3)
+    ]
+    packed = jnp.concatenate([split_rows(t, vectors) for t in terms], axis=0)
+    onehot = lax.broadcasted_iota(jnp.int32, (atoms, width), 0) == lists
+    placed = lax.dot_general(
+        packed.astype(jnp.bfloat16),
+        jnp.where(onehot, 1.0, 0.0).astype(jnp.bfloat16),
+        (((1,), (1,)), ((), ())),
+        preferred_element_type=jnp.float32,
+    )
+    return terms, [join_rows(placed[rows(a)], vectors) for a in range(3)]
+
+
+def read_back(ref, lists, a):
+    pieces = [
+        gather_lanes(ref, lists[:, j * LANES : (j + 1) * LANES], a)
+        for j in range(lists.shape[1] // LANES)
+    ]
+    return jnp.concatenate(pieces, axis=1)
+
+
+def packet_row(packet, half, vectors, width):
+    mark = vectors + 1
+    start = 2 * half * width
+    return packet[mark : mark + 1, start : start + width].astype(jnp.int32)
+
+
+def pair_merge_kernel(
+    vectors,
+    width,
+    side_ref,
+    part_ref,
+    p0_ref,
+    p1_ref,
+    p2_ref,
+    p3_ref,
+    start_ref,
+    full_ref,
+    level_ref,
+    gram_ref,
+    spread,
+):
+    atoms = part_ref.shape[1]
+    side = side_ref[...]
+    packets = (p0_ref, p1_ref, p2_ref, p3_ref)
+    for half in range(2):
+        found = []
+        for slot, n in enumerate((0, 1, 3)):
+            lists = packet_row(packets[n], half, vectors, width)
+            _, placed = placed_terms(side, packets, n, half, lists, atoms, width, vectors)
+            spread_here = spread.at[half * 3 + slot]
+            for a in range(3):
+                spread_here[rows(a), :] = placed[a]
+                if n == 0 and half == 0:
+                    full_ref[rows(a), :] = part_ref[rows(a), :] + placed[a]
+            start = 2 * half * width
+            found.append(
+                [
+                    packets[n][rows(a), start : start + width] + read_back(spread_here, lists, a)
+                    for a in range(3)
+                ]
+            )
+        for a in range(3):
+            start = 2 * half * width
+            level_ref[rows(a), start : start + width] = found[0][a]
+            level_ref[rows(a), start + width : start + 2 * width] = jnp.where(
+                side > 0.5, found[2][a], found[1][a]
+            )
+    total = jnp.zeros((2 * GROUP, LANES), jnp.float32)
+    for a in range(3):
+        stack = jnp.concatenate([start_ref[rows(a), :], full_ref[rows(a), :]], axis=0)
+        stack = only_vectors(stack, vectors)
+        total += inner(stack, stack)
+    gram_ref[...] = pack_gram(
+        jnp.concatenate([total, jnp.zeros((GROUP, LANES), jnp.float32)], axis=0),
+        jnp.zeros((GROUP, LANES), jnp.float32),
+    )
+
+
+def repeat_rows(x, vectors):
+    x = only_vectors(x, vectors)
+    return x + pltpu.roll(x, vectors, 0)
+
+
+def pair_gram_start_kernel(
+    vectors,
+    mine,
+    other,
+    got,
+    list_ref,
+    beyond_ref,
+    gram_ref,
+    beyond_gram,
+    part_ref,
+    packet_ref,
+    beyond_part,
+):
+    width = list_ref.shape[1]
+    parts = (part_ref, beyond_part)
+    pair_packet(
+        vectors,
+        mine,
+        other,
+        got,
+        pair_lists(vectors, list_ref, beyond_ref),
+        parts,
+        packet_ref,
+        width,
+    )
+    squares = []
+    for part in parts:
+        total = None
+        for a in range(3):
+            value = repeat_rows(part[rows(a), :], vectors)
+            found = shifted_products(value, value, vectors)
+            total = found if total is None else [x + y for x, y in zip(total, found)]
+        squares.append(from_shifted(total, vectors))
+    gram = gram_ref[...] + beyond_gram[...]
+    cut = slice(4 * width, 4 * width + LANES)
+    packet_ref[rows(0), cut] = gram + pltpu.roll(squares[0] + squares[1], 4 * GROUP, 1)
+    packet_ref[GROUP : 3 * GROUP, cut] = jnp.zeros((2 * GROUP, LANES), jnp.float32)
+
+
+def pair_gram_merge_kernel(
+    vectors,
+    width,
+    side_ref,
+    p3_ref,
+    p2_ref,
+    part_ref,
+    p0_ref,
+    p1_ref,
+    full_ref,
+    gram_ref,
+    spread,
+):
+    atoms = part_ref.shape[1]
+    side = side_ref[...]
+    packets = (p0_ref, p1_ref, p2_ref, p3_ref)
+    shares = []
+    for n in range(4):
+        total = []
+        for half in range(2):
+            lists = packet_row(packets[n], half, vectors, width)
+            terms, placed = placed_terms(side, packets, n, half, lists, atoms, width, vectors)
+            spread_here = spread.at[2 * n + half]
+            found = None
+            for a in range(3):
+                spread_here[rows(a), :] = placed[a]
+                if n == 0 and half == 0:
+                    full_ref[rows(a), :] = part_ref[rows(a), :] + placed[a]
+                start = 2 * half * width
+                at = repeat_rows(packets[n][rows(a), start : start + width], vectors)
+                products = shifted_products(
+                    terms[a], at + at + read_back(spread_here, lists, a), vectors
+                )
+                found = products if found is None else [x + y for x, y in zip(found, products)]
+            total.append(found)
+        share = packets[n][rows(0), 4 * width : 4 * width + LANES]
+        shares.append([share] + [x + y for x, y in zip(*total)])
+
+    def add(x, y):
+        return [p + q for p, q in zip(x, y)]
+
+    total = add(add(shares[0], shares[1]), add(shares[2], shares[3]))
+    gram_ref[...] = total[0] + pltpu.roll(from_shifted(total[1:], vectors), 4 * GROUP, 1)
+
+
 def last_kernel(vectors, scale, start_ref, first_ref, second_ref, *refs):
     gram_refs, refs = refs[:-7], refs[-7:]
     next_hbm, diag_hbm, off_hbm, next_ref, diag_ref, off_ref, sems = refs
     shape = (GROUP, LANES)
     row = lax.broadcasted_iota(jnp.int32, shape, 0)
     lane = lax.broadcasted_iota(jnp.int32, shape, 1)
-    inside = (row < vectors) & (lane < vectors)
-    eye = jnp.where((row == lane) & inside, 1.0, 0.0)
     levels = [ref[...] for ref in gram_refs]
     while len(levels) > 1:
         levels = [sum(levels[n : n + 2]) for n in range(0, len(levels), 2)]
     gram = levels[0] * scale
-
-    def block(x, n):
-        return jnp.where(inside, pltpu.roll(x, LANES - GROUP * n, 1) if n else x, 0.0)
-
-    def beside(*parts):
-        out = parts[0]
-        for n, part in enumerate(parts[1:]):
-            out = out + pltpu.roll(part, GROUP * (n + 1), 1)
+    size = range(vectors)
+
+    def block(n):
+        return [
+            [
+                jnp.broadcast_to(gram[i : i + 1, GROUP * n + j : GROUP * n + j + 1], shape)
+                for j in size
+            ]
+            for i in size
+        ]
+
+    def total(terms):
+        terms = [t for t in terms if t is not None]
+        out = terms[0] if terms else None
+        for term in terms[1:]:
+            out = out + term
         return out
 
+    def times(x, y):
+        return None if x is None or y is None else x * y
+
     def mul(x, y):
-        return sum(x[:, k : k + 1] * y[k : k + 1, :] for k in range(vectors))
+        return [[total([times(x[i][k], y[k][j]) for k in size]) for j in size] for i in size]
+
+    def even(x):
+        return [[x[min(i, j)][max(i, j)] for j in size] for i in size]
+
+    def mul_even(x, y):
+        upper = [
+            [total([times(x[i][k], y[k][j]) for k in size]) if j >= i else None for j in size]
+            for i in size
+        ]
+        return even(upper)
+
+    def add(x, y, sign=1.0):
+        def join(p, q):
+            if p is None or q is None:
+                return (q if sign > 0 else None if q is None else -q) if p is None else p
+            return p + q if sign > 0 else p - q
+
+        return [[join(p, q) for p, q in zip(u, v)] for u, v in zip(x, y)]
 
     def flip(x):
+        return [[x[j][i] for j in size] for i in size]
+
+    def factor(m):
+        m = [list(line) for line in m]
+        lower = [[None] * vectors for _ in size]
+        inverse = [[jnp.ones(shape, jnp.float32) if i == j else None for j in size] for i in size]
+        for j in size:
+            pivot = lax.rsqrt(m[j][j])
+            for i in range(j, vectors):
+                lower[i][j] = m[i][j] * pivot
+            inverse[j] = [times(x, pivot) for x in inverse[j]]
+            for i in range(j + 1, vectors):
+                for k in range(j + 1, i + 1):
+                    m[i][k] = m[i][k] - lower[i][j] * lower[k][j]
+                for k in range(j + 1):
+                    step = times(lower[i][j], inverse[j][k])
+                    if step is not None:
+                        old = inverse[i][k]
+                        inverse[i][k] = -step if old is None else old - step
+        return lower, inverse
+
+    ss, su, uu, uq, qq = (block(n) for n in range(5))
+    qq = [[0.5 * (qq[i][j] + qq[j][i]) for j in size] for i in size]
+    _, p0 = factor(ss)
+    p0t = flip(p0)
+    a1 = mul_even(mul(p0, su), p0t)
+    l1, p1 = factor(add(mul_even(mul(p0, uu), p0t), mul_even(a1, a1), -1.0))
+    b = mul(p1, p0)
+    a = [[-x for x in line] for line in mul(p1, mul(a1, p0))]
+    at, bt, up1 = flip(a), flip(b), flip(l1)
+    right_s = add(mul(su, at), mul(uu, bt))
+    right_u = add(mul(uu, at), mul(uq, bt))
+    right_q = add(mul(uq, at), mul(qq, bt))
+    a2 = even(add(mul_even(a, right_s), mul_even(b, right_u)))
+    ww = add(mul_even(a, right_u), mul_even(b, right_q))
+    l2, p2 = factor(add(add(ww, mul_even(a2, a2), -1.0), mul_even(up1, l1), -1.0))
+    up2 = flip(l2)
+    weights = (
+        [[-x for x in line] for line in mul(p2, add(mul(a2, a), mul(up1, p0)))],
+        mul(p2, add(a, mul(a2, b), -1.0)),
+        mul(p2, b),
+    )
+
+    def tile(x):
         out = jnp.zeros(shape, jnp.float32)
-        for k in range(vectors):
-            line = jnp.sum(eye * x[:, k : k + 1], axis=0, keepdims=True)
-            out = jnp.where(row == k, line, out)
-        return out
-
-    def solve(m):
-        for j in range(vectors):
-            inverse = lax.rsqrt(m[j : j + 1, j : j + 1])
-            line = m[j : j + 1, :] * inverse
-            m = jnp.where(
-                row == j, line, jnp.where(row > j, m - (m[:, j : j + 1] * inverse) * line, m)
-            )
-        return jnp.where((lane >= row) & inside, m, 0.0), m
-
-    ss, su, uu, uq, qq = (block(gram, n) for n in range(5))
-    qq = 0.5 * (qq + flip(qq))
-    _, m = solve(beside(ss, su, uu, eye))
-    p0 = block(m, 3)
-    p0t = flip(p0)
-    a1 = mul(block(m, 1), p0t)
-    up1, m = solve(beside(mul(block(m, 2), p0t) - mul(a1, a1), p0, mul(a1, p0)))
-    b, a = block(m, 1), -block(m, 2)
-    at, bt = flip(a), flip(b)
-    known = mul(up1, beside(flip(up1), p0))
-    right_s = mul(su, at) + mul(uu, bt)
-    right_u = mul(uu, at) + mul(uq, bt)
-    right_q = mul(uq, at) + mul(qq, bt)
-    a2 = mul(a, right_s) + mul(b, right_u)
-    ww = mul(a, right_u) + mul(b, right_q)
-    moved = mul(a2, beside(a2, a, b)) + known
-    up2, m = solve(
-        beside(ww - block(moved, 0), -block(moved, 1), a - block(moved, 2), b)
-    )
-    small = (slice(0, vectors), slice(0, vectors))
-    diag_ref[0] = a1[small]
-    diag_ref[1] = a2[small]
-    off_ref[0] = up1[small]
-    off_ref[1] = up2[small]
+        for i in size:
+            for j in size:
+                if x[i][j] is not None:
+                    out = jnp.where((row == i) & (lane == j), x[i][j], out)
+        return out[:vectors, :vectors]
+
+    def stacked(x, j):
+        out = jnp.zeros(shape, jnp.float32)
+        for i in size:
+            if x[i][j] is not None:
+                out = jnp.where(row == i, x[i][j], out)
+        return jnp.concatenate([out] * (start_ref.shape[1] // LANES), axis=1)
+
+    diag_ref[0] = tile(a1)
+    diag_ref[1] = tile(a2)
+    off_ref[0] = tile(up1)
+    off_ref[1] = tile(up2)
     copies = [
         pltpu.make_async_copy(diag_ref, diag_hbm, sems.at[0]),
         pltpu.make_async_copy(off_ref, off_hbm, sems.at[1]),
     ]
     for copy in copies:
         copy.start()
+    columns = [[stacked(weight, w) for w in size] for weight in weights]
     for comp in range(3):
         value = None
         for n, ref in enumerate((start_ref, first_ref, second_ref)):
-            for w in range(vectors):
+            for w in size:
                 line = GROUP * comp + w
-                place = GROUP * (n + 1) + w
-                term = m[:, place : place + 1] * ref[line : line + 1, :]
+                term = columns[n][w] * ref[line : line + 1, :]
                 value = term if value is None else value + term
         next_ref[0, 0, 0, comp] = value[:vectors]
     copies.append(pltpu.make_async_copy(next_ref, next_hbm, sems.at[2]))
@@ -1086,66 +1353,116 @@
         (GROUP * (-(-base_sums // 4)), atoms),
         (pairs * GROUP, atoms),
     ] + [(channels, edges)] * 5
+    ghost_levels = spread(octants)
     results = call(
         functools.partial(first_kernel, ghosts, vectors, basis, embedding.shape[0]),
-        [(high, atoms), (high, 7 * width)] + saved_shapes,
-        (index, own)
-        + spread(octants)
-        + (low, inward, outward, columns),
+        [(high, table_width)] + saved_shapes,
+        (index, own) + ghost_levels + (low, inward, outward, columns),
         [(high, table_width), (channels, edges), (channels, LANES)]
         + shared
         + [(base_sums * GROUP, atoms)],
     )
-    own_terms, ghost_terms, saved = results[0], results[1], results[2:]
-
-    sums, beside = return_outer(ghost_terms, width, ghosts)
-    if ring:
+    terms, saved = results[0], results[1:]
+    lifted = ring and lax.axis_size("gz") == 2
+
+    def second_product(first, levels):
+        return call(
+            functools.partial(second_kernel, ghosts, vectors, len(levels)),
+            [(high, table_width), (GROUP, LANES)],
+            (index, first) + levels + (low,) + tuple(saved),
+            [(high, table_width)] + shared,
+        )
+
+    if lifted:
+        beyond = ghost_levels[2]
+
+        def exchange(terms):
+            other = lax.ppermute(terms, "gz", swap_pairs(2, 1))
+            cut = [atoms + (kind - 1) * width for kind in range(9)]
+            both = [
+                x[:, cut[2] : cut[4]] + y[:, cut[6] : cut[8]]
+                for x, y in ((terms, other), (other, terms))
+            ]
+            return other, return_ghosts(jnp.concatenate(both, axis=1), 1, ghosts)
+
+        other, got = exchange(terms)
         part, packet = call(
-            functools.partial(start_kernel, vectors),
-            [(high, atoms), (high, 2 * width)],
-            (own_terms, sums, beside, lists),
+            functools.partial(pair_start_kernel, vectors),
+            [(high, atoms), (high, 4 * width)],
+            (terms, other, got, lists, beyond),
+            [(high, atoms)],
         )
         others = pair_exchange(packet, "gx", (1, 2, 3))
-        first, level = call(
-            functools.partial(merge_kernel, vectors),
-            [(high, atoms), (high, 2 * width)],
-            (side, part, packet, *others),
+        first, level, gram = call(
+            functools.partial(pair_merge_kernel, vectors, width),
+            [(high, atoms), (high, 4 * width), (GROUP, LANES)],
+            (side, part, packet, *others, own),
+            [(6, high, atoms)],
+        )
+        terms, edge_gram = second_product(first, (level, fetch_ghosts(level, 1, ghosts)))
+        gram = gram + jnp.roll(edge_gram, 3 * GROUP, axis=1)
+        sent = jnp.concatenate([terms, jnp.pad(gram, ((0, high - GROUP), (0, 0)))], axis=1)
+        other, got = exchange(sent)
+        part, packet = call(
+            functools.partial(pair_gram_start_kernel, vectors),
+            [(high, atoms), (high, 4 * width + LANES)],
+            (sent, other, got, lists, beyond, gram, other[:GROUP, table_width:]),
             [(high, atoms)],
-        )
-    else:
-        first, level = call(
-            functools.partial(middle_kernel, vectors),
-            [(high, atoms), (high, width)],
-            (own_terms, sums + return_ghosts(beside, 0, ghosts), lists),
-        )
-    own_terms, ghost_terms, edge_gram = call(
-        functools.partial(second_kernel, ghosts, vectors),
-        [(high, atoms), (high, 7 * width), (GROUP, LANES)],
-        (index, first) + spread(level) + (low,) + tuple(saved),
-        [(high, table_width)] + shared,
-    )
-    sums, beside = return_outer(ghost_terms, width, ghosts)
-    if ring:
-        part, packet = call(
-            functools.partial(gram_start_kernel, vectors),
-            [(high, atoms), (high, 2 * width + LANES)],
-            (own, first, own_terms, sums, beside, lists, edge_gram),
         )
         others = pair_exchange(packet, "gx", (1, 2, 3))
         second, gram = call(
-            functools.partial(gram_merge_kernel, vectors),
+            functools.partial(pair_gram_merge_kernel, vectors, width),
             [(high, atoms), (GROUP, LANES)],
             (side, *others[:0:-1], part, packet, others[0]),
-            [(high, atoms)],
-        )
-        gram = sum_across(gram)
+            [(8, high, atoms)],
+        )
+        gram = [sum_over(gram, AXES[1:2])]
     else:
-        second, gram = call(
-            functools.partial(gram_kernel, vectors),
-            [(high, atoms), (GROUP, LANES)],
-            (own, first, own_terms, sums + return_ghosts(beside, 0, ghosts), lists),
-        )
-        gram = [sum_over(gram, AXES)]
+        own_terms, ghost_terms = terms[:, :atoms], terms[:, atoms:]
+        sums, beside = return_outer(ghost_terms, width, ghosts)
+        if ring:
+            part, packet = call(
+                functools.partial(start_kernel, vectors),
+                [(high, atoms), (high, 2 * width)],
+                (own_terms, sums, beside, lists),
+            )
+            others = pair_exchange(packet, "gx", (1, 2, 3))
+            first, level = call(
+                functools.partial(merge_kernel, vectors),
+                [(high, atoms), (high, 2 * width)],
+                (side, part, packet, *others),
+                [(high, atoms)],
+            )
+        else:
+            first, level = call(
+                functools.partial(middle_kernel, vectors),
+                [(high, atoms), (high, width)],
+                (own_terms, sums + return_ghosts(beside, 0, ghosts), lists),
+            )
+        terms, edge_gram = second_product(first, spread(level))
+        own_terms, ghost_terms = terms[:, :atoms], terms[:, atoms:]
+        sums, beside = return_outer(ghost_terms, width, ghosts)
+        if ring:
+            part, packet = call(
+                functools.partial(gram_start_kernel, vectors),
+                [(high, atoms), (high, 2 * width + LANES)],
+                (own, first, own_terms, sums, beside, lists, edge_gram),
+            )
+            others = pair_exchange(packet, "gx", (1, 2, 3))
+            second, gram = call(
+                functools.partial(gram_merge_kernel, vectors),
+                [(high, atoms), (GROUP, LANES)],
+                (side, *others[:0:-1], part, packet, others[0]),
+                [(high, atoms)],
+            )
+            gram = sum_across(gram)
+        else:
+            second, gram = call(
+                functools.partial(gram_kernel, vectors),
+                [(high, atoms), (GROUP, LANES)],
+                (own, first, own_terms, sums + return_ghosts(beside, 0, ghosts), lists),
+            )
+            gram = [sum_over(gram, AXES)]
     shapes = [(1, 1, 1, 3, vectors, atoms), (2, vectors, vectors), (2, vectors, vectors)]
     following, diagonal, off = call(
         functools.partial(last_kernel, vectors, scale),

time: 81.7 us -> 78.2 us (0.957)
  starting transfers between devices: 29.1 us -> 24.5 us
  waiting for transfers between devices: 31.1 us -> 33.4 us
  Pallas kernels: 16.6 us -> 15.3 us
    ppermute x5 -> x4, starting transfers between devices: 6.64 us -> 3.44 us  [the longest x2 3.17 us: exchange(): other = lax.ppermute(terms, 'gz', swap_pairs(2, 1))]
    ppermute x17 -> x16, waiting for transfers between devices: 18 us -> 20.6 us  [pair_exchange(): lax.ppermute(x, axis, [(i, i ^ d) for i in range(size)])]
    ppermute x2 -> x1, waiting for transfers between devices: 4.27 us -> 1.69 us  [fetch_ghosts(): return lax.ppermute(x, axis, swap_pairs(2, 1))]
    ppermute x5 -> x4, waiting for transfers between devices: 8.88 us -> 11.1 us  [the longest x2 6.58 us: exchange(): other = lax.ppermute(terms, 'gz', swap_pairs(2, 1))]
    ppermute x2 -> x1, starting transfers between devices: 3.16 us -> 1.58 us  [fetch_ghosts(): return lax.ppermute(x, axis, swap_pairs(2, 1))]
    pallas_call x9, Pallas kernels: 16.6 us -> 15.3 us  [call(): pl.pallas_call(body, out_shape=[jax.ShapeDtypeStruct(shape, kind) for sha...]
    ppermute x17 -> x16, starting transfers between devices: 19.3 us -> 19.5 us  [pair_exchange(): lax.ppermute(x, axis, [(i, i ^ d) for i in range(size)])]
  transfers between devices with their start and end apart: 24 -> 21, of which waited for: 20 -> 16; matrix products, arithmetic and copies ran while one was open for 0% -> 0% of each run, Pallas kernels for 0% -> 0%
where the time goes in v6:
time: 78.2 us; the launch traced here: 77.9 us
  waiting for transfers between devices  33.4 us (43%)
  starting transfers between devices  24.5 us (31%)
  Pallas kernels  15.3 us (20%)
  local copies, waits for them, and re-layouts  3.5 us (4%)
  between operations  0.81 us (1%)
    ppermute x16, waiting for transfers between devices, pair_exchange(): lax.ppermute(x, axis, [(i, i ^ d) for i in range(size)])  20.6 us
    ppermute x16, starting transfers between devices, pair_exchange(): lax.ppermute(x, axis, [(i, i ^ d) for i in range(size)])  19.5 us
    pallas_call x9, Pallas kernels, call(): pl.pallas_call(body, out_shape=[jax.ShapeDtypeStruct(shape, kind) for sha...  15.3 us
    ppermute x2, waiting for transfers between devices, exchange(): other = lax.ppermute(terms, 'gz', swap_pairs(2, 1))  6.58 us
    ppermute x2, waiting for transfers between devices, sum_over(): x = x + lax.ppermute(x, axis, [(i, i ^ step) for i in range(size)])  4.51 us
    unnamed x18, local copies, waits for them, and re-layouts  3.43 us
    ppermute x2, starting transfers between devices, exchange(): other = lax.ppermute(terms, 'gz', swap_pairs(2, 1))  3.17 us
    ppermute x1, waiting for transfers between devices, fetch_ghosts(): return lax.ppermute(x, axis, swap_pairs(2, 1))  1.69 us
  transfers between devices with their start and end apart: 21, of which 16 were waited for; matrix products, arithmetic and copies ran while one was open for 0% of the time, Pallas kernels for 0%

profile of v6, /device:TPU:0, one launch (start us, length us, event | category | flops | bytes accessed | tf_op | source)
XLA Modules:
  0.0 77.9 jit_solution(5850101143730295478)
XLA Ops:
  1.3 0.7 copy-done.1
  3.6 5.1 %collective-permute-start = (f32[24,128]{1,0:T(8,128)S(1)}, f32[24,128]{1,0:T(8,128)S(1)}, u32[]{:S(2)}, u32[]{:S(2)}) collective-permute-start(f32[24,128]{1,0:T(8,128)S(1)} %get-tuple-element.37), channel_id=1, source_target_pairs={{0,24},{8,16},{16,8},{24,0},{1,25},{9,17},{17,9},{25,1},{2,26},{10... | collective-permute-start | bytes 36872 | tf_op jit(solution)/shard_map/ppermute | solution.py:32
  8.8 1.6 %collective-permute-done = f32[24,128]{1,0:T(8,128)S(1)} collective-permute-done((f32[24,128]{1,0:T(8,128)S(1)}, f32[24,128]{1,0:T(8,128)S(1)}, u32[]{:S(2)}, u32[]{:S(2)}) %collective-permute-start) | collective-permute-done | bytes 12320 | tf_op jit(solution)/shard_map/ppermute | solution.py:32
  10.4 2.0 %collective-permute-done.1 = f32[24,128]{1,0:T(8,128)S(1)} collective-permute-done((f32[24,128]{1,0:T(8,128)S(1)}, f32[24,128]{1,0:T(8,128)S(1)}, u32[]{:S(2)}, u32[]{:S(2)}) %collective-permute-start.1) | collective-permute-done | bytes 12320 | tf_op jit(solution)/shard_map/ppermute | solution.py:32
  12.6 1.6 %collective-permute-start.3 = (f32[24,256]{1,0:T(8,128)S(1)}, f32[24,256]{1,0:T(8,128)S(1)}, u32[]{:S(2)}, u32[]{:S(2)}) collective-permute-start(f32[24,256]{1,0:T(8,128)S(1)} %pad_maximum_fusion.3.g1_ref), channel_id=1, source_target_pairs={{0,2},{2,0},{4,6},{6,4},{1,3},{3,1},{5,7},{7,5},{8,10},{10,8},{12,... | collective-permute-start | bytes 73736 | tf_op jit(solution)/shard_map/ppermute | solution.py:32
  14.1 1.9 %collective-permute-done.2 = f32[24,256]{1,0:T(8,128)S(1)} collective-permute-done((f32[24,256]{1,0:T(8,128)S(1)}, f32[24,256]{1,0:T(8,128)S(1)}, u32[]{:S(2)}, u32[]{:S(2)}) %collective-permute-start.2) | collective-permute-done | bytes 24608 | tf_op jit(solution)/shard_map/ppermute | solution.py:32
  16.1 1.6 %collective-permute-start.4 = (f32[24,512]{1,0:T(8,128)S(1)}, f32[24,512]{1,0:T(8,128)S(1)}, u32[]{:S(2)}, u32[]{:S(2)}) collective-permute-start(f32[24,512]{1,0:T(8,128)S(1)} %pad_maximum_fusion), channel_id=1, source_target_pairs={{0,1},{1,0},{2,3},{3,2},{4,5},{5,4},{6,7},{7,6},{8,9},{9,8},{10,11... | collective-permute-start | bytes 147464 | tf_op jit(solution)/shard_map/ppermute | solution.py:52
  18.6 1.7 %collective-permute-done.4.g3_ref.beyond_ref = f32[24,512]{1,0:T(8,128)S(1)} collective-permute-done((f32[24,512]{1,0:T(8,128)S(1)}, f32[24,512]{1,0:T(8,128)S(1)}, u32[]{:S(2)}, u32[]{:S(2)}) %collective-permute-start.4) | collective-permute-done | bytes 49184 | tf_op jit(solution)/shard_map/ppermute | solution.py:52
  20.2 7.6 %shard_map.114 = (f32[24,1152]{1,0:T(8,128)S(1)}, f32[24,1536]{1,0:T(8,128)S(1)}, f32[8,1536]{1,0:T(8,128)S(1)}, f32[144,256]{1,0:T(8,128)S(1)}, f32[168,256]{1,...) custom-call(s32[1,1536]{1,0:T(1,128)S(1)} %get-tuple-element.36.idx_, ...), custom_call_target="tpu_custom_call" | custom-call | tf_op jit(solution)/shard_map/pallas_call | solution.py:1247
  27.8 1.6 %collective-permute-start.5 = (f32[24,1152]{1,0:T(8,128)S(1)}, f32[24,1152]{1,0:T(8,128)S(1)}, u32[]{:S(2)}, u32[]{:S(2)}) collective-permute-start(f32[24,1152]{1,0:T(8,128)S(1)} %get-tuple-element.42.mine), channel_id=1, source_target_pairs={{0,1},{1,0},{2,3},{3,2},{4,5},{5,4},{6,7},{7,6},{8,9},{9,8},{10,11... | collective-permute-start | bytes 331784 | tf_op jit(solution)/shard_map/ppermute | solution.py:1380
  29.4 3.2 %collective-permute-done.5.other = f32[24,1152]{1,0:T(8,128)S(1)} collective-permute-done((f32[24,1152]{1,0:T(8,128)S(1)}, f32[24,1152]{1,0:T(8,128)S(1)}, u32[]{:S(2)}, u32[]{:S(2)}) %collective-permute-start.5) | collective-permute-done | bytes 110624 | tf_op jit(solution)/shard_map/ppermute | solution.py:1380
  32.8 1.4 %collective-permute-start.7 = (f32[24,512]{1,0:T(8,128)S(1)}, f32[24,512]{1,0:T(8,128)S(1)}, u32[]{:S(2)}, u32[]{:S(2)}) collective-permute-start(f32[24,512]{1,0:T(8,128)S(1)} %pad_maximum_fusion.1), channel_id=1, source_target_pairs={{0,2},{2,0},{4,6},{6,4},{1,3},{3,1},{5,7},{7,5},{8,10},{10,8},{12,... | collective-permute-start | bytes 147464 | tf_op jit(solution)/shard_map/ppermute | solution.py:32
  34.1 2.5 %collective-permute-done.6 = f32[24,512]{1,0:T(8,128)S(1)} collective-permute-done((f32[24,512]{1,0:T(8,128)S(1)}, f32[24,512]{1,0:T(8,128)S(1)}, u32[]{:S(2)}, u32[]{:S(2)}) %collective-permute-start.6) | collective-permute-done | bytes 49184 | tf_op jit(solution)/shard_map/ppermute | solution.py:32
  36.9 1.9 %collective-permute-start.10 = (f32[24,512]{1,0:T(8,128)S(1)}, f32[24,512]{1,0:T(8,128)S(1)}, u32[]{:S(2)}, u32[]{:S(2)}) collective-permute-start(f32[24,512]{1,0:T(8,128)S(1)} %get-tuple-element.45.p0_ref), channel_id=1, source_target_pairs={{0,24},{8,16},{16,8},{24,0},{1,25},{9,17},{17,9},{25,1},{2,26},{10... | collective-permute-start | bytes 147464 | tf_op jit(solution)/shard_map/ppermute | solution.py:32
  38.8 2.6 %collective-permute-start.9 = (f32[24,512]{1,0:T(8,128)S(1)}, f32[24,512]{1,0:T(8,128)S(1)}, u32[]{:S(2)}, u32[]{:S(2)}) collective-permute-start(f32[24,512]{1,0:T(8,128)S(1)} %get-tuple-element.45.p0_ref), channel_id=1, source_target_pairs={{0,16},{8,24},{16,0},{24,8},{1,17},{9,25},{17,1},{25,9},{2,18},{10... | collective-permute-start | bytes 147464 | tf_op jit(solution)/shard_map/ppermute | solution.py:32
  41.4 1.6 %collective-permute-done.10.p3_ref = f32[24,512]{1,0:T(8,128)S(1)} collective-permute-done((f32[24,512]{1,0:T(8,128)S(1)}, f32[24,512]{1,0:T(8,128)S(1)}, u32[]{:S(2)}, u32[]{:S(2)}) %collective-permute-start.10) | collective-permute-done | bytes 49184 | tf_op jit(solution)/shard_map/ppermute | solution.py:32
  43.0 0.9 %collective-permute-done.8.p1_ref = f32[24,512]{1,0:T(8,128)S(1)} collective-permute-done((f32[24,512]{1,0:T(8,128)S(1)}, f32[24,512]{1,0:T(8,128)S(1)}, u32[]{:S(2)}, u32[]{:S(2)}) %collective-permute-start.8) | collective-permute-done | bytes 49184 | tf_op jit(solution)/shard_map/ppermute | solution.py:32
  44.7 0.7 collective-permute-start.12
  45.4 2.8 %collective-permute-done.11 = f32[24,512]{1,0:T(8,128)S(1)} collective-permute-done((f32[24,512]{1,0:T(8,128)S(1)}, f32[24,512]{1,0:T(8,128)S(1)}, u32[]{:S(2)}, u32[]{:S(2)}) %collective-permute-start.11) | collective-permute-done | bytes 49184 | tf_op jit(solution)/shard_map/ppermute | solution.py:32
  48.3 4.6 %shard_map.117 = (f32[24,1152]{1,0:T(8,128)S(1)}, f32[8,128]{1,0:T(8,128)S(1)}) custom-call(s32[1,1536]{1,0:T(1,128)S(1)} %get-tuple-element.36.idx_ref, f32[24,256]{1,0:T(8,128)S(1)} %get-tuple-element.46.own_ref.first_ref, f32[24,512]{1,0:T(8,128)S(1)} %get-tuple-element.47.refs_0_, f32[24,512]{1,0:T(8,128)S(1)} %xor_select_fusion.refs_1_, ...), custom_call_target="tpu_custom_call" | custom-call | tf_op jit(solution)/shard_map/pallas_call | solution.py:1247
  53.0 1.6 %collective-permute-start.13 = (f32[24,1280]{1,0:T(8,128)S(1)}, f32[24,1280]{1,0:T(8,128)S(1)}, u32[]{:S(2)}, u32[]{:S(2)}) collective-permute-start(f32[24,1280]{1,0:T(8,128)S(1)} %select_maximum_fusion.mine), channel_id=1, source_target_pairs={{0,1},{1,0},{2,3},{3,2},{4,5},{5,4},{6,7},{7,6},{8,9},{9,8},{10,11... | collective-permute-start | bytes 368648 | tf_op jit(solution)/shard_map/ppermute | solution.py:1380
  54.6 3.4 %collective-permute-done.13.other = f32[24,1280]{1,0:T(8,128)S(1)} collective-permute-done((f32[24,1280]{1,0:T(8,128)S(1)}, f32[24,1280]{1,0:T(8,128)S(1)}, u32[]{:S(2)}, u32[]{:S(2)}) %collective-permute-start.13) | collective-permute-done | bytes 122912 | tf_op jit(solution)/shard_map/ppermute | solution.py:1380
  58.4 1.3 %collective-permute-start.15 = (f32[24,512]{1,0:T(8,128)S(1)}, f32[24,512]{1,0:T(8,128)S(1)}, u32[]{:S(2)}, u32[]{:S(2)}) collective-permute-start(f32[24,512]{1,0:T(8,128)S(1)} %pad_maximum_fusion.2), channel_id=1, source_target_pairs={{0,2},{2,0},{4,6},{6,4},{1,3},{3,1},{5,7},{7,5},{8,10},{10,8},{12,... | collective-permute-start | bytes 147464 | tf_op jit(solution)/shard_map/ppermute | solution.py:32
  59.7 2.3 %collective-permute-done.14 = f32[24,512]{1,0:T(8,128)S(1)} collective-permute-done((f32[24,512]{1,0:T(8,128)S(1)}, f32[24,512]{1,0:T(8,128)S(1)}, u32[]{:S(2)}, u32[]{:S(2)}) %collective-permute-start.14) | collective-permute-done | bytes 49184 | tf_op jit(solution)/shard_map/ppermute | solution.py:32
  62.5 2.1 %collective-permute-start.16 = (f32[24,640]{1,0:T(8,128)S(1)}, f32[24,640]{1,0:T(8,128)S(1)}, u32[]{:S(2)}, u32[]{:S(2)}) collective-permute-start(f32[24,640]{1,0:T(8,128)S(1)} %get-tuple-element.60.p0_ref), channel_id=1, source_target_pairs={{0,24},{8,16},{16,8},{24,0},{1,25},{9,17},{17,9},{25,1},{2,26},{10... | collective-permute-start | bytes 184328 | tf_op jit(solution)/shard_map/ppermute | solution.py:32
  64.6 0.8 %collective-permute-start.17 = (f32[24,640]{1,0:T(8,128)S(1)}, f32[24,640]{1,0:T(8,128)S(1)}, u32[]{:S(2)}, u32[]{:S(2)}) collective-permute-start(f32[24,640]{1,0:T(8,128)S(1)} %get-tuple-element.60.p0_ref), channel_id=1, source_target_pairs={{0,16},{8,24},{16,0},{24,8},{1,17},{9,25},{17,1},{25,9},{2,18},{10... | collective-permute-start | bytes 184328 | tf_op jit(solution)/shard_map/ppermute | solution.py:32
  65.4 1.5 %collective-permute-start.18 = (f32[24,640]{1,0:T(8,128)S(1)}, f32[24,640]{1,0:T(8,128)S(1)}, u32[]{:S(2)}, u32[]{:S(2)}) collective-permute-start(f32[24,640]{1,0:T(8,128)S(1)} %get-tuple-element.60.p0_ref), channel_id=1, source_target_pairs={{0,8},{8,0},{16,24},{24,16},{1,9},{9,1},{17,25},{25,17},{2,10},{10... | collective-permute-start | bytes 184328 | tf_op jit(solution)/shard_map/ppermute | solution.py:32
  66.9 2.2 %collective-permute-done.16.p3_ref = f32[24,640]{1,0:T(8,128)S(1)} collective-permute-done((f32[24,640]{1,0:T(8,128)S(1)}, f32[24,640]{1,0:T(8,128)S(1)}, u32[]{:S(2)}, u32[]{:S(2)}) %collective-permute-start.16) | collective-permute-done | bytes 61472 | tf_op jit(solution)/shard_map/ppermute | solution.py:32
  69.1 2.5 %collective-permute-done.17.p2_ref = f32[24,640]{1,0:T(8,128)S(1)} collective-permute-done((f32[24,640]{1,0:T(8,128)S(1)}, f32[24,640]{1,0:T(8,128)S(1)}, u32[]{:S(2)}, u32[]{:S(2)}) %collective-permute-start.17) | collective-permute-done | bytes 61472 | tf_op jit(solution)/shard_map/ppermute | solution.py:32
  72.1 1.2 %collective-permute-done.19 = f32[8,128]{1,0:T(8,128)S(1)} collective-permute-done((f32[8,128]{1,0:T(8,128)S(1)}, f32[8,128]{1,0:T(8,128)S(1)}, u32[]{:S(2)}, u32[]{:S(2)}) %collective-permute-start.19) | collective-permute-done | bytes 4128 | tf_op jit(solution)/shard_map/ppermute | solution.py:91
  73.5 3.3 %collective-permute-done.20 = f32[8,128]{1,0:T(8,128)S(1)} collective-permute-done((f32[8,128]{1,0:T(8,128)S(1)}, f32[8,128]{1,0:T(8,128)S(1)}, u32[]{:S(2)}, u32[]{:S(2)}) %collective-permute-start.20) | collective-permute-done | bytes 4128 | tf_op jit(solution)/shard_map/ppermute | solution.py:91
  76.9 1.1 %shard_map.120 = (f32[1,1,1,3,4,256]{5,4,3,2,1,0:T(4,128)}, f32[2,4,4]{2,1,0:T(4,128)}, f32[2,4,4]{2,1,0:T(4,128)}) custom-call(f32[24,256]{1,0:T(8,128)S(1)} %get-tuple-element.35.own_ref.start_ref, f32[24,256]{1,0:T(8,128)S(1)} %get-tuple-element.46.own_ref.first_ref, f32[24,256]{1,0:T(8,128)S(1)} %get-tuple-element.62.second_ref, f32[8,128]{1,0:T(8,128)S(1)} %add.113.refs_0_), custom_call_target="tpu_custom_call" | custom-call | tf_op jit(solution)/shard_map/pallas_call | solution.py:1247
  (61 shorter events, 6.4 us)
Async XLA Ops:
  0.6 0.7 copy-start.5
  1.3 0.7 copy-start.1
  2.0 0.7 copy-start.3
  2.7 0.7 copy-start.6
  3.6 6.8 %collective-permute-start = (f32[24,128]{1,0:T(8,128)S(1)}, f32[24,128]{1,0:T(8,128)S(1)}, u32[]{:S(2)}, u32[]{:S(2)}) collective-permute-start(f32[24,128]{1,0:T(8,128)S(1)} %get-tuple-element.37), channel_id=1, source_target_pairs={{0,24},{8,16},{16,8},{24,0},{1,25},{9,17},{17,9},{25,1},{2,26},{10... | collective-permute-start | bytes 36872 | tf_op jit(solution)/shard_map/ppermute | solution.py:32
  8.7 3.7 %collective-permute-start.1 = (f32[24,128]{1,0:T(8,128)S(1)}, f32[24,128]{1,0:T(8,128)S(1)}, u32[]{:S(2)}, u32[]{:S(2)}) collective-permute-start(f32[24,128]{1,0:T(8,128)S(1)} %get-tuple-element.37), channel_id=1, source_target_pairs={{0,8},{8,0},{16,24},{24,16},{1,9},{9,1},{17,25},{25,17},{2,10},{10... | collective-permute-start | bytes 36872 | tf_op jit(solution)/shard_map/ppermute | solution.py:32
  12.5 3.5 %collective-permute-start.2 = (f32[24,256]{1,0:T(8,128)S(1)}, f32[24,256]{1,0:T(8,128)S(1)}, u32[]{:S(2)}, u32[]{:S(2)}) collective-permute-start(f32[24,256]{1,0:T(8,128)S(1)} %pad_maximum_fusion.3.g1_ref), channel_id=1, source_target_pairs={{0,6},{2,4},{4,2},{6,0},{1,7},{3,5},{5,3},{7,1},{8,14},{10,12},{12... | collective-permute-start | bytes 73736 | tf_op jit(solution)/shard_map/ppermute | solution.py:32
  12.6 3.5 %collective-permute-start.3 = (f32[24,256]{1,0:T(8,128)S(1)}, f32[24,256]{1,0:T(8,128)S(1)}, u32[]{:S(2)}, u32[]{:S(2)}) collective-permute-start(f32[24,256]{1,0:T(8,128)S(1)} %pad_maximum_fusion.3.g1_ref), channel_id=1, source_target_pairs={{0,2},{2,0},{4,6},{6,4},{1,3},{3,1},{5,7},{7,5},{8,10},{10,8},{12,... | collective-permute-start | bytes 73736 | tf_op jit(solution)/shard_map/ppermute | solution.py:32
  16.0 1.6 %copy-start = (f32[128,64]{0,1:T(8,128)S(1)}, f32[128,64]{0,1:T(8,128)}, u32[]{:S(2)}) copy-start(f32[128,64]{0,1:T(8,128)} %param.16) | copy-start | bytes 98308
  16.1 1.6 %copy-start.2 = (s32[1,1,1,6,256]{4,2,3,1,0:T(1,128)S(1)}, s32[1,1,1,6,256]{4,2,3,1,0:T(1,128)}, u32[]{:S(2)}) copy-start(s32[1,1,1,6,256]{4,2,3,1,0:T(1,128)} %param.12) | copy-start | bytes 18436
  16.1 1.6 %copy-start.4 = (f32[8,128]{1,0:T(8,128)S(1)}, f32[8,128]{1,0:T(8,128)}, u32[]{:S(2)}) copy-start(f32[8,128]{1,0:T(8,128)} %rin_ref.1) | copy-start | bytes 12292
  16.1 4.2 %collective-permute-start.4 = (f32[24,512]{1,0:T(8,128)S(1)}, f32[24,512]{1,0:T(8,128)S(1)}, u32[]{:S(2)}, u32[]{:S(2)}) collective-permute-start(f32[24,512]{1,0:T(8,128)S(1)} %pad_maximum_fusion), channel_id=1, source_target_pairs={{0,1},{1,0},{2,3},{3,2},{4,5},{5,4},{6,7},{7,6},{8,9},{9,8},{10,11... | collective-permute-start | bytes 147464 | tf_op jit(solution)/shard_map/ppermute | solution.py:52
  17.7 0.7 copy-start.7
  17.7 0.7 copy-start.8
  27.8 4.8 %collective-permute-start.5 = (f32[24,1152]{1,0:T(8,128)S(1)}, f32[24,1152]{1,0:T(8,128)S(1)}, u32[]{:S(2)}, u32[]{:S(2)}) collective-permute-start(f32[24,1152]{1,0:T(8,128)S(1)} %get-tuple-element.42.mine), channel_id=1, source_target_pairs={{0,1},{1,0},{2,3},{3,2},{4,5},{5,4},{6,7},{7,6},{8,9},{9,8},{10,11... | collective-permute-start | bytes 331784 | tf_op jit(solution)/shard_map/ppermute | solution.py:1380
  32.7 3.9 %collective-permute-start.6 = (f32[24,512]{1,0:T(8,128)S(1)}, f32[24,512]{1,0:T(8,128)S(1)}, u32[]{:S(2)}, u32[]{:S(2)}) collective-permute-start(f32[24,512]{1,0:T(8,128)S(1)} %pad_maximum_fusion.1), channel_id=1, source_target_pairs={{0,6},{2,4},{4,2},{6,0},{1,7},{3,5},{5,3},{7,1},{8,14},{10,12},{12... | collective-permute-start | bytes 147464 | tf_op jit(solution)/shard_map/ppermute | solution.py:32
  32.8 3.9 %collective-permute-start.7 = (f32[24,512]{1,0:T(8,128)S(1)}, f32[24,512]{1,0:T(8,128)S(1)}, u32[]{:S(2)}, u32[]{:S(2)}) collective-permute-start(f32[24,512]{1,0:T(8,128)S(1)} %pad_maximum_fusion.1), channel_id=1, source_target_pairs={{0,2},{2,0},{4,6},{6,4},{1,3},{3,1},{5,7},{7,5},{8,10},{10,8},{12,... | collective-permute-start | bytes 147464 | tf_op jit(solution)/shard_map/ppermute | solution.py:32
  36.9 6.1 %collective-permute-start.10 = (f32[24,512]{1,0:T(8,128)S(1)}, f32[24,512]{1,0:T(8,128)S(1)}, u32[]{:S(2)}, u32[]{:S(2)}) collective-permute-start(f32[24,512]{1,0:T(8,128)S(1)} %get-tuple-element.45.p0_ref), channel_id=1, source_target_pairs={{0,24},{8,16},{16,8},{24,0},{1,25},{9,17},{17,9},{25,1},{2,26},{10... | collective-permute-start | bytes 147464 | tf_op jit(solution)/shard_map/ppermute | solution.py:32
  38.8 5.1 %collective-permute-start.8 = (f32[24,512]{1,0:T(8,128)S(1)}, f32[24,512]{1,0:T(8,128)S(1)}, u32[]{:S(2)}, u32[]{:S(2)}) collective-permute-start(f32[24,512]{1,0:T(8,128)S(1)} %get-tuple-element.45.p0_ref), channel_id=1, source_target_pairs={{0,8},{8,0},{16,24},{24,16},{1,9},{9,1},{17,25},{25,17},{2,10},{10... | collective-permute-start | bytes 147464 | tf_op jit(solution)/shard_map/ppermute | solution.py:32
  38.8 5.4 %collective-permute-start.9 = (f32[24,512]{1,0:T(8,128)S(1)}, f32[24,512]{1,0:T(8,128)S(1)}, u32[]{:S(2)}, u32[]{:S(2)}) collective-permute-start(f32[24,512]{1,0:T(8,128)S(1)} %get-tuple-element.45.p0_ref), channel_id=1, source_target_pairs={{0,16},{8,24},{16,0},{24,8},{1,17},{9,25},{17,1},{25,9},{2,18},{10... | collective-permute-start | bytes 147464 | tf_op jit(solution)/shard_map/ppermute | solution.py:32
  44.7 3.5 %collective-permute-start.11 = (f32[24,512]{1,0:T(8,128)S(1)}, f32[24,512]{1,0:T(8,128)S(1)}, u32[]{:S(2)}, u32[]{:S(2)}) collective-permute-start(f32[24,512]{1,0:T(8,128)S(1)} %get-tuple-element.47.refs_0_), channel_id=1, source_target_pairs={{0,6},{2,4},{4,2},{6,0},{1,7},{3,5},{5,3},{7,1},{8,14},{10,12},{12... | collective-permute-start | bytes 147464 | tf_op jit(solution)/shard_map/ppermute | solution.py:32
  44.7 3.5 %collective-permute-start.12 = (f32[24,512]{1,0:T(8,128)S(1)}, f32[24,512]{1,0:T(8,128)S(1)}, u32[]{:S(2)}, u32[]{:S(2)}) collective-permute-start(f32[24,512]{1,0:T(8,128)S(1)} %get-tuple-element.47.refs_0_), channel_id=1, source_target_pairs={{0,2},{2,0},{4,6},{6,4},{1,3},{3,1},{5,7},{7,5},{8,10},{10,8},{12,... | collective-permute-start | bytes 147464 | tf_op jit(solution)/shard_map/ppermute | solution.py:32
  53.0 4.9 %collective-permute-start.13 = (f32[24,1280]{1,0:T(8,128)S(1)}, f32[24,1280]{1,0:T(8,128)S(1)}, u32[]{:S(2)}, u32[]{:S(2)}) collective-permute-start(f32[24,1280]{1,0:T(8,128)S(1)} %select_maximum_fusion.mine), channel_id=1, source_target_pairs={{0,1},{1,0},{2,3},{3,2},{4,5},{5,4},{6,7},{7,6},{8,9},{9,8},{10,11... | collective-permute-start | bytes 368648 | tf_op jit(solution)/shard_map/ppermute | solution.py:1380
  58.0 4.0 %collective-permute-start.14 = (f32[24,512]{1,0:T(8,128)S(1)}, f32[24,512]{1,0:T(8,128)S(1)}, u32[]{:S(2)}, u32[]{:S(2)}) collective-permute-start(f32[24,512]{1,0:T(8,128)S(1)} %pad_maximum_fusion.2), channel_id=1, source_target_pairs={{0,6},{2,4},{4,2},{6,0},{1,7},{3,5},{5,3},{7,1},{8,14},{10,12},{12... | collective-permute-start | bytes 147464 | tf_op jit(solution)/shard_map/ppermute | solution.py:32
  58.4 3.6 %collective-permute-start.15 = (f32[24,512]{1,0:T(8,128)S(1)}, f32[24,512]{1,0:T(8,128)S(1)}, u32[]{:S(2)}, u32[]{:S(2)}) collective-permute-start(f32[24,512]{1,0:T(8,128)S(1)} %pad_maximum_fusion.2), channel_id=1, source_target_pairs={{0,2},{2,0},{4,6},{6,4},{1,3},{3,1},{5,7},{7,5},{8,10},{10,8},{12,... | collective-permute-start | bytes 147464 | tf_op jit(solution)/shard_map/ppermute | solution.py:32
  62.5 6.6 %collective-permute-start.16 = (f32[24,640]{1,0:T(8,128)S(1)}, f32[24,640]{1,0:T(8,128)S(1)}, u32[]{:S(2)}, u32[]{:S(2)}) collective-permute-start(f32[24,640]{1,0:T(8,128)S(1)} %get-tuple-element.60.p0_ref), channel_id=1, source_target_pairs={{0,24},{8,16},{16,8},{24,0},{1,25},{9,17},{17,9},{25,1},{2,26},{10... | collective-permute-start | bytes 184328 | tf_op jit(solution)/shard_map/ppermute | solution.py:32
  64.6 6.9 %collective-permute-start.17 = (f32[24,640]{1,0:T(8,128)S(1)}, f32[24,640]{1,0:T(8,128)S(1)}, u32[]{:S(2)}, u32[]{:S(2)}) collective-permute-start(f32[24,640]{1,0:T(8,128)S(1)} %get-tuple-element.60.p0_ref), channel_id=1, source_target_pairs={{0,16},{8,24},{16,0},{24,8},{1,17},{9,25},{17,1},{25,9},{2,18},{10... | collective-permute-start | bytes 184328 | tf_op jit(solution)/shard_map/ppermute | solution.py:32
  65.4 6.1 %collective-permute-start.18 = (f32[24,640]{1,0:T(8,128)S(1)}, f32[24,640]{1,0:T(8,128)S(1)}, u32[]{:S(2)}, u32[]{:S(2)}) collective-permute-start(f32[24,640]{1,0:T(8,128)S(1)} %get-tuple-element.60.p0_ref), channel_id=1, source_target_pairs={{0,8},{8,0},{16,24},{24,16},{1,9},{9,1},{17,25},{25,17},{2,10},{10... | collective-permute-start | bytes 184328 | tf_op jit(solution)/shard_map/ppermute | solution.py:32
  72.1 1.2 %collective-permute-start.19 = (f32[8,128]{1,0:T(8,128)S(1)}, f32[8,128]{1,0:T(8,128)S(1)}, u32[]{:S(2)}, u32[]{:S(2)}) collective-permute-start(f32[8,128]{1,0:T(8,128)S(1)} %get-tuple-element.63), channel_id=1, source_target_pairs={{0,2},{2,0},{4,6},{6,4},{1,3},{3,1},{5,7},{7,5},{8,10},{10,8},{12,... | collective-permute-start | bytes 12296 | tf_op jit(solution)/shard_map/ppermute | solution.py:91
  73.2 3.6 %collective-permute-start.20 = (f32[8,128]{1,0:T(8,128)S(1)}, f32[8,128]{1,0:T(8,128)S(1)}, u32[]{:S(2)}, u32[]{:S(2)}) collective-permute-start(f32[8,128]{1,0:T(8,128)S(1)} %add.112), channel_id=1, source_target_pairs={{0,4},{2,6},{4,0},{6,2},{1,5},{3,7},{5,1},{7,3},{8,12},{10,14},{12... | collective-permute-start | bytes 12296 | tf_op jit(solution)/shard_map/ppermute | solution.py:91

commit v7 on v6

--- a/solution.py
+++ b/solution.py
@@ -138,39 +138,24 @@
     return y + pltpu.roll(y, GROUP - vectors, 0)
 
 
-def pack_kernel(pos_hbm, spec_hbm, block_hbm, raw_hbm, own_ref, oct_ref, list_ref, *scratch):
-    pos_ref, spec_ref, block_ref, raw_ref, sems = scratch
-    copies = [
-        pltpu.make_async_copy(source, target, sems.at[n])
-        for n, (source, target) in enumerate(
-            (
-                (pos_hbm, pos_ref),
-                (spec_hbm, spec_ref),
-                (block_hbm, block_ref),
-                (raw_hbm, raw_ref),
-            )
-        )
-    ]
-    for copy in copies:
-        copy.start()
-    for copy in copies:
-        copy.wait()
-    vectors = block_ref.shape[4]
-    atoms = pos_ref.shape[-1]
-    for a in range(3):
-        parts = [block_ref[0, 0, 0, a], pos_ref[a]]
-        used = vectors + 1
-        if a == 0:
-            parts.append(spec_ref[0, 0].astype(jnp.float32))
-            used += 1
-        parts.append(jnp.zeros((GROUP - used, atoms), jnp.float32))
-        own_ref[rows(a), :] = jnp.concatenate(parts, axis=0)
-    pieces = [raw_ref[n // 4, n // 2 % 2, n % 2 : n % 2 + 1, :] for n in range(8)]
-    list_ref[...] = jnp.concatenate(pieces, axis=1)
+def pack_rows(values, vectors):
+    row = lax.broadcasted_iota(jnp.int32, values[0].shape, 0)
+    return jnp.where(row < vectors, values[0], pltpu.roll(values[1], vectors, 0)), values[2]
+
+
+def unpack_rows(ref, lanes, vectors):
+    both = ref[rows(0), lanes]
+    return [both, pltpu.roll(both, GROUP - vectors, 0), ref[rows(1), lanes]]
+
+
+def pack_kernel(vectors, own_ref, oct_ref, list_ref):
+    mark = vectors + 2
+    width = oct_ref.shape[1]
+    list_ref[...] = own_ref[mark : mark + 1, :width].astype(jnp.int32)
     pick_octants(own_ref, list_ref, oct_ref)
-    row = lax.broadcasted_iota(jnp.int32, (GROUP, list_ref.shape[1]), 0)
+    row = lax.broadcasted_iota(jnp.int32, (GROUP, width), 0)
     oct_ref[rows(0), :] = jnp.where(
-        row == vectors + 2, list_ref[...].astype(jnp.float32), oct_ref[rows(0), :]
+        row == mark, own_ref[mark : mark + 1, :width], oct_ref[rows(0), :]
     )
 
 
@@ -232,6 +217,11 @@
     for kind, (ref, start) in enumerate(places):
         if kind == 0:
             continue
+        base = atoms + (kind - 1) * width
+        if len(ghost_refs) == 2:
+            for a, part in enumerate(unpack_rows(ref, slice(start, start + width), vectors)):
+                table[rows(a), base : base + width] = part
+            continue
         part = ref[:, start : start + width]
         if shifted:
             row = lax.broadcasted_iota(jnp.int32, part.shape, 0)
@@ -239,7 +229,6 @@
                 if (kind >> a) & 1:
                     move = jnp.where(octant_bit(part.shape, a, ghosts), -1.0, 1.0)
                     part = part + jnp.where(row == GROUP * a + vectors, move, 0.0)
-        base = atoms + (kind - 1) * width
         table[:, base : base + width] = part
 
 
@@ -429,12 +418,14 @@
     )
     own_tiles = atoms // LANES
     for number in range(tiles):
+        cut = slice(number * LANES, (number + 1) * LANES)
+        values = []
         for a in range(3):
             value = join_rows(spread[tile_rows(number * 3 + a)], vectors)
-            cut = slice(number * LANES, (number + 1) * LANES)
             if number < own_tiles:
                 value = value + center[a][:, cut]
-            terms_out[rows(a), cut] = value
+            values.append(value)
+        terms_out[rows(0), cut], terms_out[rows(1), cut] = pack_rows(values, vectors)
     return shifted
 
 
@@ -869,40 +860,37 @@
     gram_ref[...] = total[0] + pltpu.roll(from_shifted(total[1:], vectors), 4 * GROUP, 1)
 
 
-def pair_sums(mine, other, got, width, atoms):
-    def tile(ref, kind, a):
+def pair_sums(mine, other, got, width, atoms, vectors):
+    def tile(ref, kind):
         start = atoms + (kind - 1) * width
-        return ref[rows(a), start : start + width]
-
-    def back(n, a):
-        return got[rows(a), n * width : (n + 1) * width]
+        return ref[:, start : start + width]
+
+    def back(n):
+        return got[:, n * width : (n + 1) * width]
 
     def pick(first, second, n):
         return (
-            [first[rows(a), :atoms] for a in range(3)],
-            [tile(second, 4, a) + back(n, a) for a in range(3)],
-            [tile(first, 1, a) + tile(second, 5, a) + back(n + 1, a) for a in range(3)],
+            unpack_rows(first, slice(0, atoms), vectors),
+            tile(second, 4) + back(n),
+            tile(first, 1) + tile(second, 5) + back(n + 1),
         )
 
     return pick(mine, other, 0), pick(other, mine, 2)
 
 
-def pair_packet(vectors, mine, other, got, lists, parts, packet, ghosts_width):
+def pair_packet(vectors, mine, other, got, lists, parts, packet, width):
     atoms = parts[0].shape[1]
-    mark = vectors + 1
-    for n, (own, sums, beside) in enumerate(pair_sums(mine, other, got, ghosts_width, atoms)):
-        base = 2 * n * ghosts_width
-        for a in range(3):
-            parts[n][rows(a), :] = add_octants(own[a], sums[a], lists[n], vectors)
-        for a in range(3):
-            packet[rows(a), base + ghosts_width : base + 2 * ghosts_width] = beside[a]
-            for j in range(ghosts_width // LANES):
-                cut = slice(j * LANES, (j + 1) * LANES)
-                value = gather_lanes(parts[n], lists[n][:, cut], a)
-                if a == 0:
-                    row = lax.broadcasted_iota(jnp.int32, value.shape, 0)
-                    value = jnp.where(row == mark, lists[n][:, cut].astype(jnp.float32), value)
-                packet[rows(a), base + j * LANES : base + (j + 1) * LANES] = value
+    for n, (own, sums, beside) in enumerate(pair_sums(mine, other, got, width, atoms, vectors)):
+        base = 2 * n * width
+        for a, value in enumerate(unpack_rows(sums, slice(0, width), vectors)):
+            parts[n][rows(a), :] = add_octants(own[a], value, lists[n], vectors)
+        packet[:, base + width : base + 2 * width] = beside
+        first, last = pack_rows([read_back(parts[n], lists[n], a) for a in range(3)], vectors)
+        row = lax.broadcasted_iota(jnp.int32, last.shape, 0)
+        packet[rows(0), base : base + width] = first
+        packet[rows(1), base : base + width] = jnp.where(
+            row == vectors, lists[n].astype(jnp.float32), last
+        )
 
 
 def pair_lists(vectors, list_ref, beyond_ref):
@@ -929,16 +917,12 @@
 def placed_terms(side, packets, n, half, lists, atoms, width, vectors):
     start = (2 * half + 1) * width
     after, before = packets[(n + 1) % 4], packets[(n + 3) % 4]
+    cut = slice(start, start + width)
+    arrived = jnp.where(
+        jnp.concatenate([side, side], axis=0) > 0.5, after[:, cut], before[:, cut]
+    )
     terms = [
-        only_vectors(
-            jnp.where(
-                side > 0.5,
-                after[rows(a), start : start + width],
-                before[rows(a), start : start + width],
-            ),
-            vectors,
-        )
-        for a in range(3)
+        only_vectors(t, vectors) for t in unpack_rows(arrived, slice(0, width), vectors)
     ]
     packed = jnp.concatenate([split_rows(t, vectors) for t in terms], axis=0)
     onehot = lax.broadcasted_iota(jnp.int32, (atoms, width), 0) == lists
@@ -960,7 +944,7 @@
 
 
 def packet_row(packet, half, vectors, width):
-    mark = vectors + 1
+    mark = GROUP + vectors
     start = 2 * half * width
     return packet[mark : mark + 1, start : start + width].astype(jnp.int32)
 
@@ -994,17 +978,15 @@
                 if n == 0 and half == 0:
                     full_ref[rows(a), :] = part_ref[rows(a), :] + placed[a]
             start = 2 * half * width
+            change = pack_rows([read_back(spread_here, lists, a) for a in range(3)], vectors)
             found.append(
-                [
-                    packets[n][rows(a), start : start + width] + read_back(spread_here, lists, a)
-                    for a in range(3)
-                ]
+                [packets[n][rows(g), start : start + width] + change[g] for g in range(2)]
             )
-        for a in range(3):
+        for g in range(2):
             start = 2 * half * width
-            level_ref[rows(a), start : start + width] = found[0][a]
-            level_ref[rows(a), start + width : start + 2 * width] = jnp.where(
-                side > 0.5, found[2][a], found[1][a]
+            level_ref[rows(g), start : start + width] = found[0][g]
+            level_ref[rows(g), start + width : start + 2 * width] = jnp.where(
+                side > 0.5, found[2][g], found[1][g]
             )
     total = jnp.zeros((2 * GROUP, LANES), jnp.float32)
     for a in range(3):
@@ -1058,7 +1040,7 @@
     gram = gram_ref[...] + beyond_gram[...]
     cut = slice(4 * width, 4 * width + LANES)
     packet_ref[rows(0), cut] = gram + pltpu.roll(squares[0] + squares[1], 4 * GROUP, 1)
-    packet_ref[GROUP : 3 * GROUP, cut] = jnp.zeros((2 * GROUP, LANES), jnp.float32)
+    packet_ref[rows(1), cut] = jnp.zeros((GROUP, LANES), jnp.float32)
 
 
 def pair_gram_merge_kernel(
@@ -1085,12 +1067,13 @@
             terms, placed = placed_terms(side, packets, n, half, lists, atoms, width, vectors)
             spread_here = spread.at[2 * n + half]
             found = None
+            start = 2 * half * width
+            values = unpack_rows(packets[n], slice(start, start + width), vectors)
             for a in range(3):
                 spread_here[rows(a), :] = placed[a]
                 if n == 0 and half == 0:
                     full_ref[rows(a), :] = part_ref[rows(a), :] + placed[a]
-                start = 2 * half * width
-                at = repeat_rows(packets[n][rows(a), start : start + width], vectors)
+                at = repeat_rows(values[a], vectors)
                 products = shifted_products(
                     terms[a], at + at + read_back(spread_here, lists, a), vectors
                 )
@@ -1307,19 +1290,28 @@
         jnp.float32
     )
 
-    inputs = (
-        positions.transpose(0, 1, 3, 2, 4).reshape(3, 1, atoms),
-        species,
-        start_block.transpose(0, 1, 2, 4, 3, 5),
-        ghost_lists,
-    )
-    own, octants, lists = call(
-        pack_kernel,
-        [(high, atoms), (high, width), ((1, width), jnp.int32)],
-        inputs,
-        [pltpu.VMEM(x.shape, x.dtype) for x in inputs]
-        + [pltpu.SemaphoreType.DMA((len(inputs),))],
-        spaces=pltpu.HBM,
+    block = start_block[0, 0, 0]
+    blank = jnp.zeros((GROUP - vectors - 1, atoms), jnp.float32)
+    extra = jnp.concatenate(
+        [
+            species[0, 0].astype(jnp.float32),
+            jnp.pad(ghost_lists.reshape(1, width).astype(jnp.float32), ((0, 0), (0, atoms - width))),
+            blank[2:],
+        ],
+        axis=0,
+    )
+    own = jnp.concatenate(
+        [
+            part
+            for a in range(3)
+            for part in (block[:, a], positions[0, 0, 0, a : a + 1], extra if a == 0 else blank)
+        ],
+        axis=0,
+    )
+    octants, lists = call(
+        functools.partial(pack_kernel, vectors),
+        [(high, width), ((1, width), jnp.int32)],
+        (own,),
     )
     basis, hidden = radial_in.shape
     index, low, inward, outward, columns = call(
@@ -1356,7 +1348,7 @@
     ghost_levels = spread(octants)
     results = call(
         functools.partial(first_kernel, ghosts, vectors, basis, embedding.shape[0]),
-        [(high, table_width)] + saved_shapes,
+        [(2 * GROUP, table_width)] + saved_shapes,
         (index, own) + ghost_levels + (low, inward, outward, columns),
         [(high, table_width), (channels, edges), (channels, LANES)]
         + shared
@@ -1368,10 +1360,15 @@
     def second_product(first, levels):
         return call(
             functools.partial(second_kernel, ghosts, vectors, len(levels)),
-            [(high, table_width), (GROUP, LANES)],
+            [(2 * GROUP, table_width), (GROUP, LANES)],
             (index, first) + levels + (low,) + tuple(saved),
             [(high, table_width)] + shared,
         )
+
+    def loose(terms):
+        parts = [terms[GROUP // 2 * n : GROUP // 2 * (n + 1)] for n in range(3)]
+        rest = jnp.zeros_like(parts[0])
+        return jnp.concatenate([x for part in parts for x in (part, rest)], axis=0)
 
     if lifted:
         beyond = ghost_levels[2]
@@ -1388,24 +1385,24 @@
         other, got = exchange(terms)
         part, packet = call(
             functools.partial(pair_start_kernel, vectors),
-            [(high, atoms), (high, 4 * width)],
+            [(high, atoms), (2 * GROUP, 4 * width)],
             (terms, other, got, lists, beyond),
             [(high, atoms)],
         )
         others = pair_exchange(packet, "gx", (1, 2, 3))
         first, level, gram = call(
             functools.partial(pair_merge_kernel, vectors, width),
-            [(high, atoms), (high, 4 * width), (GROUP, LANES)],
+            [(high, atoms), (2 * GROUP, 4 * width), (GROUP, LANES)],
             (side, part, packet, *others, own),
             [(6, high, atoms)],
         )
         terms, edge_gram = second_product(first, (level, fetch_ghosts(level, 1, ghosts)))
         gram = gram + jnp.roll(edge_gram, 3 * GROUP, axis=1)
-        sent = jnp.concatenate([terms, jnp.pad(gram, ((0, high - GROUP), (0, 0)))], axis=1)
+        sent = jnp.concatenate([terms, jnp.pad(gram, ((0, GROUP), (0, 0)))], axis=1)
         other, got = exchange(sent)
         part, packet = call(
             functools.partial(pair_gram_start_kernel, vectors),
-            [(high, atoms), (high, 4 * width + LANES)],
+            [(high, atoms), (2 * GROUP, 4 * width + LANES)],
             (sent, other, got, lists, beyond, gram, other[:GROUP, table_width:]),
             [(high, atoms)],
         )
@@ -1418,6 +1415,7 @@
         )
         gram = [sum_over(gram, AXES[1:2])]
     else:
+        terms = loose(terms)
         own_terms, ghost_terms = terms[:, :atoms], terms[:, atoms:]
         sums, beside = return_outer(ghost_terms, width, ghosts)
         if ring:
@@ -1440,6 +1438,7 @@
                 (own_terms, sums + return_ghosts(beside, 0, ghosts), lists),
             )
         terms, edge_gram = second_product(first, spread(level))
+        terms = loose(terms)
         own_terms, ghost_terms = terms[:, :atoms], terms[:, atoms:]
         sums, beside = return_outer(ghost_terms, width, ghosts)
         if ring:

time: 78.2 us -> 73.4 us (0.939)
  waiting for transfers between devices: 33.4 us -> 28.8 us
    ppermute x16, waiting for transfers between devices: 20.6 us -> 17.7 us  [pair_exchange(): lax.ppermute(x, axis, [(i, i ^ d) for i in range(size)])]
    unnamed x18 -> x16, local copies, waits for them, and re-layouts: 3.43 us -> 1.96 us
    ppermute x2, starting transfers between devices: 0.27 us -> 1.17 us  [sum_over(): x = x + lax.ppermute(x, axis, [(i, i ^ step) for i in range(size)])]
    ppermute x2, waiting for transfers between devices: 4.51 us -> 3.61 us  [sum_over(): x = x + lax.ppermute(x, axis, [(i, i ^ step) for i in range(size)])]
    ppermute x2, waiting for transfers between devices: 6.58 us -> 5.76 us  [exchange(): other = lax.ppermute(terms, 'gz', swap_pairs(2, 1))]
where the time goes in v7:
time: 73.4 us; the launch traced here: 73.1 us
  waiting for transfers between devices  28.8 us (39%)
  starting transfers between devices  25 us (34%)
  Pallas kernels  15.3 us (21%)
  local copies, waits for them, and re-layouts  2.92 us (4%)
  between operations  0.81 us (1%)
    ppermute x16, starting transfers between devices, pair_exchange(): lax.ppermute(x, axis, [(i, i ^ d) for i in range(size)])  19.1 us
    ppermute x16, waiting for transfers between devices, pair_exchange(): lax.ppermute(x, axis, [(i, i ^ d) for i in range(size)])  17.7 us
    pallas_call x9, Pallas kernels, call(): pl.pallas_call(body, out_shape=[jax.ShapeDtypeStruct(shape, kind) for sha...  15.3 us
    ppermute x2, waiting for transfers between devices, exchange(): other = lax.ppermute(terms, 'gz', swap_pairs(2, 1))  5.76 us
    ppermute x2, waiting for transfers between devices, sum_over(): x = x + lax.ppermute(x, axis, [(i, i ^ step) for i in range(size)])  3.61 us
    ppermute x2, starting transfers between devices, exchange(): other = lax.ppermute(terms, 'gz', swap_pairs(2, 1))  3.15 us
    unnamed x16, local copies, waits for them, and re-layouts  1.96 us
    ppermute x1, waiting for transfers between devices, fetch_ghosts(): return lax.ppermute(x, axis, swap_pairs(2, 1))  1.69 us
  transfers between devices with their start and end apart: 21, of which 16 were waited for; matrix products, arithmetic and copies ran while one was open for 0% of the time, Pallas kernels for 0%

profile of v7, /device:TPU:0, one launch (start us, length us, event | category | flops | bytes accessed | tf_op | source)
XLA Modules:
  0.0 73.1 jit_solution(1767454615849326617)
XLA Ops:
  2.9 5.1 %collective-permute-start = (f32[24,128]{1,0:T(8,128)S(1)}, f32[24,128]{1,0:T(8,128)S(1)}, u32[]{:S(2)}, u32[]{:S(2)}) collective-permute-start(f32[24,128]{1,0:T(8,128)S(1)} %get-tuple-element.35), channel_id=1, source_target_pairs={{0,24},{8,16},{16,8},{24,0},{1,25},{9,17},{17,9},{25,1},{2,26},{10... | collective-permute-start | bytes 36872 | tf_op jit(solution)/shard_map/ppermute | solution.py:32
  8.0 1.6 %collective-permute-done = f32[24,128]{1,0:T(8,128)S(1)} collective-permute-done((f32[24,128]{1,0:T(8,128)S(1)}, f32[24,128]{1,0:T(8,128)S(1)}, u32[]{:S(2)}, u32[]{:S(2)}) %collective-permute-start) | collective-permute-done | bytes 12320 | tf_op jit(solution)/shard_map/ppermute | solution.py:32
  9.7 2.0 %collective-permute-done.1 = f32[24,128]{1,0:T(8,128)S(1)} collective-permute-done((f32[24,128]{1,0:T(8,128)S(1)}, f32[24,128]{1,0:T(8,128)S(1)}, u32[]{:S(2)}, u32[]{:S(2)}) %collective-permute-start.1) | collective-permute-done | bytes 12320 | tf_op jit(solution)/shard_map/ppermute | solution.py:32
  11.8 1.6 %collective-permute-start.3 = (f32[24,256]{1,0:T(8,128)S(1)}, f32[24,256]{1,0:T(8,128)S(1)}, u32[]{:S(2)}, u32[]{:S(2)}) collective-permute-start(f32[24,256]{1,0:T(8,128)S(1)} %pad_maximum_fusion.3.g1_ref), channel_id=1, source_target_pairs={{0,2},{2,0},{4,6},{6,4},{1,3},{3,1},{5,7},{7,5},{8,10},{10,8},{12,... | collective-permute-start | bytes 73736 | tf_op jit(solution)/shard_map/ppermute | solution.py:32
  13.4 1.9 %collective-permute-done.2 = f32[24,256]{1,0:T(8,128)S(1)} collective-permute-done((f32[24,256]{1,0:T(8,128)S(1)}, f32[24,256]{1,0:T(8,128)S(1)}, u32[]{:S(2)}, u32[]{:S(2)}) %collective-permute-start.2) | collective-permute-done | bytes 24608 | tf_op jit(solution)/shard_map/ppermute | solution.py:32
  15.3 1.6 %collective-permute-start.4 = (f32[24,512]{1,0:T(8,128)S(1)}, f32[24,512]{1,0:T(8,128)S(1)}, u32[]{:S(2)}, u32[]{:S(2)}) collective-permute-start(f32[24,512]{1,0:T(8,128)S(1)} %pad_maximum_fusion), channel_id=1, source_target_pairs={{0,1},{1,0},{2,3},{3,2},{4,5},{5,4},{6,7},{7,6},{8,9},{9,8},{10,11... | collective-permute-start | bytes 147464 | tf_op jit(solution)/shard_map/ppermute | solution.py:52
  17.8 1.7 %collective-permute-done.4.g3_ref.beyond_ref = f32[24,512]{1,0:T(8,128)S(1)} collective-permute-done((f32[24,512]{1,0:T(8,128)S(1)}, f32[24,512]{1,0:T(8,128)S(1)}, u32[]{:S(2)}, u32[]{:S(2)}) %collective-permute-start.4) | collective-permute-done | bytes 49184 | tf_op jit(solution)/shard_map/ppermute | solution.py:52
  19.5 7.5 %shard_map.114 = (f32[16,1152]{1,0:T(8,128)S(1)}, f32[24,1536]{1,0:T(8,128)S(1)}, f32[8,1536]{1,0:T(8,128)S(1)}, f32[144,256]{1,0:T(8,128)S(1)}, f32[168,256]{1,...) custom-call(s32[1,1536]{1,0:T(1,128)S(1)} %get-tuple-element.34.idx_, ...), custom_call_target="tpu_custom_call" | custom-call | tf_op jit(solution)/shard_map/pallas_call | solution.py:1230
  27.0 1.6 %collective-permute-start.5 = (f32[16,1152]{1,0:T(8,128)S(1)}, f32[16,1152]{1,0:T(8,128)S(1)}, u32[]{:S(2)}, u32[]{:S(2)}) collective-permute-start(f32[16,1152]{1,0:T(8,128)S(1)} %get-tuple-element.40.mine), channel_id=1, source_target_pairs={{0,1},{1,0},{2,3},{3,2},{4,5},{5,4},{6,7},{7,6},{8,9},{9,8},{10,11... | collective-permute-start | bytes 221192 | tf_op jit(solution)/shard_map/ppermute | solution.py:1377
  28.6 2.8 %collective-permute-done.5.other = f32[16,1152]{1,0:T(8,128)S(1)} collective-permute-done((f32[16,1152]{1,0:T(8,128)S(1)}, f32[16,1152]{1,0:T(8,128)S(1)}, u32[]{:S(2)}, u32[]{:S(2)}) %collective-permute-start.5) | collective-permute-done | bytes 73760 | tf_op jit(solution)/shard_map/ppermute | solution.py:1377
  31.6 1.4 %collective-permute-start.7 = (f32[16,512]{1,0:T(8,128)S(1)}, f32[16,512]{1,0:T(8,128)S(1)}, u32[]{:S(2)}, u32[]{:S(2)}) collective-permute-start(f32[16,512]{1,0:T(8,128)S(1)} %pad_maximum_fusion.1), channel_id=1, source_target_pairs={{0,2},{2,0},{4,6},{6,4},{1,3},{3,1},{5,7},{7,5},{8,10},{10,8},{12,... | collective-permute-start | bytes 98312 | tf_op jit(solution)/shard_map/ppermute | solution.py:32
  32.9 2.1 %collective-permute-done.6 = f32[16,512]{1,0:T(8,128)S(1)} collective-permute-done((f32[16,512]{1,0:T(8,128)S(1)}, f32[16,512]{1,0:T(8,128)S(1)}, u32[]{:S(2)}, u32[]{:S(2)}) %collective-permute-start.6) | collective-permute-done | bytes 32800 | tf_op jit(solution)/shard_map/ppermute | solution.py:32
  35.4 1.8 %collective-permute-start.10 = (f32[16,512]{1,0:T(8,128)S(1)}, f32[16,512]{1,0:T(8,128)S(1)}, u32[]{:S(2)}, u32[]{:S(2)}) collective-permute-start(f32[16,512]{1,0:T(8,128)S(1)} %get-tuple-element.43.p0_ref), channel_id=1, source_target_pairs={{0,24},{8,16},{16,8},{24,0},{1,25},{9,17},{17,9},{25,1},{2,26},{10... | collective-permute-start | bytes 98312 | tf_op jit(solution)/shard_map/ppermute | solution.py:32
  37.2 2.6 %collective-permute-start.9 = (f32[16,512]{1,0:T(8,128)S(1)}, f32[16,512]{1,0:T(8,128)S(1)}, u32[]{:S(2)}, u32[]{:S(2)}) collective-permute-start(f32[16,512]{1,0:T(8,128)S(1)} %get-tuple-element.43.p0_ref), channel_id=1, source_target_pairs={{0,16},{8,24},{16,0},{24,8},{1,17},{9,25},{17,1},{25,9},{2,18},{10... | collective-permute-start | bytes 98312 | tf_op jit(solution)/shard_map/ppermute | solution.py:32
  39.9 1.3 %collective-permute-done.10.p3_ref = f32[16,512]{1,0:T(8,128)S(1)} collective-permute-done((f32[16,512]{1,0:T(8,128)S(1)}, f32[16,512]{1,0:T(8,128)S(1)}, u32[]{:S(2)}, u32[]{:S(2)}) %collective-permute-start.10) | collective-permute-done | bytes 32800 | tf_op jit(solution)/shard_map/ppermute | solution.py:32
  41.5 0.8 %collective-permute-done.9.p2_ref = f32[16,512]{1,0:T(8,128)S(1)} collective-permute-done((f32[16,512]{1,0:T(8,128)S(1)}, f32[16,512]{1,0:T(8,128)S(1)}, u32[]{:S(2)}, u32[]{:S(2)}) %collective-permute-start.9) | collective-permute-done | bytes 32800 | tf_op jit(solution)/shard_map/ppermute | solution.py:32
  42.8 1.0 %collective-permute-start.12 = (f32[16,512]{1,0:T(8,128)S(1)}, f32[16,512]{1,0:T(8,128)S(1)}, u32[]{:S(2)}, u32[]{:S(2)}) collective-permute-start(f32[16,512]{1,0:T(8,128)S(1)} %get-tuple-element.45.refs_0_), channel_id=1, source_target_pairs={{0,2},{2,0},{4,6},{6,4},{1,3},{3,1},{5,7},{7,5},{8,10},{10,8},{12,... | collective-permute-start | bytes 98312 | tf_op jit(solution)/shard_map/ppermute | solution.py:32
  43.8 2.4 %collective-permute-done.11 = f32[16,512]{1,0:T(8,128)S(1)} collective-permute-done((f32[16,512]{1,0:T(8,128)S(1)}, f32[16,512]{1,0:T(8,128)S(1)}, u32[]{:S(2)}, u32[]{:S(2)}) %collective-permute-start.11) | collective-permute-done | bytes 32800 | tf_op jit(solution)/shard_map/ppermute | solution.py:32
  46.2 4.7 %shard_map.117 = (f32[16,1152]{1,0:T(8,128)S(1)}, f32[8,128]{1,0:T(8,128)S(1)}) custom-call(s32[1,1536]{1,0:T(1,128)S(1)} %get-tuple-element.34.idx_ref, f32[24,256]{1,0:T(8,128)S(1)} %get-tuple-element.44.own_ref.first_ref, f32[16,512]{1,0:T(8,128)S(1)} %get-tuple-element.45.refs_0_, f32[16,512]{1,0:T(8,128)S(1)} %xor_select_fusion.refs_1_, ...), custom_call_target="tpu_custom_call" | custom-call | tf_op jit(solution)/shard_map/pallas_call | solution.py:1230
  51.0 1.6 %collective-permute-start.13 = (f32[16,1280]{1,0:T(8,128)S(1)}, f32[16,1280]{1,0:T(8,128)S(1)}, u32[]{:S(2)}, u32[]{:S(2)}) collective-permute-start(f32[16,1280]{1,0:T(8,128)S(1)} %select_maximum_fusion.mine), channel_id=1, source_target_pairs={{0,1},{1,0},{2,3},{3,2},{4,5},{5,4},{6,7},{7,6},{8,9},{9,8},{10,11... | collective-permute-start | bytes 245768 | tf_op jit(solution)/shard_map/ppermute | solution.py:1377
  52.6 2.9 %collective-permute-done.13.other = f32[16,1280]{1,0:T(8,128)S(1)} collective-permute-done((f32[16,1280]{1,0:T(8,128)S(1)}, f32[16,1280]{1,0:T(8,128)S(1)}, u32[]{:S(2)}, u32[]{:S(2)}) %collective-permute-start.13) | collective-permute-done | bytes 81952 | tf_op jit(solution)/shard_map/ppermute | solution.py:1377
  55.6 1.0 %collective-permute-start.15 = (f32[16,512]{1,0:T(8,128)S(1)}, f32[16,512]{1,0:T(8,128)S(1)}, u32[]{:S(2)}, u32[]{:S(2)}) collective-permute-start(f32[16,512]{1,0:T(8,128)S(1)} %pad_maximum_fusion.2), channel_id=1, source_target_pairs={{0,2},{2,0},{4,6},{6,4},{1,3},{3,1},{5,7},{7,5},{8,10},{10,8},{12,... | collective-permute-start | bytes 98312 | tf_op jit(solution)/shard_map/ppermute | solution.py:32
  56.6 2.3 %collective-permute-done.14 = f32[16,512]{1,0:T(8,128)S(1)} collective-permute-done((f32[16,512]{1,0:T(8,128)S(1)}, f32[16,512]{1,0:T(8,128)S(1)}, u32[]{:S(2)}, u32[]{:S(2)}) %collective-permute-start.14) | collective-permute-done | bytes 32800 | tf_op jit(solution)/shard_map/ppermute | solution.py:32
  59.4 2.0 %collective-permute-start.16 = (f32[16,640]{1,0:T(8,128)S(1)}, f32[16,640]{1,0:T(8,128)S(1)}, u32[]{:S(2)}, u32[]{:S(2)}) collective-permute-start(f32[16,640]{1,0:T(8,128)S(1)} %get-tuple-element.58.p0_ref), channel_id=1, source_target_pairs={{0,24},{8,16},{16,8},{24,0},{1,25},{9,17},{17,9},{25,1},{2,26},{10... | collective-permute-start | bytes 122888 | tf_op jit(solution)/shard_map/ppermute | solution.py:32
  61.4 1.2 %collective-permute-start.17 = (f32[16,640]{1,0:T(8,128)S(1)}, f32[16,640]{1,0:T(8,128)S(1)}, u32[]{:S(2)}, u32[]{:S(2)}) collective-permute-start(f32[16,640]{1,0:T(8,128)S(1)} %get-tuple-element.58.p0_ref), channel_id=1, source_target_pairs={{0,16},{8,24},{16,0},{24,8},{1,17},{9,25},{17,1},{25,9},{2,18},{10... | collective-permute-start | bytes 122888 | tf_op jit(solution)/shard_map/ppermute | solution.py:32
  62.7 1.1 %collective-permute-start.18 = (f32[16,640]{1,0:T(8,128)S(1)}, f32[16,640]{1,0:T(8,128)S(1)}, u32[]{:S(2)}, u32[]{:S(2)}) collective-permute-start(f32[16,640]{1,0:T(8,128)S(1)} %get-tuple-element.58.p0_ref), channel_id=1, source_target_pairs={{0,8},{8,0},{16,24},{24,16},{1,9},{9,1},{17,25},{25,17},{2,10},{10... | collective-permute-start | bytes 122888 | tf_op jit(solution)/shard_map/ppermute | solution.py:32
  63.8 1.7 %collective-permute-done.16.p3_ref = f32[16,640]{1,0:T(8,128)S(1)} collective-permute-done((f32[16,640]{1,0:T(8,128)S(1)}, f32[16,640]{1,0:T(8,128)S(1)}, u32[]{:S(2)}, u32[]{:S(2)}) %collective-permute-start.16) | collective-permute-done | bytes 40992 | tf_op jit(solution)/shard_map/ppermute | solution.py:32
  65.5 1.3 %collective-permute-done.17.p2_ref = f32[16,640]{1,0:T(8,128)S(1)} collective-permute-done((f32[16,640]{1,0:T(8,128)S(1)}, f32[16,640]{1,0:T(8,128)S(1)}, u32[]{:S(2)}, u32[]{:S(2)}) %collective-permute-start.17) | collective-permute-done | bytes 40992 | tf_op jit(solution)/shard_map/ppermute | solution.py:32
  67.3 1.2 %collective-permute-done.19 = f32[8,128]{1,0:T(8,128)S(1)} collective-permute-done((f32[8,128]{1,0:T(8,128)S(1)}, f32[8,128]{1,0:T(8,128)S(1)}, u32[]{:S(2)}, u32[]{:S(2)}) %collective-permute-start.19) | collective-permute-done | bytes 4128 | tf_op jit(solution)/shard_map/ppermute | solution.py:91
  68.5 1.2 %collective-permute-start.20 = (f32[8,128]{1,0:T(8,128)S(1)}, f32[8,128]{1,0:T(8,128)S(1)}, u32[]{:S(2)}, u32[]{:S(2)}) collective-permute-start(f32[8,128]{1,0:T(8,128)S(1)} %add.114), channel_id=1, source_target_pairs={{0,4},{2,6},{4,0},{6,2},{1,5},{3,7},{5,1},{7,3},{8,12},{10,14},{12... | collective-permute-start | bytes 12296 | tf_op jit(solution)/shard_map/ppermute | solution.py:91
  69.6 2.4 %collective-permute-done.20 = f32[8,128]{1,0:T(8,128)S(1)} collective-permute-done((f32[8,128]{1,0:T(8,128)S(1)}, f32[8,128]{1,0:T(8,128)S(1)}, u32[]{:S(2)}, u32[]{:S(2)}) %collective-permute-start.20) | collective-permute-done | bytes 4128 | tf_op jit(solution)/shard_map/ppermute | solution.py:91
  72.1 1.1 %shard_map.120 = (f32[1,1,1,3,4,256]{5,4,3,2,1,0:T(4,128)}, f32[2,4,4]{2,1,0:T(4,128)}, f32[2,4,4]{2,1,0:T(4,128)}) custom-call(f32[24,256]{1,0:T(8,128)S(1)} %concatenate.23.own_ref.start_ref, f32[24,256]{1,0:T(8,128)S(1)} %get-tuple-element.44.own_ref.first_ref, f32[24,256]{1,0:T(8,128)S(1)} %get-tuple-element.60.second_ref, f32[8,128]{1,0:T(8,128)S(1)} %add.115.refs_0_), custom_call_target="tpu_custom_call" | custom-call | tf_op jit(solution)/shard_map/pallas_call | solution.py:1230
  (68 shorter events, 5.8 us)
Async XLA Ops:
  0.6 0.7 %copy-start.6 = (f32[1,1,1,3,256]{4,2,3,1,0:T(1,128)S(1)}, f32[1,1,1,3,256]{4,2,3,1,0:T(1,128)}, u32[]{:S(2)}) copy-start(f32[1,1,1,3,256]{4,2,3,1,0:T(1,128)} %param.9) | copy-start | bytes 9220
  1.4 0.7 copy-start.5
  2.1 0.7 copy-start.7
  2.9 6.7 %collective-permute-start = (f32[24,128]{1,0:T(8,128)S(1)}, f32[24,128]{1,0:T(8,128)S(1)}, u32[]{:S(2)}, u32[]{:S(2)}) collective-permute-start(f32[24,128]{1,0:T(8,128)S(1)} %get-tuple-element.35), channel_id=1, source_target_pairs={{0,24},{8,16},{16,8},{24,0},{1,25},{9,17},{17,9},{25,1},{2,26},{10... | collective-permute-start | bytes 36872 | tf_op jit(solution)/shard_map/ppermute | solution.py:32
  8.0 3.7 %collective-permute-start.1 = (f32[24,128]{1,0:T(8,128)S(1)}, f32[24,128]{1,0:T(8,128)S(1)}, u32[]{:S(2)}, u32[]{:S(2)}) collective-permute-start(f32[24,128]{1,0:T(8,128)S(1)} %get-tuple-element.35), channel_id=1, source_target_pairs={{0,8},{8,0},{16,24},{24,16},{1,9},{9,1},{17,25},{25,17},{2,10},{10... | collective-permute-start | bytes 36872 | tf_op jit(solution)/shard_map/ppermute | solution.py:32
  11.7 3.5 %collective-permute-start.2 = (f32[24,256]{1,0:T(8,128)S(1)}, f32[24,256]{1,0:T(8,128)S(1)}, u32[]{:S(2)}, u32[]{:S(2)}) collective-permute-start(f32[24,256]{1,0:T(8,128)S(1)} %pad_maximum_fusion.3.g1_ref), channel_id=1, source_target_pairs={{0,6},{2,4},{4,2},{6,0},{1,7},{3,5},{5,3},{7,1},{8,14},{10,12},{12... | collective-permute-start | bytes 73736 | tf_op jit(solution)/shard_map/ppermute | solution.py:32
  11.8 3.5 %collective-permute-start.3 = (f32[24,256]{1,0:T(8,128)S(1)}, f32[24,256]{1,0:T(8,128)S(1)}, u32[]{:S(2)}, u32[]{:S(2)}) collective-permute-start(f32[24,256]{1,0:T(8,128)S(1)} %pad_maximum_fusion.3.g1_ref), channel_id=1, source_target_pairs={{0,2},{2,0},{4,6},{6,4},{1,3},{3,1},{5,7},{7,5},{8,10},{10,8},{12,... | collective-permute-start | bytes 73736 | tf_op jit(solution)/shard_map/ppermute | solution.py:32
  15.3 1.6 %copy-start = (f32[128,64]{0,1:T(8,128)S(1)}, f32[128,64]{0,1:T(8,128)}, u32[]{:S(2)}) copy-start(f32[128,64]{0,1:T(8,128)} %param.16) | copy-start | bytes 98308
  15.3 1.6 %copy-start.1 = (s32[1,1,1,6,256]{4,2,3,1,0:T(1,128)S(1)}, s32[1,1,1,6,256]{4,2,3,1,0:T(1,128)}, u32[]{:S(2)}) copy-start(s32[1,1,1,6,256]{4,2,3,1,0:T(1,128)} %param.12) | copy-start | bytes 18436
  15.3 1.6 %copy-start.2 = (f32[8,128]{1,0:T(8,128)S(1)}, f32[8,128]{1,0:T(8,128)}, u32[]{:S(2)}) copy-start(f32[8,128]{1,0:T(8,128)} %rin_ref.1) | copy-start | bytes 12292
  15.3 4.2 %collective-permute-start.4 = (f32[24,512]{1,0:T(8,128)S(1)}, f32[24,512]{1,0:T(8,128)S(1)}, u32[]{:S(2)}, u32[]{:S(2)}) collective-permute-start(f32[24,512]{1,0:T(8,128)S(1)} %pad_maximum_fusion), channel_id=1, source_target_pairs={{0,1},{1,0},{2,3},{3,2},{4,5},{5,4},{6,7},{7,6},{8,9},{9,8},{10,11... | collective-permute-start | bytes 147464 | tf_op jit(solution)/shard_map/ppermute | solution.py:52
  16.9 0.7 copy-start.3
  16.9 0.7 copy-start.4
  27.0 4.4 %collective-permute-start.5 = (f32[16,1152]{1,0:T(8,128)S(1)}, f32[16,1152]{1,0:T(8,128)S(1)}, u32[]{:S(2)}, u32[]{:S(2)}) collective-permute-start(f32[16,1152]{1,0:T(8,128)S(1)} %get-tuple-element.40.mine), channel_id=1, source_target_pairs={{0,1},{1,0},{2,3},{3,2},{4,5},{5,4},{6,7},{7,6},{8,9},{9,8},{10,11... | collective-permute-start | bytes 221192 | tf_op jit(solution)/shard_map/ppermute | solution.py:1377
  31.5 3.6 %collective-permute-start.6 = (f32[16,512]{1,0:T(8,128)S(1)}, f32[16,512]{1,0:T(8,128)S(1)}, u32[]{:S(2)}, u32[]{:S(2)}) collective-permute-start(f32[16,512]{1,0:T(8,128)S(1)} %pad_maximum_fusion.1), channel_id=1, source_target_pairs={{0,6},{2,4},{4,2},{6,0},{1,7},{3,5},{5,3},{7,1},{8,14},{10,12},{12... | collective-permute-start | bytes 98312 | tf_op jit(solution)/shard_map/ppermute | solution.py:32
  31.6 3.5 %collective-permute-start.7 = (f32[16,512]{1,0:T(8,128)S(1)}, f32[16,512]{1,0:T(8,128)S(1)}, u32[]{:S(2)}, u32[]{:S(2)}) collective-permute-start(f32[16,512]{1,0:T(8,128)S(1)} %pad_maximum_fusion.1), channel_id=1, source_target_pairs={{0,2},{2,0},{4,6},{6,4},{1,3},{3,1},{5,7},{7,5},{8,10},{10,8},{12,... | collective-permute-start | bytes 98312 | tf_op jit(solution)/shard_map/ppermute | solution.py:32
  35.4 5.8 %collective-permute-start.10 = (f32[16,512]{1,0:T(8,128)S(1)}, f32[16,512]{1,0:T(8,128)S(1)}, u32[]{:S(2)}, u32[]{:S(2)}) collective-permute-start(f32[16,512]{1,0:T(8,128)S(1)} %get-tuple-element.43.p0_ref), channel_id=1, source_target_pairs={{0,24},{8,16},{16,8},{24,0},{1,25},{9,17},{17,9},{25,1},{2,26},{10... | collective-permute-start | bytes 98312 | tf_op jit(solution)/shard_map/ppermute | solution.py:32
  37.2 4.3 %collective-permute-start.8 = (f32[16,512]{1,0:T(8,128)S(1)}, f32[16,512]{1,0:T(8,128)S(1)}, u32[]{:S(2)}, u32[]{:S(2)}) collective-permute-start(f32[16,512]{1,0:T(8,128)S(1)} %get-tuple-element.43.p0_ref), channel_id=1, source_target_pairs={{0,8},{8,0},{16,24},{24,16},{1,9},{9,1},{17,25},{25,17},{2,10},{10... | collective-permute-start | bytes 98312 | tf_op jit(solution)/shard_map/ppermute | solution.py:32
  37.2 5.0 %collective-permute-start.9 = (f32[16,512]{1,0:T(8,128)S(1)}, f32[16,512]{1,0:T(8,128)S(1)}, u32[]{:S(2)}, u32[]{:S(2)}) collective-permute-start(f32[16,512]{1,0:T(8,128)S(1)} %get-tuple-element.43.p0_ref), channel_id=1, source_target_pairs={{0,16},{8,24},{16,0},{24,8},{1,17},{9,25},{17,1},{25,9},{2,18},{10... | collective-permute-start | bytes 98312 | tf_op jit(solution)/shard_map/ppermute | solution.py:32
  42.8 3.4 %collective-permute-start.11 = (f32[16,512]{1,0:T(8,128)S(1)}, f32[16,512]{1,0:T(8,128)S(1)}, u32[]{:S(2)}, u32[]{:S(2)}) collective-permute-start(f32[16,512]{1,0:T(8,128)S(1)} %get-tuple-element.45.refs_0_), channel_id=1, source_target_pairs={{0,6},{2,4},{4,2},{6,0},{1,7},{3,5},{5,3},{7,1},{8,14},{10,12},{12... | collective-permute-start | bytes 98312 | tf_op jit(solution)/shard_map/ppermute | solution.py:32
  42.8 3.4 %collective-permute-start.12 = (f32[16,512]{1,0:T(8,128)S(1)}, f32[16,512]{1,0:T(8,128)S(1)}, u32[]{:S(2)}, u32[]{:S(2)}) collective-permute-start(f32[16,512]{1,0:T(8,128)S(1)} %get-tuple-element.45.refs_0_), channel_id=1, source_target_pairs={{0,2},{2,0},{4,6},{6,4},{1,3},{3,1},{5,7},{7,5},{8,10},{10,8},{12,... | collective-permute-start | bytes 98312 | tf_op jit(solution)/shard_map/ppermute | solution.py:32
  51.0 4.5 %collective-permute-start.13 = (f32[16,1280]{1,0:T(8,128)S(1)}, f32[16,1280]{1,0:T(8,128)S(1)}, u32[]{:S(2)}, u32[]{:S(2)}) collective-permute-start(f32[16,1280]{1,0:T(8,128)S(1)} %select_maximum_fusion.mine), channel_id=1, source_target_pairs={{0,1},{1,0},{2,3},{3,2},{4,5},{5,4},{6,7},{7,6},{8,9},{9,8},{10,11... | collective-permute-start | bytes 245768 | tf_op jit(solution)/shard_map/ppermute | solution.py:1377
  55.5 3.4 %collective-permute-start.14 = (f32[16,512]{1,0:T(8,128)S(1)}, f32[16,512]{1,0:T(8,128)S(1)}, u32[]{:S(2)}, u32[]{:S(2)}) collective-permute-start(f32[16,512]{1,0:T(8,128)S(1)} %pad_maximum_fusion.2), channel_id=1, source_target_pairs={{0,6},{2,4},{4,2},{6,0},{1,7},{3,5},{5,3},{7,1},{8,14},{10,12},{12... | collective-permute-start | bytes 98312 | tf_op jit(solution)/shard_map/ppermute | solution.py:32
  55.6 3.3 %collective-permute-start.15 = (f32[16,512]{1,0:T(8,128)S(1)}, f32[16,512]{1,0:T(8,128)S(1)}, u32[]{:S(2)}, u32[]{:S(2)}) collective-permute-start(f32[16,512]{1,0:T(8,128)S(1)} %pad_maximum_fusion.2), channel_id=1, source_target_pairs={{0,2},{2,0},{4,6},{6,4},{1,3},{3,1},{5,7},{7,5},{8,10},{10,8},{12,... | collective-permute-start | bytes 98312 | tf_op jit(solution)/shard_map/ppermute | solution.py:32
  59.4 6.1 %collective-permute-start.16 = (f32[16,640]{1,0:T(8,128)S(1)}, f32[16,640]{1,0:T(8,128)S(1)}, u32[]{:S(2)}, u32[]{:S(2)}) collective-permute-start(f32[16,640]{1,0:T(8,128)S(1)} %get-tuple-element.58.p0_ref), channel_id=1, source_target_pairs={{0,24},{8,16},{16,8},{24,0},{1,25},{9,17},{17,9},{25,1},{2,26},{10... | collective-permute-start | bytes 122888 | tf_op jit(solution)/shard_map/ppermute | solution.py:32
  61.4 5.3 %collective-permute-start.17 = (f32[16,640]{1,0:T(8,128)S(1)}, f32[16,640]{1,0:T(8,128)S(1)}, u32[]{:S(2)}, u32[]{:S(2)}) collective-permute-start(f32[16,640]{1,0:T(8,128)S(1)} %get-tuple-element.58.p0_ref), channel_id=1, source_target_pairs={{0,16},{8,24},{16,0},{24,8},{1,17},{9,25},{17,1},{25,9},{2,18},{10... | collective-permute-start | bytes 122888 | tf_op jit(solution)/shard_map/ppermute | solution.py:32
  62.7 4.1 %collective-permute-start.18 = (f32[16,640]{1,0:T(8,128)S(1)}, f32[16,640]{1,0:T(8,128)S(1)}, u32[]{:S(2)}, u32[]{:S(2)}) collective-permute-start(f32[16,640]{1,0:T(8,128)S(1)} %get-tuple-element.58.p0_ref), channel_id=1, source_target_pairs={{0,8},{8,0},{16,24},{24,16},{1,9},{9,1},{17,25},{25,17},{2,10},{10... | collective-permute-start | bytes 122888 | tf_op jit(solution)/shard_map/ppermute | solution.py:32
  67.3 1.2 %collective-permute-start.19 = (f32[8,128]{1,0:T(8,128)S(1)}, f32[8,128]{1,0:T(8,128)S(1)}, u32[]{:S(2)}, u32[]{:S(2)}) collective-permute-start(f32[8,128]{1,0:T(8,128)S(1)} %get-tuple-element.61), channel_id=1, source_target_pairs={{0,2},{2,0},{4,6},{6,4},{1,3},{3,1},{5,7},{7,5},{8,10},{10,8},{12,... | collective-permute-start | bytes 12296 | tf_op jit(solution)/shard_map/ppermute | solution.py:91
  68.5 3.6 %collective-permute-start.20 = (f32[8,128]{1,0:T(8,128)S(1)}, f32[8,128]{1,0:T(8,128)S(1)}, u32[]{:S(2)}, u32[]{:S(2)}) collective-permute-start(f32[8,128]{1,0:T(8,128)S(1)} %add.114), channel_id=1, source_target_pairs={{0,4},{2,6},{4,0},{6,2},{1,5},{3,7},{5,1},{7,3},{8,12},{10,14},{12... | collective-permute-start | bytes 12296 | tf_op jit(solution)/shard_map/ppermute | solution.py:91

commit v8 on v7

--- a/solution.py
+++ b/solution.py
@@ -598,7 +598,7 @@
             channel_products(f, f1, q, rp, rpp, cosine, tn, acc, lanes, fanout, vectors)
         return carry
 
-    lax.fori_loop(0, channels // GROUP, tile, 0)
+    lax.fori_loop(0, channels // GROUP, tile, 0, unroll=2)
     count = acc2.shape[0] // GROUP
     for n in range(0, count, 4):
         parts = [acc2[tile_rows(min(n + j, count - 1)), :] for j in range(4)]
@@ -648,7 +648,7 @@
             channel_products(*parts, cosine, tn, acc, lanes, fanout, vectors)
         return carry
 
-    lax.fori_loop(0, channels // GROUP, tile, 0)
+    lax.fori_loop(0, channels // GROUP, tile, 0, unroll=2)
     shifted = finish_product(
         idx_ref,
         low_ref,

time: 73.4 us -> 73.6 us (level)
  no operation moved by 1% of the time
where the time goes in v8:
time: 73.6 us; the launch traced here: 73.3 us
  waiting for transfers between devices  28.8 us (39%)
  starting transfers between devices  25 us (34%)
  Pallas kernels  15.4 us (21%)
  local copies, waits for them, and re-layouts  2.92 us (4%)
  between operations  0.81 us (1%)
    ppermute x16, starting transfers between devices, pair_exchange(): lax.ppermute(x, axis, [(i, i ^ d) for i in range(size)])  19.1 us
    ppermute x16, waiting for transfers between devices, pair_exchange(): lax.ppermute(x, axis, [(i, i ^ d) for i in range(size)])  17.7 us
    pallas_call x9, Pallas kernels, call(): pl.pallas_call(body, out_shape=[jax.ShapeDtypeStruct(shape, kind) for sha...  15.4 us
    ppermute x2, waiting for transfers between devices, exchange(): other = lax.ppermute(terms, 'gz', swap_pairs(2, 1))  5.76 us
    ppermute x2, waiting for transfers between devices, sum_over(): x = x + lax.ppermute(x, axis, [(i, i ^ step) for i in range(size)])  3.61 us
    ppermute x2, starting transfers between devices, exchange(): other = lax.ppermute(terms, 'gz', swap_pairs(2, 1))  3.15 us
    unnamed x16, local copies, waits for them, and re-layouts  1.96 us
    ppermute x1, waiting for transfers between devices, fetch_ghosts(): return lax.ppermute(x, axis, swap_pairs(2, 1))  1.69 us
  transfers between devices with their start and end apart: 21, of which 16 were waited for; matrix products, arithmetic and copies ran while one was open for 0% of the time, Pallas kernels for 0%

profile of v8, /device:TPU:0, one launch (start us, length us, event | category | flops | bytes accessed | tf_op | source)
XLA Modules:
  0.0 73.3 jit_solution(9236481748382618214)
XLA Ops:
  2.9 5.1 %collective-permute-start = (f32[24,128]{1,0:T(8,128)S(1)}, f32[24,128]{1,0:T(8,128)S(1)}, u32[]{:S(2)}, u32[]{:S(2)}) collective-permute-start(f32[24,128]{1,0:T(8,128)S(1)} %get-tuple-element.35), channel_id=1, source_target_pairs={{0,24},{8,16},{16,8},{24,0},{1,25},{9,17},{17,9},{25,1},{2,26},{10... | collective-permute-start | bytes 36872 | tf_op jit(solution)/shard_map/ppermute | solution.py:32
  8.0 1.6 %collective-permute-done = f32[24,128]{1,0:T(8,128)S(1)} collective-permute-done((f32[24,128]{1,0:T(8,128)S(1)}, f32[24,128]{1,0:T(8,128)S(1)}, u32[]{:S(2)}, u32[]{:S(2)}) %collective-permute-start) | collective-permute-done | bytes 12320 | tf_op jit(solution)/shard_map/ppermute | solution.py:32
  9.7 2.0 %collective-permute-done.1 = f32[24,128]{1,0:T(8,128)S(1)} collective-permute-done((f32[24,128]{1,0:T(8,128)S(1)}, f32[24,128]{1,0:T(8,128)S(1)}, u32[]{:S(2)}, u32[]{:S(2)}) %collective-permute-start.1) | collective-permute-done | bytes 12320 | tf_op jit(solution)/shard_map/ppermute | solution.py:32
  11.8 1.6 %collective-permute-start.3 = (f32[24,256]{1,0:T(8,128)S(1)}, f32[24,256]{1,0:T(8,128)S(1)}, u32[]{:S(2)}, u32[]{:S(2)}) collective-permute-start(f32[24,256]{1,0:T(8,128)S(1)} %pad_maximum_fusion.3.g1_ref), channel_id=1, source_target_pairs={{0,2},{2,0},{4,6},{6,4},{1,3},{3,1},{5,7},{7,5},{8,10},{10,8},{12,... | collective-permute-start | bytes 73736 | tf_op jit(solution)/shard_map/ppermute | solution.py:32
  13.4 1.9 %collective-permute-done.2 = f32[24,256]{1,0:T(8,128)S(1)} collective-permute-done((f32[24,256]{1,0:T(8,128)S(1)}, f32[24,256]{1,0:T(8,128)S(1)}, u32[]{:S(2)}, u32[]{:S(2)}) %collective-permute-start.2) | collective-permute-done | bytes 24608 | tf_op jit(solution)/shard_map/ppermute | solution.py:32
  15.3 1.6 %collective-permute-start.4 = (f32[24,512]{1,0:T(8,128)S(1)}, f32[24,512]{1,0:T(8,128)S(1)}, u32[]{:S(2)}, u32[]{:S(2)}) collective-permute-start(f32[24,512]{1,0:T(8,128)S(1)} %pad_maximum_fusion), channel_id=1, source_target_pairs={{0,1},{1,0},{2,3},{3,2},{4,5},{5,4},{6,7},{7,6},{8,9},{9,8},{10,11... | collective-permute-start | bytes 147464 | tf_op jit(solution)/shard_map/ppermute | solution.py:52
  17.8 1.7 %collective-permute-done.4.g3_ref.beyond_ref = f32[24,512]{1,0:T(8,128)S(1)} collective-permute-done((f32[24,512]{1,0:T(8,128)S(1)}, f32[24,512]{1,0:T(8,128)S(1)}, u32[]{:S(2)}, u32[]{:S(2)}) %collective-permute-start.4) | collective-permute-done | bytes 49184 | tf_op jit(solution)/shard_map/ppermute | solution.py:52
  19.5 7.8 %shard_map.114 = (f32[16,1152]{1,0:T(8,128)S(1)}, f32[24,1536]{1,0:T(8,128)S(1)}, f32[8,1536]{1,0:T(8,128)S(1)}, f32[144,256]{1,0:T(8,128)S(1)}, f32[168,256]{1,...) custom-call(s32[1,1536]{1,0:T(1,128)S(1)} %get-tuple-element.34.idx_, ...), custom_call_target="tpu_custom_call" | custom-call | tf_op jit(solution)/shard_map/pallas_call | solution.py:1230
  27.3 1.6 %collective-permute-start.5 = (f32[16,1152]{1,0:T(8,128)S(1)}, f32[16,1152]{1,0:T(8,128)S(1)}, u32[]{:S(2)}, u32[]{:S(2)}) collective-permute-start(f32[16,1152]{1,0:T(8,128)S(1)} %get-tuple-element.40.mine), channel_id=1, source_target_pairs={{0,1},{1,0},{2,3},{3,2},{4,5},{5,4},{6,7},{7,6},{8,9},{9,8},{10,11... | collective-permute-start | bytes 221192 | tf_op jit(solution)/shard_map/ppermute | solution.py:1377
  28.9 2.8 %collective-permute-done.5.other = f32[16,1152]{1,0:T(8,128)S(1)} collective-permute-done((f32[16,1152]{1,0:T(8,128)S(1)}, f32[16,1152]{1,0:T(8,128)S(1)}, u32[]{:S(2)}, u32[]{:S(2)}) %collective-permute-start.5) | collective-permute-done | bytes 73760 | tf_op jit(solution)/shard_map/ppermute | solution.py:1377
  31.8 1.4 %collective-permute-start.7 = (f32[16,512]{1,0:T(8,128)S(1)}, f32[16,512]{1,0:T(8,128)S(1)}, u32[]{:S(2)}, u32[]{:S(2)}) collective-permute-start(f32[16,512]{1,0:T(8,128)S(1)} %pad_maximum_fusion.1), channel_id=1, source_target_pairs={{0,2},{2,0},{4,6},{6,4},{1,3},{3,1},{5,7},{7,5},{8,10},{10,8},{12,... | collective-permute-start | bytes 98312 | tf_op jit(solution)/shard_map/ppermute | solution.py:32
  33.2 2.1 %collective-permute-done.6 = f32[16,512]{1,0:T(8,128)S(1)} collective-permute-done((f32[16,512]{1,0:T(8,128)S(1)}, f32[16,512]{1,0:T(8,128)S(1)}, u32[]{:S(2)}, u32[]{:S(2)}) %collective-permute-start.6) | collective-permute-done | bytes 32800 | tf_op jit(solution)/shard_map/ppermute | solution.py:32
  35.6 1.8 %collective-permute-start.10 = (f32[16,512]{1,0:T(8,128)S(1)}, f32[16,512]{1,0:T(8,128)S(1)}, u32[]{:S(2)}, u32[]{:S(2)}) collective-permute-start(f32[16,512]{1,0:T(8,128)S(1)} %get-tuple-element.43.p0_ref), channel_id=1, source_target_pairs={{0,24},{8,16},{16,8},{24,0},{1,25},{9,17},{17,9},{25,1},{2,26},{10... | collective-permute-start | bytes 98312 | tf_op jit(solution)/shard_map/ppermute | solution.py:32
  37.5 2.6 %collective-permute-start.9 = (f32[16,512]{1,0:T(8,128)S(1)}, f32[16,512]{1,0:T(8,128)S(1)}, u32[]{:S(2)}, u32[]{:S(2)}) collective-permute-start(f32[16,512]{1,0:T(8,128)S(1)} %get-tuple-element.43.p0_ref), channel_id=1, source_target_pairs={{0,16},{8,24},{16,0},{24,8},{1,17},{9,25},{17,1},{25,9},{2,18},{10... | collective-permute-start | bytes 98312 | tf_op jit(solution)/shard_map/ppermute | solution.py:32
  40.1 1.3 %collective-permute-done.10.p3_ref = f32[16,512]{1,0:T(8,128)S(1)} collective-permute-done((f32[16,512]{1,0:T(8,128)S(1)}, f32[16,512]{1,0:T(8,128)S(1)}, u32[]{:S(2)}, u32[]{:S(2)}) %collective-permute-start.10) | collective-permute-done | bytes 32800 | tf_op jit(solution)/shard_map/ppermute | solution.py:32
  41.7 0.8 %collective-permute-done.9.p2_ref = f32[16,512]{1,0:T(8,128)S(1)} collective-permute-done((f32[16,512]{1,0:T(8,128)S(1)}, f32[16,512]{1,0:T(8,128)S(1)}, u32[]{:S(2)}, u32[]{:S(2)}) %collective-permute-start.9) | collective-permute-done | bytes 32800 | tf_op jit(solution)/shard_map/ppermute | solution.py:32
  43.0 1.0 %collective-permute-start.12 = (f32[16,512]{1,0:T(8,128)S(1)}, f32[16,512]{1,0:T(8,128)S(1)}, u32[]{:S(2)}, u32[]{:S(2)}) collective-permute-start(f32[16,512]{1,0:T(8,128)S(1)} %get-tuple-element.45.refs_0_), channel_id=1, source_target_pairs={{0,2},{2,0},{4,6},{6,4},{1,3},{3,1},{5,7},{7,5},{8,10},{10,8},{12,... | collective-permute-start | bytes 98312 | tf_op jit(solution)/shard_map/ppermute | solution.py:32
  44.0 2.4 %collective-permute-done.11 = f32[16,512]{1,0:T(8,128)S(1)} collective-permute-done((f32[16,512]{1,0:T(8,128)S(1)}, f32[16,512]{1,0:T(8,128)S(1)}, u32[]{:S(2)}, u32[]{:S(2)}) %collective-permute-start.11) | collective-permute-done | bytes 32800 | tf_op jit(solution)/shard_map/ppermute | solution.py:32
  46.4 4.6 %shard_map.117 = (f32[16,1152]{1,0:T(8,128)S(1)}, f32[8,128]{1,0:T(8,128)S(1)}) custom-call(s32[1,1536]{1,0:T(1,128)S(1)} %get-tuple-element.34.idx_ref, f32[24,256]{1,0:T(8,128)S(1)} %get-tuple-element.44.own_ref.first_ref, f32[16,512]{1,0:T(8,128)S(1)} %get-tuple-element.45.refs_0_, f32[16,512]{1,0:T(8,128)S(1)} %xor_select_fusion.refs_1_, ...), custom_call_target="tpu_custom_call" | custom-call | tf_op jit(solution)/shard_map/pallas_call | solution.py:1230
  51.2 1.6 %collective-permute-start.13 = (f32[16,1280]{1,0:T(8,128)S(1)}, f32[16,1280]{1,0:T(8,128)S(1)}, u32[]{:S(2)}, u32[]{:S(2)}) collective-permute-start(f32[16,1280]{1,0:T(8,128)S(1)} %select_maximum_fusion.mine), channel_id=1, source_target_pairs={{0,1},{1,0},{2,3},{3,2},{4,5},{5,4},{6,7},{7,6},{8,9},{9,8},{10,11... | collective-permute-start | bytes 245768 | tf_op jit(solution)/shard_map/ppermute | solution.py:1377
  52.8 2.9 %collective-permute-done.13.other = f32[16,1280]{1,0:T(8,128)S(1)} collective-permute-done((f32[16,1280]{1,0:T(8,128)S(1)}, f32[16,1280]{1,0:T(8,128)S(1)}, u32[]{:S(2)}, u32[]{:S(2)}) %collective-permute-start.13) | collective-permute-done | bytes 81952 | tf_op jit(solution)/shard_map/ppermute | solution.py:1377
  55.8 1.0 %collective-permute-start.15 = (f32[16,512]{1,0:T(8,128)S(1)}, f32[16,512]{1,0:T(8,128)S(1)}, u32[]{:S(2)}, u32[]{:S(2)}) collective-permute-start(f32[16,512]{1,0:T(8,128)S(1)} %pad_maximum_fusion.2), channel_id=1, source_target_pairs={{0,2},{2,0},{4,6},{6,4},{1,3},{3,1},{5,7},{7,5},{8,10},{10,8},{12,... | collective-permute-start | bytes 98312 | tf_op jit(solution)/shard_map/ppermute | solution.py:32
  56.8 2.3 %collective-permute-done.14 = f32[16,512]{1,0:T(8,128)S(1)} collective-permute-done((f32[16,512]{1,0:T(8,128)S(1)}, f32[16,512]{1,0:T(8,128)S(1)}, u32[]{:S(2)}, u32[]{:S(2)}) %collective-permute-start.14) | collective-permute-done | bytes 32800 | tf_op jit(solution)/shard_map/ppermute | solution.py:32
  59.5 2.0 %collective-permute-start.16 = (f32[16,640]{1,0:T(8,128)S(1)}, f32[16,640]{1,0:T(8,128)S(1)}, u32[]{:S(2)}, u32[]{:S(2)}) collective-permute-start(f32[16,640]{1,0:T(8,128)S(1)} %get-tuple-element.58.p0_ref), channel_id=1, source_target_pairs={{0,24},{8,16},{16,8},{24,0},{1,25},{9,17},{17,9},{25,1},{2,26},{10... | collective-permute-start | bytes 122888 | tf_op jit(solution)/shard_map/ppermute | solution.py:32
  61.6 1.2 %collective-permute-start.17 = (f32[16,640]{1,0:T(8,128)S(1)}, f32[16,640]{1,0:T(8,128)S(1)}, u32[]{:S(2)}, u32[]{:S(2)}) collective-permute-start(f32[16,640]{1,0:T(8,128)S(1)} %get-tuple-element.58.p0_ref), channel_id=1, source_target_pairs={{0,16},{8,24},{16,0},{24,8},{1,17},{9,25},{17,1},{25,9},{2,18},{10... | collective-permute-start | bytes 122888 | tf_op jit(solution)/shard_map/ppermute | solution.py:32
  62.8 1.1 %collective-permute-start.18 = (f32[16,640]{1,0:T(8,128)S(1)}, f32[16,640]{1,0:T(8,128)S(1)}, u32[]{:S(2)}, u32[]{:S(2)}) collective-permute-start(f32[16,640]{1,0:T(8,128)S(1)} %get-tuple-element.58.p0_ref), channel_id=1, source_target_pairs={{0,8},{8,0},{16,24},{24,16},{1,9},{9,1},{17,25},{25,17},{2,10},{10... | collective-permute-start | bytes 122888 | tf_op jit(solution)/shard_map/ppermute | solution.py:32
  64.0 1.7 %collective-permute-done.16.p3_ref = f32[16,640]{1,0:T(8,128)S(1)} collective-permute-done((f32[16,640]{1,0:T(8,128)S(1)}, f32[16,640]{1,0:T(8,128)S(1)}, u32[]{:S(2)}, u32[]{:S(2)}) %collective-permute-start.16) | collective-permute-done | bytes 40992 | tf_op jit(solution)/shard_map/ppermute | solution.py:32
  65.7 1.2 %collective-permute-done.17.p2_ref = f32[16,640]{1,0:T(8,128)S(1)} collective-permute-done((f32[16,640]{1,0:T(8,128)S(1)}, f32[16,640]{1,0:T(8,128)S(1)}, u32[]{:S(2)}, u32[]{:S(2)}) %collective-permute-start.17) | collective-permute-done | bytes 40992 | tf_op jit(solution)/shard_map/ppermute | solution.py:32
  67.5 1.2 %collective-permute-done.19 = f32[8,128]{1,0:T(8,128)S(1)} collective-permute-done((f32[8,128]{1,0:T(8,128)S(1)}, f32[8,128]{1,0:T(8,128)S(1)}, u32[]{:S(2)}, u32[]{:S(2)}) %collective-permute-start.19) | collective-permute-done | bytes 4128 | tf_op jit(solution)/shard_map/ppermute | solution.py:91
  68.6 1.2 %collective-permute-start.20 = (f32[8,128]{1,0:T(8,128)S(1)}, f32[8,128]{1,0:T(8,128)S(1)}, u32[]{:S(2)}, u32[]{:S(2)}) collective-permute-start(f32[8,128]{1,0:T(8,128)S(1)} %add.114), channel_id=1, source_target_pairs={{0,4},{2,6},{4,0},{6,2},{1,5},{3,7},{5,1},{7,3},{8,12},{10,14},{12... | collective-permute-start | bytes 12296 | tf_op jit(solution)/shard_map/ppermute | solution.py:91
  69.8 2.4 %collective-permute-done.20 = f32[8,128]{1,0:T(8,128)S(1)} collective-permute-done((f32[8,128]{1,0:T(8,128)S(1)}, f32[8,128]{1,0:T(8,128)S(1)}, u32[]{:S(2)}, u32[]{:S(2)}) %collective-permute-start.20) | collective-permute-done | bytes 4128 | tf_op jit(solution)/shard_map/ppermute | solution.py:91
  72.3 1.1 %shard_map.120 = (f32[1,1,1,3,4,256]{5,4,3,2,1,0:T(4,128)}, f32[2,4,4]{2,1,0:T(4,128)}, f32[2,4,4]{2,1,0:T(4,128)}) custom-call(f32[24,256]{1,0:T(8,128)S(1)} %concatenate.23.own_ref.start_ref, f32[24,256]{1,0:T(8,128)S(1)} %get-tuple-element.44.own_ref.first_ref, f32[24,256]{1,0:T(8,128)S(1)} %get-tuple-element.60.second_ref, f32[8,128]{1,0:T(8,128)S(1)} %add.115.refs_0_), custom_call_target="tpu_custom_call" | custom-call | tf_op jit(solution)/shard_map/pallas_call | solution.py:1230
  (68 shorter events, 5.8 us)
Async XLA Ops:
  0.6 0.7 %copy-start.6 = (f32[1,1,1,3,256]{4,2,3,1,0:T(1,128)S(1)}, f32[1,1,1,3,256]{4,2,3,1,0:T(1,128)}, u32[]{:S(2)}) copy-start(f32[1,1,1,3,256]{4,2,3,1,0:T(1,128)} %param.9) | copy-start | bytes 9220
  1.4 0.7 copy-start.5
  2.1 0.7 copy-start.7
  2.9 6.7 %collective-permute-start = (f32[24,128]{1,0:T(8,128)S(1)}, f32[24,128]{1,0:T(8,128)S(1)}, u32[]{:S(2)}, u32[]{:S(2)}) collective-permute-start(f32[24,128]{1,0:T(8,128)S(1)} %get-tuple-element.35), channel_id=1, source_target_pairs={{0,24},{8,16},{16,8},{24,0},{1,25},{9,17},{17,9},{25,1},{2,26},{10... | collective-permute-start | bytes 36872 | tf_op jit(solution)/shard_map/ppermute | solution.py:32
  8.0 3.7 %collective-permute-start.1 = (f32[24,128]{1,0:T(8,128)S(1)}, f32[24,128]{1,0:T(8,128)S(1)}, u32[]{:S(2)}, u32[]{:S(2)}) collective-permute-start(f32[24,128]{1,0:T(8,128)S(1)} %get-tuple-element.35), channel_id=1, source_target_pairs={{0,8},{8,0},{16,24},{24,16},{1,9},{9,1},{17,25},{25,17},{2,10},{10... | collective-permute-start | bytes 36872 | tf_op jit(solution)/shard_map/ppermute | solution.py:32
  11.7 3.5 %collective-permute-start.2 = (f32[24,256]{1,0:T(8,128)S(1)}, f32[24,256]{1,0:T(8,128)S(1)}, u32[]{:S(2)}, u32[]{:S(2)}) collective-permute-start(f32[24,256]{1,0:T(8,128)S(1)} %pad_maximum_fusion.3.g1_ref), channel_id=1, source_target_pairs={{0,6},{2,4},{4,2},{6,0},{1,7},{3,5},{5,3},{7,1},{8,14},{10,12},{12... | collective-permute-start | bytes 73736 | tf_op jit(solution)/shard_map/ppermute | solution.py:32
  11.8 3.5 %collective-permute-start.3 = (f32[24,256]{1,0:T(8,128)S(1)}, f32[24,256]{1,0:T(8,128)S(1)}, u32[]{:S(2)}, u32[]{:S(2)}) collective-permute-start(f32[24,256]{1,0:T(8,128)S(1)} %pad_maximum_fusion.3.g1_ref), channel_id=1, source_target_pairs={{0,2},{2,0},{4,6},{6,4},{1,3},{3,1},{5,7},{7,5},{8,10},{10,8},{12,... | collective-permute-start | bytes 73736 | tf_op jit(solution)/shard_map/ppermute | solution.py:32
  15.3 1.6 %copy-start = (f32[128,64]{0,1:T(8,128)S(1)}, f32[128,64]{0,1:T(8,128)}, u32[]{:S(2)}) copy-start(f32[128,64]{0,1:T(8,128)} %param.16) | copy-start | bytes 98308
  15.3 1.6 %copy-start.1 = (s32[1,1,1,6,256]{4,2,3,1,0:T(1,128)S(1)}, s32[1,1,1,6,256]{4,2,3,1,0:T(1,128)}, u32[]{:S(2)}) copy-start(s32[1,1,1,6,256]{4,2,3,1,0:T(1,128)} %param.12) | copy-start | bytes 18436
  15.3 1.6 %copy-start.2 = (f32[8,128]{1,0:T(8,128)S(1)}, f32[8,128]{1,0:T(8,128)}, u32[]{:S(2)}) copy-start(f32[8,128]{1,0:T(8,128)} %rin_ref.1) | copy-start | bytes 12292
  15.3 4.2 %collective-permute-start.4 = (f32[24,512]{1,0:T(8,128)S(1)}, f32[24,512]{1,0:T(8,128)S(1)}, u32[]{:S(2)}, u32[]{:S(2)}) collective-permute-start(f32[24,512]{1,0:T(8,128)S(1)} %pad_maximum_fusion), channel_id=1, source_target_pairs={{0,1},{1,0},{2,3},{3,2},{4,5},{5,4},{6,7},{7,6},{8,9},{9,8},{10,11... | collective-permute-start | bytes 147464 | tf_op jit(solution)/shard_map/ppermute | solution.py:52
  16.9 0.7 copy-start.3
  16.9 0.7 copy-start.4
  27.3 4.4 %collective-permute-start.5 = (f32[16,1152]{1,0:T(8,128)S(1)}, f32[16,1152]{1,0:T(8,128)S(1)}, u32[]{:S(2)}, u32[]{:S(2)}) collective-permute-start(f32[16,1152]{1,0:T(8,128)S(1)} %get-tuple-element.40.mine), channel_id=1, source_target_pairs={{0,1},{1,0},{2,3},{3,2},{4,5},{5,4},{6,7},{7,6},{8,9},{9,8},{10,11... | collective-permute-start | bytes 221192 | tf_op jit(solution)/shard_map/ppermute | solution.py:1377
  31.7 3.6 %collective-permute-start.6 = (f32[16,512]{1,0:T(8,128)S(1)}, f32[16,512]{1,0:T(8,128)S(1)}, u32[]{:S(2)}, u32[]{:S(2)}) collective-permute-start(f32[16,512]{1,0:T(8,128)S(1)} %pad_maximum_fusion.1), channel_id=1, source_target_pairs={{0,6},{2,4},{4,2},{6,0},{1,7},{3,5},{5,3},{7,1},{8,14},{10,12},{12... | collective-permute-start | bytes 98312 | tf_op jit(solution)/shard_map/ppermute | solution.py:32
  31.8 3.5 %collective-permute-start.7 = (f32[16,512]{1,0:T(8,128)S(1)}, f32[16,512]{1,0:T(8,128)S(1)}, u32[]{:S(2)}, u32[]{:S(2)}) collective-permute-start(f32[16,512]{1,0:T(8,128)S(1)} %pad_maximum_fusion.1), channel_id=1, source_target_pairs={{0,2},{2,0},{4,6},{6,4},{1,3},{3,1},{5,7},{7,5},{8,10},{10,8},{12,... | collective-permute-start | bytes 98312 | tf_op jit(solution)/shard_map/ppermute | solution.py:32
  35.6 5.8 %collective-permute-start.10 = (f32[16,512]{1,0:T(8,128)S(1)}, f32[16,512]{1,0:T(8,128)S(1)}, u32[]{:S(2)}, u32[]{:S(2)}) collective-permute-start(f32[16,512]{1,0:T(8,128)S(1)} %get-tuple-element.43.p0_ref), channel_id=1, source_target_pairs={{0,24},{8,16},{16,8},{24,0},{1,25},{9,17},{17,9},{25,1},{2,26},{10... | collective-permute-start | bytes 98312 | tf_op jit(solution)/shard_map/ppermute | solution.py:32
  37.5 4.3 %collective-permute-start.8 = (f32[16,512]{1,0:T(8,128)S(1)}, f32[16,512]{1,0:T(8,128)S(1)}, u32[]{:S(2)}, u32[]{:S(2)}) collective-permute-start(f32[16,512]{1,0:T(8,128)S(1)} %get-tuple-element.43.p0_ref), channel_id=1, source_target_pairs={{0,8},{8,0},{16,24},{24,16},{1,9},{9,1},{17,25},{25,17},{2,10},{10... | collective-permute-start | bytes 98312 | tf_op jit(solution)/shard_map/ppermute | solution.py:32
  37.5 5.0 %collective-permute-start.9 = (f32[16,512]{1,0:T(8,128)S(1)}, f32[16,512]{1,0:T(8,128)S(1)}, u32[]{:S(2)}, u32[]{:S(2)}) collective-permute-start(f32[16,512]{1,0:T(8,128)S(1)} %get-tuple-element.43.p0_ref), channel_id=1, source_target_pairs={{0,16},{8,24},{16,0},{24,8},{1,17},{9,25},{17,1},{25,9},{2,18},{10... | collective-permute-start | bytes 98312 | tf_op jit(solution)/shard_map/ppermute | solution.py:32
  43.0 3.4 %collective-permute-start.11 = (f32[16,512]{1,0:T(8,128)S(1)}, f32[16,512]{1,0:T(8,128)S(1)}, u32[]{:S(2)}, u32[]{:S(2)}) collective-permute-start(f32[16,512]{1,0:T(8,128)S(1)} %get-tuple-element.45.refs_0_), channel_id=1, source_target_pairs={{0,6},{2,4},{4,2},{6,0},{1,7},{3,5},{5,3},{7,1},{8,14},{10,12},{12... | collective-permute-start | bytes 98312 | tf_op jit(solution)/shard_map/ppermute | solution.py:32
  43.0 3.4 %collective-permute-start.12 = (f32[16,512]{1,0:T(8,128)S(1)}, f32[16,512]{1,0:T(8,128)S(1)}, u32[]{:S(2)}, u32[]{:S(2)}) collective-permute-start(f32[16,512]{1,0:T(8,128)S(1)} %get-tuple-element.45.refs_0_), channel_id=1, source_target_pairs={{0,2},{2,0},{4,6},{6,4},{1,3},{3,1},{5,7},{7,5},{8,10},{10,8},{12,... | collective-permute-start | bytes 98312 | tf_op jit(solution)/shard_map/ppermute | solution.py:32
  51.2 4.5 %collective-permute-start.13 = (f32[16,1280]{1,0:T(8,128)S(1)}, f32[16,1280]{1,0:T(8,128)S(1)}, u32[]{:S(2)}, u32[]{:S(2)}) collective-permute-start(f32[16,1280]{1,0:T(8,128)S(1)} %select_maximum_fusion.mine), channel_id=1, source_target_pairs={{0,1},{1,0},{2,3},{3,2},{4,5},{5,4},{6,7},{7,6},{8,9},{9,8},{10,11... | collective-permute-start | bytes 245768 | tf_op jit(solution)/shard_map/ppermute | solution.py:1377
  55.7 3.4 %collective-permute-start.14 = (f32[16,512]{1,0:T(8,128)S(1)}, f32[16,512]{1,0:T(8,128)S(1)}, u32[]{:S(2)}, u32[]{:S(2)}) collective-permute-start(f32[16,512]{1,0:T(8,128)S(1)} %pad_maximum_fusion.2), channel_id=1, source_target_pairs={{0,6},{2,4},{4,2},{6,0},{1,7},{3,5},{5,3},{7,1},{8,14},{10,12},{12... | collective-permute-start | bytes 98312 | tf_op jit(solution)/shard_map/ppermute | solution.py:32
  55.8 3.3 %collective-permute-start.15 = (f32[16,512]{1,0:T(8,128)S(1)}, f32[16,512]{1,0:T(8,128)S(1)}, u32[]{:S(2)}, u32[]{:S(2)}) collective-permute-start(f32[16,512]{1,0:T(8,128)S(1)} %pad_maximum_fusion.2), channel_id=1, source_target_pairs={{0,2},{2,0},{4,6},{6,4},{1,3},{3,1},{5,7},{7,5},{8,10},{10,8},{12,... | collective-permute-start | bytes 98312 | tf_op jit(solution)/shard_map/ppermute | solution.py:32
  59.5 6.1 %collective-permute-start.16 = (f32[16,640]{1,0:T(8,128)S(1)}, f32[16,640]{1,0:T(8,128)S(1)}, u32[]{:S(2)}, u32[]{:S(2)}) collective-permute-start(f32[16,640]{1,0:T(8,128)S(1)} %get-tuple-element.58.p0_ref), channel_id=1, source_target_pairs={{0,24},{8,16},{16,8},{24,0},{1,25},{9,17},{17,9},{25,1},{2,26},{10... | collective-permute-start | bytes 122888 | tf_op jit(solution)/shard_map/ppermute | solution.py:32
  61.6 5.3 %collective-permute-start.17 = (f32[16,640]{1,0:T(8,128)S(1)}, f32[16,640]{1,0:T(8,128)S(1)}, u32[]{:S(2)}, u32[]{:S(2)}) collective-permute-start(f32[16,640]{1,0:T(8,128)S(1)} %get-tuple-element.58.p0_ref), channel_id=1, source_target_pairs={{0,16},{8,24},{16,0},{24,8},{1,17},{9,25},{17,1},{25,9},{2,18},{10... | collective-permute-start | bytes 122888 | tf_op jit(solution)/shard_map/ppermute | solution.py:32
  62.8 4.1 %collective-permute-start.18 = (f32[16,640]{1,0:T(8,128)S(1)}, f32[16,640]{1,0:T(8,128)S(1)}, u32[]{:S(2)}, u32[]{:S(2)}) collective-permute-start(f32[16,640]{1,0:T(8,128)S(1)} %get-tuple-element.58.p0_ref), channel_id=1, source_target_pairs={{0,8},{8,0},{16,24},{24,16},{1,9},{9,1},{17,25},{25,17},{2,10},{10... | collective-permute-start | bytes 122888 | tf_op jit(solution)/shard_map/ppermute | solution.py:32
  67.5 1.2 %collective-permute-start.19 = (f32[8,128]{1,0:T(8,128)S(1)}, f32[8,128]{1,0:T(8,128)S(1)}, u32[]{:S(2)}, u32[]{:S(2)}) collective-permute-start(f32[8,128]{1,0:T(8,128)S(1)} %get-tuple-element.61), channel_id=1, source_target_pairs={{0,2},{2,0},{4,6},{6,4},{1,3},{3,1},{5,7},{7,5},{8,10},{10,8},{12,... | collective-permute-start | bytes 12296 | tf_op jit(solution)/shard_map/ppermute | solution.py:91
  68.6 3.6 %collective-permute-start.20 = (f32[8,128]{1,0:T(8,128)S(1)}, f32[8,128]{1,0:T(8,128)S(1)}, u32[]{:S(2)}, u32[]{:S(2)}) collective-permute-start(f32[8,128]{1,0:T(8,128)S(1)} %add.114), channel_id=1, source_target_pairs={{0,4},{2,6},{4,0},{6,2},{1,5},{3,7},{5,1},{7,3},{8,12},{10,14},{12... | collective-permute-start | bytes 12296 | tf_op jit(solution)/shard_map/ppermute | solution.py:91
